TPU v7x, 32 devices: a whole 2x2x4 slice. The times are simulated.
32 devices in a mesh: lat: 8 (over y, x, core), lon: 4 (over z).
Axes of the slice: x: 2, y: 2, z: 4, core: 2. Of those that a mesh axis runs over, the one named last changes fastest.
Arguments:
- fields: bfloat16 [256, 128, 256], P('lat', 'lon'), may hold values from -6 to 6
- w_conv1: bfloat16 [3, 3, 256, 256], replicated, may hold values from -0.125 to 0.125
- b_conv1: float32 [256], replicated, may hold values from -3 to 3
- w_conv2: bfloat16 [3, 3, 256, 256], replicated, may hold values from -0.125 to 0.125
- b_conv2: float32 [256], replicated, may hold values from -3 to 3
- w_query: bfloat16 [256, 256], replicated, may hold values from -16 to 16
- w_key: bfloat16 [256, 64], replicated, may hold values from -1 to 1
- w_value: bfloat16 [256, 64], replicated, may hold values from -0.375 to 0.375
- w_out: bfloat16 [256, 256], replicated, may hold values from -0.375 to 0.375
- rotation: int32 [8, 4], replicated, may hold values from 0 to 3
- owner: int32 [8, 4], replicated, may hold values from 0 to 3, as said below
- counts: int32 [256], replicated, may hold values from 4 to 128
Outputs:
- fields_out: bfloat16 [256, 128, 256], P('lat', 'lon')
Inputs may be any that keep to these rules, and one draw needn't show every extreme that they name: Each row of owner holds every number from 0 to 3 exactly once.
All inputs are finite; a program needn't handle non-finite values.
Results may differ from a plain program's by a relative error of at most 0.014.
Values may be sent and summed in bfloat16 or wider, within the bound.
No kernel may reach another device: no remote copies, remote signals or barrier semaphores. Data moves between devices by JAX's collectives and lax.ppermute only.
A program may use at most 64 MiB of HBM per device.

v0:
```python
import functools
import math

import jax
import jax.numpy as jnp
from jax import lax
from jax.experimental import pallas as pl
from jax.experimental.pallas import tpu as pltpu
from jax.sharding import PartitionSpec as P

HALO = 2
LANES = 128
GROUP = 256
VMEM_BYTES = 28 * 1024 * 1024


def group_of(band, shard, n):
    outer = jnp.where((shard == n - 2) == (band % 2 == 0), 0, n - 1)
    return jnp.where(shard < n - 2, shard + 1, outer)


def shard_of(band, group, n):
    if 0 < group < n - 1:
        return group - 1
    return n - 2 if (group == 0) == (band % 2 == 0) else n - 1


def first_held(group, rows):
    return group * rows - HALO * (group % 2)


def turn(quarter, staged, block, out, ready, done):
    size, _, chans = block.shape
    tiles = staged.shape[0]
    depth = GROUP // size
    pieces = size // depth

    def column(col):
        parts = [staged[t, pl.ds(col, size, stride=size), :] for t in range(tiles)]
        return jnp.concatenate(parts, axis=1).astype(jnp.bfloat16)

    def keep(i, row):
        for t in range(tiles):
            staged[t, pl.ds(i * size, size), :] = row[:, t * LANES : (t + 1) * LANES]

    @pl.when(quarter == 0)
    def _():
        for g in range(pieces):
            ready(g)
            out[g * depth : (g + 1) * depth] = block[g * depth : (g + 1) * depth]
            done(g)

    @pl.when(quarter == 1)
    def _():
        for i in range(size):
            if i % depth == 0:
                ready(i // depth)
            keep(i, block[i].astype(jnp.float32))
        for i in range(size):
            out[i] = column(size - 1 - i)
            if i % depth == depth - 1:
                done(i // depth)

    @pl.when(quarter == 2)
    def _():
        i = lax.broadcasted_iota(jnp.int32, (GROUP, GROUP), 0)
        j = lax.broadcasted_iota(jnp.int32, (GROUP, GROUP), 1)
        backwards = jnp.where(i + j == GROUP - 1, 1.0, 0.0).astype(jnp.bfloat16)
        for g in reversed(range(pieces)):
            ready(pieces - 1 - g)
            cells = block[size - (g + 1) * depth : size - g * depth].reshape(GROUP, chans)
            turned = jnp.dot(backwards, cells, preferred_element_type=jnp.float32).astype(jnp.bfloat16)
            out[g * depth : (g + 1) * depth] = turned.reshape(depth, size, chans)
            done(g)

    @pl.when(quarter == 3)
    def _():
        for i in range(size):
            if i % depth == 0:
                ready(i // depth)
            keep(size - 1 - i, block[i].astype(jnp.float32))
        for i in range(size):
            out[i] = column(i)
            if i % depth == depth - 1:
                done(i // depth)


def send_kernel(n, rows, rotation_in, fields, *rest):
    edges, slabs = rest[:n], rest[n : 2 * n]
    staged, block, upright, rotation, scalar_sem, sems = rest[2 * n :]
    band = lax.axis_index("lat")
    me = lax.axis_index("lon")
    depth = GROUP // fields.shape[0]

    def piece(g):
        at = pl.ds(g * depth, depth)
        return pltpu.make_async_copy(fields.at[at], block.at[at], sems.at[g])

    scalars = pltpu.make_async_copy(rotation_in, rotation, scalar_sem)
    scalars.start()
    for g in range(fields.shape[0] // depth):
        piece(g).start()
    scalars.wait()
    turn((4 - rotation[me, band]) % 4, staged, block, upright, lambda g: piece(g).wait(), lambda g: None)
    for d in range(n):
        group = group_of(band, lax.rem(me + d, n), n)
        top, odd = first_held(group, rows), group % 2
        edges[d][...] = upright[pl.ds(top + rows * odd, HALO)]
        slabs[d][...] = upright[pl.ds(top + HALO * (1 - odd), rows)]


def load_kernel(n, rows, after, *refs):
    del after
    count = (len(refs) - 9) // 2
    direct, (query, key, value) = refs[:count], refs[count : count + 3]
    loaded, (w_key, w_qv) = refs[count + 3 : 2 * count + 3], refs[2 * count + 3 : 2 * count + 5]
    query_in, key_in, value_in, sems = refs[2 * count + 5 :]
    chans = query.shape[0]
    pairs = list(zip(direct, loaded)) + [(query, query_in), (key, key_in), (value, value_in)]
    copies = [pltpu.make_async_copy(*pair, sems.at[i]) for i, pair in enumerate(pairs)]
    for copy in copies:
        copy.start()
    for copy in copies:
        copy.wait()
    w_key[...] = key_in[...].T
    w_qv[:chans] = query_in[...].T
    w_qv[chans:] = value_in[...]


def columns_of(segment, size):
    return pl.ds(pl.multiple_of(segment * size, size), size)


def whole_rows(n, owner, slabs, out, first):
    band = lax.axis_index("lat")
    me = lax.axis_index("lon")
    count, size = slabs[0].shape[:2]
    for d in range(n):
        segment = owner[lax.rem(me + n - d, n), band]
        out[pl.ds(first, count), columns_of(segment, size)] = slabs[d][...]


def edge_kernel(n, rows, owner, *rest):
    del rows
    whole_rows(n, owner, rest[:n], rest[n], 0)


def spread(taps, r, row):
    cols, chans = row.shape
    taps[r, :, :chans] = pltpu.roll(row, 1, 0).astype(jnp.bfloat16)
    taps[r, :, chans : 2 * chans] = row.astype(jnp.bfloat16)
    taps[r, :, 2 * chans :] = pltpu.roll(row, cols - 1, 0).astype(jnp.bfloat16)


def convolve(taps, weight, bias, count):
    cols, width = taps.shape[1:]
    total = bias[...]
    for i in range(3):
        window = taps[i : i + count].reshape(count * cols, width)
        total = total + jnp.dot(window, weight[i], preferred_element_type=jnp.float32)
    return total


def silu(x):
    return x / (1.0 + jnp.exp(-x))


def live_count(counts, row):
    inside = (row >= 0) & (row < counts.shape[0])
    return jnp.where(inside, counts[jnp.clip(row, 0, counts.shape[0] - 1)], 0)


def finish(n, count, first_row, grid_row, second, counts, owner, w_key, w_qv, w_out, results, *scratch):
    mixed, attended, scores, expo = scratch
    band = lax.axis_index("lat")
    me = lax.axis_index("lon")
    chans = mixed.shape[1]
    cols = mixed.shape[0] // count
    head_dim = w_key.shape[1]
    heads = chans // head_dim
    scale = math.log2(math.e) / head_dim**0.5
    cell = lax.broadcasted_iota(jnp.int32, (cols, chans), 0)
    spans = [slice(r * cols, (r + 1) * cols) for r in range(count)]
    lanes = [slice(h * cols, (h + 1) * cols) for h in range(heads)]
    limits = [counts[first_row + r] for r in range(count)]
    for r, at in enumerate(spans):
        part = jnp.where(cell < limits[r], grid_row(r).astype(jnp.float32) + second[at], 0.0)
        mixed[at, :] = part.astype(jnp.bfloat16)
    flat = mixed[...].astype(jnp.float32)
    normed = (flat * lax.rsqrt(jnp.mean(flat * flat, axis=1, keepdims=True) + 1e-06)).astype(jnp.bfloat16)

    keys = jnp.dot(normed, w_key[...], preferred_element_type=jnp.float32).astype(jnp.bfloat16)
    flipped = jnp.dot(w_qv[...], normed.T, preferred_element_type=jnp.float32).astype(jnp.bfloat16)
    for r, at in enumerate(spans):
        queries = jnp.concatenate([flipped[h * head_dim : (h + 1) * head_dim, at] for h in range(heads)], axis=1)
        scores[r] = jnp.dot(keys[at], queries, preferred_element_type=jnp.float32)
    key_at = lax.broadcasted_iota(jnp.int32, (cols, cols), 0)
    shares = []
    for r in range(count):
        live = key_at < limits[r]
        for h in range(heads):
            part = jnp.where(live, scores[r, :, lanes[h]], -jnp.inf)
            part = jnp.exp2((part - jnp.max(part, axis=0, keepdims=True)) * scale)
            shares.append(1.0 / jnp.sum(part, axis=0, keepdims=True))
            expo[r, :, lanes[h]] = part.astype(jnp.bfloat16)
    for r, at in enumerate(spans):
        summed = jnp.dot(flipped[chans:, at], expo[r], preferred_element_type=jnp.float32)
        for h in range(heads):
            part = summed[:, lanes[h]] * shares[r * heads + h]
            attended[h * head_dim : (h + 1) * head_dim, at] = part.astype(jnp.bfloat16)
    update = lax.dot_general(attended[...], w_out[...], (((0,), (0,)), ((), ())), preferred_element_type=jnp.float32)
    for r, at in enumerate(spans):
        mixed[at, :] = (flat[at] + jnp.where(cell < limits[r], update[at], 0.0)).astype(jnp.bfloat16)
    for d in range(n):
        segment = owner[lax.rem(me + d, n), band]
        for r in range(count):
            results[d][r] = mixed[columns_of(segment + r * n, cols // n), :]


def main_kernel(n, rows, owner, counts, *rest):
    slabs, sent, received = rest[:n], rest[n], rest[n + 1]
    w_conv1, b_conv1, w_conv2, b_conv2 = rest[n + 2 : n + 6]
    weights = rest[n + 6 : n + 9]
    inner = rows - HALO
    last_grid, last_acts, *rest = rest[n + 9 :]
    results = rest[: n if inner else 0]
    grid, taps, acts, *scratch = rest[len(results) :]
    band = lax.axis_index("lat")
    group = group_of(band, lax.axis_index("lon"), n)
    odd = group % 2
    cols, chans = sent.shape[1:]
    cell = lax.broadcasted_iota(jnp.int32, (cols, chans), 0)
    first_row = band * (rows * n) + group * rows
    whole_rows(n, owner, slabs, grid, 2 * HALO * (1 - odd))
    grid[pl.ds(HALO + (rows - HALO) * odd, HALO)] = sent[...]
    grid[pl.ds((rows + HALO) * odd, HALO)] = received[...]
    for r in range(rows + 2 * HALO):
        spread(taps, r, grid[r].astype(jnp.float32))
    act = silu(convolve(taps, w_conv1, b_conv1, rows + HALO))
    for r in range(rows + HALO):
        live = cell < live_count(counts, first_row - 1 + r)
        spread(acts, r, jnp.where(live, act[r * cols : (r + 1) * cols], 0.0))
    last_grid[...] = grid[rows : rows + HALO]
    last_acts[...] = acts[inner:]
    if inner:
        second = convolve(acts, w_conv2, b_conv2, inner)
        finish(n, inner, first_row, lambda r: grid[r + HALO], second, counts, owner, *weights, results, *scratch)


def last_kernel(n, rows, owner, counts, *rest):
    grid, acts, w_conv2, b_conv2 = rest[:4]
    weights, results, scratch = rest[4:7], rest[7 : 7 + n], rest[7 + n :]
    band = lax.axis_index("lat")
    group = group_of(band, lax.axis_index("lon"), n)
    first_row = band * (rows * n) + group * rows + rows - HALO
    second = convolve(acts, w_conv2, b_conv2, HALO)
    finish(n, HALO, first_row, lambda r: grid[r], second, counts, owner, *weights, results, *scratch)


def store_kernel(n, rows, rotation, *rest):
    inner = rows - HALO
    slabs = rest[: n if inner else 0]
    lasts = rest[len(slabs) : len(slabs) + n]
    out, staged, upright, turned, sems = rest[len(slabs) + n :]
    band = lax.axis_index("lat")
    me = lax.axis_index("lon")
    depth = GROUP // out.shape[0]
    pieces = out.shape[0] // depth
    for d in range(n):
        group = group_of(band, lax.rem(me + n - d, n), n)
        if inner:
            upright[pl.ds(group * rows, inner)] = slabs[d][...]
        upright[pl.ds(group * rows + inner, HALO)] = lasts[d][...]

    def piece(g):
        at = pl.ds(g * depth, depth)
        return pltpu.make_async_copy(turned.at[at], out.at[at], sems.at[g])

    turn(rotation[me, band] % 4, staged, upright, turned, lambda g: None, lambda g: piece(g).start())
    for g in range(pieces):
        piece(g).wait()


def on_device(
    bands,
    n,
    fields,
    w_conv1,
    b_conv1,
    w_conv2,
    b_conv2,
    w_query,
    w_key,
    w_value,
    w_out,
    rotation,
    owner,
    counts,
):
    size, _, chans = fields.shape
    rows = size // n
    inner = rows - HALO
    cols = size * n
    bf16 = jnp.bfloat16
    smem = pl.BlockSpec(memory_space=pltpu.SMEM)
    vmem = pl.BlockSpec(memory_space=pltpu.VMEM)
    hbm = pl.BlockSpec(memory_space=pltpu.HBM)
    params = pltpu.CompilerParams(vmem_limit_bytes=VMEM_BYTES)
    pieces = size * size // GROUP

    def call(kernel, name, out, scalars, arrays, scratch, array_spec=vmem, scalar_spec=smem, out_spec=vmem):
        many = isinstance(out, list)
        return pl.pallas_call(
            functools.partial(kernel, n, rows),
            out_shape=out,
            in_specs=[scalar_spec] * len(scalars) + [array_spec] * len(arrays),
            out_specs=[out_spec] * len(out) if many else out_spec,
            scratch_shapes=scratch,
            compiler_params=params,
            name=name,
        )(*scalars, *arrays)

    def array(*shape):
        return jax.ShapeDtypeStruct(shape, bf16)

    def around(parts):
        order = sorted(range(1, n), key=lambda d: -min(d, n - d))
        moved = {d: lax.ppermute(parts[d], "lon", [(i, (i + d) % n) for i in range(n)]) for d in order}
        return [parts[0]] + [moved[d] for d in range(1, n)]

    def in_hbm(x):
        return pltpu.with_memory_space_constraint(x, pltpu.HBM)

    loaded = [rotation.T, owner.T, counts]
    loaded += [w_conv1.reshape(3, 3 * chans, chans), b_conv1.reshape(1, chans)]
    loaded += [w_conv2.reshape(3, 3 * chans, chans), b_conv2.reshape(1, chans), w_out]
    loaded = [in_hbm(x) for x in loaded]
    turned = [in_hbm(x) for x in (w_query, w_key.T, w_value.T)]
    staging = pltpu.VMEM((chans // LANES, size * size, LANES), jnp.float32)
    block = pltpu.VMEM((size, size, chans), bf16)

    slabs = [array(HALO, size, chans)] * n + [array(rows, size, chans)] * n
    scratch = [staging, block, block, pltpu.SMEM(rotation.T.shape, rotation.dtype)]
    scratch += [pltpu.SemaphoreType.DMA, pltpu.SemaphoreType.DMA((pieces,))]
    slabs = call(send_kernel, "send", slabs, loaded[:1], [in_hbm(fields)], scratch, hbm, hbm)
    held = [pltpu.VMEM(x.shape, x.dtype) for x in loaded]
    held += [pltpu.VMEM(w_key.shape, bf16), pltpu.VMEM((chans + w_key.shape[1], chans), bf16)]
    scratch = [pltpu.VMEM(x.shape, bf16) for x in turned] + [pltpu.SemaphoreType.DMA((len(loaded) + 3,))]
    loaded = call(load_kernel, "load", held, slabs[:1], loaded + turned, scratch, hbm, hbm)
    rotation, owner, counts, *convs, w_out, w_key, w_qv = loaded
    weights = [*convs, w_key, w_qv, w_out]
    edges = around(slabs[:n])
    slabs = around(slabs[n:])

    snake = [a * n + shard_of(a, g, n) for a in range(bands) for g in range(n)]
    pairs = [(snake[i], snake[i + 1 if i % 2 else i - 1]) for i in range(1, bands * n - 1)]
    sent = call(edge_kernel, "edge", array(HALO, cols, chans), [owner], edges, [])
    received = lax.ppermute(sent, ("lat", "lon"), pairs)

    def taps(count):
        return pltpu.VMEM((count, cols, 3 * chans), bf16)

    def working(count):
        count, heads = max(count, 1), chans // w_key.shape[1]
        return [
            pltpu.VMEM((count * cols, chans), bf16),
            pltpu.VMEM((chans, count * cols), bf16),
            pltpu.VMEM((count, cols, heads * cols), jnp.float32),
            pltpu.VMEM((count, cols, heads * cols), bf16),
        ]

    held = [array(HALO, cols, chans), array(2 * HALO, cols, 3 * chans)]
    last_grid, last_acts, *results = call(
        main_kernel,
        "main",
        held + [array(inner, size, chans)] * (n if inner else 0),
        [owner, counts],
        slabs + [sent, received] + weights,
        [pltpu.VMEM((rows + 2 * HALO, cols, chans), bf16), taps(rows + 2 * HALO), taps(rows + HALO)] + working(inner),
    )
    results = around(results) if inner else []
    lasts = call(
        last_kernel,
        "last",
        [array(HALO, size, chans)] * n,
        [owner, counts],
        [last_grid, last_acts] + weights[2:],
        working(HALO),
    )
    lasts = around(lasts)
    scratch = [staging, block, block, pltpu.SemaphoreType.DMA((pieces,))]
    return call(store_kernel, "store", array(*fields.shape), [rotation], results + lasts, scratch, out_spec=hbm)


def solution(mesh):
    in_specs = (P("lat", "lon", None), P(), P(), P(), P(), P(), P(), P(), P(), P(), P(), P())
    out_specs = P("lat", "lon", None)
    body = functools.partial(on_device, mesh.shape["lat"], mesh.shape["lon"])
    return jax.shard_map(body, mesh=mesh, in_specs=in_specs, out_specs=out_specs, check_vma=False)
```

profile of v0, /device:TPU:0, one launch (start us, length us, event | category | flops | bytes accessed | tf_op | source)
XLA Modules:
  0.0 48.5 jit_solution(6180290306843192711)
XLA Ops:
  0.0 1.8 %send.1 = (bf16[2,32,256]{2,1,0:T(8,128)(2,1)S(1)}, bf16[2,32,256]{2,1,0:T(8,128)(2,1)S(1)}, bf16[2,32,256]{2,1,0:T(8,128)(2,1)S(1)}, bf16[2,32,256]{2,1,0:T(8,1...) custom-call(s32[4,8]{1,0:T(4,128)} %bitcast.12, ...), custom_call_target="tpu_custom_call" | custom-call | tf_op jit(solution)/shard_map/send/pallas_call | solution.py:313
  1.8 3.1 %collective-permute-start.3 = (bf16[2,32,256]{2,1,0:T(8,128)(2,1)S(1)}, bf16[2,32,256]{2,1,0:T(8,128)(2,1)S(1)}, u32[]{:S(2)}, u32[]{:S(2)}) collective-permute-start(bf16[2,32,256]{2,1,0:T(8,128)(2,1)S(1)} %get-tuple-element.41), channel_id=1, source_target_pairs={{0,1},{1,2},{2,3},{3,0},{4,5},{5,6},{6,7},{7,4},{8,9},{9,10},{10,1... | collective-permute-start | bytes 98312 | tf_op jit(solution)/shard_map/ppermute | solution.py:328
  4.9 2.6 %collective-permute-start.4 = (bf16[2,32,256]{2,1,0:T(8,128)(2,1)S(1)}, bf16[2,32,256]{2,1,0:T(8,128)(2,1)S(1)}, u32[]{:S(2)}, u32[]{:S(2)}) collective-permute-start(bf16[2,32,256]{2,1,0:T(8,128)(2,1)S(1)} %get-tuple-element.42), channel_id=1, source_target_pairs={{0,2},{1,3},{2,0},{3,1},{4,6},{5,7},{6,4},{7,5},{8,10},{9,11},{10,... | collective-permute-start | bytes 98312 | tf_op jit(solution)/shard_map/ppermute | solution.py:328
  7.5 1.3 %collective-permute-start.5 = (bf16[2,32,256]{2,1,0:T(8,128)(2,1)S(1)}, bf16[2,32,256]{2,1,0:T(8,128)(2,1)S(1)}, u32[]{:S(2)}, u32[]{:S(2)}) collective-permute-start(bf16[2,32,256]{2,1,0:T(8,128)(2,1)S(1)} %get-tuple-element.43), channel_id=1, source_target_pairs={{0,3},{1,0},{2,1},{3,2},{4,7},{5,4},{6,5},{7,6},{8,11},{9,8},{10,9... | collective-permute-start | bytes 98312 | tf_op jit(solution)/shard_map/ppermute | solution.py:328
  8.8 0.7 %collective-permute-start = (bf16[8,32,256]{2,1,0:T(8,128)(2,1)S(1)}, bf16[8,32,256]{2,1,0:T(8,128)(2,1)S(1)}, u32[]{:S(2)}, u32[]{:S(2)}) collective-permute-start(bf16[8,32,256]{2,1,0:T(8,128)(2,1)S(1)} %get-tuple-element.38), channel_id=1, source_target_pairs={{0,1},{1,2},{2,3},{3,0},{4,5},{5,6},{6,7},{7,4},{8,9},{9,10},{10,1... | collective-permute-start | bytes 393224 | tf_op jit(solution)/shard_map/ppermute | solution.py:328
  9.5 0.3 collective-permute-start.1
  9.9 1.9 %load.1 = (s32[4,8]{1,0:T(4,128)S(1)}, s32[4,8]{1,0:T(4,128)S(1)}, s32[256]{0:T(256)S(1)}, bf16[3,768,256]{2,1,0:T(8,128)(2,1)S(1)}, f32[1,256]{1,0:T(1,128)S(1)...) custom-call(bf16[2,32,256]{2,1,0:T(8,128)(2,1)S(1)} %get-tuple-eleme, ...), custom_call_target="tpu_custom_call" | custom-call | tf_op jit(solution)/shard_map/load/pallas_call | solution.py:313
  11.8 2.9 %collective-permute-start.2 = (bf16[8,32,256]{2,1,0:T(8,128)(2,1)S(1)}, bf16[8,32,256]{2,1,0:T(8,128)(2,1)S(1)}, u32[]{:S(2)}, u32[]{:S(2)}) collective-permute-start(bf16[8,32,256]{2,1,0:T(8,128)(2,1)S(1)} %get-tuple-element.40), channel_id=1, source_target_pairs={{0,3},{1,0},{2,1},{3,2},{4,7},{5,4},{6,5},{7,6},{8,11},{9,8},{10,9... | collective-permute-start | bytes 393224 | tf_op jit(solution)/shard_map/ppermute | solution.py:328
  14.7 0.6 %edge.1.rest_4_ = bf16[2,128,256]{2,1,0:T(8,128)(2,1)S(1)} custom-call(s32[4,8]{1,0:T(4,128)S(1)} %get-tuple-element.35.owner, bf16[2,32,256]{2,1,0:T(8,128)(2,1)S(1)} %get-tuple-element.33.after.rest_0_, bf16[2,32,256]{2,1,0:T(8,128)(2,1)S(1)} %collective-permute-done.3.rest_1_, bf16[2,32,256]{2,1,0:T(8,128)(2,1)S(1)} %collective-permute-done.4.rest_2_, ...), custom_call_target="tpu_custom_call" | custom-call | tf_op jit(solution)/shard_map/edge/pallas_call | solution.py:313
  15.3 2.5 %collective-permute-start.6 = (bf16[2,128,256]{2,1,0:T(8,128)(2,1)S(1)}, bf16[2,128,256]{2,1,0:T(8,128)(2,1)S(1)}, u32[]{:S(2)}, u32[]{:S(2)}) collective-permute-start(bf16[2,128,256]{2,1,0:T(8,128)(2,1)S(1)} %edge.1.rest_4_), channel_id=1, source_target_pairs={{0,1},{1,0},{3,7},{7,3},{4,5},{5,4},{6,10},{10,6},{8,9},{9,8},{11,... | collective-permute-start | bytes 393224 | tf_op jit(solution)/shard_map/ppermute | solution.py:358
  17.8 3.1 %collective-permute-done.1.rest_2_ = bf16[8,32,256]{2,1,0:T(8,128)(2,1)S(1)} collective-permute-done((bf16[8,32,256]{2,1,0:T(8,128)(2,1)S(1)}, bf16[8,32,256]{2,1,0:T(8,128)(2,1)S(1)}, u32[]{:S(2)}, u32[]{:S(2)}) %collective-permute-start.1) | collective-permute-done | bytes 131104 | tf_op jit(solution)/shard_map/ppermute | solution.py:328
  20.9 0.5 collective-permute-done.2.rest_3_
  21.3 1.9 %collective-permute-done.6.rest_5_ = bf16[2,128,256]{2,1,0:T(8,128)(2,1)S(1)} collective-permute-done((bf16[2,128,256]{2,1,0:T(8,128)(2,1)S(1)}, bf16[2,128,256]{2,1,0:T(8,128)(2,1)S(1)}, u32[]{:S(2)}, u32[]{:S(2)}) %collective-permute-start.6) | collective-permute-done | bytes 131104 | tf_op jit(solution)/shard_map/ppermute | solution.py:358
  23.3 7.3 %main.1 = (bf16[2,128,256]{2,1,0:T(8,128)(2,1)S(1)}, bf16[4,128,768]{2,1,0:T(8,128)(2,1)S(1)}, bf16[6,32,256]{2,1,0:T(8,128)(2,1)S(1)}, bf16[6,32,256]{2,1,0:T(8...) custom-call(s32[4,8]{1,0:T(4,128)S(1)} %get-tuple-element.35.owner, ...), custom_call_target="tpu_custom_call" | custom-call | tf_op jit(solution)/shard_map/main/pallas_call | solution.py:313
  30.7 1.1 %collective-permute-start.8 = (bf16[6,32,256]{2,1,0:T(8,128)(2,1)S(1)}, bf16[6,32,256]{2,1,0:T(8,128)(2,1)S(1)}, u32[]{:S(2)}, u32[]{:S(2)}) collective-permute-start(bf16[6,32,256]{2,1,0:T(8,128)(2,1)S(1)} %get-tuple-element.53), channel_id=1, source_target_pairs={{0,2},{1,3},{2,0},{3,1},{4,6},{5,7},{6,4},{7,5},{8,10},{9,11},{10,... | collective-permute-start | bytes 294920 | tf_op jit(solution)/shard_map/ppermute | solution.py:328
  31.8 2.7 %collective-permute-start.9 = (bf16[6,32,256]{2,1,0:T(8,128)(2,1)S(1)}, bf16[6,32,256]{2,1,0:T(8,128)(2,1)S(1)}, u32[]{:S(2)}, u32[]{:S(2)}) collective-permute-start(bf16[6,32,256]{2,1,0:T(8,128)(2,1)S(1)} %get-tuple-element.54), channel_id=1, source_target_pairs={{0,3},{1,0},{2,1},{3,2},{4,7},{5,4},{6,5},{7,6},{8,11},{9,8},{10,9... | collective-permute-start | bytes 294920 | tf_op jit(solution)/shard_map/ppermute | solution.py:328
  34.5 2.2 %last.1 = (bf16[2,32,256]{2,1,0:T(8,128)(2,1)S(1)}, bf16[2,32,256]{2,1,0:T(8,128)(2,1)S(1)}, bf16[2,32,256]{2,1,0:T(8,128)(2,1)S(1)}, bf16[2,32,256]{2,1,0:T(8,128)(2,1)S(1)}) custom-call(s32[4,8]{1,0:T(4,128)S(1)} %get-tuple-element.35.owner, s32[256]{0:T(256)S(1)} %get-tuple-element.36.counts, bf16[2,128,256]{2,1,0:T(8,128)(2,1)S(1)} %get-tuple-element.55.rest_0_, ...), custom_call_target="tpu_custom_call" | custom-call | tf_op jit(solution)/shard_map/last/pallas_call | solution.py:313
  36.7 0.6 %collective-permute-start.10 = (bf16[2,32,256]{2,1,0:T(8,128)(2,1)S(1)}, bf16[2,32,256]{2,1,0:T(8,128)(2,1)S(1)}, u32[]{:S(2)}, u32[]{:S(2)}) collective-permute-start(bf16[2,32,256]{2,1,0:T(8,128)(2,1)S(1)} %get-tuple-element.58), channel_id=1, source_target_pairs={{0,1},{1,2},{2,3},{3,0},{4,5},{5,6},{6,7},{7,4},{8,9},{9,10},{10,1... | collective-permute-start | bytes 98312 | tf_op jit(solution)/shard_map/ppermute | solution.py:328
  37.3 1.5 %collective-permute-start.11 = (bf16[2,32,256]{2,1,0:T(8,128)(2,1)S(1)}, bf16[2,32,256]{2,1,0:T(8,128)(2,1)S(1)}, u32[]{:S(2)}, u32[]{:S(2)}) collective-permute-start(bf16[2,32,256]{2,1,0:T(8,128)(2,1)S(1)} %get-tuple-element.59), channel_id=1, source_target_pairs={{0,2},{1,3},{2,0},{3,1},{4,6},{5,7},{6,4},{7,5},{8,10},{9,11},{10,... | collective-permute-start | bytes 98312 | tf_op jit(solution)/shard_map/ppermute | solution.py:328
  38.8 3.7 %collective-permute-done.10.rest_5_ = bf16[2,32,256]{2,1,0:T(8,128)(2,1)S(1)} collective-permute-done((bf16[2,32,256]{2,1,0:T(8,128)(2,1)S(1)}, bf16[2,32,256]{2,1,0:T(8,128)(2,1)S(1)}, u32[]{:S(2)}, u32[]{:S(2)}) %collective-permute-start.10) | collective-permute-done | bytes 32800 | tf_op jit(solution)/shard_map/ppermute | solution.py:328
  42.5 0.8 %collective-permute-start.12 = (bf16[2,32,256]{2,1,0:T(8,128)(2,1)S(1)}, bf16[2,32,256]{2,1,0:T(8,128)(2,1)S(1)}, u32[]{:S(2)}, u32[]{:S(2)}) collective-permute-start(bf16[2,32,256]{2,1,0:T(8,128)(2,1)S(1)} %get-tuple-element.60), channel_id=1, source_target_pairs={{0,3},{1,0},{2,1},{3,2},{4,7},{5,4},{6,5},{7,6},{8,11},{9,8},{10,9... | collective-permute-start | bytes 98312 | tf_op jit(solution)/shard_map/ppermute | solution.py:328
  43.4 0.7 %collective-permute-done.11.rest_6_ = bf16[2,32,256]{2,1,0:T(8,128)(2,1)S(1)} collective-permute-done((bf16[2,32,256]{2,1,0:T(8,128)(2,1)S(1)}, bf16[2,32,256]{2,1,0:T(8,128)(2,1)S(1)}, u32[]{:S(2)}, u32[]{:S(2)}) %collective-permute-start.11) | collective-permute-done | bytes 32800 | tf_op jit(solution)/shard_map/ppermute | solution.py:328
  44.0 2.4 %collective-permute-done.12.rest_7_ = bf16[2,32,256]{2,1,0:T(8,128)(2,1)S(1)} collective-permute-done((bf16[2,32,256]{2,1,0:T(8,128)(2,1)S(1)}, bf16[2,32,256]{2,1,0:T(8,128)(2,1)S(1)}, u32[]{:S(2)}, u32[]{:S(2)}) %collective-permute-start.12) | collective-permute-done | bytes 32800 | tf_op jit(solution)/shard_map/ppermute | solution.py:328
  46.5 2.0 %store.1 = bf16[32,32,256]{2,1,0:T(8,128)(2,1)} custom-call(s32[4,8]{1,0:T(4,128)S(1)} %get-tuple-element.34.rotation, bf16[6,32,256]{2,1,0:T(8,128)(2,1)S(1)} %get-tuple-element.51.rest_0_, bf16[6,32,256]{2,1,0:T(8,128)(2,1)S(1)} %collective-permute-done.7.rest_1_, bf16[6,32,256]{2,1,0:T(8,128)(2,1)S(1)} %collective-permute-done.8.rest_2_, ...), custom_call_target="tpu_custom_call" | custom-call | tf_op jit(solution)/shard_map/store/pallas_call | solution.py:313
  (8 shorter events, 0.1 us)
Async XLA Ops:
  1.8 10.0 %collective-permute-start.3 = (bf16[2,32,256]{2,1,0:T(8,128)(2,1)S(1)}, bf16[2,32,256]{2,1,0:T(8,128)(2,1)S(1)}, u32[]{:S(2)}, u32[]{:S(2)}) collective-permute-start(bf16[2,32,256]{2,1,0:T(8,128)(2,1)S(1)} %get-tuple-element.41), channel_id=1, source_target_pairs={{0,1},{1,2},{2,3},{3,0},{4,5},{5,6},{6,7},{7,4},{8,9},{9,10},{10,1... | collective-permute-start | bytes 98312 | tf_op jit(solution)/shard_map/ppermute | solution.py:328
  4.9 9.8 %collective-permute-start.4 = (bf16[2,32,256]{2,1,0:T(8,128)(2,1)S(1)}, bf16[2,32,256]{2,1,0:T(8,128)(2,1)S(1)}, u32[]{:S(2)}, u32[]{:S(2)}) collective-permute-start(bf16[2,32,256]{2,1,0:T(8,128)(2,1)S(1)} %get-tuple-element.42), channel_id=1, source_target_pairs={{0,2},{1,3},{2,0},{3,1},{4,6},{5,7},{6,4},{7,5},{8,10},{9,11},{10,... | collective-permute-start | bytes 98312 | tf_op jit(solution)/shard_map/ppermute | solution.py:328
  7.5 7.2 %collective-permute-start.5 = (bf16[2,32,256]{2,1,0:T(8,128)(2,1)S(1)}, bf16[2,32,256]{2,1,0:T(8,128)(2,1)S(1)}, u32[]{:S(2)}, u32[]{:S(2)}) collective-permute-start(bf16[2,32,256]{2,1,0:T(8,128)(2,1)S(1)} %get-tuple-element.43), channel_id=1, source_target_pairs={{0,3},{1,0},{2,1},{3,2},{4,7},{5,4},{6,5},{7,6},{8,11},{9,8},{10,9... | collective-permute-start | bytes 98312 | tf_op jit(solution)/shard_map/ppermute | solution.py:328
  8.8 9.0 %collective-permute-start = (bf16[8,32,256]{2,1,0:T(8,128)(2,1)S(1)}, bf16[8,32,256]{2,1,0:T(8,128)(2,1)S(1)}, u32[]{:S(2)}, u32[]{:S(2)}) collective-permute-start(bf16[8,32,256]{2,1,0:T(8,128)(2,1)S(1)} %get-tuple-element.38), channel_id=1, source_target_pairs={{0,1},{1,2},{2,3},{3,0},{4,5},{5,6},{6,7},{7,4},{8,9},{9,10},{10,1... | collective-permute-start | bytes 393224 | tf_op jit(solution)/shard_map/ppermute | solution.py:328
  9.5 11.4 %collective-permute-start.1 = (bf16[8,32,256]{2,1,0:T(8,128)(2,1)S(1)}, bf16[8,32,256]{2,1,0:T(8,128)(2,1)S(1)}, u32[]{:S(2)}, u32[]{:S(2)}) collective-permute-start(bf16[8,32,256]{2,1,0:T(8,128)(2,1)S(1)} %get-tuple-element.39), channel_id=1, source_target_pairs={{0,2},{1,3},{2,0},{3,1},{4,6},{5,7},{6,4},{7,5},{8,10},{9,11},{10,... | collective-permute-start | bytes 393224 | tf_op jit(solution)/shard_map/ppermute | solution.py:328
  11.8 9.5 %collective-permute-start.2 = (bf16[8,32,256]{2,1,0:T(8,128)(2,1)S(1)}, bf16[8,32,256]{2,1,0:T(8,128)(2,1)S(1)}, u32[]{:S(2)}, u32[]{:S(2)}) collective-permute-start(bf16[8,32,256]{2,1,0:T(8,128)(2,1)S(1)} %get-tuple-element.40), channel_id=1, source_target_pairs={{0,3},{1,0},{2,1},{3,2},{4,7},{5,4},{6,5},{7,6},{8,11},{9,8},{10,9... | collective-permute-start | bytes 393224 | tf_op jit(solution)/shard_map/ppermute | solution.py:328
  15.3 8.0 %collective-permute-start.6 = (bf16[2,128,256]{2,1,0:T(8,128)(2,1)S(1)}, bf16[2,128,256]{2,1,0:T(8,128)(2,1)S(1)}, u32[]{:S(2)}, u32[]{:S(2)}) collective-permute-start(bf16[2,128,256]{2,1,0:T(8,128)(2,1)S(1)} %edge.1.rest_4_), channel_id=1, source_target_pairs={{0,1},{1,0},{3,7},{7,3},{4,5},{5,4},{6,10},{10,6},{8,9},{9,8},{11,... | collective-permute-start | bytes 393224 | tf_op jit(solution)/shard_map/ppermute | solution.py:358
  30.6 15.9 %collective-permute-start.7 = (bf16[6,32,256]{2,1,0:T(8,128)(2,1)S(1)}, bf16[6,32,256]{2,1,0:T(8,128)(2,1)S(1)}, u32[]{:S(2)}, u32[]{:S(2)}) collective-permute-start(bf16[6,32,256]{2,1,0:T(8,128)(2,1)S(1)} %get-tuple-element.52), channel_id=1, source_target_pairs={{0,1},{1,2},{2,3},{3,0},{4,5},{5,6},{6,7},{7,4},{8,9},{9,10},{10,1... | collective-permute-start | bytes 294920 | tf_op jit(solution)/shard_map/ppermute | solution.py:328
  30.7 15.8 %collective-permute-start.8 = (bf16[6,32,256]{2,1,0:T(8,128)(2,1)S(1)}, bf16[6,32,256]{2,1,0:T(8,128)(2,1)S(1)}, u32[]{:S(2)}, u32[]{:S(2)}) collective-permute-start(bf16[6,32,256]{2,1,0:T(8,128)(2,1)S(1)} %get-tuple-element.53), channel_id=1, source_target_pairs={{0,2},{1,3},{2,0},{3,1},{4,6},{5,7},{6,4},{7,5},{8,10},{9,11},{10,... | collective-permute-start | bytes 294920 | tf_op jit(solution)/shard_map/ppermute | solution.py:328
  31.8 14.7 %collective-permute-start.9 = (bf16[6,32,256]{2,1,0:T(8,128)(2,1)S(1)}, bf16[6,32,256]{2,1,0:T(8,128)(2,1)S(1)}, u32[]{:S(2)}, u32[]{:S(2)}) collective-permute-start(bf16[6,32,256]{2,1,0:T(8,128)(2,1)S(1)} %get-tuple-element.54), channel_id=1, source_target_pairs={{0,3},{1,0},{2,1},{3,2},{4,7},{5,4},{6,5},{7,6},{8,11},{9,8},{10,9... | collective-permute-start | bytes 294920 | tf_op jit(solution)/shard_map/ppermute | solution.py:328
  36.7 5.9 %collective-permute-start.10 = (bf16[2,32,256]{2,1,0:T(8,128)(2,1)S(1)}, bf16[2,32,256]{2,1,0:T(8,128)(2,1)S(1)}, u32[]{:S(2)}, u32[]{:S(2)}) collective-permute-start(bf16[2,32,256]{2,1,0:T(8,128)(2,1)S(1)} %get-tuple-element.58), channel_id=1, source_target_pairs={{0,1},{1,2},{2,3},{3,0},{4,5},{5,6},{6,7},{7,4},{8,9},{9,10},{10,1... | collective-permute-start | bytes 98312 | tf_op jit(solution)/shard_map/ppermute | solution.py:328
  37.3 6.7 %collective-permute-start.11 = (bf16[2,32,256]{2,1,0:T(8,128)(2,1)S(1)}, bf16[2,32,256]{2,1,0:T(8,128)(2,1)S(1)}, u32[]{:S(2)}, u32[]{:S(2)}) collective-permute-start(bf16[2,32,256]{2,1,0:T(8,128)(2,1)S(1)} %get-tuple-element.59), channel_id=1, source_target_pairs={{0,2},{1,3},{2,0},{3,1},{4,6},{5,7},{6,4},{7,5},{8,10},{9,11},{10,... | collective-permute-start | bytes 98312 | tf_op jit(solution)/shard_map/ppermute | solution.py:328
  42.5 3.9 %collective-permute-start.12 = (bf16[2,32,256]{2,1,0:T(8,128)(2,1)S(1)}, bf16[2,32,256]{2,1,0:T(8,128)(2,1)S(1)}, u32[]{:S(2)}, u32[]{:S(2)}) collective-permute-start(bf16[2,32,256]{2,1,0:T(8,128)(2,1)S(1)} %get-tuple-element.60), channel_id=1, source_target_pairs={{0,3},{1,0},{2,1},{3,2},{4,7},{5,4},{6,5},{7,6},{8,11},{9,8},{10,9... | collective-permute-start | bytes 98312 | tf_op jit(solution)/shard_map/ppermute | solution.py:328
where the time goes:
time: 48.5 us
  starting transfers between devices  20.2 us (42%)
  Pallas kernels  15.9 us (33%)
  waiting for transfers between devices  12.3 us (25%)
    ppermute x12, starting transfers between devices, around(): lax.ppermute(parts[d], 'lon', [(i, (i + d) % n) for i in range(n)])  17.7 us
    pallas_call x6, Pallas kernels, call(): pl.pallas_call(functools.partial(kernel, n, rows), out_shape=out, in_spec...  15.9 us
    ppermute x12, waiting for transfers between devices, around(): lax.ppermute(parts[d], 'lon', [(i, (i + d) % n) for i in range(n)])  10.4 us
    ppermute x1, starting transfers between devices, on_device(): received = lax.ppermute(sent, ('lat', 'lon'), pairs)  2.5 us
    ppermute x1, waiting for transfers between devices, on_device(): received = lax.ppermute(sent, ('lat', 'lon'), pairs)  1.91 us
  transfers between devices with their start and end apart: 13, of which 6 were waited for; matrix products, arithmetic and copies ran while one was open for 0% of the time, Pallas kernels for 10%

commit v1 on v0

v1 whole, which is shorter than its diff:
```python
import functools
import math

import jax
import jax.numpy as jnp
from jax import lax
from jax.experimental import pallas as pl
from jax.experimental.pallas import tpu as pltpu
from jax.sharding import PartitionSpec as P

HALO = 2
LANES = 128
GROUP = 256
AHEAD = 16
VMEM_BYTES = 28 * 1024 * 1024


def group_of(band, shard, n):
    outer = jnp.where((shard == n - 2) == (band % 2 == 0), 0, n - 1)
    return jnp.where(shard < n - 2, shard + 1, outer)


def shard_of(band, group, n):
    if 0 < group < n - 1:
        return group - 1
    return n - 2 if (group == 0) == (band % 2 == 0) else n - 1


def first_held(group, rows):
    return group * rows - HALO * (group % 2)


def turn(quarter, staged, block, out, ready, done):
    size, _, chans = block.shape
    tiles = staged.shape[0]
    depth = GROUP // size
    pieces = size // depth

    def column(col):
        parts = [staged[t, pl.ds(col, size, stride=size), :] for t in range(tiles)]
        return jnp.concatenate(parts, axis=1).astype(jnp.bfloat16)

    def keep(i, row):
        for t in range(tiles):
            staged[t, pl.ds(i * size, size), :] = row[:, t * LANES : (t + 1) * LANES]

    @pl.when(quarter == 0)
    def _():
        for g in range(pieces):
            ready(g)
            out[g * depth : (g + 1) * depth] = block[g * depth : (g + 1) * depth]
            done(g)

    @pl.when(quarter == 1)
    def _():
        for i in range(size):
            if i % depth == 0:
                ready(i // depth)
            keep(i, block[i].astype(jnp.float32))
        for i in range(size):
            out[i] = column(size - 1 - i)
            if i % depth == depth - 1:
                done(i // depth)

    @pl.when(quarter == 2)
    def _():
        i = lax.broadcasted_iota(jnp.int32, (GROUP, GROUP), 0)
        j = lax.broadcasted_iota(jnp.int32, (GROUP, GROUP), 1)
        backwards = jnp.where(i + j == GROUP - 1, 1.0, 0.0).astype(jnp.bfloat16)
        for g in reversed(range(pieces)):
            ready(pieces - 1 - g)
            cells = block[size - (g + 1) * depth : size - g * depth].reshape(GROUP, chans)
            turned = jnp.dot(backwards, cells, preferred_element_type=jnp.float32).astype(jnp.bfloat16)
            out[g * depth : (g + 1) * depth] = turned.reshape(depth, size, chans)
            done(g)

    @pl.when(quarter == 3)
    def _():
        for i in range(size):
            if i % depth == 0:
                ready(i // depth)
            keep(size - 1 - i, block[i].astype(jnp.float32))
        for i in range(size):
            out[i] = column(i)
            if i % depth == depth - 1:
                done(i // depth)


def send_kernel(n, rows, rotation_in, owner_in, fields, *rest):
    edges, slabs, (rotation_out, owner_out) = rest[:n], rest[n : 2 * n], rest[2 * n : 2 * n + 2]
    staged, block, upright, rotation, scalar_sems, sems = rest[2 * n + 2 :]
    band = lax.axis_index("lat")
    me = lax.axis_index("lon")
    depth = GROUP // fields.shape[0]

    def piece(g):
        at = pl.ds(g * depth, depth)
        return pltpu.make_async_copy(fields.at[at], block.at[at], sems.at[g])

    scalars = [
        pltpu.make_async_copy(rotation_in, rotation, scalar_sems.at[0]),
        pltpu.make_async_copy(rotation_in, rotation_out, scalar_sems.at[1]),
        pltpu.make_async_copy(owner_in, owner_out, scalar_sems.at[2]),
    ]
    for copy in scalars:
        copy.start()
    for g in range(fields.shape[0] // depth):
        piece(g).start()
    scalars[0].wait()
    turn((4 - rotation[me, band]) % 4, staged, block, upright, lambda g: piece(g).wait(), lambda g: None)
    for d in range(n):
        group = group_of(band, lax.rem(me + d, n), n)
        top, odd = first_held(group, rows), group % 2
        edges[d][...] = upright[pl.ds(top + rows * odd, HALO)]
        slabs[d][...] = upright[pl.ds(top + HALO * (1 - odd), rows)]
    scalars[1].wait()
    scalars[2].wait()


def load_kernel(n, rows, after, *refs):
    del after
    count = (len(refs) - 7) // 2
    direct, (query, key) = refs[:count], refs[count : count + 2]
    loaded, (w_query, w_key) = refs[count + 2 : 2 * count + 2], refs[2 * count + 2 : 2 * count + 4]
    query_in, key_in, sems = refs[2 * count + 4 :]
    heads, _, head_dim = w_query.shape
    pairs = list(zip(direct, loaded)) + [(query, query_in), (key, key_in)]
    copies = [pltpu.make_async_copy(*pair, sems.at[i]) for i, pair in enumerate(pairs)]
    for copy in copies:
        copy.start()
    for copy in copies:
        copy.wait()
    w_key[...] = key_in[...].T
    for h in range(heads):
        w_query[h] = query_in[:, h * head_dim : (h + 1) * head_dim]


def columns_of(segment, size):
    return pl.ds(pl.multiple_of(segment * size, size), size)


def whole_rows(n, owner, slabs, out, first):
    band = lax.axis_index("lat")
    me = lax.axis_index("lon")
    count, size = slabs[0].shape[:2]
    for d in range(n):
        segment = owner[lax.rem(me + n - d, n), band]
        out[pl.ds(first, count), columns_of(segment, size)] = slabs[d][...]


def edge_kernel(n, rows, owner, *rest):
    del rows
    whole_rows(n, owner, rest[:n], rest[n], 0)


def spread(taps, r, row):
    cols, chans = row.shape
    taps[r, :, :chans] = pltpu.roll(row, 1, 0).astype(jnp.bfloat16)
    taps[r, :, chans : 2 * chans] = row.astype(jnp.bfloat16)
    taps[r, :, 2 * chans :] = pltpu.roll(row, cols - 1, 0).astype(jnp.bfloat16)


def convolve(taps, weight, bias, count):
    cols, width = taps.shape[1:]
    total = bias[...]
    for i in range(3):
        window = taps[i : i + count].reshape(count * cols, width)
        total = total + jnp.dot(window, weight[i], preferred_element_type=jnp.float32)
    return total


def silu(x):
    return x / (1.0 + jnp.exp(-x))


def live_count(counts, row):
    inside = (row >= 0) & (row < counts.shape[0])
    return jnp.where(inside, counts[jnp.clip(row, 0, counts.shape[0] - 1)], 0)


def by_last(a, b):
    return lax.dot_general(a, b, (((1,), (1,)), ((), ())), preferred_element_type=jnp.float32)


def attend(segments, limits, mixed, normed, keys, values, w_query, w_out, results, here, scores, expo, turned):
    rows, chans = len(limits), mixed.shape[1]
    size = here.shape[0] // (rows * len(segments))
    heads, _, head_dim = w_query.shape
    cols = mixed.shape[0] // rows
    width = heads * size
    blocks = [(s, r) for s in range(len(segments)) for r in range(rows)]

    def cells(s, r):
        return columns_of(segments[s] + r * (cols // size), size)

    for b, (s, r) in enumerate(blocks):
        here[b * size : (b + 1) * size, :] = normed[cells(s, r), :]
    queries = [jnp.dot(here[...], w_query[h], preferred_element_type=jnp.float32) for h in range(heads)]
    queries = [query.astype(jnp.bfloat16) for query in queries]
    for b, (s, r) in enumerate(blocks):
        own = jnp.concatenate([query[b * size : (b + 1) * size] for query in queries], axis=0)
        scores[b] = by_last(keys[r * cols : (r + 1) * cols, :], own)
    key_at = lax.broadcasted_iota(jnp.int32, (cols, width), 0)
    scale = math.log2(math.e) / head_dim**0.5
    shares = []
    for b, (s, r) in enumerate(blocks):
        part = jnp.where(key_at < limits[r], scores[b], -jnp.inf)
        part = jnp.exp2((part - jnp.max(part, axis=0, keepdims=True)) * scale)
        shares.append(1.0 / jnp.sum(part, axis=0, keepdims=True))
        expo[b] = part.astype(jnp.bfloat16)
    for b, (s, r) in enumerate(blocks):
        summed = jnp.dot(values[:, r * cols : (r + 1) * cols], expo[b], preferred_element_type=jnp.float32)
        turned[:, b * width : (b + 1) * width] = (summed * shares[b]).astype(jnp.bfloat16)
    attended = turned[...].T
    update = jnp.zeros(here.shape, jnp.float32)
    for h in range(heads):
        starts = [b * width + h * size for b in range(len(blocks))]
        part = jnp.concatenate([attended[start : start + size] for start in starts], axis=0)
        weight = w_out[h * head_dim : (h + 1) * head_dim, :]
        update = update + jnp.dot(part, weight, preferred_element_type=jnp.float32)
    for b, (s, r) in enumerate(blocks):
        cell = segments[s] * size + lax.broadcasted_iota(jnp.int32, (size, chans), 0)
        part = jnp.where(cell < limits[r], update[b * size : (b + 1) * size], 0.0)
        results[s][r * size : (r + 1) * size, :] = (mixed[cells(s, r), :].astype(jnp.float32) + part).astype(jnp.bfloat16)


def main_kernel(first, n, rows, owner, counts, *rest):
    slabs, sent, received = rest[:n], rest[n], rest[n + 1]
    w_conv1, b_conv1, w_conv2, b_conv2, w_key, w_value, w_query, w_out = rest[n + 2 : n + 10]
    result, mixed, normed, keys, values = rest[n + 10 : n + 15]
    grid, taps, acts, *scratch = rest[n + 15 :]
    band = lax.axis_index("lat")
    me = lax.axis_index("lon")
    group = group_of(band, me, n)
    odd = group % 2
    cols, chans = sent.shape[1:]
    cell = lax.broadcasted_iota(jnp.int32, (cols, chans), 0)
    first_row = band * (rows * n) + group * rows
    whole_rows(n, owner, slabs, grid, 2 * HALO * (1 - odd))
    grid[pl.ds(HALO + (rows - HALO) * odd, HALO)] = sent[...]
    grid[pl.ds((rows + HALO) * odd, HALO)] = received[...]
    for r in range(rows + 2 * HALO):
        spread(taps, r, grid[r].astype(jnp.float32))
    act = silu(convolve(taps, w_conv1, b_conv1, rows + HALO))
    limits = [live_count(counts, first_row - 1 + r) for r in range(rows + HALO)]
    for r in range(rows + HALO):
        spread(acts, r, jnp.where(cell < limits[r], act[r * cols : (r + 1) * cols], 0.0))
    limits = limits[1 : rows + 1]
    second = convolve(acts, w_conv2, b_conv2, rows)
    for r in range(rows):
        at = slice(r * cols, (r + 1) * cols)
        part = jnp.where(cell < limits[r], grid[r + HALO].astype(jnp.float32) + second[at], 0.0)
        mixed[at, :] = part.astype(jnp.bfloat16)
    flat = mixed[...].astype(jnp.float32)
    scaled = (flat * lax.rsqrt(jnp.mean(flat * flat, axis=1, keepdims=True) + 1e-06)).astype(jnp.bfloat16)
    normed[...] = scaled
    keys[...] = jnp.dot(scaled, w_key[...], preferred_element_type=jnp.float32).astype(jnp.bfloat16)
    values[...] = by_last(w_value[...], scaled).astype(jnp.bfloat16)
    result[rows * (cols // n) :, :] = jnp.zeros((AHEAD, chans), result.dtype)
    segments = [owner[lax.rem(me + first, n), band]]
    attend(segments, limits, mixed, normed, keys, values, w_query, w_out, [result], *scratch)


def rest_kernel(moves, n, rows, owner, counts, *rest):
    mixed, normed, keys, values, w_query, w_out = rest[:6]
    results, scratch = rest[6 : 6 + len(moves)], rest[6 + len(moves) :]
    band = lax.axis_index("lat")
    me = lax.axis_index("lon")
    first_row = band * (rows * n) + group_of(band, me, n) * rows
    limits = [counts[first_row + r] for r in range(rows)]
    segments = [owner[lax.rem(me + d, n), band] for d in moves]
    attend(segments, limits, mixed, normed, keys, values, w_query, w_out, results, *scratch)


def store_kernel(n, rows, rotation, *rest):
    slabs, (out, staged, upright, turned, sems) = rest[:n], rest[n:]
    band = lax.axis_index("lat")
    me = lax.axis_index("lon")
    depth = GROUP // out.shape[0]
    pieces = out.shape[0] // depth
    for d in range(n):
        top = group_of(band, lax.rem(me + n - d, n), n) * rows
        upright[pl.ds(top, rows)] = slabs[d][: rows * out.shape[0], :].reshape(rows, *out.shape[1:])

    def piece(g):
        at = pl.ds(g * depth, depth)
        return pltpu.make_async_copy(turned.at[at], out.at[at], sems.at[g])

    turn(rotation[me, band] % 4, staged, upright, turned, lambda g: None, lambda g: piece(g).start())
    for g in range(pieces):
        piece(g).wait()


def on_device(
    bands,
    n,
    fields,
    w_conv1,
    b_conv1,
    w_conv2,
    b_conv2,
    w_query,
    w_key,
    w_value,
    w_out,
    rotation,
    owner,
    counts,
):
    size, _, chans = fields.shape
    rows = size // n
    inner = rows - HALO
    cols = size * n
    bf16 = jnp.bfloat16
    smem = pl.BlockSpec(memory_space=pltpu.SMEM)
    vmem = pl.BlockSpec(memory_space=pltpu.VMEM)
    hbm = pl.BlockSpec(memory_space=pltpu.HBM)
    params = pltpu.CompilerParams(vmem_limit_bytes=VMEM_BYTES)
    pieces = size * size // GROUP

    def call(kernel, name, out, scalars, arrays, scratch, array_spec=vmem, scalar_spec=smem, out_spec=vmem):
        many = isinstance(out, list)
        return pl.pallas_call(
            functools.partial(kernel, n, rows),
            out_shape=out,
            in_specs=[scalar_spec] * len(scalars) + [array_spec] * len(arrays),
            out_specs=[out_spec] * len(out) if many else out_spec,
            scratch_shapes=scratch,
            compiler_params=params,
            name=name,
        )(*scalars, *arrays)

    def array(*shape):
        return jax.ShapeDtypeStruct(shape, bf16)

    order = sorted(range(1, n), key=lambda d: -min(d, n - d))

    def around_by(x, d):
        return lax.ppermute(x, "lon", [(i, (i + d) % n) for i in range(n)])

    def around(parts):
        moved = {d: around_by(parts[d], d) for d in order}
        return [parts[0]] + [moved[d] for d in range(1, n)]

    def in_hbm(x):
        return pltpu.with_memory_space_constraint(x, pltpu.HBM)

    rotation, owner = in_hbm(rotation.T), in_hbm(owner.T)
    loaded = [counts]
    loaded += [w_conv1.reshape(3, 3 * chans, chans), b_conv1.reshape(1, chans)]
    loaded += [w_conv2.reshape(3, 3 * chans, chans), b_conv2.reshape(1, chans), w_value.T, w_out]
    loaded = [in_hbm(x) for x in loaded]
    turned = [in_hbm(x) for x in (w_query, w_key.T)]
    staging = pltpu.VMEM((chans // LANES, size * size, LANES), jnp.float32)
    block = pltpu.VMEM((size, size, chans), bf16)

    slabs = [array(HALO, size, chans)] * n + [array(rows, size, chans)] * n
    scratch = [staging, block, block, pltpu.SMEM(rotation.shape, rotation.dtype)]
    scratch += [pltpu.SemaphoreType.DMA((3,)), pltpu.SemaphoreType.DMA((pieces,))]
    held = slabs + [pltpu.VMEM(x.shape, x.dtype) for x in (rotation, owner)]
    *slabs, rotation, owner = call(send_kernel, "send", held, [rotation, owner], [in_hbm(fields)], scratch, hbm, hbm)
    edges = around(slabs[:n])
    slabs = around(slabs[n:])

    snake = [a * n + shard_of(a, g, n) for a in range(bands) for g in range(n)]
    pairs = [(snake[i], snake[i + 1 if i % 2 else i - 1]) for i in range(1, bands * n - 1)]
    sent = call(edge_kernel, "edge", array(HALO, cols, chans), [owner], edges, [])
    received = lax.ppermute(sent, ("lat", "lon"), pairs)

    head_dim = w_key.shape[1]
    heads = chans // head_dim
    held = [pltpu.VMEM(x.shape, x.dtype) for x in loaded]
    held += [pltpu.VMEM((heads, chans, head_dim), bf16), pltpu.VMEM(w_key.shape, bf16)]
    scratch = [pltpu.VMEM(x.shape, bf16) for x in turned] + [pltpu.SemaphoreType.DMA((len(loaded) + 2,))]
    loaded = call(load_kernel, "load", held, [sent], loaded + turned, scratch, hbm, hbm)
    counts, *convs, w_value, w_out, w_query, w_key = loaded

    def taps(count):
        return pltpu.VMEM((count, cols, 3 * chans), bf16)

    def working(segments):
        blocks, width = segments * rows, heads * size
        return [
            pltpu.VMEM((blocks * size, chans), bf16),
            pltpu.VMEM((blocks, cols, width), jnp.float32),
            pltpu.VMEM((blocks, cols, width), bf16),
            pltpu.VMEM((head_dim, blocks * width), bf16),
        ]

    cells = rows * cols
    result = array(rows * size, chans)
    first, *others = [*order, 0]
    results = {}
    results[first], *held = call(
        functools.partial(main_kernel, first),
        "main",
        [array(rows * size + AHEAD, chans), array(cells, chans), array(cells, chans), array(cells, head_dim), array(head_dim, cells)],
        [owner, counts],
        slabs + [sent, received, *convs, w_key, w_value, w_query, w_out],
        [pltpu.VMEM((rows + 2 * HALO, cols, chans), bf16), taps(rows + 2 * HALO), taps(rows + HALO)] + working(1),
    )
    moved = {first: around_by(results[first], first)}
    rest = call(
        functools.partial(rest_kernel, others),
        "rest",
        [result] * len(others),
        [owner, counts],
        held + [w_query, w_out],
        working(len(others)),
    )
    for d, x in zip(others, rest):
        moved[d] = around_by(x, d) if d else x
    slabs = [moved[d] for d in range(n)]
    scratch = [staging, block, block, pltpu.SemaphoreType.DMA((pieces,))]
    return call(store_kernel, "store", array(*fields.shape), [rotation], slabs, scratch, out_spec=hbm)


def solution(mesh):
    in_specs = (P("lat", "lon", None), P(), P(), P(), P(), P(), P(), P(), P(), P(), P(), P())
    out_specs = P("lat", "lon", None)
    body = functools.partial(on_device, mesh.shape["lat"], mesh.shape["lon"])
    return jax.shard_map(body, mesh=mesh, in_specs=in_specs, out_specs=out_specs, check_vma=False)
```

time: 48.5 us -> 46.8 us (0.965)
  starting transfers between devices: 20.2 us -> 17.9 us
    ppermute x12 -> x9, starting transfers between devices: 17.7 us -> 15.4 us  [around_by(): return lax.ppermute(x, 'lon', [(i, (i + d) % n) for i in range(n)])]
    pallas_call x6, Pallas kernels: 15.9 us -> 16.3 us  [call(): pl.pallas_call(functools.partial(kernel, n, rows), out_shape=out, in_spec...]
    ppermute x12 -> x9, waiting for transfers between devices: 10.4 us -> 10.3 us  [around_by(): return lax.ppermute(x, 'lon', [(i, (i + d) % n) for i in range(n)])]
  transfers between devices with their start and end apart: 13 -> 10, of which waited for: 6 -> 4; matrix products, arithmetic and copies ran while one was open for 0% -> 0% of each run, Pallas kernels for 10% -> 12%
where the time goes in v1:
time: 46.8 us; the launch traced here: 46.3 us
  starting transfers between devices  17.9 us (38%)
  Pallas kernels  16.3 us (35%)
  waiting for transfers between devices  12 us (26%)
    pallas_call x6, Pallas kernels, call(): pl.pallas_call(functools.partial(kernel, n, rows), out_shape=out, in_spec...  16.3 us
    ppermute x9, starting transfers between devices, around_by(): return lax.ppermute(x, 'lon', [(i, (i + d) % n) for i in range(n)])  15.4 us
    ppermute x9, waiting for transfers between devices, around_by(): return lax.ppermute(x, 'lon', [(i, (i + d) % n) for i in range(n)])  10.3 us
    ppermute x1, starting transfers between devices, on_device(): received = lax.ppermute(sent, ('lat', 'lon'), pairs)  2.48 us
    ppermute x1, waiting for transfers between devices, on_device(): received = lax.ppermute(sent, ('lat', 'lon'), pairs)  1.7 us
  transfers between devices with their start and end apart: 10, of which 4 were waited for; matrix products, arithmetic and copies ran while one was open for 0% of the time, Pallas kernels for 12%

profile of v1, /device:TPU:0, one launch (start us, length us, event | category | flops | bytes accessed | tf_op | source)
XLA Modules:
  0.0 46.3 jit_solution(2572383509037086418)
XLA Ops:
  0.0 1.2 %send.1 = (bf16[2,32,256]{2,1,0:T(8,128)(2,1)S(1)}, bf16[2,32,256]{2,1,0:T(8,128)(2,1)S(1)}, bf16[2,32,256]{2,1,0:T(8,128)(2,1)S(1)}, bf16[2,32,256]{2,1,0:T(8,1...) custom-call(s32[4,8]{1,0:T(4,128)} %bitcast.12, ...), custom_call_target="tpu_custom_call" | custom-call | tf_op jit(solution)/shard_map/send/pallas_call | solution.py:323
  1.2 3.7 %collective-permute-start = (bf16[2,32,256]{2,1,0:T(8,128)(2,1)S(1)}, bf16[2,32,256]{2,1,0:T(8,128)(2,1)S(1)}, u32[]{:S(2)}, u32[]{:S(2)}) collective-permute-start(bf16[2,32,256]{2,1,0:T(8,128)(2,1)S(1)} %get-tuple-element.35), channel_id=1, source_target_pairs={{0,1},{1,2},{2,3},{3,0},{4,5},{5,6},{6,7},{7,4},{8,9},{9,10},{10,1... | collective-permute-start | bytes 98312 | tf_op jit(solution)/shard_map/ppermute | solution.py:339
  5.0 2.0 %collective-permute-start.1 = (bf16[2,32,256]{2,1,0:T(8,128)(2,1)S(1)}, bf16[2,32,256]{2,1,0:T(8,128)(2,1)S(1)}, u32[]{:S(2)}, u32[]{:S(2)}) collective-permute-start(bf16[2,32,256]{2,1,0:T(8,128)(2,1)S(1)} %get-tuple-element.36), channel_id=1, source_target_pairs={{0,2},{1,3},{2,0},{3,1},{4,6},{5,7},{6,4},{7,5},{8,10},{9,11},{10,... | collective-permute-start | bytes 98312 | tf_op jit(solution)/shard_map/ppermute | solution.py:339
  6.9 2.0 %collective-permute-start.2 = (bf16[2,32,256]{2,1,0:T(8,128)(2,1)S(1)}, bf16[2,32,256]{2,1,0:T(8,128)(2,1)S(1)}, u32[]{:S(2)}, u32[]{:S(2)}) collective-permute-start(bf16[2,32,256]{2,1,0:T(8,128)(2,1)S(1)} %get-tuple-element.37), channel_id=1, source_target_pairs={{0,3},{1,0},{2,1},{3,2},{4,7},{5,4},{6,5},{7,6},{8,11},{9,8},{10,9... | collective-permute-start | bytes 98312 | tf_op jit(solution)/shard_map/ppermute | solution.py:339
  8.9 0.0 collective-permute-start.3
  8.9 1.0 %collective-permute-start.4 = (bf16[8,32,256]{2,1,0:T(8,128)(2,1)S(1)}, bf16[8,32,256]{2,1,0:T(8,128)(2,1)S(1)}, u32[]{:S(2)}, u32[]{:S(2)}) collective-permute-start(bf16[8,32,256]{2,1,0:T(8,128)(2,1)S(1)} %get-tuple-element.41), channel_id=1, source_target_pairs={{0,2},{1,3},{2,0},{3,1},{4,6},{5,7},{6,4},{7,5},{8,10},{9,11},{10,... | collective-permute-start | bytes 393224 | tf_op jit(solution)/shard_map/ppermute | solution.py:339
  9.9 0.0 collective-permute-done.rest_1_
  9.9 2.8 %collective-permute-start.5 = (bf16[8,32,256]{2,1,0:T(8,128)(2,1)S(1)}, bf16[8,32,256]{2,1,0:T(8,128)(2,1)S(1)}, u32[]{:S(2)}, u32[]{:S(2)}) collective-permute-start(bf16[8,32,256]{2,1,0:T(8,128)(2,1)S(1)} %get-tuple-element.42), channel_id=1, source_target_pairs={{0,3},{1,0},{2,1},{3,2},{4,7},{5,4},{6,5},{7,6},{8,11},{9,8},{10,9... | collective-permute-start | bytes 393224 | tf_op jit(solution)/shard_map/ppermute | solution.py:339
  12.7 0.0 collective-permute-done.1.rest_2_
  12.7 0.0 collective-permute-done.2.rest_3_
  12.7 0.6 %edge.1.after.rest_4_ = bf16[2,128,256]{2,1,0:T(8,128)(2,1)S(1)} custom-call(s32[4,8]{1,0:T(4,128)S(1)} %get-tuple-element.33.owner, bf16[2,32,256]{2,1,0:T(8,128)(2,1)S(1)} %get-tuple-element.34.rest_0_, bf16[2,32,256]{2,1,0:T(8,128)(2,1)S(1)} %collective-permute-done.rest_1_, bf16[2,32,256]{2,1,0:T(8,128)(2,1)S(1)} %collective-permute-done.1.rest_2_, ...), custom_call_target="tpu_custom_call" | custom-call | tf_op jit(solution)/shard_map/edge/pallas_call | solution.py:323
  13.3 2.5 %collective-permute-start.6 = (bf16[2,128,256]{2,1,0:T(8,128)(2,1)S(1)}, bf16[2,128,256]{2,1,0:T(8,128)(2,1)S(1)}, u32[]{:S(2)}, u32[]{:S(2)}) collective-permute-start(bf16[2,128,256]{2,1,0:T(8,128)(2,1)S(1)} %edge.1.after.rest_4_), channel_id=1, source_target_pairs={{0,1},{1,0},{3,7},{7,3},{4,5},{5,4},{6,10},{10,6},{8,9},{9,8},{11,... | collective-permute-start | bytes 393224 | tf_op jit(solution)/shard_map/ppermute | solution.py:368
  15.8 2.0 %load.1 = (s32[256]{0:T(256)S(1)}, bf16[3,768,256]{2,1,0:T(8,128)(2,1)S(1)}, f32[1,256]{1,0:T(1,128)S(1)}, bf16[3,768,256]{2,1,0:T(8,128)(2,1)S(1)}, f32[1,256]{...) custom-call(bf16[2,128,256]{2,1,0:T(8,128)(2,1)S(1)} %edge.1.after.r, ...), custom_call_target="tpu_custom_call" | custom-call | tf_op jit(solution)/shard_map/load/pallas_call | solution.py:323
  17.8 3.1 %collective-permute-done.4.rest_2_ = bf16[8,32,256]{2,1,0:T(8,128)(2,1)S(1)} collective-permute-done((bf16[8,32,256]{2,1,0:T(8,128)(2,1)S(1)}, bf16[8,32,256]{2,1,0:T(8,128)(2,1)S(1)}, u32[]{:S(2)}, u32[]{:S(2)}) %collective-permute-start.4) | collective-permute-done | bytes 131104 | tf_op jit(solution)/shard_map/ppermute | solution.py:339
  20.9 0.0 collective-permute-done.5.rest_3_
  20.9 1.7 %collective-permute-done.6.rest_5_ = bf16[2,128,256]{2,1,0:T(8,128)(2,1)S(1)} collective-permute-done((bf16[2,128,256]{2,1,0:T(8,128)(2,1)S(1)}, bf16[2,128,256]{2,1,0:T(8,128)(2,1)S(1)}, u32[]{:S(2)}, u32[]{:S(2)}) %collective-permute-start.6) | collective-permute-done | bytes 131104 | tf_op jit(solution)/shard_map/ppermute | solution.py:368
  22.6 8.0 %main.1 = (bf16[272,256]{1,0:T(8,128)(2,1)S(1)}, bf16[1024,256]{1,0:T(8,128)(2,1)S(1)}, bf16[1024,256]{1,0:T(8,128)(2,1)S(1)}, bf16[1024,64]{1,0:T(8,128)(2,1)S(1)}, bf16[64,1024]{1,0:T(8,128)(2,1)S(1)}) custom-call(s32[4,8]{1,0:T(4,128)S(1)} %get-tuple-element.33.owner, s32[256]{0:T(256)S(1)} %get-tuple-element.38.counts, ...), custom_call_target="tpu_custom_call" | custom-call | tf_op jit(solution)/shard_map/main/pallas_call | solution.py:323
  30.7 0.1 collective-permute-start.8
  30.7 3.1 %rest.1 = (bf16[256,256]{1,0:T(8,128)(2,1)S(1)}, bf16[256,256]{1,0:T(8,128)(2,1)S(1)}, bf16[256,256]{1,0:T(8,128)(2,1)S(1)}) custom-call(s32[4,8]{1,0:T(4,128)S(1)} %get-tuple-element.33.owner, s32[256]{0:T(256)S(1)} %get-tuple-element.38.counts, bf16[1024,256]{1,0:T(8,128)(2,1)S(1)} %get-tuple-element.51.rest_0_, ...), custom_call_target="tpu_custom_call" | custom-call | tf_op jit(solution)/shard_map/rest/pallas_call | solution.py:323
  33.8 1.8 %collective-permute-start.7 = (bf16[256,256]{1,0:T(8,128)(2,1)S(1)}, bf16[256,256]{1,0:T(8,128)(2,1)S(1)}, u32[]{:S(2)}, u32[]{:S(2)}) collective-permute-start(bf16[256,256]{1,0:T(8,128)(2,1)S(1)} %get-tuple-element.56), channel_id=1, source_target_pairs={{0,1},{1,2},{2,3},{3,0},{4,5},{5,6},{6,7},{7,4},{8,9},{9,10},{10,1... | collective-permute-start | bytes 393224 | tf_op jit(solution)/shard_map/ppermute | solution.py:339
  35.6 2.1 %collective-permute-start.9 = (bf16[256,256]{1,0:T(8,128)(2,1)S(1)}, bf16[256,256]{1,0:T(8,128)(2,1)S(1)}, u32[]{:S(2)}, u32[]{:S(2)}) collective-permute-start(bf16[256,256]{1,0:T(8,128)(2,1)S(1)} %get-tuple-element.58), channel_id=1, source_target_pairs={{0,3},{1,0},{2,1},{3,2},{4,7},{5,4},{6,5},{7,6},{8,11},{9,8},{10,9... | collective-permute-start | bytes 393224 | tf_op jit(solution)/shard_map/ppermute | solution.py:339
  37.7 4.1 %collective-permute-done.7.rest_1_ = bf16[256,256]{1,0:T(8,128)(2,1)S(1)} collective-permute-done((bf16[256,256]{1,0:T(8,128)(2,1)S(1)}, bf16[256,256]{1,0:T(8,128)(2,1)S(1)}, u32[]{:S(2)}, u32[]{:S(2)}) %collective-permute-start.7) | collective-permute-done | bytes 131104 | tf_op jit(solution)/shard_map/ppermute | solution.py:339
  41.8 3.1 %collective-permute-done.9.rest_3_ = bf16[256,256]{1,0:T(8,128)(2,1)S(1)} collective-permute-done((bf16[256,256]{1,0:T(8,128)(2,1)S(1)}, bf16[256,256]{1,0:T(8,128)(2,1)S(1)}, u32[]{:S(2)}, u32[]{:S(2)}) %collective-permute-start.9) | collective-permute-done | bytes 131104 | tf_op jit(solution)/shard_map/ppermute | solution.py:339
  44.9 1.4 %store.1 = bf16[32,32,256]{2,1,0:T(8,128)(2,1)} custom-call(s32[4,8]{1,0:T(4,128)S(1)} %get-tuple-element.32.rotation, bf16[256,256]{1,0:T(8,128)(2,1)S(1)} %get-tuple-element.55.rest_0_, bf16[256,256]{1,0:T(8,128)(2,1)S(1)} %collective-permute-done.7.rest_1_, bf16[272,256]{1,0:T(8,128)(2,1)S(1)} %collective-permute-done.8.rest_2_, ...), custom_call_target="tpu_custom_call" | custom-call | tf_op jit(solution)/shard_map/store/pallas_call | solution.py:323
  (2 shorter events, 0.0 us)
Async XLA Ops:
  1.2 8.7 %collective-permute-start = (bf16[2,32,256]{2,1,0:T(8,128)(2,1)S(1)}, bf16[2,32,256]{2,1,0:T(8,128)(2,1)S(1)}, u32[]{:S(2)}, u32[]{:S(2)}) collective-permute-start(bf16[2,32,256]{2,1,0:T(8,128)(2,1)S(1)} %get-tuple-element.35), channel_id=1, source_target_pairs={{0,1},{1,2},{2,3},{3,0},{4,5},{5,6},{6,7},{7,4},{8,9},{9,10},{10,1... | collective-permute-start | bytes 98312 | tf_op jit(solution)/shard_map/ppermute | solution.py:339
  5.0 7.8 %collective-permute-start.1 = (bf16[2,32,256]{2,1,0:T(8,128)(2,1)S(1)}, bf16[2,32,256]{2,1,0:T(8,128)(2,1)S(1)}, u32[]{:S(2)}, u32[]{:S(2)}) collective-permute-start(bf16[2,32,256]{2,1,0:T(8,128)(2,1)S(1)} %get-tuple-element.36), channel_id=1, source_target_pairs={{0,2},{1,3},{2,0},{3,1},{4,6},{5,7},{6,4},{7,5},{8,10},{9,11},{10,... | collective-permute-start | bytes 98312 | tf_op jit(solution)/shard_map/ppermute | solution.py:339
  6.9 5.8 %collective-permute-start.2 = (bf16[2,32,256]{2,1,0:T(8,128)(2,1)S(1)}, bf16[2,32,256]{2,1,0:T(8,128)(2,1)S(1)}, u32[]{:S(2)}, u32[]{:S(2)}) collective-permute-start(bf16[2,32,256]{2,1,0:T(8,128)(2,1)S(1)} %get-tuple-element.37), channel_id=1, source_target_pairs={{0,3},{1,0},{2,1},{3,2},{4,7},{5,4},{6,5},{7,6},{8,11},{9,8},{10,9... | collective-permute-start | bytes 98312 | tf_op jit(solution)/shard_map/ppermute | solution.py:339
  8.9 8.9 %collective-permute-start.3 = (bf16[8,32,256]{2,1,0:T(8,128)(2,1)S(1)}, bf16[8,32,256]{2,1,0:T(8,128)(2,1)S(1)}, u32[]{:S(2)}, u32[]{:S(2)}) collective-permute-start(bf16[8,32,256]{2,1,0:T(8,128)(2,1)S(1)} %get-tuple-element.40), channel_id=1, source_target_pairs={{0,1},{1,2},{2,3},{3,0},{4,5},{5,6},{6,7},{7,4},{8,9},{9,10},{10,1... | collective-permute-start | bytes 393224 | tf_op jit(solution)/shard_map/ppermute | solution.py:339
  8.9 12.0 %collective-permute-start.4 = (bf16[8,32,256]{2,1,0:T(8,128)(2,1)S(1)}, bf16[8,32,256]{2,1,0:T(8,128)(2,1)S(1)}, u32[]{:S(2)}, u32[]{:S(2)}) collective-permute-start(bf16[8,32,256]{2,1,0:T(8,128)(2,1)S(1)} %get-tuple-element.41), channel_id=1, source_target_pairs={{0,2},{1,3},{2,0},{3,1},{4,6},{5,7},{6,4},{7,5},{8,10},{9,11},{10,... | collective-permute-start | bytes 393224 | tf_op jit(solution)/shard_map/ppermute | solution.py:339
  9.9 11.0 %collective-permute-start.5 = (bf16[8,32,256]{2,1,0:T(8,128)(2,1)S(1)}, bf16[8,32,256]{2,1,0:T(8,128)(2,1)S(1)}, u32[]{:S(2)}, u32[]{:S(2)}) collective-permute-start(bf16[8,32,256]{2,1,0:T(8,128)(2,1)S(1)} %get-tuple-element.42), channel_id=1, source_target_pairs={{0,3},{1,0},{2,1},{3,2},{4,7},{5,4},{6,5},{7,6},{8,11},{9,8},{10,9... | collective-permute-start | bytes 393224 | tf_op jit(solution)/shard_map/ppermute | solution.py:339
  13.3 9.3 %collective-permute-start.6 = (bf16[2,128,256]{2,1,0:T(8,128)(2,1)S(1)}, bf16[2,128,256]{2,1,0:T(8,128)(2,1)S(1)}, u32[]{:S(2)}, u32[]{:S(2)}) collective-permute-start(bf16[2,128,256]{2,1,0:T(8,128)(2,1)S(1)} %edge.1.after.rest_4_), channel_id=1, source_target_pairs={{0,1},{1,0},{3,7},{7,3},{4,5},{5,4},{6,10},{10,6},{8,9},{9,8},{11,... | collective-permute-start | bytes 393224 | tf_op jit(solution)/shard_map/ppermute | solution.py:368
  30.7 14.2 %collective-permute-start.8 = (bf16[272,256]{1,0:T(8,128)(2,1)S(1)}, bf16[272,256]{1,0:T(8,128)(2,1)S(1)}, u32[]{:S(2)}, u32[]{:S(2)}) collective-permute-start(bf16[272,256]{1,0:T(8,128)(2,1)S(1)} %get-tuple-element.57), channel_id=1, source_target_pairs={{0,2},{1,3},{2,0},{3,1},{4,6},{5,7},{6,4},{7,5},{8,10},{9,11},{10,... | collective-permute-start | bytes 417800 | tf_op jit(solution)/shard_map/ppermute | solution.py:339
  33.8 8.0 %collective-permute-start.7 = (bf16[256,256]{1,0:T(8,128)(2,1)S(1)}, bf16[256,256]{1,0:T(8,128)(2,1)S(1)}, u32[]{:S(2)}, u32[]{:S(2)}) collective-permute-start(bf16[256,256]{1,0:T(8,128)(2,1)S(1)} %get-tuple-element.56), channel_id=1, source_target_pairs={{0,1},{1,2},{2,3},{3,0},{4,5},{5,6},{6,7},{7,4},{8,9},{9,10},{10,1... | collective-permute-start | bytes 393224 | tf_op jit(solution)/shard_map/ppermute | solution.py:339
  35.6 9.3 %collective-permute-start.9 = (bf16[256,256]{1,0:T(8,128)(2,1)S(1)}, bf16[256,256]{1,0:T(8,128)(2,1)S(1)}, u32[]{:S(2)}, u32[]{:S(2)}) collective-permute-start(bf16[256,256]{1,0:T(8,128)(2,1)S(1)} %get-tuple-element.58), channel_id=1, source_target_pairs={{0,3},{1,0},{2,1},{3,2},{4,7},{5,4},{6,5},{7,6},{8,11},{9,8},{10,9... | collective-permute-start | bytes 393224 | tf_op jit(solution)/shard_map/ppermute | solution.py:339

commit v2 on v1

--- a/solution.py
+++ b/solution.py
@@ -160,13 +160,16 @@
     taps[r, :, 2 * chans :] = pltpu.roll(row, cols - 1, 0).astype(jnp.bfloat16)
 
 
-def convolve(taps, weight, bias, count):
+def convolve(taps, weight, bias, first, count):
     cols, width = taps.shape[1:]
-    total = bias[...]
-    for i in range(3):
-        window = taps[i : i + count].reshape(count * cols, width)
-        total = total + jnp.dot(window, weight[i], preferred_element_type=jnp.float32)
-    return total
+    windows = [taps[first + i : first + i + count].reshape(count * cols, width) for i in range(3)]
+    depth = weight.shape[0] * width
+    product = jnp.dot(
+        jnp.concatenate(windows, axis=1),
+        weight[...].reshape(depth, weight.shape[2]),
+        preferred_element_type=jnp.float32,
+    )
+    return product + bias[...]
 
 
 def silu(x):
@@ -239,18 +242,32 @@
     whole_rows(n, owner, slabs, grid, 2 * HALO * (1 - odd))
     grid[pl.ds(HALO + (rows - HALO) * odd, HALO)] = sent[...]
     grid[pl.ds((rows + HALO) * odd, HALO)] = received[...]
-    for r in range(rows + 2 * HALO):
-        spread(taps, r, grid[r].astype(jnp.float32))
-    act = silu(convolve(taps, w_conv1, b_conv1, rows + HALO))
     limits = [live_count(counts, first_row - 1 + r) for r in range(rows + HALO)]
-    for r in range(rows + HALO):
-        spread(acts, r, jnp.where(cell < limits[r], act[r * cols : (r + 1) * cols], 0.0))
+    half = (rows + HALO) // 2
+    spans = [(0, half), (half, rows + HALO)]
+    done = 0
+    convolved = []
+    for low, high in spans:
+        for r in range(done, high + HALO):
+            spread(taps, r, grid[r].astype(jnp.float32))
+        done = high + HALO
+        convolved.append(convolve(taps, w_conv1, b_conv1, low, high - low))
+    low = 0
+    for (start, stop), first_conv in zip(spans, convolved):
+        act = silu(first_conv)
+        for r in range(start, stop):
+            at = slice((r - start) * cols, (r - start + 1) * cols)
+            spread(acts, r, jnp.where(cell < limits[r], act[at], 0.0))
+        high = stop - HALO
+        if high <= low:
+            continue
+        second = convolve(acts, w_conv2, b_conv2, low, high - low)
+        for r in range(low, high):
+            here = grid[r + HALO].astype(jnp.float32) + second[(r - low) * cols : (r - low + 1) * cols]
+            here = jnp.where(cell < limits[r + 1], here, 0.0)
+            mixed[r * cols : (r + 1) * cols, :] = here.astype(jnp.bfloat16)
+        low = high
     limits = limits[1 : rows + 1]
-    second = convolve(acts, w_conv2, b_conv2, rows)
-    for r in range(rows):
-        at = slice(r * cols, (r + 1) * cols)
-        part = jnp.where(cell < limits[r], grid[r + HALO].astype(jnp.float32) + second[at], 0.0)
-        mixed[at, :] = part.astype(jnp.bfloat16)
     flat = mixed[...].astype(jnp.float32)
     scaled = (flat * lax.rsqrt(jnp.mean(flat * flat, axis=1, keepdims=True) + 1e-06)).astype(jnp.bfloat16)
     normed[...] = scaled

time: 46.8 us -> 45.2 us (0.966); the launches traced: 46.3 us -> 45.2 us
  Pallas kernels: 16.3 us -> 15.4 us
  starting transfers between devices: 17.9 us -> 17.3 us
  waiting for transfers between devices: 12 us -> 12.5 us
    pallas_call x6, Pallas kernels: 16.3 us -> 15.4 us  [call(): pl.pallas_call(functools.partial(kernel, n, rows), out_shape=out, in_spec...]
    ppermute x9, starting transfers between devices: 15.4 us -> 14.8 us  [around_by(): return lax.ppermute(x, 'lon', [(i, (i + d) % n) for i in range(n)])]
  transfers between devices with their start and end apart: 10 -> 10, of which waited for: 4 -> 5; matrix products, arithmetic and copies ran while one was open for 0% -> 0% of each run, Pallas kernels for 12% -> 13%
where the time goes in v2:
time: 45.2 us
  starting transfers between devices  17.3 us (38%)
  Pallas kernels  15.4 us (34%)
  waiting for transfers between devices  12.5 us (28%)
    pallas_call x6, Pallas kernels, call(): pl.pallas_call(functools.partial(kernel, n, rows), out_shape=out, in_spec...  15.4 us
    ppermute x9, starting transfers between devices, around_by(): return lax.ppermute(x, 'lon', [(i, (i + d) % n) for i in range(n)])  14.8 us
    ppermute x9, waiting for transfers between devices, around_by(): return lax.ppermute(x, 'lon', [(i, (i + d) % n) for i in range(n)])  10.6 us
    ppermute x1, starting transfers between devices, on_device(): received = lax.ppermute(sent, ('lat', 'lon'), pairs)  2.48 us
    ppermute x1, waiting for transfers between devices, on_device(): received = lax.ppermute(sent, ('lat', 'lon'), pairs)  1.93 us
  transfers between devices with their start and end apart: 10, of which 5 were waited for; matrix products, arithmetic and copies ran while one was open for 0% of the time, Pallas kernels for 13%

profile of v2, /device:TPU:0, one launch (start us, length us, event | category | flops | bytes accessed | tf_op | source)
XLA Modules:
  0.0 45.2 jit_solution(5710433204527444764)
XLA Ops:
  0.0 1.9 %send.1 = (bf16[2,32,256]{2,1,0:T(8,128)(2,1)S(1)}, bf16[2,32,256]{2,1,0:T(8,128)(2,1)S(1)}, bf16[2,32,256]{2,1,0:T(8,128)(2,1)S(1)}, bf16[2,32,256]{2,1,0:T(8,1...) custom-call(s32[4,8]{1,0:T(4,128)} %bitcast.12, ...), custom_call_target="tpu_custom_call" | custom-call | tf_op jit(solution)/shard_map/send/pallas_call | solution.py:340
  1.9 3.1 %collective-permute-start = (bf16[2,32,256]{2,1,0:T(8,128)(2,1)S(1)}, bf16[2,32,256]{2,1,0:T(8,128)(2,1)S(1)}, u32[]{:S(2)}, u32[]{:S(2)}) collective-permute-start(bf16[2,32,256]{2,1,0:T(8,128)(2,1)S(1)} %get-tuple-element.35), channel_id=1, source_target_pairs={{0,1},{1,2},{2,3},{3,0},{4,5},{5,6},{6,7},{7,4},{8,9},{9,10},{10,1... | collective-permute-start | bytes 98312 | tf_op jit(solution)/shard_map/ppermute | solution.py:356
  5.0 2.6 %collective-permute-start.1 = (bf16[2,32,256]{2,1,0:T(8,128)(2,1)S(1)}, bf16[2,32,256]{2,1,0:T(8,128)(2,1)S(1)}, u32[]{:S(2)}, u32[]{:S(2)}) collective-permute-start(bf16[2,32,256]{2,1,0:T(8,128)(2,1)S(1)} %get-tuple-element.36), channel_id=1, source_target_pairs={{0,2},{1,3},{2,0},{3,1},{4,6},{5,7},{6,4},{7,5},{8,10},{9,11},{10,... | collective-permute-start | bytes 98312 | tf_op jit(solution)/shard_map/ppermute | solution.py:356
  7.6 1.3 %collective-permute-start.2 = (bf16[2,32,256]{2,1,0:T(8,128)(2,1)S(1)}, bf16[2,32,256]{2,1,0:T(8,128)(2,1)S(1)}, u32[]{:S(2)}, u32[]{:S(2)}) collective-permute-start(bf16[2,32,256]{2,1,0:T(8,128)(2,1)S(1)} %get-tuple-element.37), channel_id=1, source_target_pairs={{0,3},{1,0},{2,1},{3,2},{4,7},{5,4},{6,5},{7,6},{8,11},{9,8},{10,9... | collective-permute-start | bytes 98312 | tf_op jit(solution)/shard_map/ppermute | solution.py:356
  8.9 0.7 %collective-permute-start.3 = (bf16[8,32,256]{2,1,0:T(8,128)(2,1)S(1)}, bf16[8,32,256]{2,1,0:T(8,128)(2,1)S(1)}, u32[]{:S(2)}, u32[]{:S(2)}) collective-permute-start(bf16[8,32,256]{2,1,0:T(8,128)(2,1)S(1)} %get-tuple-element.40), channel_id=1, source_target_pairs={{0,1},{1,2},{2,3},{3,0},{4,5},{5,6},{6,7},{7,4},{8,9},{9,10},{10,1... | collective-permute-start | bytes 393224 | tf_op jit(solution)/shard_map/ppermute | solution.py:356
  9.6 0.3 collective-permute-start.4
  9.9 0.0 collective-permute-done.rest_1_
  9.9 2.8 %collective-permute-start.5 = (bf16[8,32,256]{2,1,0:T(8,128)(2,1)S(1)}, bf16[8,32,256]{2,1,0:T(8,128)(2,1)S(1)}, u32[]{:S(2)}, u32[]{:S(2)}) collective-permute-start(bf16[8,32,256]{2,1,0:T(8,128)(2,1)S(1)} %get-tuple-element.42), channel_id=1, source_target_pairs={{0,3},{1,0},{2,1},{3,2},{4,7},{5,4},{6,5},{7,6},{8,11},{9,8},{10,9... | collective-permute-start | bytes 393224 | tf_op jit(solution)/shard_map/ppermute | solution.py:356
  12.7 0.0 collective-permute-done.1.rest_2_
  12.7 0.6 %edge.1.after.rest_4_ = bf16[2,128,256]{2,1,0:T(8,128)(2,1)S(1)} custom-call(s32[4,8]{1,0:T(4,128)S(1)} %get-tuple-element.33.owner, bf16[2,32,256]{2,1,0:T(8,128)(2,1)S(1)} %get-tuple-element.34.rest_0_, bf16[2,32,256]{2,1,0:T(8,128)(2,1)S(1)} %collective-permute-done.rest_1_, bf16[2,32,256]{2,1,0:T(8,128)(2,1)S(1)} %collective-permute-done.1.rest_2_, ...), custom_call_target="tpu_custom_call" | custom-call | tf_op jit(solution)/shard_map/edge/pallas_call | solution.py:340
  13.3 2.5 %collective-permute-start.6 = (bf16[2,128,256]{2,1,0:T(8,128)(2,1)S(1)}, bf16[2,128,256]{2,1,0:T(8,128)(2,1)S(1)}, u32[]{:S(2)}, u32[]{:S(2)}) collective-permute-start(bf16[2,128,256]{2,1,0:T(8,128)(2,1)S(1)} %edge.1.after.rest_4_), channel_id=1, source_target_pairs={{0,1},{1,0},{3,7},{7,3},{4,5},{5,4},{6,10},{10,6},{8,9},{9,8},{11,... | collective-permute-start | bytes 393224 | tf_op jit(solution)/shard_map/ppermute | solution.py:385
  15.8 2.0 %load.1 = (s32[256]{0:T(256)S(1)}, bf16[3,768,256]{2,1,0:T(8,128)(2,1)S(1)}, f32[1,256]{1,0:T(1,128)S(1)}, bf16[3,768,256]{2,1,0:T(8,128)(2,1)S(1)}, f32[1,256]{...) custom-call(bf16[2,128,256]{2,1,0:T(8,128)(2,1)S(1)} %edge.1.after.r, ...), custom_call_target="tpu_custom_call" | custom-call | tf_op jit(solution)/shard_map/load/pallas_call | solution.py:340
  17.8 0.0 collective-permute-done.3.rest_1_
  17.8 3.1 %collective-permute-done.4.rest_2_ = bf16[8,32,256]{2,1,0:T(8,128)(2,1)S(1)} collective-permute-done((bf16[8,32,256]{2,1,0:T(8,128)(2,1)S(1)}, bf16[8,32,256]{2,1,0:T(8,128)(2,1)S(1)}, u32[]{:S(2)}, u32[]{:S(2)}) %collective-permute-start.4) | collective-permute-done | bytes 131104 | tf_op jit(solution)/shard_map/ppermute | solution.py:356
  20.9 0.2 collective-permute-done.5.rest_3_
  21.1 1.9 %collective-permute-done.6.rest_5_ = bf16[2,128,256]{2,1,0:T(8,128)(2,1)S(1)} collective-permute-done((bf16[2,128,256]{2,1,0:T(8,128)(2,1)S(1)}, bf16[2,128,256]{2,1,0:T(8,128)(2,1)S(1)}, u32[]{:S(2)}, u32[]{:S(2)}) %collective-permute-start.6) | collective-permute-done | bytes 131104 | tf_op jit(solution)/shard_map/ppermute | solution.py:385
  23.0 5.9 %main.1 = (bf16[272,256]{1,0:T(8,128)(2,1)S(1)}, bf16[1024,256]{1,0:T(8,128)(2,1)S(1)}, bf16[1024,256]{1,0:T(8,128)(2,1)S(1)}, bf16[1024,64]{1,0:T(8,128)(2,1)S(1)}, bf16[64,1024]{1,0:T(8,128)(2,1)S(1)}) custom-call(s32[4,8]{1,0:T(4,128)S(1)} %get-tuple-element.33.owner, s32[256]{0:T(256)S(1)} %get-tuple-element.38.counts, ...), custom_call_target="tpu_custom_call" | custom-call | tf_op jit(solution)/shard_map/main/pallas_call | solution.py:340
  28.9 0.1 collective-permute-start.8
  28.9 3.1 %rest.1 = (bf16[256,256]{1,0:T(8,128)(2,1)S(1)}, bf16[256,256]{1,0:T(8,128)(2,1)S(1)}, bf16[256,256]{1,0:T(8,128)(2,1)S(1)}) custom-call(s32[4,8]{1,0:T(4,128)S(1)} %get-tuple-element.33.owner, s32[256]{0:T(256)S(1)} %get-tuple-element.38.counts, bf16[1024,256]{1,0:T(8,128)(2,1)S(1)} %get-tuple-element.51.rest_0_, ...), custom_call_target="tpu_custom_call" | custom-call | tf_op jit(solution)/shard_map/rest/pallas_call | solution.py:340
  32.0 2.1 %collective-permute-start.7 = (bf16[256,256]{1,0:T(8,128)(2,1)S(1)}, bf16[256,256]{1,0:T(8,128)(2,1)S(1)}, u32[]{:S(2)}, u32[]{:S(2)}) collective-permute-start(bf16[256,256]{1,0:T(8,128)(2,1)S(1)} %get-tuple-element.56), channel_id=1, source_target_pairs={{0,1},{1,2},{2,3},{3,0},{4,5},{5,6},{6,7},{7,4},{8,9},{9,10},{10,1... | collective-permute-start | bytes 393224 | tf_op jit(solution)/shard_map/ppermute | solution.py:356
  34.1 1.8 %collective-permute-start.9 = (bf16[256,256]{1,0:T(8,128)(2,1)S(1)}, bf16[256,256]{1,0:T(8,128)(2,1)S(1)}, u32[]{:S(2)}, u32[]{:S(2)}) collective-permute-start(bf16[256,256]{1,0:T(8,128)(2,1)S(1)} %get-tuple-element.58), channel_id=1, source_target_pairs={{0,3},{1,0},{2,1},{3,2},{4,7},{5,4},{6,5},{7,6},{8,11},{9,8},{10,9... | collective-permute-start | bytes 393224 | tf_op jit(solution)/shard_map/ppermute | solution.py:356
  35.9 4.2 %collective-permute-done.7.rest_1_ = bf16[256,256]{1,0:T(8,128)(2,1)S(1)} collective-permute-done((bf16[256,256]{1,0:T(8,128)(2,1)S(1)}, bf16[256,256]{1,0:T(8,128)(2,1)S(1)}, u32[]{:S(2)}, u32[]{:S(2)}) %collective-permute-start.7) | collective-permute-done | bytes 131104 | tf_op jit(solution)/shard_map/ppermute | solution.py:356
  40.1 3.1 %collective-permute-done.9.rest_3_ = bf16[256,256]{1,0:T(8,128)(2,1)S(1)} collective-permute-done((bf16[256,256]{1,0:T(8,128)(2,1)S(1)}, bf16[256,256]{1,0:T(8,128)(2,1)S(1)}, u32[]{:S(2)}, u32[]{:S(2)}) %collective-permute-start.9) | collective-permute-done | bytes 131104 | tf_op jit(solution)/shard_map/ppermute | solution.py:356
  43.2 2.0 %store.1 = bf16[32,32,256]{2,1,0:T(8,128)(2,1)} custom-call(s32[4,8]{1,0:T(4,128)S(1)} %get-tuple-element.32.rotation, bf16[256,256]{1,0:T(8,128)(2,1)S(1)} %get-tuple-element.55.rest_0_, bf16[256,256]{1,0:T(8,128)(2,1)S(1)} %collective-permute-done.7.rest_1_, bf16[272,256]{1,0:T(8,128)(2,1)S(1)} %collective-permute-done.8.rest_2_, ...), custom_call_target="tpu_custom_call" | custom-call | tf_op jit(solution)/shard_map/store/pallas_call | solution.py:340
  (2 shorter events, 0.0 us)
Async XLA Ops:
  1.9 8.0 %collective-permute-start = (bf16[2,32,256]{2,1,0:T(8,128)(2,1)S(1)}, bf16[2,32,256]{2,1,0:T(8,128)(2,1)S(1)}, u32[]{:S(2)}, u32[]{:S(2)}) collective-permute-start(bf16[2,32,256]{2,1,0:T(8,128)(2,1)S(1)} %get-tuple-element.35), channel_id=1, source_target_pairs={{0,1},{1,2},{2,3},{3,0},{4,5},{5,6},{6,7},{7,4},{8,9},{9,10},{10,1... | collective-permute-start | bytes 98312 | tf_op jit(solution)/shard_map/ppermute | solution.py:356
  5.0 7.8 %collective-permute-start.1 = (bf16[2,32,256]{2,1,0:T(8,128)(2,1)S(1)}, bf16[2,32,256]{2,1,0:T(8,128)(2,1)S(1)}, u32[]{:S(2)}, u32[]{:S(2)}) collective-permute-start(bf16[2,32,256]{2,1,0:T(8,128)(2,1)S(1)} %get-tuple-element.36), channel_id=1, source_target_pairs={{0,2},{1,3},{2,0},{3,1},{4,6},{5,7},{6,4},{7,5},{8,10},{9,11},{10,... | collective-permute-start | bytes 98312 | tf_op jit(solution)/shard_map/ppermute | solution.py:356
  7.6 5.2 %collective-permute-start.2 = (bf16[2,32,256]{2,1,0:T(8,128)(2,1)S(1)}, bf16[2,32,256]{2,1,0:T(8,128)(2,1)S(1)}, u32[]{:S(2)}, u32[]{:S(2)}) collective-permute-start(bf16[2,32,256]{2,1,0:T(8,128)(2,1)S(1)} %get-tuple-element.37), channel_id=1, source_target_pairs={{0,3},{1,0},{2,1},{3,2},{4,7},{5,4},{6,5},{7,6},{8,11},{9,8},{10,9... | collective-permute-start | bytes 98312 | tf_op jit(solution)/shard_map/ppermute | solution.py:356
  8.9 8.9 %collective-permute-start.3 = (bf16[8,32,256]{2,1,0:T(8,128)(2,1)S(1)}, bf16[8,32,256]{2,1,0:T(8,128)(2,1)S(1)}, u32[]{:S(2)}, u32[]{:S(2)}) collective-permute-start(bf16[8,32,256]{2,1,0:T(8,128)(2,1)S(1)} %get-tuple-element.40), channel_id=1, source_target_pairs={{0,1},{1,2},{2,3},{3,0},{4,5},{5,6},{6,7},{7,4},{8,9},{9,10},{10,1... | collective-permute-start | bytes 393224 | tf_op jit(solution)/shard_map/ppermute | solution.py:356
  9.6 11.3 %collective-permute-start.4 = (bf16[8,32,256]{2,1,0:T(8,128)(2,1)S(1)}, bf16[8,32,256]{2,1,0:T(8,128)(2,1)S(1)}, u32[]{:S(2)}, u32[]{:S(2)}) collective-permute-start(bf16[8,32,256]{2,1,0:T(8,128)(2,1)S(1)} %get-tuple-element.41), channel_id=1, source_target_pairs={{0,2},{1,3},{2,0},{3,1},{4,6},{5,7},{6,4},{7,5},{8,10},{9,11},{10,... | collective-permute-start | bytes 393224 | tf_op jit(solution)/shard_map/ppermute | solution.py:356
  9.9 11.2 %collective-permute-start.5 = (bf16[8,32,256]{2,1,0:T(8,128)(2,1)S(1)}, bf16[8,32,256]{2,1,0:T(8,128)(2,1)S(1)}, u32[]{:S(2)}, u32[]{:S(2)}) collective-permute-start(bf16[8,32,256]{2,1,0:T(8,128)(2,1)S(1)} %get-tuple-element.42), channel_id=1, source_target_pairs={{0,3},{1,0},{2,1},{3,2},{4,7},{5,4},{6,5},{7,6},{8,11},{9,8},{10,9... | collective-permute-start | bytes 393224 | tf_op jit(solution)/shard_map/ppermute | solution.py:356
  13.3 9.7 %collective-permute-start.6 = (bf16[2,128,256]{2,1,0:T(8,128)(2,1)S(1)}, bf16[2,128,256]{2,1,0:T(8,128)(2,1)S(1)}, u32[]{:S(2)}, u32[]{:S(2)}) collective-permute-start(bf16[2,128,256]{2,1,0:T(8,128)(2,1)S(1)} %edge.1.after.rest_4_), channel_id=1, source_target_pairs={{0,1},{1,0},{3,7},{7,3},{4,5},{5,4},{6,10},{10,6},{8,9},{9,8},{11,... | collective-permute-start | bytes 393224 | tf_op jit(solution)/shard_map/ppermute | solution.py:385
  28.9 14.4 %collective-permute-start.8 = (bf16[272,256]{1,0:T(8,128)(2,1)S(1)}, bf16[272,256]{1,0:T(8,128)(2,1)S(1)}, u32[]{:S(2)}, u32[]{:S(2)}) collective-permute-start(bf16[272,256]{1,0:T(8,128)(2,1)S(1)} %get-tuple-element.57), channel_id=1, source_target_pairs={{0,2},{1,3},{2,0},{3,1},{4,6},{5,7},{6,4},{7,5},{8,10},{9,11},{10,... | collective-permute-start | bytes 417800 | tf_op jit(solution)/shard_map/ppermute | solution.py:356
  32.0 8.1 %collective-permute-start.7 = (bf16[256,256]{1,0:T(8,128)(2,1)S(1)}, bf16[256,256]{1,0:T(8,128)(2,1)S(1)}, u32[]{:S(2)}, u32[]{:S(2)}) collective-permute-start(bf16[256,256]{1,0:T(8,128)(2,1)S(1)} %get-tuple-element.56), channel_id=1, source_target_pairs={{0,1},{1,2},{2,3},{3,0},{4,5},{5,6},{6,7},{7,4},{8,9},{9,10},{10,1... | collective-permute-start | bytes 393224 | tf_op jit(solution)/shard_map/ppermute | solution.py:356
  34.1 9.1 %collective-permute-start.9 = (bf16[256,256]{1,0:T(8,128)(2,1)S(1)}, bf16[256,256]{1,0:T(8,128)(2,1)S(1)}, u32[]{:S(2)}, u32[]{:S(2)}) collective-permute-start(bf16[256,256]{1,0:T(8,128)(2,1)S(1)} %get-tuple-element.58), channel_id=1, source_target_pairs={{0,3},{1,0},{2,1},{3,2},{4,7},{5,4},{6,5},{7,6},{8,11},{9,8},{10,9... | collective-permute-start | bytes 393224 | tf_op jit(solution)/shard_map/ppermute | solution.py:356

commit v3 on v2

--- a/solution.py
+++ b/solution.py
@@ -33,16 +33,17 @@
 def turn(quarter, staged, block, out, ready, done):
     size, _, chans = block.shape
     tiles = staged.shape[0]
+    pitch = staged.shape[1] // size
     depth = GROUP // size
     pieces = size // depth
 
     def column(col):
-        parts = [staged[t, pl.ds(col, size, stride=size), :] for t in range(tiles)]
+        parts = [staged[t, pl.ds(col, size, stride=pitch), :] for t in range(tiles)]
         return jnp.concatenate(parts, axis=1).astype(jnp.bfloat16)
 
     def keep(i, row):
         for t in range(tiles):
-            staged[t, pl.ds(i * size, size), :] = row[:, t * LANES : (t + 1) * LANES]
+            staged[t, pl.ds(i * pitch, size), :] = row[:, t * LANES : (t + 1) * LANES]
 
     @pl.when(quarter == 0)
     def _():
@@ -150,7 +151,13 @@
 
 def edge_kernel(n, rows, owner, *rest):
     del rows
-    whole_rows(n, owner, rest[:n], rest[n], 0)
+    held, (out, *passed, rows_out) = rest[: 2 * n - 2], rest[2 * n - 2 :]
+    _, cols, chans = rows_out.shape
+    whole_rows(n, owner, held[:n], rows_out, 0)
+    out[: HALO * cols, :] = rows_out[...].reshape(HALO * cols, chans)
+    out[HALO * cols :, :] = jnp.zeros((AHEAD, chans), out.dtype)
+    for slab, copy in zip(held[n:], passed):
+        copy[...] = slab[...]
 
 
 def spread(taps, r, row):
@@ -236,12 +243,13 @@
     me = lax.axis_index("lon")
     group = group_of(band, me, n)
     odd = group % 2
-    cols, chans = sent.shape[1:]
+    cols, chans = grid.shape[1:]
+    edge = (HALO, cols, chans)
     cell = lax.broadcasted_iota(jnp.int32, (cols, chans), 0)
     first_row = band * (rows * n) + group * rows
     whole_rows(n, owner, slabs, grid, 2 * HALO * (1 - odd))
-    grid[pl.ds(HALO + (rows - HALO) * odd, HALO)] = sent[...]
-    grid[pl.ds((rows + HALO) * odd, HALO)] = received[...]
+    grid[pl.ds(HALO + (rows - HALO) * odd, HALO)] = sent[: HALO * cols, :].reshape(edge)
+    grid[pl.ds((rows + HALO) * odd, HALO)] = received[: HALO * cols, :].reshape(edge)
     limits = [live_count(counts, first_row - 1 + r) for r in range(rows + HALO)]
     half = (rows + HALO) // 2
     spans = [(0, half), (half, rows + HALO)]
@@ -368,7 +376,7 @@
     loaded += [w_conv2.reshape(3, 3 * chans, chans), b_conv2.reshape(1, chans), w_value.T, w_out]
     loaded = [in_hbm(x) for x in loaded]
     turned = [in_hbm(x) for x in (w_query, w_key.T)]
-    staging = pltpu.VMEM((chans // LANES, size * size, LANES), jnp.float32)
+    staging = pltpu.VMEM((chans // LANES, size * (size + 8), LANES), jnp.float32)
     block = pltpu.VMEM((size, size, chans), bf16)
 
     slabs = [array(HALO, size, chans)] * n + [array(rows, size, chans)] * n
@@ -377,12 +385,18 @@
     held = slabs + [pltpu.VMEM(x.shape, x.dtype) for x in (rotation, owner)]
     *slabs, rotation, owner = call(send_kernel, "send", held, [rotation, owner], [in_hbm(fields)], scratch, hbm, hbm)
     edges = around(slabs[:n])
-    slabs = around(slabs[n:])
+    slabs = slabs[n:]
+    first, *others = order
 
     snake = [a * n + shard_of(a, g, n) for a in range(bands) for g in range(n)]
     pairs = [(snake[i], snake[i + 1 if i % 2 else i - 1]) for i in range(1, bands * n - 1)]
-    sent = call(edge_kernel, "edge", array(HALO, cols, chans), [owner], edges, [])
+    moved = {first: around_by(slabs[first], first)}
+    held = [array(HALO * cols + AHEAD, chans)] + [array(*slabs[0].shape)] * len(others)
+    scratch = [pltpu.VMEM((HALO, cols, chans), bf16)]
+    sent, *passed = call(edge_kernel, "edge", held, [owner], edges + [slabs[d] for d in others], scratch)
     received = lax.ppermute(sent, ("lat", "lon"), pairs)
+    moved |= {d: around_by(x, d) for d, x in zip(others, passed)}
+    slabs = [slabs[0]] + [moved[d] for d in range(1, n)]
 
     head_dim = w_key.shape[1]
     heads = chans // head_dim
@@ -406,7 +420,7 @@
 
     cells = rows * cols
     result = array(rows * size, chans)
-    first, *others = [*order, 0]
+    others = [*others, 0]
     results = {}
     results[first], *held = call(
         functools.partial(main_kernel, first),

time: 45.2 us -> 51.1 us (1.13)
  starting transfers between devices: 17.3 us -> 21.2 us
  waiting for transfers between devices: 12.5 us -> 15.2 us
  Pallas kernels: 15.4 us -> 14.5 us
    ppermute x9, waiting for transfers between devices: 10.6 us -> 15.2 us  [around_by(): return lax.ppermute(x, 'lon', [(i, (i + d) % n) for i in range(n)])]
    ppermute x9, starting transfers between devices: 14.8 us -> 19 us  [around_by(): return lax.ppermute(x, 'lon', [(i, (i + d) % n) for i in range(n)])]
    ppermute x1, waiting for transfers between devices: 1.93 us -> 0.01 us  [on_device(): received = lax.ppermute(sent, ('lat', 'lon'), pairs)]
    pallas_call x6, Pallas kernels: 15.4 us -> 14.5 us  [call(): pl.pallas_call(functools.partial(kernel, n, rows), out_shape=out, in_spec...]
  transfers between devices with their start and end apart: 10 -> 10, of which waited for: 5 -> 7; matrix products, arithmetic and copies ran while one was open for 0% -> 0% of each run, Pallas kernels for 13% -> 10%
where the time goes in v3:
time: 51.1 us; the launch traced here: 51 us
  starting transfers between devices  21.2 us (41%)
  waiting for transfers between devices  15.2 us (30%)
  Pallas kernels  14.5 us (28%)
    ppermute x9, starting transfers between devices, around_by(): return lax.ppermute(x, 'lon', [(i, (i + d) % n) for i in range(n)])  19 us
    ppermute x9, waiting for transfers between devices, around_by(): return lax.ppermute(x, 'lon', [(i, (i + d) % n) for i in range(n)])  15.2 us
    pallas_call x6, Pallas kernels, call(): pl.pallas_call(functools.partial(kernel, n, rows), out_shape=out, in_spec...  14.5 us
    ppermute x1, starting transfers between devices, on_device(): received = lax.ppermute(sent, ('lat', 'lon'), pairs)  2.15 us
  transfers between devices with their start and end apart: 10, of which 7 were waited for; matrix products, arithmetic and copies ran while one was open for 0% of the time, Pallas kernels for 10%

profile of v3, /device:TPU:0, one launch (start us, length us, event | category | flops | bytes accessed | tf_op | source)
XLA Modules:
  0.0 51.0 jit_solution(16762531462380144741)
XLA Ops:
  0.0 1.4 %send.1 = (bf16[2,32,256]{2,1,0:T(8,128)(2,1)S(1)}, bf16[2,32,256]{2,1,0:T(8,128)(2,1)S(1)}, bf16[2,32,256]{2,1,0:T(8,128)(2,1)S(1)}, bf16[2,32,256]{2,1,0:T(8,1...) custom-call(s32[4,8]{1,0:T(4,128)} %bitcast.12, ...), custom_call_target="tpu_custom_call" | custom-call | tf_op jit(solution)/shard_map/send/pallas_call | solution.py:348
  1.5 3.1 %collective-permute-start = (bf16[2,32,256]{2,1,0:T(8,128)(2,1)S(1)}, bf16[2,32,256]{2,1,0:T(8,128)(2,1)S(1)}, u32[]{:S(2)}, u32[]{:S(2)}) collective-permute-start(bf16[2,32,256]{2,1,0:T(8,128)(2,1)S(1)} %get-tuple-element.38), channel_id=1, source_target_pairs={{0,1},{1,2},{2,3},{3,0},{4,5},{5,6},{6,7},{7,4},{8,9},{9,10},{10,1... | collective-permute-start | bytes 98312 | tf_op jit(solution)/shard_map/ppermute | solution.py:364
  4.5 2.6 %collective-permute-start.1 = (bf16[2,32,256]{2,1,0:T(8,128)(2,1)S(1)}, bf16[2,32,256]{2,1,0:T(8,128)(2,1)S(1)}, u32[]{:S(2)}, u32[]{:S(2)}) collective-permute-start(bf16[2,32,256]{2,1,0:T(8,128)(2,1)S(1)} %get-tuple-element.39), channel_id=1, source_target_pairs={{0,2},{1,3},{2,0},{3,1},{4,6},{5,7},{6,4},{7,5},{8,10},{9,11},{10,... | collective-permute-start | bytes 98312 | tf_op jit(solution)/shard_map/ppermute | solution.py:364
  7.1 1.3 %collective-permute-start.2 = (bf16[2,32,256]{2,1,0:T(8,128)(2,1)S(1)}, bf16[2,32,256]{2,1,0:T(8,128)(2,1)S(1)}, u32[]{:S(2)}, u32[]{:S(2)}) collective-permute-start(bf16[2,32,256]{2,1,0:T(8,128)(2,1)S(1)} %get-tuple-element.40), channel_id=1, source_target_pairs={{0,3},{1,0},{2,1},{3,2},{4,7},{5,4},{6,5},{7,6},{8,11},{9,8},{10,9... | collective-permute-start | bytes 98312 | tf_op jit(solution)/shard_map/ppermute | solution.py:364
  8.5 0.1 collective-permute-done.rest_1_
  8.6 1.1 %collective-permute-done.1.rest_2_ = bf16[2,32,256]{2,1,0:T(8,128)(2,1)S(1)} collective-permute-done((bf16[2,32,256]{2,1,0:T(8,128)(2,1)S(1)}, bf16[2,32,256]{2,1,0:T(8,128)(2,1)S(1)}, u32[]{:S(2)}, u32[]{:S(2)}) %collective-permute-start.1) | collective-permute-done | bytes 32800 | tf_op jit(solution)/shard_map/ppermute | solution.py:364
  9.7 1.3 %collective-permute-done.2.rest_3_ = bf16[2,32,256]{2,1,0:T(8,128)(2,1)S(1)} collective-permute-done((bf16[2,32,256]{2,1,0:T(8,128)(2,1)S(1)}, bf16[2,32,256]{2,1,0:T(8,128)(2,1)S(1)}, u32[]{:S(2)}, u32[]{:S(2)}) %collective-permute-start.2) | collective-permute-done | bytes 32800 | tf_op jit(solution)/shard_map/ppermute | solution.py:364
  11.0 0.6 %edge.1 = (bf16[272,256]{1,0:T(8,128)(2,1)S(1)}, bf16[8,32,256]{2,1,0:T(8,128)(2,1)S(1)}, bf16[8,32,256]{2,1,0:T(8,128)(2,1)S(1)}) custom-call(s32[4,8]{1,0:T(4,128)S(1)} %get-tuple-element.36.owner, bf16[2,32,256]{2,1,0:T(8,128)(2,1)S(1)} %get-tuple-element.37.rest_0_, bf16[2,32,256]{2,1,0:T(8,128)(2,1)S(1)} %collective-permute-done.rest_1_, ...), custom_call_target="tpu_custom_call" | custom-call | tf_op jit(solution)/shard_map/edge/pallas_call | solution.py:348
  11.6 2.1 %collective-permute-start.6 = (bf16[272,256]{1,0:T(8,128)(2,1)S(1)}, bf16[272,256]{1,0:T(8,128)(2,1)S(1)}, u32[]{:S(2)}, u32[]{:S(2)}) collective-permute-start(bf16[272,256]{1,0:T(8,128)(2,1)S(1)} %get-tuple-element.43.after.rest_4_), channel_id=1, source_target_pairs={{0,1},{1,0},{3,7},{7,3},{4,5},{5,4},{6,10},{10,6},{8,9},{9,8},{11,... | collective-permute-start | bytes 417800 | tf_op jit(solution)/shard_map/ppermute | solution.py:397
  13.8 0.1 collective-permute-start.4
  13.9 3.5 %collective-permute-start.3 = (bf16[8,32,256]{2,1,0:T(8,128)(2,1)S(1)}, bf16[8,32,256]{2,1,0:T(8,128)(2,1)S(1)}, u32[]{:S(2)}, u32[]{:S(2)}) collective-permute-start(bf16[8,32,256]{2,1,0:T(8,128)(2,1)S(1)} %get-tuple-element.46), channel_id=1, source_target_pairs={{0,1},{1,2},{2,3},{3,0},{4,5},{5,6},{6,7},{7,4},{8,9},{9,10},{10,1... | collective-permute-start | bytes 393224 | tf_op jit(solution)/shard_map/ppermute | solution.py:364
  17.3 0.7 %collective-permute-start.5 = (bf16[8,32,256]{2,1,0:T(8,128)(2,1)S(1)}, bf16[8,32,256]{2,1,0:T(8,128)(2,1)S(1)}, u32[]{:S(2)}, u32[]{:S(2)}) collective-permute-start(bf16[8,32,256]{2,1,0:T(8,128)(2,1)S(1)} %get-tuple-element.48), channel_id=1, source_target_pairs={{0,3},{1,0},{2,1},{3,2},{4,7},{5,4},{6,5},{7,6},{8,11},{9,8},{10,9... | collective-permute-start | bytes 393224 | tf_op jit(solution)/shard_map/ppermute | solution.py:364
  18.0 2.0 %load.1 = (s32[256]{0:T(256)S(1)}, bf16[3,768,256]{2,1,0:T(8,128)(2,1)S(1)}, f32[1,256]{1,0:T(1,128)S(1)}, bf16[3,768,256]{2,1,0:T(8,128)(2,1)S(1)}, f32[1,256]{...) custom-call(bf16[272,256]{1,0:T(8,128)(2,1)S(1)} %get-tuple-element., ...), custom_call_target="tpu_custom_call" | custom-call | tf_op jit(solution)/shard_map/load/pallas_call | solution.py:348
  20.0 6.7 %collective-permute-done.4.rest_2_ = bf16[8,32,256]{2,1,0:T(8,128)(2,1)S(1)} collective-permute-done((bf16[8,32,256]{2,1,0:T(8,128)(2,1)S(1)}, bf16[8,32,256]{2,1,0:T(8,128)(2,1)S(1)}, u32[]{:S(2)}, u32[]{:S(2)}) %collective-permute-start.4) | collective-permute-done | bytes 131104 | tf_op jit(solution)/shard_map/ppermute | solution.py:364
  26.7 0.0 collective-permute-done.3.rest_1_
  26.7 0.4 collective-permute-done.5.rest_3_
  27.1 5.9 %main.1 = (bf16[272,256]{1,0:T(8,128)(2,1)S(1)}, bf16[1024,256]{1,0:T(8,128)(2,1)S(1)}, bf16[1024,256]{1,0:T(8,128)(2,1)S(1)}, bf16[1024,64]{1,0:T(8,128)(2,1)S(1)}, bf16[64,1024]{1,0:T(8,128)(2,1)S(1)}) custom-call(s32[4,8]{1,0:T(4,128)S(1)} %get-tuple-element.36.owner, s32[256]{0:T(256)S(1)} %get-tuple-element.44.counts, ...), custom_call_target="tpu_custom_call" | custom-call | tf_op jit(solution)/shard_map/main/pallas_call | solution.py:348
  32.9 4.0 %collective-permute-start.8 = (bf16[272,256]{1,0:T(8,128)(2,1)S(1)}, bf16[272,256]{1,0:T(8,128)(2,1)S(1)}, u32[]{:S(2)}, u32[]{:S(2)}) collective-permute-start(bf16[272,256]{1,0:T(8,128)(2,1)S(1)} %get-tuple-element.63), channel_id=1, source_target_pairs={{0,2},{1,3},{2,0},{3,1},{4,6},{5,7},{6,4},{7,5},{8,10},{9,11},{10,... | collective-permute-start | bytes 417800 | tf_op jit(solution)/shard_map/ppermute | solution.py:364
  36.9 3.1 %rest.1 = (bf16[256,256]{1,0:T(8,128)(2,1)S(1)}, bf16[256,256]{1,0:T(8,128)(2,1)S(1)}, bf16[256,256]{1,0:T(8,128)(2,1)S(1)}) custom-call(s32[4,8]{1,0:T(4,128)S(1)} %get-tuple-element.36.owner, s32[256]{0:T(256)S(1)} %get-tuple-element.44.counts, bf16[1024,256]{1,0:T(8,128)(2,1)S(1)} %get-tuple-element.57.rest_0_, ...), custom_call_target="tpu_custom_call" | custom-call | tf_op jit(solution)/shard_map/rest/pallas_call | solution.py:348
  40.0 0.1 collective-permute-start.7
  40.0 3.8 %collective-permute-start.9 = (bf16[256,256]{1,0:T(8,128)(2,1)S(1)}, bf16[256,256]{1,0:T(8,128)(2,1)S(1)}, u32[]{:S(2)}, u32[]{:S(2)}) collective-permute-start(bf16[256,256]{1,0:T(8,128)(2,1)S(1)} %get-tuple-element.64), channel_id=1, source_target_pairs={{0,3},{1,0},{2,1},{3,2},{4,7},{5,4},{6,5},{7,6},{8,11},{9,8},{10,9... | collective-permute-start | bytes 393224 | tf_op jit(solution)/shard_map/ppermute | solution.py:364
  43.9 4.4 %collective-permute-done.7.rest_1_ = bf16[256,256]{1,0:T(8,128)(2,1)S(1)} collective-permute-done((bf16[256,256]{1,0:T(8,128)(2,1)S(1)}, bf16[256,256]{1,0:T(8,128)(2,1)S(1)}, u32[]{:S(2)}, u32[]{:S(2)}) %collective-permute-start.7) | collective-permute-done | bytes 131104 | tf_op jit(solution)/shard_map/ppermute | solution.py:364
  48.2 1.2 %collective-permute-done.9.rest_3_ = bf16[256,256]{1,0:T(8,128)(2,1)S(1)} collective-permute-done((bf16[256,256]{1,0:T(8,128)(2,1)S(1)}, bf16[256,256]{1,0:T(8,128)(2,1)S(1)}, u32[]{:S(2)}, u32[]{:S(2)}) %collective-permute-start.9) | collective-permute-done | bytes 131104 | tf_op jit(solution)/shard_map/ppermute | solution.py:364
  49.4 1.6 %store.1 = bf16[32,32,256]{2,1,0:T(8,128)(2,1)} custom-call(s32[4,8]{1,0:T(4,128)S(1)} %get-tuple-element.35.rotation, bf16[256,256]{1,0:T(8,128)(2,1)S(1)} %get-tuple-element.61.rest_0_, bf16[256,256]{1,0:T(8,128)(2,1)S(1)} %collective-permute-done.7.rest_1_, bf16[272,256]{1,0:T(8,128)(2,1)S(1)} %collective-permute-done.8.rest_2_, ...), custom_call_target="tpu_custom_call" | custom-call | tf_op jit(solution)/shard_map/store/pallas_call | solution.py:348
  (2 shorter events, 0.0 us)
Async XLA Ops:
  1.5 7.1 %collective-permute-start = (bf16[2,32,256]{2,1,0:T(8,128)(2,1)S(1)}, bf16[2,32,256]{2,1,0:T(8,128)(2,1)S(1)}, u32[]{:S(2)}, u32[]{:S(2)}) collective-permute-start(bf16[2,32,256]{2,1,0:T(8,128)(2,1)S(1)} %get-tuple-element.38), channel_id=1, source_target_pairs={{0,1},{1,2},{2,3},{3,0},{4,5},{5,6},{6,7},{7,4},{8,9},{9,10},{10,1... | collective-permute-start | bytes 98312 | tf_op jit(solution)/shard_map/ppermute | solution.py:364
  4.5 5.2 %collective-permute-start.1 = (bf16[2,32,256]{2,1,0:T(8,128)(2,1)S(1)}, bf16[2,32,256]{2,1,0:T(8,128)(2,1)S(1)}, u32[]{:S(2)}, u32[]{:S(2)}) collective-permute-start(bf16[2,32,256]{2,1,0:T(8,128)(2,1)S(1)} %get-tuple-element.39), channel_id=1, source_target_pairs={{0,2},{1,3},{2,0},{3,1},{4,6},{5,7},{6,4},{7,5},{8,10},{9,11},{10,... | collective-permute-start | bytes 98312 | tf_op jit(solution)/shard_map/ppermute | solution.py:364
  7.1 3.9 %collective-permute-start.2 = (bf16[2,32,256]{2,1,0:T(8,128)(2,1)S(1)}, bf16[2,32,256]{2,1,0:T(8,128)(2,1)S(1)}, u32[]{:S(2)}, u32[]{:S(2)}) collective-permute-start(bf16[2,32,256]{2,1,0:T(8,128)(2,1)S(1)} %get-tuple-element.40), channel_id=1, source_target_pairs={{0,3},{1,0},{2,1},{3,2},{4,7},{5,4},{6,5},{7,6},{8,11},{9,8},{10,9... | collective-permute-start | bytes 98312 | tf_op jit(solution)/shard_map/ppermute | solution.py:364
  11.6 15.4 %collective-permute-start.6 = (bf16[272,256]{1,0:T(8,128)(2,1)S(1)}, bf16[272,256]{1,0:T(8,128)(2,1)S(1)}, u32[]{:S(2)}, u32[]{:S(2)}) collective-permute-start(bf16[272,256]{1,0:T(8,128)(2,1)S(1)} %get-tuple-element.43.after.rest_4_), channel_id=1, source_target_pairs={{0,1},{1,0},{3,7},{7,3},{4,5},{5,4},{6,10},{10,6},{8,9},{9,8},{11,... | collective-permute-start | bytes 417800 | tf_op jit(solution)/shard_map/ppermute | solution.py:397
  13.8 12.9 %collective-permute-start.4 = (bf16[8,32,256]{2,1,0:T(8,128)(2,1)S(1)}, bf16[8,32,256]{2,1,0:T(8,128)(2,1)S(1)}, u32[]{:S(2)}, u32[]{:S(2)}) collective-permute-start(bf16[8,32,256]{2,1,0:T(8,128)(2,1)S(1)} %get-tuple-element.47), channel_id=1, source_target_pairs={{0,2},{1,3},{2,0},{3,1},{4,6},{5,7},{6,4},{7,5},{8,10},{9,11},{10,... | collective-permute-start | bytes 393224 | tf_op jit(solution)/shard_map/ppermute | solution.py:364
  13.9 12.8 %collective-permute-start.3 = (bf16[8,32,256]{2,1,0:T(8,128)(2,1)S(1)}, bf16[8,32,256]{2,1,0:T(8,128)(2,1)S(1)}, u32[]{:S(2)}, u32[]{:S(2)}) collective-permute-start(bf16[8,32,256]{2,1,0:T(8,128)(2,1)S(1)} %get-tuple-element.46), channel_id=1, source_target_pairs={{0,1},{1,2},{2,3},{3,0},{4,5},{5,6},{6,7},{7,4},{8,9},{9,10},{10,1... | collective-permute-start | bytes 393224 | tf_op jit(solution)/shard_map/ppermute | solution.py:364
  17.3 9.7 %collective-permute-start.5 = (bf16[8,32,256]{2,1,0:T(8,128)(2,1)S(1)}, bf16[8,32,256]{2,1,0:T(8,128)(2,1)S(1)}, u32[]{:S(2)}, u32[]{:S(2)}) collective-permute-start(bf16[8,32,256]{2,1,0:T(8,128)(2,1)S(1)} %get-tuple-element.48), channel_id=1, source_target_pairs={{0,3},{1,0},{2,1},{3,2},{4,7},{5,4},{6,5},{7,6},{8,11},{9,8},{10,9... | collective-permute-start | bytes 393224 | tf_op jit(solution)/shard_map/ppermute | solution.py:364
  32.9 16.5 %collective-permute-start.8 = (bf16[272,256]{1,0:T(8,128)(2,1)S(1)}, bf16[272,256]{1,0:T(8,128)(2,1)S(1)}, u32[]{:S(2)}, u32[]{:S(2)}) collective-permute-start(bf16[272,256]{1,0:T(8,128)(2,1)S(1)} %get-tuple-element.63), channel_id=1, source_target_pairs={{0,2},{1,3},{2,0},{3,1},{4,6},{5,7},{6,4},{7,5},{8,10},{9,11},{10,... | collective-permute-start | bytes 417800 | tf_op jit(solution)/shard_map/ppermute | solution.py:364
  40.0 8.2 %collective-permute-start.7 = (bf16[256,256]{1,0:T(8,128)(2,1)S(1)}, bf16[256,256]{1,0:T(8,128)(2,1)S(1)}, u32[]{:S(2)}, u32[]{:S(2)}) collective-permute-start(bf16[256,256]{1,0:T(8,128)(2,1)S(1)} %get-tuple-element.62), channel_id=1, source_target_pairs={{0,1},{1,2},{2,3},{3,0},{4,5},{5,6},{6,7},{7,4},{8,9},{9,10},{10,1... | collective-permute-start | bytes 393224 | tf_op jit(solution)/shard_map/ppermute | solution.py:364
  40.0 9.4 %collective-permute-start.9 = (bf16[256,256]{1,0:T(8,128)(2,1)S(1)}, bf16[256,256]{1,0:T(8,128)(2,1)S(1)}, u32[]{:S(2)}, u32[]{:S(2)}) collective-permute-start(bf16[256,256]{1,0:T(8,128)(2,1)S(1)} %get-tuple-element.64), channel_id=1, source_target_pairs={{0,3},{1,0},{2,1},{3,2},{4,7},{5,4},{6,5},{7,6},{8,11},{9,8},{10,9... | collective-permute-start | bytes 393224 | tf_op jit(solution)/shard_map/ppermute | solution.py:364

commit v4 on v3

--- a/solution.py
+++ b/solution.py
@@ -92,7 +92,8 @@
     staged, block, upright, rotation, scalar_sems, sems = rest[2 * n + 2 :]
     band = lax.axis_index("lat")
     me = lax.axis_index("lon")
-    depth = GROUP // fields.shape[0]
+    size, _, chans = fields.shape
+    depth = GROUP // size
 
     def piece(g):
         at = pl.ds(g * depth, depth)
@@ -105,15 +106,18 @@
     ]
     for copy in scalars:
         copy.start()
-    for g in range(fields.shape[0] // depth):
+    for g in range(size // depth):
         piece(g).start()
     scalars[0].wait()
     turn((4 - rotation[me, band]) % 4, staged, block, upright, lambda g: piece(g).wait(), lambda g: None)
     for d in range(n):
         group = group_of(band, lax.rem(me + d, n), n)
         top, odd = first_held(group, rows), group % 2
-        edges[d][...] = upright[pl.ds(top + rows * odd, HALO)]
-        slabs[d][...] = upright[pl.ds(top + HALO * (1 - odd), rows)]
+        edges[d][...] = upright[pl.ds(top + rows * odd, HALO)].reshape(HALO * size, chans)
+        slab = upright[pl.ds(top + HALO * (1 - odd), rows)]
+        slabs[d][: rows * size, :] = slab.reshape(rows * size, chans)
+        if slabs[d].shape[0] > rows * size:
+            slabs[d][rows * size :, :] = jnp.zeros((slabs[d].shape[0] - rows * size, chans), slab.dtype)
     scalars[1].wait()
     scalars[2].wait()
 
@@ -140,20 +144,21 @@
     return pl.ds(pl.multiple_of(segment * size, size), size)
 
 
-def whole_rows(n, owner, slabs, out, first):
+def whole_rows(n, count, owner, slabs, out, first):
     band = lax.axis_index("lat")
     me = lax.axis_index("lon")
-    count, size = slabs[0].shape[:2]
+    size, chans = out.shape[1] // n, out.shape[2]
     for d in range(n):
         segment = owner[lax.rem(me + n - d, n), band]
-        out[pl.ds(first, count), columns_of(segment, size)] = slabs[d][...]
+        piece = slabs[d][: count * size, :].reshape(count, size, chans)
+        out[pl.ds(first, count), columns_of(segment, size)] = piece
 
 
 def edge_kernel(n, rows, owner, *rest):
     del rows
     held, (out, *passed, rows_out) = rest[: 2 * n - 2], rest[2 * n - 2 :]
     _, cols, chans = rows_out.shape
-    whole_rows(n, owner, held[:n], rows_out, 0)
+    whole_rows(n, HALO, owner, held[:n], rows_out, 0)
     out[: HALO * cols, :] = rows_out[...].reshape(HALO * cols, chans)
     out[HALO * cols :, :] = jnp.zeros((AHEAD, chans), out.dtype)
     for slab, copy in zip(held[n:], passed):
@@ -247,7 +252,7 @@
     edge = (HALO, cols, chans)
     cell = lax.broadcasted_iota(jnp.int32, (cols, chans), 0)
     first_row = band * (rows * n) + group * rows
-    whole_rows(n, owner, slabs, grid, 2 * HALO * (1 - odd))
+    whole_rows(n, rows, owner, slabs, grid, 2 * HALO * (1 - odd))
     grid[pl.ds(HALO + (rows - HALO) * odd, HALO)] = sent[: HALO * cols, :].reshape(edge)
     grid[pl.ds((rows + HALO) * odd, HALO)] = received[: HALO * cols, :].reshape(edge)
     limits = [live_count(counts, first_row - 1 + r) for r in range(rows + HALO)]
@@ -379,14 +384,15 @@
     staging = pltpu.VMEM((chans // LANES, size * (size + 8), LANES), jnp.float32)
     block = pltpu.VMEM((size, size, chans), bf16)
 
-    slabs = [array(HALO, size, chans)] * n + [array(rows, size, chans)] * n
+    first, *others = order
+    slabs = [array(HALO * size, chans)] * n
+    slabs += [array(rows * size + (2 * AHEAD if d == first else 0), chans) for d in range(n)]
     scratch = [staging, block, block, pltpu.SMEM(rotation.shape, rotation.dtype)]
     scratch += [pltpu.SemaphoreType.DMA((3,)), pltpu.SemaphoreType.DMA((pieces,))]
     held = slabs + [pltpu.VMEM(x.shape, x.dtype) for x in (rotation, owner)]
     *slabs, rotation, owner = call(send_kernel, "send", held, [rotation, owner], [in_hbm(fields)], scratch, hbm, hbm)
     edges = around(slabs[:n])
     slabs = slabs[n:]
-    first, *others = order
 
     snake = [a * n + shard_of(a, g, n) for a in range(bands) for g in range(n)]
     pairs = [(snake[i], snake[i + 1 if i % 2 else i - 1]) for i in range(1, bands * n - 1)]

time: 51.1 us -> 47.3 us (0.926)
  starting transfers between devices: 21.2 us -> 17 us
    ppermute x9, starting transfers between devices: 19 us -> 14.8 us  [around_by(): return lax.ppermute(x, 'lon', [(i, (i + d) % n) for i in range(n)])]
  transfers between devices with their start and end apart: 10 -> 10, of which waited for: 7 -> 6; matrix products, arithmetic and copies ran while one was open for 0% -> 0% of each run, Pallas kernels for 10% -> 12%
where the time goes in v4:
time: 47.3 us; the launch traced here: 46.8 us
  starting transfers between devices  17 us (36%)
  waiting for transfers between devices  15.2 us (32%)
  Pallas kernels  14.5 us (31%)
    ppermute x9, waiting for transfers between devices, around_by(): return lax.ppermute(x, 'lon', [(i, (i + d) % n) for i in range(n)])  15.2 us
    ppermute x9, starting transfers between devices, around_by(): return lax.ppermute(x, 'lon', [(i, (i + d) % n) for i in range(n)])  14.8 us
    pallas_call x6, Pallas kernels, call(): pl.pallas_call(functools.partial(kernel, n, rows), out_shape=out, in_spec...  14.5 us
    ppermute x1, starting transfers between devices, on_device(): received = lax.ppermute(sent, ('lat', 'lon'), pairs)  2.15 us
  transfers between devices with their start and end apart: 10, of which 6 were waited for; matrix products, arithmetic and copies ran while one was open for 0% of the time, Pallas kernels for 12%

profile of v4, /device:TPU:0, one launch (start us, length us, event | category | flops | bytes accessed | tf_op | source)
XLA Modules:
  0.0 46.8 jit_solution(12254702495243300590)
XLA Ops:
  0.0 1.4 %send.1 = (bf16[64,256]{1,0:T(8,128)(2,1)S(1)}, bf16[64,256]{1,0:T(8,128)(2,1)S(1)}, bf16[64,256]{1,0:T(8,128)(2,1)S(1)}, bf16[64,256]{1,0:T(8,128)(2,1)S(1)}, b...) custom-call(s32[4,8]{1,0:T(4,128)} %bitcast.12, ...), custom_call_target="tpu_custom_call" | custom-call | tf_op jit(solution)/shard_map/send/pallas_call | solution.py:353
  1.5 3.5 %collective-permute-start = (bf16[64,256]{1,0:T(8,128)(2,1)S(1)}, bf16[64,256]{1,0:T(8,128)(2,1)S(1)}, u32[]{:S(2)}, u32[]{:S(2)}) collective-permute-start(bf16[64,256]{1,0:T(8,128)(2,1)S(1)} %get-tuple-element.38), channel_id=1, source_target_pairs={{0,1},{1,2},{2,3},{3,0},{4,5},{5,6},{6,7},{7,4},{8,9},{9,10},{10,1... | collective-permute-start | bytes 98312 | tf_op jit(solution)/shard_map/ppermute | solution.py:369
  5.0 1.9 %collective-permute-start.1 = (bf16[64,256]{1,0:T(8,128)(2,1)S(1)}, bf16[64,256]{1,0:T(8,128)(2,1)S(1)}, u32[]{:S(2)}, u32[]{:S(2)}) collective-permute-start(bf16[64,256]{1,0:T(8,128)(2,1)S(1)} %get-tuple-element.39), channel_id=1, source_target_pairs={{0,2},{1,3},{2,0},{3,1},{4,6},{5,7},{6,4},{7,5},{8,10},{9,11},{10,... | collective-permute-start | bytes 98312 | tf_op jit(solution)/shard_map/ppermute | solution.py:369
  6.9 1.3 %collective-permute-start.2 = (bf16[64,256]{1,0:T(8,128)(2,1)S(1)}, bf16[64,256]{1,0:T(8,128)(2,1)S(1)}, u32[]{:S(2)}, u32[]{:S(2)}) collective-permute-start(bf16[64,256]{1,0:T(8,128)(2,1)S(1)} %get-tuple-element.40), channel_id=1, source_target_pairs={{0,3},{1,0},{2,1},{3,2},{4,7},{5,4},{6,5},{7,6},{8,11},{9,8},{10,9... | collective-permute-start | bytes 98312 | tf_op jit(solution)/shard_map/ppermute | solution.py:369
  8.3 0.2 collective-permute-start.4
  8.5 1.3 %collective-permute-done.1.rest_2_ = bf16[64,256]{1,0:T(8,128)(2,1)S(1)} collective-permute-done((bf16[64,256]{1,0:T(8,128)(2,1)S(1)}, bf16[64,256]{1,0:T(8,128)(2,1)S(1)}, u32[]{:S(2)}, u32[]{:S(2)}) %collective-permute-start.1) | collective-permute-done | bytes 32800 | tf_op jit(solution)/shard_map/ppermute | solution.py:369
  9.8 1.1 %collective-permute-done.2.rest_3_ = bf16[64,256]{1,0:T(8,128)(2,1)S(1)} collective-permute-done((bf16[64,256]{1,0:T(8,128)(2,1)S(1)}, bf16[64,256]{1,0:T(8,128)(2,1)S(1)}, u32[]{:S(2)}, u32[]{:S(2)}) %collective-permute-start.2) | collective-permute-done | bytes 32800 | tf_op jit(solution)/shard_map/ppermute | solution.py:369
  10.8 0.6 %edge.1 = (bf16[272,256]{1,0:T(8,128)(2,1)S(1)}, bf16[256,256]{1,0:T(8,128)(2,1)S(1)}, bf16[256,256]{1,0:T(8,128)(2,1)S(1)}) custom-call(s32[4,8]{1,0:T(4,128)S(1)} %get-tuple-element.36.owner, bf16[64,256]{1,0:T(8,128)(2,1)S(1)} %get-tuple-element.37.rest_0_, bf16[64,256]{1,0:T(8,128)(2,1)S(1)} %collective-permute-done.rest_1_, ...), custom_call_target="tpu_custom_call" | custom-call | tf_op jit(solution)/shard_map/edge/pallas_call | solution.py:353
  11.5 2.1 %collective-permute-start.6 = (bf16[272,256]{1,0:T(8,128)(2,1)S(1)}, bf16[272,256]{1,0:T(8,128)(2,1)S(1)}, u32[]{:S(2)}, u32[]{:S(2)}) collective-permute-start(bf16[272,256]{1,0:T(8,128)(2,1)S(1)} %get-tuple-element.43.after.rest_4_), channel_id=1, source_target_pairs={{0,1},{1,0},{3,7},{7,3},{4,5},{5,4},{6,10},{10,6},{8,9},{9,8},{11,... | collective-permute-start | bytes 417800 | tf_op jit(solution)/shard_map/ppermute | solution.py:403
  13.6 1.8 %collective-permute-start.3 = (bf16[256,256]{1,0:T(8,128)(2,1)S(1)}, bf16[256,256]{1,0:T(8,128)(2,1)S(1)}, u32[]{:S(2)}, u32[]{:S(2)}) collective-permute-start(bf16[256,256]{1,0:T(8,128)(2,1)S(1)} %get-tuple-element.46), channel_id=1, source_target_pairs={{0,1},{1,2},{2,3},{3,0},{4,5},{5,6},{6,7},{7,4},{8,9},{9,10},{10,1... | collective-permute-start | bytes 393224 | tf_op jit(solution)/shard_map/ppermute | solution.py:369
  15.5 2.0 %collective-permute-start.5 = (bf16[256,256]{1,0:T(8,128)(2,1)S(1)}, bf16[256,256]{1,0:T(8,128)(2,1)S(1)}, u32[]{:S(2)}, u32[]{:S(2)}) collective-permute-start(bf16[256,256]{1,0:T(8,128)(2,1)S(1)} %get-tuple-element.48), channel_id=1, source_target_pairs={{0,3},{1,0},{2,1},{3,2},{4,7},{5,4},{6,5},{7,6},{8,11},{9,8},{10,9... | collective-permute-start | bytes 393224 | tf_op jit(solution)/shard_map/ppermute | solution.py:369
  17.5 2.0 %load.1 = (s32[256]{0:T(256)S(1)}, bf16[3,768,256]{2,1,0:T(8,128)(2,1)S(1)}, f32[1,256]{1,0:T(1,128)S(1)}, bf16[3,768,256]{2,1,0:T(8,128)(2,1)S(1)}, f32[1,256]{...) custom-call(bf16[272,256]{1,0:T(8,128)(2,1)S(1)} %get-tuple-element., ...), custom_call_target="tpu_custom_call" | custom-call | tf_op jit(solution)/shard_map/load/pallas_call | solution.py:353
  19.5 0.0 collective-permute-done.4.rest_2_
  19.5 2.3 %collective-permute-done.3.rest_1_ = bf16[256,256]{1,0:T(8,128)(2,1)S(1)} collective-permute-done((bf16[256,256]{1,0:T(8,128)(2,1)S(1)}, bf16[256,256]{1,0:T(8,128)(2,1)S(1)}, u32[]{:S(2)}, u32[]{:S(2)}) %collective-permute-start.3) | collective-permute-done | bytes 131104 | tf_op jit(solution)/shard_map/ppermute | solution.py:369
  21.8 3.8 %collective-permute-done.5.rest_3_ = bf16[256,256]{1,0:T(8,128)(2,1)S(1)} collective-permute-done((bf16[256,256]{1,0:T(8,128)(2,1)S(1)}, bf16[256,256]{1,0:T(8,128)(2,1)S(1)}, u32[]{:S(2)}, u32[]{:S(2)}) %collective-permute-start.5) | collective-permute-done | bytes 131104 | tf_op jit(solution)/shard_map/ppermute | solution.py:369
  25.6 0.0 collective-permute-done.6.rest_5_
  25.6 5.9 %main.1 = (bf16[272,256]{1,0:T(8,128)(2,1)S(1)}, bf16[1024,256]{1,0:T(8,128)(2,1)S(1)}, bf16[1024,256]{1,0:T(8,128)(2,1)S(1)}, bf16[1024,64]{1,0:T(8,128)(2,1)S(1)}, bf16[64,1024]{1,0:T(8,128)(2,1)S(1)}) custom-call(s32[4,8]{1,0:T(4,128)S(1)} %get-tuple-element.36.owner, s32[256]{0:T(256)S(1)} %get-tuple-element.44.counts, ...), custom_call_target="tpu_custom_call" | custom-call | tf_op jit(solution)/shard_map/main/pallas_call | solution.py:353
  31.5 0.1 collective-permute-start.8
  31.5 3.1 %rest.1 = (bf16[256,256]{1,0:T(8,128)(2,1)S(1)}, bf16[256,256]{1,0:T(8,128)(2,1)S(1)}, bf16[256,256]{1,0:T(8,128)(2,1)S(1)}) custom-call(s32[4,8]{1,0:T(4,128)S(1)} %get-tuple-element.36.owner, s32[256]{0:T(256)S(1)} %get-tuple-element.44.counts, bf16[1024,256]{1,0:T(8,128)(2,1)S(1)} %get-tuple-element.57.rest_0_, ...), custom_call_target="tpu_custom_call" | custom-call | tf_op jit(solution)/shard_map/rest/pallas_call | solution.py:353
  34.6 0.8 %collective-permute-start.7 = (bf16[256,256]{1,0:T(8,128)(2,1)S(1)}, bf16[256,256]{1,0:T(8,128)(2,1)S(1)}, u32[]{:S(2)}, u32[]{:S(2)}) collective-permute-start(bf16[256,256]{1,0:T(8,128)(2,1)S(1)} %get-tuple-element.62), channel_id=1, source_target_pairs={{0,1},{1,2},{2,3},{3,0},{4,5},{5,6},{6,7},{7,4},{8,9},{9,10},{10,1... | collective-permute-start | bytes 393224 | tf_op jit(solution)/shard_map/ppermute | solution.py:369
  35.4 3.1 %collective-permute-start.9 = (bf16[256,256]{1,0:T(8,128)(2,1)S(1)}, bf16[256,256]{1,0:T(8,128)(2,1)S(1)}, u32[]{:S(2)}, u32[]{:S(2)}) collective-permute-start(bf16[256,256]{1,0:T(8,128)(2,1)S(1)} %get-tuple-element.64), channel_id=1, source_target_pairs={{0,3},{1,0},{2,1},{3,2},{4,7},{5,4},{6,5},{7,6},{8,11},{9,8},{10,9... | collective-permute-start | bytes 393224 | tf_op jit(solution)/shard_map/ppermute | solution.py:369
  38.5 4.4 %collective-permute-done.7.rest_1_ = bf16[256,256]{1,0:T(8,128)(2,1)S(1)} collective-permute-done((bf16[256,256]{1,0:T(8,128)(2,1)S(1)}, bf16[256,256]{1,0:T(8,128)(2,1)S(1)}, u32[]{:S(2)}, u32[]{:S(2)}) %collective-permute-start.7) | collective-permute-done | bytes 131104 | tf_op jit(solution)/shard_map/ppermute | solution.py:369
  42.9 2.4 %collective-permute-done.9.rest_3_ = bf16[256,256]{1,0:T(8,128)(2,1)S(1)} collective-permute-done((bf16[256,256]{1,0:T(8,128)(2,1)S(1)}, bf16[256,256]{1,0:T(8,128)(2,1)S(1)}, u32[]{:S(2)}, u32[]{:S(2)}) %collective-permute-start.9) | collective-permute-done | bytes 131104 | tf_op jit(solution)/shard_map/ppermute | solution.py:369
  45.3 1.6 %store.1 = bf16[32,32,256]{2,1,0:T(8,128)(2,1)} custom-call(s32[4,8]{1,0:T(4,128)S(1)} %get-tuple-element.35.rotation, bf16[256,256]{1,0:T(8,128)(2,1)S(1)} %get-tuple-element.61.rest_0_, bf16[256,256]{1,0:T(8,128)(2,1)S(1)} %collective-permute-done.7.rest_1_, bf16[272,256]{1,0:T(8,128)(2,1)S(1)} %collective-permute-done.8.rest_2_, ...), custom_call_target="tpu_custom_call" | custom-call | tf_op jit(solution)/shard_map/store/pallas_call | solution.py:353
  (2 shorter events, 0.0 us)
Async XLA Ops:
  1.5 7.0 %collective-permute-start = (bf16[64,256]{1,0:T(8,128)(2,1)S(1)}, bf16[64,256]{1,0:T(8,128)(2,1)S(1)}, u32[]{:S(2)}, u32[]{:S(2)}) collective-permute-start(bf16[64,256]{1,0:T(8,128)(2,1)S(1)} %get-tuple-element.38), channel_id=1, source_target_pairs={{0,1},{1,2},{2,3},{3,0},{4,5},{5,6},{6,7},{7,4},{8,9},{9,10},{10,1... | collective-permute-start | bytes 98312 | tf_op jit(solution)/shard_map/ppermute | solution.py:369
  5.0 4.8 %collective-permute-start.1 = (bf16[64,256]{1,0:T(8,128)(2,1)S(1)}, bf16[64,256]{1,0:T(8,128)(2,1)S(1)}, u32[]{:S(2)}, u32[]{:S(2)}) collective-permute-start(bf16[64,256]{1,0:T(8,128)(2,1)S(1)} %get-tuple-element.39), channel_id=1, source_target_pairs={{0,2},{1,3},{2,0},{3,1},{4,6},{5,7},{6,4},{7,5},{8,10},{9,11},{10,... | collective-permute-start | bytes 98312 | tf_op jit(solution)/shard_map/ppermute | solution.py:369
  6.9 3.9 %collective-permute-start.2 = (bf16[64,256]{1,0:T(8,128)(2,1)S(1)}, bf16[64,256]{1,0:T(8,128)(2,1)S(1)}, u32[]{:S(2)}, u32[]{:S(2)}) collective-permute-start(bf16[64,256]{1,0:T(8,128)(2,1)S(1)} %get-tuple-element.40), channel_id=1, source_target_pairs={{0,3},{1,0},{2,1},{3,2},{4,7},{5,4},{6,5},{7,6},{8,11},{9,8},{10,9... | collective-permute-start | bytes 98312 | tf_op jit(solution)/shard_map/ppermute | solution.py:369
  8.3 11.2 %collective-permute-start.4 = (bf16[288,256]{1,0:T(8,128)(2,1)S(1)}, bf16[288,256]{1,0:T(8,128)(2,1)S(1)}, u32[]{:S(2)}, u32[]{:S(2)}) collective-permute-start(bf16[288,256]{1,0:T(8,128)(2,1)S(1)} %get-tuple-element.47), channel_id=1, source_target_pairs={{0,2},{1,3},{2,0},{3,1},{4,6},{5,7},{6,4},{7,5},{8,10},{9,11},{10,... | collective-permute-start | bytes 442376 | tf_op jit(solution)/shard_map/ppermute | solution.py:369
  11.5 14.1 %collective-permute-start.6 = (bf16[272,256]{1,0:T(8,128)(2,1)S(1)}, bf16[272,256]{1,0:T(8,128)(2,1)S(1)}, u32[]{:S(2)}, u32[]{:S(2)}) collective-permute-start(bf16[272,256]{1,0:T(8,128)(2,1)S(1)} %get-tuple-element.43.after.rest_4_), channel_id=1, source_target_pairs={{0,1},{1,0},{3,7},{7,3},{4,5},{5,4},{6,10},{10,6},{8,9},{9,8},{11,... | collective-permute-start | bytes 417800 | tf_op jit(solution)/shard_map/ppermute | solution.py:403
  13.6 8.2 %collective-permute-start.3 = (bf16[256,256]{1,0:T(8,128)(2,1)S(1)}, bf16[256,256]{1,0:T(8,128)(2,1)S(1)}, u32[]{:S(2)}, u32[]{:S(2)}) collective-permute-start(bf16[256,256]{1,0:T(8,128)(2,1)S(1)} %get-tuple-element.46), channel_id=1, source_target_pairs={{0,1},{1,2},{2,3},{3,0},{4,5},{5,6},{6,7},{7,4},{8,9},{9,10},{10,1... | collective-permute-start | bytes 393224 | tf_op jit(solution)/shard_map/ppermute | solution.py:369
  15.5 10.1 %collective-permute-start.5 = (bf16[256,256]{1,0:T(8,128)(2,1)S(1)}, bf16[256,256]{1,0:T(8,128)(2,1)S(1)}, u32[]{:S(2)}, u32[]{:S(2)}) collective-permute-start(bf16[256,256]{1,0:T(8,128)(2,1)S(1)} %get-tuple-element.48), channel_id=1, source_target_pairs={{0,3},{1,0},{2,1},{3,2},{4,7},{5,4},{6,5},{7,6},{8,11},{9,8},{10,9... | collective-permute-start | bytes 393224 | tf_op jit(solution)/shard_map/ppermute | solution.py:369
  31.5 13.8 %collective-permute-start.8 = (bf16[272,256]{1,0:T(8,128)(2,1)S(1)}, bf16[272,256]{1,0:T(8,128)(2,1)S(1)}, u32[]{:S(2)}, u32[]{:S(2)}) collective-permute-start(bf16[272,256]{1,0:T(8,128)(2,1)S(1)} %get-tuple-element.63), channel_id=1, source_target_pairs={{0,2},{1,3},{2,0},{3,1},{4,6},{5,7},{6,4},{7,5},{8,10},{9,11},{10,... | collective-permute-start | bytes 417800 | tf_op jit(solution)/shard_map/ppermute | solution.py:369
  34.6 8.3 %collective-permute-start.7 = (bf16[256,256]{1,0:T(8,128)(2,1)S(1)}, bf16[256,256]{1,0:T(8,128)(2,1)S(1)}, u32[]{:S(2)}, u32[]{:S(2)}) collective-permute-start(bf16[256,256]{1,0:T(8,128)(2,1)S(1)} %get-tuple-element.62), channel_id=1, source_target_pairs={{0,1},{1,2},{2,3},{3,0},{4,5},{5,6},{6,7},{7,4},{8,9},{9,10},{10,1... | collective-permute-start | bytes 393224 | tf_op jit(solution)/shard_map/ppermute | solution.py:369
  35.4 9.8 %collective-permute-start.9 = (bf16[256,256]{1,0:T(8,128)(2,1)S(1)}, bf16[256,256]{1,0:T(8,128)(2,1)S(1)}, u32[]{:S(2)}, u32[]{:S(2)}) collective-permute-start(bf16[256,256]{1,0:T(8,128)(2,1)S(1)} %get-tuple-element.64), channel_id=1, source_target_pairs={{0,3},{1,0},{2,1},{3,2},{4,7},{5,4},{6,5},{7,6},{8,11},{9,8},{10,9... | collective-permute-start | bytes 393224 | tf_op jit(solution)/shard_map/ppermute | solution.py:369

commit v5 on v2

--- a/solution.py
+++ b/solution.py
@@ -11,6 +11,7 @@
 HALO = 2
 LANES = 128
 GROUP = 256
+CHUNKS = 3
 AHEAD = 16
 VMEM_BYTES = 28 * 1024 * 1024
 
@@ -33,16 +34,17 @@
 def turn(quarter, staged, block, out, ready, done):
     size, _, chans = block.shape
     tiles = staged.shape[0]
+    pitch = staged.shape[1] // size
     depth = GROUP // size
     pieces = size // depth
 
     def column(col):
-        parts = [staged[t, pl.ds(col, size, stride=size), :] for t in range(tiles)]
+        parts = [staged[t, pl.ds(col, size, stride=pitch), :] for t in range(tiles)]
         return jnp.concatenate(parts, axis=1).astype(jnp.bfloat16)
 
     def keep(i, row):
         for t in range(tiles):
-            staged[t, pl.ds(i * size, size), :] = row[:, t * LANES : (t + 1) * LANES]
+            staged[t, pl.ds(i * pitch, size), :] = row[:, t * LANES : (t + 1) * LANES]
 
     @pl.when(quarter == 0)
     def _():
@@ -243,18 +245,15 @@
     grid[pl.ds(HALO + (rows - HALO) * odd, HALO)] = sent[...]
     grid[pl.ds((rows + HALO) * odd, HALO)] = received[...]
     limits = [live_count(counts, first_row - 1 + r) for r in range(rows + HALO)]
-    half = (rows + HALO) // 2
-    spans = [(0, half), (half, rows + HALO)]
-    done = 0
-    convolved = []
-    for low, high in spans:
-        for r in range(done, high + HALO):
+    total = rows + HALO
+    chunks = min(CHUNKS, total // HALO)
+    cuts = [-(-total * i // chunks) for i in range(chunks + 1)]
+    done = low = 0
+    for start, stop in zip(cuts, cuts[1:]):
+        for r in range(done, stop + HALO):
             spread(taps, r, grid[r].astype(jnp.float32))
-        done = high + HALO
-        convolved.append(convolve(taps, w_conv1, b_conv1, low, high - low))
-    low = 0
-    for (start, stop), first_conv in zip(spans, convolved):
-        act = silu(first_conv)
+        done = stop + HALO
+        act = silu(convolve(taps, w_conv1, b_conv1, start, stop - start))
         for r in range(start, stop):
             at = slice((r - start) * cols, (r - start + 1) * cols)
             spread(acts, r, jnp.where(cell < limits[r], act[at], 0.0))
@@ -266,13 +265,14 @@
             here = grid[r + HALO].astype(jnp.float32) + second[(r - low) * cols : (r - low + 1) * cols]
             here = jnp.where(cell < limits[r + 1], here, 0.0)
             mixed[r * cols : (r + 1) * cols, :] = here.astype(jnp.bfloat16)
+        at = slice(low * cols, high * cols)
+        flat = mixed[at, :].astype(jnp.float32)
+        scaled = (flat * lax.rsqrt(jnp.mean(flat * flat, axis=1, keepdims=True) + 1e-06)).astype(jnp.bfloat16)
+        normed[at, :] = scaled
+        keys[at, :] = jnp.dot(scaled, w_key[...], preferred_element_type=jnp.float32).astype(jnp.bfloat16)
+        values[:, at] = by_last(w_value[...], scaled).astype(jnp.bfloat16)
         low = high
     limits = limits[1 : rows + 1]
-    flat = mixed[...].astype(jnp.float32)
-    scaled = (flat * lax.rsqrt(jnp.mean(flat * flat, axis=1, keepdims=True) + 1e-06)).astype(jnp.bfloat16)
-    normed[...] = scaled
-    keys[...] = jnp.dot(scaled, w_key[...], preferred_element_type=jnp.float32).astype(jnp.bfloat16)
-    values[...] = by_last(w_value[...], scaled).astype(jnp.bfloat16)
     result[rows * (cols // n) :, :] = jnp.zeros((AHEAD, chans), result.dtype)
     segments = [owner[lax.rem(me + first, n), band]]
     attend(segments, limits, mixed, normed, keys, values, w_query, w_out, [result], *scratch)
@@ -368,7 +368,7 @@
     loaded += [w_conv2.reshape(3, 3 * chans, chans), b_conv2.reshape(1, chans), w_value.T, w_out]
     loaded = [in_hbm(x) for x in loaded]
     turned = [in_hbm(x) for x in (w_query, w_key.T)]
-    staging = pltpu.VMEM((chans // LANES, size * size, LANES), jnp.float32)
+    staging = pltpu.VMEM((chans // LANES, size * (size + 8), LANES), jnp.float32)
     block = pltpu.VMEM((size, size, chans), bf16)
 
     slabs = [array(HALO, size, chans)] * n + [array(rows, size, chans)] * n

time: 45.2 us -> 46.7 us (1.033)
  Pallas kernels: 15.4 us -> 17.4 us
  starting transfers between devices: 17.3 us -> 16.7 us
    pallas_call x6, Pallas kernels: 15.4 us -> 17.4 us  [call(): pl.pallas_call(functools.partial(kernel, n, rows), out_shape=out, in_spec...]
    ppermute x1, starting transfers between devices: 2.48 us -> 1.92 us  [on_device(): received = lax.ppermute(sent, ('lat', 'lon'), pairs)]
  transfers between devices with their start and end apart: 10 -> 10, of which waited for: 5 -> 6; matrix products, arithmetic and copies ran while one was open for 0% -> 0% of each run, Pallas kernels for 13% -> 12%
where the time goes in v5:
time: 46.7 us
  Pallas kernels  17.4 us (37%)
  starting transfers between devices  16.7 us (36%)
  waiting for transfers between devices  12.5 us (27%)
    pallas_call x6, Pallas kernels, call(): pl.pallas_call(functools.partial(kernel, n, rows), out_shape=out, in_spec...  17.4 us
    ppermute x9, starting transfers between devices, around_by(): return lax.ppermute(x, 'lon', [(i, (i + d) % n) for i in range(n)])  14.8 us
    ppermute x9, waiting for transfers between devices, around_by(): return lax.ppermute(x, 'lon', [(i, (i + d) % n) for i in range(n)])  10.8 us
    ppermute x1, starting transfers between devices, on_device(): received = lax.ppermute(sent, ('lat', 'lon'), pairs)  1.92 us
    ppermute x1, waiting for transfers between devices, on_device(): received = lax.ppermute(sent, ('lat', 'lon'), pairs)  1.61 us
  transfers between devices with their start and end apart: 10, of which 6 were waited for; matrix products, arithmetic and copies ran while one was open for 0% of the time, Pallas kernels for 12%

profile of v5, /device:TPU:0, one launch (start us, length us, event | category | flops | bytes accessed | tf_op | source)
XLA Modules:
  0.0 46.7 jit_solution(11656224556029003232)
XLA Ops:
  0.0 1.9 %send.1 = (bf16[2,32,256]{2,1,0:T(8,128)(2,1)S(1)}, bf16[2,32,256]{2,1,0:T(8,128)(2,1)S(1)}, bf16[2,32,256]{2,1,0:T(8,128)(2,1)S(1)}, bf16[2,32,256]{2,1,0:T(8,1...) custom-call(s32[4,8]{1,0:T(4,128)} %bitcast.12, ...), custom_call_target="tpu_custom_call" | custom-call | tf_op jit(solution)/shard_map/send/pallas_call | solution.py:340
  1.9 3.1 %collective-permute-start = (bf16[2,32,256]{2,1,0:T(8,128)(2,1)S(1)}, bf16[2,32,256]{2,1,0:T(8,128)(2,1)S(1)}, u32[]{:S(2)}, u32[]{:S(2)}) collective-permute-start(bf16[2,32,256]{2,1,0:T(8,128)(2,1)S(1)} %get-tuple-element.35), channel_id=1, source_target_pairs={{0,1},{1,2},{2,3},{3,0},{4,5},{5,6},{6,7},{7,4},{8,9},{9,10},{10,1... | collective-permute-start | bytes 98312 | tf_op jit(solution)/shard_map/ppermute | solution.py:356
  5.0 2.6 %collective-permute-start.1 = (bf16[2,32,256]{2,1,0:T(8,128)(2,1)S(1)}, bf16[2,32,256]{2,1,0:T(8,128)(2,1)S(1)}, u32[]{:S(2)}, u32[]{:S(2)}) collective-permute-start(bf16[2,32,256]{2,1,0:T(8,128)(2,1)S(1)} %get-tuple-element.36), channel_id=1, source_target_pairs={{0,2},{1,3},{2,0},{3,1},{4,6},{5,7},{6,4},{7,5},{8,10},{9,11},{10,... | collective-permute-start | bytes 98312 | tf_op jit(solution)/shard_map/ppermute | solution.py:356
  7.6 1.3 %collective-permute-start.2 = (bf16[2,32,256]{2,1,0:T(8,128)(2,1)S(1)}, bf16[2,32,256]{2,1,0:T(8,128)(2,1)S(1)}, u32[]{:S(2)}, u32[]{:S(2)}) collective-permute-start(bf16[2,32,256]{2,1,0:T(8,128)(2,1)S(1)} %get-tuple-element.37), channel_id=1, source_target_pairs={{0,3},{1,0},{2,1},{3,2},{4,7},{5,4},{6,5},{7,6},{8,11},{9,8},{10,9... | collective-permute-start | bytes 98312 | tf_op jit(solution)/shard_map/ppermute | solution.py:356
  8.9 0.7 %collective-permute-start.3 = (bf16[8,32,256]{2,1,0:T(8,128)(2,1)S(1)}, bf16[8,32,256]{2,1,0:T(8,128)(2,1)S(1)}, u32[]{:S(2)}, u32[]{:S(2)}) collective-permute-start(bf16[8,32,256]{2,1,0:T(8,128)(2,1)S(1)} %get-tuple-element.40), channel_id=1, source_target_pairs={{0,1},{1,2},{2,3},{3,0},{4,5},{5,6},{6,7},{7,4},{8,9},{9,10},{10,1... | collective-permute-start | bytes 393224 | tf_op jit(solution)/shard_map/ppermute | solution.py:356
  9.6 0.3 collective-permute-start.4
  9.9 2.8 %collective-permute-start.5 = (bf16[8,32,256]{2,1,0:T(8,128)(2,1)S(1)}, bf16[8,32,256]{2,1,0:T(8,128)(2,1)S(1)}, u32[]{:S(2)}, u32[]{:S(2)}) collective-permute-start(bf16[8,32,256]{2,1,0:T(8,128)(2,1)S(1)} %get-tuple-element.42), channel_id=1, source_target_pairs={{0,3},{1,0},{2,1},{3,2},{4,7},{5,4},{6,5},{7,6},{8,11},{9,8},{10,9... | collective-permute-start | bytes 393224 | tf_op jit(solution)/shard_map/ppermute | solution.py:356
  12.8 0.0 collective-permute-done.1.rest_2_
  12.8 0.8 %collective-permute-done.2.rest_3_ = bf16[2,32,256]{2,1,0:T(8,128)(2,1)S(1)} collective-permute-done((bf16[2,32,256]{2,1,0:T(8,128)(2,1)S(1)}, bf16[2,32,256]{2,1,0:T(8,128)(2,1)S(1)}, u32[]{:S(2)}, u32[]{:S(2)}) %collective-permute-start.2) | collective-permute-done | bytes 32800 | tf_op jit(solution)/shard_map/ppermute | solution.py:356
  13.5 0.6 %edge.1.after.rest_4_ = bf16[2,128,256]{2,1,0:T(8,128)(2,1)S(1)} custom-call(s32[4,8]{1,0:T(4,128)S(1)} %get-tuple-element.33.owner, bf16[2,32,256]{2,1,0:T(8,128)(2,1)S(1)} %get-tuple-element.34.rest_0_, bf16[2,32,256]{2,1,0:T(8,128)(2,1)S(1)} %collective-permute-done.rest_1_, bf16[2,32,256]{2,1,0:T(8,128)(2,1)S(1)} %collective-permute-done.1.rest_2_, ...), custom_call_target="tpu_custom_call" | custom-call | tf_op jit(solution)/shard_map/edge/pallas_call | solution.py:340
  14.1 1.9 %collective-permute-start.6 = (bf16[2,128,256]{2,1,0:T(8,128)(2,1)S(1)}, bf16[2,128,256]{2,1,0:T(8,128)(2,1)S(1)}, u32[]{:S(2)}, u32[]{:S(2)}) collective-permute-start(bf16[2,128,256]{2,1,0:T(8,128)(2,1)S(1)} %edge.1.after.rest_4_), channel_id=1, source_target_pairs={{0,1},{1,0},{3,7},{7,3},{4,5},{5,4},{6,10},{10,6},{8,9},{9,8},{11,... | collective-permute-start | bytes 393224 | tf_op jit(solution)/shard_map/ppermute | solution.py:385
  16.1 2.0 %load.1 = (s32[256]{0:T(256)S(1)}, bf16[3,768,256]{2,1,0:T(8,128)(2,1)S(1)}, f32[1,256]{1,0:T(1,128)S(1)}, bf16[3,768,256]{2,1,0:T(8,128)(2,1)S(1)}, f32[1,256]{...) custom-call(bf16[2,128,256]{2,1,0:T(8,128)(2,1)S(1)} %edge.1.after.r, ...), custom_call_target="tpu_custom_call" | custom-call | tf_op jit(solution)/shard_map/load/pallas_call | solution.py:340
  18.1 0.0 collective-permute-done.3.rest_1_
  18.1 2.4 %collective-permute-done.4.rest_2_ = bf16[8,32,256]{2,1,0:T(8,128)(2,1)S(1)} collective-permute-done((bf16[8,32,256]{2,1,0:T(8,128)(2,1)S(1)}, bf16[8,32,256]{2,1,0:T(8,128)(2,1)S(1)}, u32[]{:S(2)}, u32[]{:S(2)}) %collective-permute-start.4) | collective-permute-done | bytes 131104 | tf_op jit(solution)/shard_map/ppermute | solution.py:356
  20.5 0.6 %collective-permute-done.5.rest_3_ = bf16[8,32,256]{2,1,0:T(8,128)(2,1)S(1)} collective-permute-done((bf16[8,32,256]{2,1,0:T(8,128)(2,1)S(1)}, bf16[8,32,256]{2,1,0:T(8,128)(2,1)S(1)}, u32[]{:S(2)}, u32[]{:S(2)}) %collective-permute-start.5) | collective-permute-done | bytes 131104 | tf_op jit(solution)/shard_map/ppermute | solution.py:356
  21.1 1.6 %collective-permute-done.6.rest_5_ = bf16[2,128,256]{2,1,0:T(8,128)(2,1)S(1)} collective-permute-done((bf16[2,128,256]{2,1,0:T(8,128)(2,1)S(1)}, bf16[2,128,256]{2,1,0:T(8,128)(2,1)S(1)}, u32[]{:S(2)}, u32[]{:S(2)}) %collective-permute-start.6) | collective-permute-done | bytes 131104 | tf_op jit(solution)/shard_map/ppermute | solution.py:385
  22.7 8.2 %main.1 = (bf16[272,256]{1,0:T(8,128)(2,1)S(1)}, bf16[1024,256]{1,0:T(8,128)(2,1)S(1)}, bf16[1024,256]{1,0:T(8,128)(2,1)S(1)}, bf16[1024,64]{1,0:T(8,128)(2,1)S(1)}, bf16[64,1024]{1,0:T(8,128)(2,1)S(1)}) custom-call(s32[4,8]{1,0:T(4,128)S(1)} %get-tuple-element.33.owner, s32[256]{0:T(256)S(1)} %get-tuple-element.38.counts, ...), custom_call_target="tpu_custom_call" | custom-call | tf_op jit(solution)/shard_map/main/pallas_call | solution.py:340
  30.9 0.1 collective-permute-start.8
  31.0 3.1 %rest.1 = (bf16[256,256]{1,0:T(8,128)(2,1)S(1)}, bf16[256,256]{1,0:T(8,128)(2,1)S(1)}, bf16[256,256]{1,0:T(8,128)(2,1)S(1)}) custom-call(s32[4,8]{1,0:T(4,128)S(1)} %get-tuple-element.33.owner, s32[256]{0:T(256)S(1)} %get-tuple-element.38.counts, bf16[1024,256]{1,0:T(8,128)(2,1)S(1)} %get-tuple-element.51.rest_0_, ...), custom_call_target="tpu_custom_call" | custom-call | tf_op jit(solution)/shard_map/rest/pallas_call | solution.py:340
  34.1 1.9 %collective-permute-start.7 = (bf16[256,256]{1,0:T(8,128)(2,1)S(1)}, bf16[256,256]{1,0:T(8,128)(2,1)S(1)}, u32[]{:S(2)}, u32[]{:S(2)}) collective-permute-start(bf16[256,256]{1,0:T(8,128)(2,1)S(1)} %get-tuple-element.56), channel_id=1, source_target_pairs={{0,1},{1,2},{2,3},{3,0},{4,5},{5,6},{6,7},{7,4},{8,9},{9,10},{10,1... | collective-permute-start | bytes 393224 | tf_op jit(solution)/shard_map/ppermute | solution.py:356
  36.0 1.9 %collective-permute-start.9 = (bf16[256,256]{1,0:T(8,128)(2,1)S(1)}, bf16[256,256]{1,0:T(8,128)(2,1)S(1)}, u32[]{:S(2)}, u32[]{:S(2)}) collective-permute-start(bf16[256,256]{1,0:T(8,128)(2,1)S(1)} %get-tuple-element.58), channel_id=1, source_target_pairs={{0,3},{1,0},{2,1},{3,2},{4,7},{5,4},{6,5},{7,6},{8,11},{9,8},{10,9... | collective-permute-start | bytes 393224 | tf_op jit(solution)/shard_map/ppermute | solution.py:356
  37.9 3.9 %collective-permute-done.7.rest_1_ = bf16[256,256]{1,0:T(8,128)(2,1)S(1)} collective-permute-done((bf16[256,256]{1,0:T(8,128)(2,1)S(1)}, bf16[256,256]{1,0:T(8,128)(2,1)S(1)}, u32[]{:S(2)}, u32[]{:S(2)}) %collective-permute-start.7) | collective-permute-done | bytes 131104 | tf_op jit(solution)/shard_map/ppermute | solution.py:356
  41.8 3.1 %collective-permute-done.9.rest_3_ = bf16[256,256]{1,0:T(8,128)(2,1)S(1)} collective-permute-done((bf16[256,256]{1,0:T(8,128)(2,1)S(1)}, bf16[256,256]{1,0:T(8,128)(2,1)S(1)}, u32[]{:S(2)}, u32[]{:S(2)}) %collective-permute-start.9) | collective-permute-done | bytes 131104 | tf_op jit(solution)/shard_map/ppermute | solution.py:356
  45.0 1.7 %store.1 = bf16[32,32,256]{2,1,0:T(8,128)(2,1)} custom-call(s32[4,8]{1,0:T(4,128)S(1)} %get-tuple-element.32.rotation, bf16[256,256]{1,0:T(8,128)(2,1)S(1)} %get-tuple-element.55.rest_0_, bf16[256,256]{1,0:T(8,128)(2,1)S(1)} %collective-permute-done.7.rest_1_, bf16[272,256]{1,0:T(8,128)(2,1)S(1)} %collective-permute-done.8.rest_2_, ...), custom_call_target="tpu_custom_call" | custom-call | tf_op jit(solution)/shard_map/store/pallas_call | solution.py:340
  (2 shorter events, 0.0 us)
Async XLA Ops:
  1.9 8.0 %collective-permute-start = (bf16[2,32,256]{2,1,0:T(8,128)(2,1)S(1)}, bf16[2,32,256]{2,1,0:T(8,128)(2,1)S(1)}, u32[]{:S(2)}, u32[]{:S(2)}) collective-permute-start(bf16[2,32,256]{2,1,0:T(8,128)(2,1)S(1)} %get-tuple-element.35), channel_id=1, source_target_pairs={{0,1},{1,2},{2,3},{3,0},{4,5},{5,6},{6,7},{7,4},{8,9},{9,10},{10,1... | collective-permute-start | bytes 98312 | tf_op jit(solution)/shard_map/ppermute | solution.py:356
  5.0 7.8 %collective-permute-start.1 = (bf16[2,32,256]{2,1,0:T(8,128)(2,1)S(1)}, bf16[2,32,256]{2,1,0:T(8,128)(2,1)S(1)}, u32[]{:S(2)}, u32[]{:S(2)}) collective-permute-start(bf16[2,32,256]{2,1,0:T(8,128)(2,1)S(1)} %get-tuple-element.36), channel_id=1, source_target_pairs={{0,2},{1,3},{2,0},{3,1},{4,6},{5,7},{6,4},{7,5},{8,10},{9,11},{10,... | collective-permute-start | bytes 98312 | tf_op jit(solution)/shard_map/ppermute | solution.py:356
  7.6 6.0 %collective-permute-start.2 = (bf16[2,32,256]{2,1,0:T(8,128)(2,1)S(1)}, bf16[2,32,256]{2,1,0:T(8,128)(2,1)S(1)}, u32[]{:S(2)}, u32[]{:S(2)}) collective-permute-start(bf16[2,32,256]{2,1,0:T(8,128)(2,1)S(1)} %get-tuple-element.37), channel_id=1, source_target_pairs={{0,3},{1,0},{2,1},{3,2},{4,7},{5,4},{6,5},{7,6},{8,11},{9,8},{10,9... | collective-permute-start | bytes 98312 | tf_op jit(solution)/shard_map/ppermute | solution.py:356
  8.9 9.1 %collective-permute-start.3 = (bf16[8,32,256]{2,1,0:T(8,128)(2,1)S(1)}, bf16[8,32,256]{2,1,0:T(8,128)(2,1)S(1)}, u32[]{:S(2)}, u32[]{:S(2)}) collective-permute-start(bf16[8,32,256]{2,1,0:T(8,128)(2,1)S(1)} %get-tuple-element.40), channel_id=1, source_target_pairs={{0,1},{1,2},{2,3},{3,0},{4,5},{5,6},{6,7},{7,4},{8,9},{9,10},{10,1... | collective-permute-start | bytes 393224 | tf_op jit(solution)/shard_map/ppermute | solution.py:356
  9.6 10.9 %collective-permute-start.4 = (bf16[8,32,256]{2,1,0:T(8,128)(2,1)S(1)}, bf16[8,32,256]{2,1,0:T(8,128)(2,1)S(1)}, u32[]{:S(2)}, u32[]{:S(2)}) collective-permute-start(bf16[8,32,256]{2,1,0:T(8,128)(2,1)S(1)} %get-tuple-element.41), channel_id=1, source_target_pairs={{0,2},{1,3},{2,0},{3,1},{4,6},{5,7},{6,4},{7,5},{8,10},{9,11},{10,... | collective-permute-start | bytes 393224 | tf_op jit(solution)/shard_map/ppermute | solution.py:356
  9.9 11.2 %collective-permute-start.5 = (bf16[8,32,256]{2,1,0:T(8,128)(2,1)S(1)}, bf16[8,32,256]{2,1,0:T(8,128)(2,1)S(1)}, u32[]{:S(2)}, u32[]{:S(2)}) collective-permute-start(bf16[8,32,256]{2,1,0:T(8,128)(2,1)S(1)} %get-tuple-element.42), channel_id=1, source_target_pairs={{0,3},{1,0},{2,1},{3,2},{4,7},{5,4},{6,5},{7,6},{8,11},{9,8},{10,9... | collective-permute-start | bytes 393224 | tf_op jit(solution)/shard_map/ppermute | solution.py:356
  14.1 8.6 %collective-permute-start.6 = (bf16[2,128,256]{2,1,0:T(8,128)(2,1)S(1)}, bf16[2,128,256]{2,1,0:T(8,128)(2,1)S(1)}, u32[]{:S(2)}, u32[]{:S(2)}) collective-permute-start(bf16[2,128,256]{2,1,0:T(8,128)(2,1)S(1)} %edge.1.after.rest_4_), channel_id=1, source_target_pairs={{0,1},{1,0},{3,7},{7,3},{4,5},{5,4},{6,10},{10,6},{8,9},{9,8},{11,... | collective-permute-start | bytes 393224 | tf_op jit(solution)/shard_map/ppermute | solution.py:385
  30.9 14.1 %collective-permute-start.8 = (bf16[272,256]{1,0:T(8,128)(2,1)S(1)}, bf16[272,256]{1,0:T(8,128)(2,1)S(1)}, u32[]{:S(2)}, u32[]{:S(2)}) collective-permute-start(bf16[272,256]{1,0:T(8,128)(2,1)S(1)} %get-tuple-element.57), channel_id=1, source_target_pairs={{0,2},{1,3},{2,0},{3,1},{4,6},{5,7},{6,4},{7,5},{8,10},{9,11},{10,... | collective-permute-start | bytes 417800 | tf_op jit(solution)/shard_map/ppermute | solution.py:356
  34.1 7.8 %collective-permute-start.7 = (bf16[256,256]{1,0:T(8,128)(2,1)S(1)}, bf16[256,256]{1,0:T(8,128)(2,1)S(1)}, u32[]{:S(2)}, u32[]{:S(2)}) collective-permute-start(bf16[256,256]{1,0:T(8,128)(2,1)S(1)} %get-tuple-element.56), channel_id=1, source_target_pairs={{0,1},{1,2},{2,3},{3,0},{4,5},{5,6},{6,7},{7,4},{8,9},{9,10},{10,1... | collective-permute-start | bytes 393224 | tf_op jit(solution)/shard_map/ppermute | solution.py:356
  36.0 9.0 %collective-permute-start.9 = (bf16[256,256]{1,0:T(8,128)(2,1)S(1)}, bf16[256,256]{1,0:T(8,128)(2,1)S(1)}, u32[]{:S(2)}, u32[]{:S(2)}) collective-permute-start(bf16[256,256]{1,0:T(8,128)(2,1)S(1)} %get-tuple-element.58), channel_id=1, source_target_pairs={{0,3},{1,0},{2,1},{3,2},{4,7},{5,4},{6,5},{7,6},{8,11},{9,8},{10,9... | collective-permute-start | bytes 393224 | tf_op jit(solution)/shard_map/ppermute | solution.py:356

commit v6 on v5

--- a/solution.py
+++ b/solution.py
@@ -11,7 +11,6 @@
 HALO = 2
 LANES = 128
 GROUP = 256
-CHUNKS = 3
 AHEAD = 16
 VMEM_BYTES = 28 * 1024 * 1024
 
@@ -202,20 +201,28 @@
         here[b * size : (b + 1) * size, :] = normed[cells(s, r), :]
     queries = [jnp.dot(here[...], w_query[h], preferred_element_type=jnp.float32) for h in range(heads)]
     queries = [query.astype(jnp.bfloat16) for query in queries]
-    for b, (s, r) in enumerate(blocks):
+    key_at = lax.broadcasted_iota(jnp.int32, (cols, width), 0)
+    scale = math.log2(math.e) / head_dim**0.5
+    shares = {}
+
+    def score(b, r):
         own = jnp.concatenate([query[b * size : (b + 1) * size] for query in queries], axis=0)
         scores[b] = by_last(keys[r * cols : (r + 1) * cols, :], own)
-    key_at = lax.broadcasted_iota(jnp.int32, (cols, width), 0)
-    scale = math.log2(math.e) / head_dim**0.5
-    shares = []
-    for b, (s, r) in enumerate(blocks):
+
+    def weigh(b, r):
         part = jnp.where(key_at < limits[r], scores[b], -jnp.inf)
         part = jnp.exp2((part - jnp.max(part, axis=0, keepdims=True)) * scale)
-        shares.append(1.0 / jnp.sum(part, axis=0, keepdims=True))
+        shares[b] = 1.0 / jnp.sum(part, axis=0, keepdims=True)
         expo[b] = part.astype(jnp.bfloat16)
-    for b, (s, r) in enumerate(blocks):
+
+    def add_up(b, r):
         summed = jnp.dot(values[:, r * cols : (r + 1) * cols], expo[b], preferred_element_type=jnp.float32)
         turned[:, b * width : (b + 1) * width] = (summed * shares[b]).astype(jnp.bfloat16)
+
+    for turn_at in range(len(blocks) + 4):
+        for lag, step in ((0, score), (2, weigh), (4, add_up)):
+            if 0 <= turn_at - lag < len(blocks):
+                step(turn_at - lag, blocks[turn_at - lag][1])
     attended = turned[...].T
     update = jnp.zeros(here.shape, jnp.float32)
     for h in range(heads):
@@ -245,33 +252,44 @@
     grid[pl.ds(HALO + (rows - HALO) * odd, HALO)] = sent[...]
     grid[pl.ds((rows + HALO) * odd, HALO)] = received[...]
     limits = [live_count(counts, first_row - 1 + r) for r in range(rows + HALO)]
-    total = rows + HALO
-    chunks = min(CHUNKS, total // HALO)
-    cuts = [-(-total * i // chunks) for i in range(chunks + 1)]
-    done = low = 0
-    for start, stop in zip(cuts, cuts[1:]):
-        for r in range(done, stop + HALO):
+
+    def spread_inputs(start, stop):
+        for r in range(start, stop):
             spread(taps, r, grid[r].astype(jnp.float32))
-        done = stop + HALO
-        act = silu(convolve(taps, w_conv1, b_conv1, start, stop - start))
+
+    def spread_acts(start, stop, product):
+        act = silu(product)
         for r in range(start, stop):
             at = slice((r - start) * cols, (r - start + 1) * cols)
             spread(acts, r, jnp.where(cell < limits[r], act[at], 0.0))
-        high = stop - HALO
-        if high <= low:
-            continue
-        second = convolve(acts, w_conv2, b_conv2, low, high - low)
-        for r in range(low, high):
-            here = grid[r + HALO].astype(jnp.float32) + second[(r - low) * cols : (r - low + 1) * cols]
+
+    def mix(start, stop, product):
+        for r in range(start, stop):
+            here = grid[r + HALO].astype(jnp.float32) + product[(r - start) * cols : (r - start + 1) * cols]
             here = jnp.where(cell < limits[r + 1], here, 0.0)
             mixed[r * cols : (r + 1) * cols, :] = here.astype(jnp.bfloat16)
-        at = slice(low * cols, high * cols)
+        at = slice(start * cols, stop * cols)
         flat = mixed[at, :].astype(jnp.float32)
         scaled = (flat * lax.rsqrt(jnp.mean(flat * flat, axis=1, keepdims=True) + 1e-06)).astype(jnp.bfloat16)
         normed[at, :] = scaled
         keys[at, :] = jnp.dot(scaled, w_key[...], preferred_element_type=jnp.float32).astype(jnp.bfloat16)
         values[:, at] = by_last(w_value[...], scaled).astype(jnp.bfloat16)
-        low = high
+
+    total = rows + HALO
+    half = total // 2
+    low = half - HALO
+    spread_inputs(0, half + HALO)
+    first_low = convolve(taps, w_conv1, b_conv1, 0, half)
+    spread_inputs(half + HALO, total + HALO)
+    first_high = convolve(taps, w_conv1, b_conv1, half, total - half)
+    spread_acts(0, half, first_low)
+    if low:
+        second_low = convolve(acts, w_conv2, b_conv2, 0, low)
+    spread_acts(half, total, first_high)
+    second_high = convolve(acts, w_conv2, b_conv2, low, rows - low)
+    if low:
+        mix(0, low, second_low)
+    mix(low, rows, second_high)
     limits = limits[1 : rows + 1]
     result[rows * (cols // n) :, :] = jnp.zeros((AHEAD, chans), result.dtype)
     segments = [owner[lax.rem(me + first, n), band]]

time: 46.7 us -> 44.7 us (0.957)
  Pallas kernels: 17.4 us -> 15 us
    pallas_call x6, Pallas kernels: 17.4 us -> 15 us  [call(): pl.pallas_call(functools.partial(kernel, n, rows), out_shape=out, in_spec...]
  transfers between devices with their start and end apart: 10 -> 10, of which waited for: 6 -> 6; matrix products, arithmetic and copies ran while one was open for 0% -> 0% of each run, Pallas kernels for 12% -> 14%
where the time goes in v6:
time: 44.7 us; the launch traced here: 44.6 us
  starting transfers between devices  16.7 us (37%)
  Pallas kernels  15 us (34%)
  waiting for transfers between devices  12.9 us (29%)
    pallas_call x6, Pallas kernels, call(): pl.pallas_call(functools.partial(kernel, n, rows), out_shape=out, in_spec...  15 us
    ppermute x9, starting transfers between devices, around_by(): return lax.ppermute(x, 'lon', [(i, (i + d) % n) for i in range(n)])  14.8 us
    ppermute x9, waiting for transfers between devices, around_by(): return lax.ppermute(x, 'lon', [(i, (i + d) % n) for i in range(n)])  10.8 us
    ppermute x1, waiting for transfers between devices, on_device(): received = lax.ppermute(sent, ('lat', 'lon'), pairs)  2.06 us
    ppermute x1, starting transfers between devices, on_device(): received = lax.ppermute(sent, ('lat', 'lon'), pairs)  1.92 us
  transfers between devices with their start and end apart: 10, of which 6 were waited for; matrix products, arithmetic and copies ran while one was open for 0% of the time, Pallas kernels for 14%

profile of v6, /device:TPU:0, one launch (start us, length us, event | category | flops | bytes accessed | tf_op | source)
XLA Modules:
  0.0 44.6 jit_solution(435609278361675306)
XLA Ops:
  0.0 1.4 %send.1 = (bf16[2,32,256]{2,1,0:T(8,128)(2,1)S(1)}, bf16[2,32,256]{2,1,0:T(8,128)(2,1)S(1)}, bf16[2,32,256]{2,1,0:T(8,128)(2,1)S(1)}, bf16[2,32,256]{2,1,0:T(8,1...) custom-call(s32[4,8]{1,0:T(4,128)} %bitcast.12, ...), custom_call_target="tpu_custom_call" | custom-call | tf_op jit(solution)/shard_map/send/pallas_call | solution.py:358
  1.4 3.1 %collective-permute-start = (bf16[2,32,256]{2,1,0:T(8,128)(2,1)S(1)}, bf16[2,32,256]{2,1,0:T(8,128)(2,1)S(1)}, u32[]{:S(2)}, u32[]{:S(2)}) collective-permute-start(bf16[2,32,256]{2,1,0:T(8,128)(2,1)S(1)} %get-tuple-element.35), channel_id=1, source_target_pairs={{0,1},{1,2},{2,3},{3,0},{4,5},{5,6},{6,7},{7,4},{8,9},{9,10},{10,1... | collective-permute-start | bytes 98312 | tf_op jit(solution)/shard_map/ppermute | solution.py:374
  4.5 3.0 %collective-permute-start.1 = (bf16[2,32,256]{2,1,0:T(8,128)(2,1)S(1)}, bf16[2,32,256]{2,1,0:T(8,128)(2,1)S(1)}, u32[]{:S(2)}, u32[]{:S(2)}) collective-permute-start(bf16[2,32,256]{2,1,0:T(8,128)(2,1)S(1)} %get-tuple-element.36), channel_id=1, source_target_pairs={{0,2},{1,3},{2,0},{3,1},{4,6},{5,7},{6,4},{7,5},{8,10},{9,11},{10,... | collective-permute-start | bytes 98312 | tf_op jit(solution)/shard_map/ppermute | solution.py:374
  7.6 0.9 %collective-permute-start.2 = (bf16[2,32,256]{2,1,0:T(8,128)(2,1)S(1)}, bf16[2,32,256]{2,1,0:T(8,128)(2,1)S(1)}, u32[]{:S(2)}, u32[]{:S(2)}) collective-permute-start(bf16[2,32,256]{2,1,0:T(8,128)(2,1)S(1)} %get-tuple-element.37), channel_id=1, source_target_pairs={{0,3},{1,0},{2,1},{3,2},{4,7},{5,4},{6,5},{7,6},{8,11},{9,8},{10,9... | collective-permute-start | bytes 98312 | tf_op jit(solution)/shard_map/ppermute | solution.py:374
  8.5 1.1 %collective-permute-start.3 = (bf16[8,32,256]{2,1,0:T(8,128)(2,1)S(1)}, bf16[8,32,256]{2,1,0:T(8,128)(2,1)S(1)}, u32[]{:S(2)}, u32[]{:S(2)}) collective-permute-start(bf16[8,32,256]{2,1,0:T(8,128)(2,1)S(1)} %get-tuple-element.40), channel_id=1, source_target_pairs={{0,1},{1,2},{2,3},{3,0},{4,5},{5,6},{6,7},{7,4},{8,9},{9,10},{10,1... | collective-permute-start | bytes 393224 | tf_op jit(solution)/shard_map/ppermute | solution.py:374
  9.6 0.0 collective-permute-start.4
  9.6 0.0 collective-permute-done.rest_1_
  9.6 2.7 %collective-permute-start.5 = (bf16[8,32,256]{2,1,0:T(8,128)(2,1)S(1)}, bf16[8,32,256]{2,1,0:T(8,128)(2,1)S(1)}, u32[]{:S(2)}, u32[]{:S(2)}) collective-permute-start(bf16[8,32,256]{2,1,0:T(8,128)(2,1)S(1)} %get-tuple-element.42), channel_id=1, source_target_pairs={{0,3},{1,0},{2,1},{3,2},{4,7},{5,4},{6,5},{7,6},{8,11},{9,8},{10,9... | collective-permute-start | bytes 393224 | tf_op jit(solution)/shard_map/ppermute | solution.py:374
  12.3 1.2 %collective-permute-done.2.rest_3_ = bf16[2,32,256]{2,1,0:T(8,128)(2,1)S(1)} collective-permute-done((bf16[2,32,256]{2,1,0:T(8,128)(2,1)S(1)}, bf16[2,32,256]{2,1,0:T(8,128)(2,1)S(1)}, u32[]{:S(2)}, u32[]{:S(2)}) %collective-permute-start.2) | collective-permute-done | bytes 32800 | tf_op jit(solution)/shard_map/ppermute | solution.py:374
  13.5 0.6 %edge.1.after.rest_4_ = bf16[2,128,256]{2,1,0:T(8,128)(2,1)S(1)} custom-call(s32[4,8]{1,0:T(4,128)S(1)} %get-tuple-element.33.owner, bf16[2,32,256]{2,1,0:T(8,128)(2,1)S(1)} %get-tuple-element.34.rest_0_, bf16[2,32,256]{2,1,0:T(8,128)(2,1)S(1)} %collective-permute-done.rest_1_, bf16[2,32,256]{2,1,0:T(8,128)(2,1)S(1)} %collective-permute-done.1.rest_2_, ...), custom_call_target="tpu_custom_call" | custom-call | tf_op jit(solution)/shard_map/edge/pallas_call | solution.py:358
  14.1 1.9 %collective-permute-start.6 = (bf16[2,128,256]{2,1,0:T(8,128)(2,1)S(1)}, bf16[2,128,256]{2,1,0:T(8,128)(2,1)S(1)}, u32[]{:S(2)}, u32[]{:S(2)}) collective-permute-start(bf16[2,128,256]{2,1,0:T(8,128)(2,1)S(1)} %edge.1.after.rest_4_), channel_id=1, source_target_pairs={{0,1},{1,0},{3,7},{7,3},{4,5},{5,4},{6,10},{10,6},{8,9},{9,8},{11,... | collective-permute-start | bytes 393224 | tf_op jit(solution)/shard_map/ppermute | solution.py:403
  16.1 2.0 %load.1 = (s32[256]{0:T(256)S(1)}, bf16[3,768,256]{2,1,0:T(8,128)(2,1)S(1)}, f32[1,256]{1,0:T(1,128)S(1)}, bf16[3,768,256]{2,1,0:T(8,128)(2,1)S(1)}, f32[1,256]{...) custom-call(bf16[2,128,256]{2,1,0:T(8,128)(2,1)S(1)} %edge.1.after.r, ...), custom_call_target="tpu_custom_call" | custom-call | tf_op jit(solution)/shard_map/load/pallas_call | solution.py:358
  18.1 2.5 %collective-permute-done.4.rest_2_ = bf16[8,32,256]{2,1,0:T(8,128)(2,1)S(1)} collective-permute-done((bf16[8,32,256]{2,1,0:T(8,128)(2,1)S(1)}, bf16[8,32,256]{2,1,0:T(8,128)(2,1)S(1)}, u32[]{:S(2)}, u32[]{:S(2)}) %collective-permute-start.4) | collective-permute-done | bytes 131104 | tf_op jit(solution)/shard_map/ppermute | solution.py:374
  20.5 0.1 collective-permute-done.5.rest_3_
  20.7 2.1 %collective-permute-done.6.rest_5_ = bf16[2,128,256]{2,1,0:T(8,128)(2,1)S(1)} collective-permute-done((bf16[2,128,256]{2,1,0:T(8,128)(2,1)S(1)}, bf16[2,128,256]{2,1,0:T(8,128)(2,1)S(1)}, u32[]{:S(2)}, u32[]{:S(2)}) %collective-permute-start.6) | collective-permute-done | bytes 131104 | tf_op jit(solution)/shard_map/ppermute | solution.py:403
  22.7 5.9 %main.1 = (bf16[272,256]{1,0:T(8,128)(2,1)S(1)}, bf16[1024,256]{1,0:T(8,128)(2,1)S(1)}, bf16[1024,256]{1,0:T(8,128)(2,1)S(1)}, bf16[1024,64]{1,0:T(8,128)(2,1)S(1)}, bf16[64,1024]{1,0:T(8,128)(2,1)S(1)}) custom-call(s32[4,8]{1,0:T(4,128)S(1)} %get-tuple-element.33.owner, s32[256]{0:T(256)S(1)} %get-tuple-element.38.counts, ...), custom_call_target="tpu_custom_call" | custom-call | tf_op jit(solution)/shard_map/main/pallas_call | solution.py:358
  28.6 0.1 collective-permute-start.8
  28.7 3.5 %rest.1 = (bf16[256,256]{1,0:T(8,128)(2,1)S(1)}, bf16[256,256]{1,0:T(8,128)(2,1)S(1)}, bf16[256,256]{1,0:T(8,128)(2,1)S(1)}) custom-call(s32[4,8]{1,0:T(4,128)S(1)} %get-tuple-element.33.owner, s32[256]{0:T(256)S(1)} %get-tuple-element.38.counts, bf16[1024,256]{1,0:T(8,128)(2,1)S(1)} %get-tuple-element.51.rest_0_, ...), custom_call_target="tpu_custom_call" | custom-call | tf_op jit(solution)/shard_map/rest/pallas_call | solution.py:358
  32.2 1.9 %collective-permute-start.7 = (bf16[256,256]{1,0:T(8,128)(2,1)S(1)}, bf16[256,256]{1,0:T(8,128)(2,1)S(1)}, u32[]{:S(2)}, u32[]{:S(2)}) collective-permute-start(bf16[256,256]{1,0:T(8,128)(2,1)S(1)} %get-tuple-element.56), channel_id=1, source_target_pairs={{0,1},{1,2},{2,3},{3,0},{4,5},{5,6},{6,7},{7,4},{8,9},{9,10},{10,1... | collective-permute-start | bytes 393224 | tf_op jit(solution)/shard_map/ppermute | solution.py:374
  34.2 1.9 %collective-permute-start.9 = (bf16[256,256]{1,0:T(8,128)(2,1)S(1)}, bf16[256,256]{1,0:T(8,128)(2,1)S(1)}, u32[]{:S(2)}, u32[]{:S(2)}) collective-permute-start(bf16[256,256]{1,0:T(8,128)(2,1)S(1)} %get-tuple-element.58), channel_id=1, source_target_pairs={{0,3},{1,0},{2,1},{3,2},{4,7},{5,4},{6,5},{7,6},{8,11},{9,8},{10,9... | collective-permute-start | bytes 393224 | tf_op jit(solution)/shard_map/ppermute | solution.py:374
  36.1 4.2 %collective-permute-done.7.rest_1_ = bf16[256,256]{1,0:T(8,128)(2,1)S(1)} collective-permute-done((bf16[256,256]{1,0:T(8,128)(2,1)S(1)}, bf16[256,256]{1,0:T(8,128)(2,1)S(1)}, u32[]{:S(2)}, u32[]{:S(2)}) %collective-permute-start.7) | collective-permute-done | bytes 131104 | tf_op jit(solution)/shard_map/ppermute | solution.py:374
  40.3 2.8 %collective-permute-done.9.rest_3_ = bf16[256,256]{1,0:T(8,128)(2,1)S(1)} collective-permute-done((bf16[256,256]{1,0:T(8,128)(2,1)S(1)}, bf16[256,256]{1,0:T(8,128)(2,1)S(1)}, u32[]{:S(2)}, u32[]{:S(2)}) %collective-permute-start.9) | collective-permute-done | bytes 131104 | tf_op jit(solution)/shard_map/ppermute | solution.py:374
  43.1 0.0 collective-permute-done.8.rest_2_
  43.1 1.5 %store.1 = bf16[32,32,256]{2,1,0:T(8,128)(2,1)} custom-call(s32[4,8]{1,0:T(4,128)S(1)} %get-tuple-element.32.rotation, bf16[256,256]{1,0:T(8,128)(2,1)S(1)} %get-tuple-element.55.rest_0_, bf16[256,256]{1,0:T(8,128)(2,1)S(1)} %collective-permute-done.7.rest_1_, bf16[272,256]{1,0:T(8,128)(2,1)S(1)} %collective-permute-done.8.rest_2_, ...), custom_call_target="tpu_custom_call" | custom-call | tf_op jit(solution)/shard_map/store/pallas_call | solution.py:358
  (2 shorter events, 0.0 us)
Async XLA Ops:
  1.4 8.2 %collective-permute-start = (bf16[2,32,256]{2,1,0:T(8,128)(2,1)S(1)}, bf16[2,32,256]{2,1,0:T(8,128)(2,1)S(1)}, u32[]{:S(2)}, u32[]{:S(2)}) collective-permute-start(bf16[2,32,256]{2,1,0:T(8,128)(2,1)S(1)} %get-tuple-element.35), channel_id=1, source_target_pairs={{0,1},{1,2},{2,3},{3,0},{4,5},{5,6},{6,7},{7,4},{8,9},{9,10},{10,1... | collective-permute-start | bytes 98312 | tf_op jit(solution)/shard_map/ppermute | solution.py:374
  4.5 7.8 %collective-permute-start.1 = (bf16[2,32,256]{2,1,0:T(8,128)(2,1)S(1)}, bf16[2,32,256]{2,1,0:T(8,128)(2,1)S(1)}, u32[]{:S(2)}, u32[]{:S(2)}) collective-permute-start(bf16[2,32,256]{2,1,0:T(8,128)(2,1)S(1)} %get-tuple-element.36), channel_id=1, source_target_pairs={{0,2},{1,3},{2,0},{3,1},{4,6},{5,7},{6,4},{7,5},{8,10},{9,11},{10,... | collective-permute-start | bytes 98312 | tf_op jit(solution)/shard_map/ppermute | solution.py:374
  7.6 6.0 %collective-permute-start.2 = (bf16[2,32,256]{2,1,0:T(8,128)(2,1)S(1)}, bf16[2,32,256]{2,1,0:T(8,128)(2,1)S(1)}, u32[]{:S(2)}, u32[]{:S(2)}) collective-permute-start(bf16[2,32,256]{2,1,0:T(8,128)(2,1)S(1)} %get-tuple-element.37), channel_id=1, source_target_pairs={{0,3},{1,0},{2,1},{3,2},{4,7},{5,4},{6,5},{7,6},{8,11},{9,8},{10,9... | collective-permute-start | bytes 98312 | tf_op jit(solution)/shard_map/ppermute | solution.py:374
  8.5 9.6 %collective-permute-start.3 = (bf16[8,32,256]{2,1,0:T(8,128)(2,1)S(1)}, bf16[8,32,256]{2,1,0:T(8,128)(2,1)S(1)}, u32[]{:S(2)}, u32[]{:S(2)}) collective-permute-start(bf16[8,32,256]{2,1,0:T(8,128)(2,1)S(1)} %get-tuple-element.40), channel_id=1, source_target_pairs={{0,1},{1,2},{2,3},{3,0},{4,5},{5,6},{6,7},{7,4},{8,9},{9,10},{10,1... | collective-permute-start | bytes 393224 | tf_op jit(solution)/shard_map/ppermute | solution.py:374
  9.6 10.9 %collective-permute-start.4 = (bf16[8,32,256]{2,1,0:T(8,128)(2,1)S(1)}, bf16[8,32,256]{2,1,0:T(8,128)(2,1)S(1)}, u32[]{:S(2)}, u32[]{:S(2)}) collective-permute-start(bf16[8,32,256]{2,1,0:T(8,128)(2,1)S(1)} %get-tuple-element.41), channel_id=1, source_target_pairs={{0,2},{1,3},{2,0},{3,1},{4,6},{5,7},{6,4},{7,5},{8,10},{9,11},{10,... | collective-permute-start | bytes 393224 | tf_op jit(solution)/shard_map/ppermute | solution.py:374
  9.6 11.1 %collective-permute-start.5 = (bf16[8,32,256]{2,1,0:T(8,128)(2,1)S(1)}, bf16[8,32,256]{2,1,0:T(8,128)(2,1)S(1)}, u32[]{:S(2)}, u32[]{:S(2)}) collective-permute-start(bf16[8,32,256]{2,1,0:T(8,128)(2,1)S(1)} %get-tuple-element.42), channel_id=1, source_target_pairs={{0,3},{1,0},{2,1},{3,2},{4,7},{5,4},{6,5},{7,6},{8,11},{9,8},{10,9... | collective-permute-start | bytes 393224 | tf_op jit(solution)/shard_map/ppermute | solution.py:374
  14.1 8.6 %collective-permute-start.6 = (bf16[2,128,256]{2,1,0:T(8,128)(2,1)S(1)}, bf16[2,128,256]{2,1,0:T(8,128)(2,1)S(1)}, u32[]{:S(2)}, u32[]{:S(2)}) collective-permute-start(bf16[2,128,256]{2,1,0:T(8,128)(2,1)S(1)} %edge.1.after.rest_4_), channel_id=1, source_target_pairs={{0,1},{1,0},{3,7},{7,3},{4,5},{5,4},{6,10},{10,6},{8,9},{9,8},{11,... | collective-permute-start | bytes 393224 | tf_op jit(solution)/shard_map/ppermute | solution.py:403
  28.6 14.5 %collective-permute-start.8 = (bf16[272,256]{1,0:T(8,128)(2,1)S(1)}, bf16[272,256]{1,0:T(8,128)(2,1)S(1)}, u32[]{:S(2)}, u32[]{:S(2)}) collective-permute-start(bf16[272,256]{1,0:T(8,128)(2,1)S(1)} %get-tuple-element.57), channel_id=1, source_target_pairs={{0,2},{1,3},{2,0},{3,1},{4,6},{5,7},{6,4},{7,5},{8,10},{9,11},{10,... | collective-permute-start | bytes 417800 | tf_op jit(solution)/shard_map/ppermute | solution.py:374
  32.2 8.1 %collective-permute-start.7 = (bf16[256,256]{1,0:T(8,128)(2,1)S(1)}, bf16[256,256]{1,0:T(8,128)(2,1)S(1)}, u32[]{:S(2)}, u32[]{:S(2)}) collective-permute-start(bf16[256,256]{1,0:T(8,128)(2,1)S(1)} %get-tuple-element.56), channel_id=1, source_target_pairs={{0,1},{1,2},{2,3},{3,0},{4,5},{5,6},{6,7},{7,4},{8,9},{9,10},{10,1... | collective-permute-start | bytes 393224 | tf_op jit(solution)/shard_map/ppermute | solution.py:374
  34.2 8.9 %collective-permute-start.9 = (bf16[256,256]{1,0:T(8,128)(2,1)S(1)}, bf16[256,256]{1,0:T(8,128)(2,1)S(1)}, u32[]{:S(2)}, u32[]{:S(2)}) collective-permute-start(bf16[256,256]{1,0:T(8,128)(2,1)S(1)} %get-tuple-element.58), channel_id=1, source_target_pairs={{0,3},{1,0},{2,1},{3,2},{4,7},{5,4},{6,5},{7,6},{8,11},{9,8},{10,9... | collective-permute-start | bytes 393224 | tf_op jit(solution)/shard_map/ppermute | solution.py:374

commit v7 on v6

--- a/solution.py
+++ b/solution.py
@@ -87,9 +87,15 @@
                 done(i // depth)
 
 
+def parts(rows):
+    if rows > 2 * HALO:
+        return [(0, rows, HALO), (HALO, HALO, rows - HALO), (rows, 0, HALO)]
+    return [(0, rows, HALO), (HALO, 0, rows)]
+
+
 def send_kernel(n, rows, rotation_in, owner_in, fields, *rest):
-    edges, slabs, (rotation_out, owner_out) = rest[:n], rest[n : 2 * n], rest[2 * n : 2 * n + 2]
-    staged, block, upright, rotation, scalar_sems, sems = rest[2 * n + 2 :]
+    pieces, (rotation_out, owner_out) = rest[:-8], rest[-8:-6]
+    staged, block, upright, rotation, scalar_sems, sems = rest[-6:]
     band = lax.axis_index("lat")
     me = lax.axis_index("lon")
     depth = GROUP // fields.shape[0]
@@ -112,14 +118,18 @@
     for d in range(n):
         group = group_of(band, lax.rem(me + d, n), n)
         top, odd = first_held(group, rows), group % 2
-        edges[d][...] = upright[pl.ds(top + rows * odd, HALO)]
-        slabs[d][...] = upright[pl.ds(top + HALO * (1 - odd), rows)]
+        for slab, (even_at, odd_at, count) in zip(pieces[d::n], parts(rows)):
+            slab[...] = upright[pl.ds(top + jnp.where(odd == 0, even_at, odd_at), count)]
     scalars[1].wait()
     scalars[2].wait()
 
 
 def load_kernel(n, rows, after, *refs):
     del after
+    passed = n - 1 if rows > 2 * HALO else 0
+    for i in range(passed):
+        refs[len(refs) - 3 - passed + i][...] = refs[i][...]
+    refs = refs[passed : len(refs) - 3 - passed] + refs[-3:]
     count = (len(refs) - 7) // 2
     direct, (query, key) = refs[:count], refs[count : count + 2]
     loaded, (w_query, w_key) = refs[count + 2 : 2 * count + 2], refs[2 * count + 2 : 2 * count + 4]
@@ -201,28 +211,20 @@
         here[b * size : (b + 1) * size, :] = normed[cells(s, r), :]
     queries = [jnp.dot(here[...], w_query[h], preferred_element_type=jnp.float32) for h in range(heads)]
     queries = [query.astype(jnp.bfloat16) for query in queries]
+    for b, (s, r) in enumerate(blocks):
+        own = jnp.concatenate([query[b * size : (b + 1) * size] for query in queries], axis=0)
+        scores[b] = by_last(keys[r * cols : (r + 1) * cols, :], own)
     key_at = lax.broadcasted_iota(jnp.int32, (cols, width), 0)
     scale = math.log2(math.e) / head_dim**0.5
-    shares = {}
-
-    def score(b, r):
-        own = jnp.concatenate([query[b * size : (b + 1) * size] for query in queries], axis=0)
-        scores[b] = by_last(keys[r * cols : (r + 1) * cols, :], own)
-
-    def weigh(b, r):
+    shares = []
+    for b, (s, r) in enumerate(blocks):
         part = jnp.where(key_at < limits[r], scores[b], -jnp.inf)
         part = jnp.exp2((part - jnp.max(part, axis=0, keepdims=True)) * scale)
-        shares[b] = 1.0 / jnp.sum(part, axis=0, keepdims=True)
+        shares.append(1.0 / jnp.sum(part, axis=0, keepdims=True))
         expo[b] = part.astype(jnp.bfloat16)
-
-    def add_up(b, r):
+    for b, (s, r) in enumerate(blocks):
         summed = jnp.dot(values[:, r * cols : (r + 1) * cols], expo[b], preferred_element_type=jnp.float32)
         turned[:, b * width : (b + 1) * width] = (summed * shares[b]).astype(jnp.bfloat16)
-
-    for turn_at in range(len(blocks) + 4):
-        for lag, step in ((0, score), (2, weigh), (4, add_up)):
-            if 0 <= turn_at - lag < len(blocks):
-                step(turn_at - lag, blocks[turn_at - lag][1])
     attended = turned[...].T
     update = jnp.zeros(here.shape, jnp.float32)
     for h in range(heads):
@@ -294,6 +296,108 @@
     result[rows * (cols // n) :, :] = jnp.zeros((AHEAD, chans), result.dtype)
     segments = [owner[lax.rem(me + first, n), band]]
     attend(segments, limits, mixed, normed, keys, values, w_query, w_out, [result], *scratch)
+
+
+def mix(start, stop, product, grid_row, limits, mixed, normed, keys, values, w_key, w_value):
+    cols = product.shape[0] // (stop - start)
+    cell = lax.broadcasted_iota(jnp.int32, (cols, product.shape[1]), 0)
+    for r in range(start, stop):
+        here = grid_row(r).astype(jnp.float32) + product[(r - start) * cols : (r - start + 1) * cols]
+        here = jnp.where(cell < limits[r], here, 0.0)
+        mixed[r * cols : (r + 1) * cols, :] = here.astype(jnp.bfloat16)
+    at = slice(start * cols, stop * cols)
+    flat = mixed[at, :].astype(jnp.float32)
+    scaled = (flat * lax.rsqrt(jnp.mean(flat * flat, axis=1, keepdims=True) + 1e-06)).astype(jnp.bfloat16)
+    normed[at, :] = scaled
+    keys[at, :] = jnp.dot(scaled, w_key[...], preferred_element_type=jnp.float32).astype(jnp.bfloat16)
+    values[:, at] = by_last(w_value[...], scaled).astype(jnp.bfloat16)
+
+
+def activate(start, stop, product, limits, acts, at):
+    cols = product.shape[0] // (stop - start)
+    cell = lax.broadcasted_iota(jnp.int32, (cols, product.shape[1]), 0)
+    act = silu(product)
+    for r in range(start, stop):
+        here = act[(r - start) * cols : (r - start + 1) * cols]
+        spread(acts, r - start + at, jnp.where(cell < limits[r], here, 0.0))
+
+
+def inner_kernel(n, rows, owner, counts, *rest):
+    slabs, (sent, w_conv1, b_conv1, w_conv2, b_conv2, w_key, w_value) = rest[:n], rest[n : n + 7]
+    edge_taps, edge_acts, mixed, normed, keys, values = rest[n + 7 : n + 13]
+    grid, taps, acts = rest[n + 13 :]
+    band = lax.axis_index("lat")
+    group = group_of(band, lax.axis_index("lon"), n)
+    odd = group % 2
+    first_row = band * (rows * n) + group * rows
+    whole_rows(n, owner, slabs, grid, HALO * (1 - odd))
+    grid[pl.ds((rows - HALO) * odd, HALO)] = sent[...]
+    limits = [counts[first_row + 1 + r] for r in range(rows - HALO)]
+    half = rows // 2 - 1
+    last = rows - HALO
+
+    def spread_inputs(start, stop):
+        for r in range(start, stop):
+            spread(taps, r, grid[r].astype(jnp.float32))
+
+    def mix_rows(start, stop, product):
+        row = lambda r: grid[r + HALO]
+        mix(start, stop, product, row, limits[1:], mixed, normed, keys, values, w_key, w_value)
+
+    spread_inputs(0, half + HALO)
+    first_low = convolve(taps, w_conv1, b_conv1, 0, half)
+    spread_inputs(half + HALO, rows)
+    first_high = convolve(taps, w_conv1, b_conv1, half, last - half)
+    activate(0, half, first_low, limits, acts, 0)
+    edge_taps[:HALO] = taps[:HALO]
+    edge_taps[HALO:] = taps[rows - HALO :]
+    activate(half, last, first_high, limits, acts, half)
+    second = convolve(acts, w_conv2, b_conv2, 0, last - HALO)
+    edge_acts[:HALO] = acts[:HALO]
+    edge_acts[HALO:] = acts[last - HALO :]
+    mix_rows(0, last - HALO, second)
+
+
+def outer_kernel(first, n, rows, owner, counts, *rest):
+    slabs, (received, edge_taps, edge_acts, *inner), rest = rest[:n], rest[n : n + 7], rest[n + 7 :]
+    w_conv1, b_conv1, w_conv2, b_conv2, w_key, w_value, w_query, w_out = rest[:8]
+    result, mixed, normed, keys, values, ends, taps, acts, *scratch = rest[8:]
+    band = lax.axis_index("lat")
+    me = lax.axis_index("lon")
+    group = group_of(band, me, n)
+    odd = group % 2
+    cols, chans = ends.shape[1:]
+    first_row = band * (rows * n) + group * rows
+    limits = [live_count(counts, first_row - 1 + r) for r in range(rows + HALO)]
+    low, high = HALO * cols, (rows - HALO) * cols
+    whole_rows(n, owner, slabs, ends, HALO * (1 - odd))
+    ends[pl.ds(HALO * odd, HALO)] = received[...]
+    tops = [0, 1, 6, 7]
+    taps[HALO : 3 * HALO] = edge_taps[...]
+    acts[HALO : 3 * HALO] = edge_acts[...]
+
+    def mix_rows(start, product, at):
+        row = lambda r: taps[r - start + at, :, chans : 2 * chans]
+        mix(start, start + HALO, product, row, limits[1:], mixed, normed, keys, values, w_key, w_value)
+
+    for r in range(HALO):
+        spread(taps, tops[r], ends[r].astype(jnp.float32))
+    first_top = convolve(taps, w_conv1, b_conv1, 0, HALO)
+    for r in range(HALO, 2 * HALO):
+        spread(taps, tops[r], ends[r].astype(jnp.float32))
+    first_end = convolve(taps, w_conv1, b_conv1, 2 * HALO, HALO)
+    activate(0, HALO, first_top, limits, acts, 0)
+    second_top = convolve(acts, w_conv2, b_conv2, 0, HALO)
+    activate(rows, rows + HALO, first_end, limits, acts, 3 * HALO)
+    second_end = convolve(acts, w_conv2, b_conv2, 2 * HALO, HALO)
+    for whole, part in zip((mixed, normed, keys), inner):
+        whole[low:high, :] = part[...]
+    values[:, low:high] = inner[3][...]
+    mix_rows(0, second_top, HALO)
+    mix_rows(rows - HALO, second_end, 2 * HALO)
+    result[rows * (cols // n) :, :] = jnp.zeros((AHEAD, chans), result.dtype)
+    segments = [owner[lax.rem(me + first, n), band]]
+    attend(segments, limits[1 : rows + 1], mixed, normed, keys, values, w_query, w_out, [result], *scratch)
 
 
 def rest_kernel(moves, n, rows, owner, counts, *rest):
@@ -353,12 +457,13 @@
     params = pltpu.CompilerParams(vmem_limit_bytes=VMEM_BYTES)
     pieces = size * size // GROUP
 
-    def call(kernel, name, out, scalars, arrays, scratch, array_spec=vmem, scalar_spec=smem, out_spec=vmem):
+    def call(kernel, name, out, scalars, arrays, scratch, array_spec=vmem, scalar_spec=smem, out_spec=vmem, in_place=None):
         many = isinstance(out, list)
+        specs = [array_spec if in_place is None or i >= in_place else vmem for i in range(len(arrays))]
         return pl.pallas_call(
             functools.partial(kernel, n, rows),
             out_shape=out,
-            in_specs=[scalar_spec] * len(scalars) + [array_spec] * len(arrays),
+            in_specs=[scalar_spec] * len(scalars) + specs,
             out_specs=[out_spec] * len(out) if many else out_spec,
             scratch_shapes=scratch,
             compiler_params=params,
@@ -389,13 +494,14 @@
     staging = pltpu.VMEM((chans // LANES, size * (size + 8), LANES), jnp.float32)
     block = pltpu.VMEM((size, size, chans), bf16)
 
-    slabs = [array(HALO, size, chans)] * n + [array(rows, size, chans)] * n
+    slabs = [array(count, size, chans) for *_, count in parts(rows) for _ in range(n)]
     scratch = [staging, block, block, pltpu.SMEM(rotation.shape, rotation.dtype)]
     scratch += [pltpu.SemaphoreType.DMA((3,)), pltpu.SemaphoreType.DMA((pieces,))]
     held = slabs + [pltpu.VMEM(x.shape, x.dtype) for x in (rotation, owner)]
     *slabs, rotation, owner = call(send_kernel, "send", held, [rotation, owner], [in_hbm(fields)], scratch, hbm, hbm)
-    edges = around(slabs[:n])
-    slabs = around(slabs[n:])
+    edges, *slabs = [slabs[i : i + n] for i in range(0, len(slabs), n)]
+    edges = around(edges)
+    slabs[0] = around(slabs[0])
 
     snake = [a * n + shard_of(a, g, n) for a in range(bands) for g in range(n)]
     pairs = [(snake[i], snake[i + 1 if i % 2 else i - 1]) for i in range(1, bands * n - 1)]
@@ -407,8 +513,13 @@
     held = [pltpu.VMEM(x.shape, x.dtype) for x in loaded]
     held += [pltpu.VMEM((heads, chans, head_dim), bf16), pltpu.VMEM(w_key.shape, bf16)]
     scratch = [pltpu.VMEM(x.shape, bf16) for x in turned] + [pltpu.SemaphoreType.DMA((len(loaded) + 2,))]
-    loaded = call(load_kernel, "load", held, [sent], loaded + turned, scratch, hbm, hbm)
+    passed = [x for late in slabs[1:] for x in late[1:]]
+    held += [array(*x.shape) for x in passed]
+    loaded = call(load_kernel, "load", held, [sent], passed + loaded + turned, scratch, hbm, hbm, in_place=len(passed))
+    loaded, passed = loaded[: len(loaded) - len(passed)], loaded[len(loaded) - len(passed) :]
     counts, *convs, w_value, w_out, w_query, w_key = loaded
+    if passed:
+        slabs[1] = around([slabs[1][0], *passed])
 
     def taps(count):
         return pltpu.VMEM((count, cols, 3 * chans), bf16)
@@ -422,18 +533,46 @@
             pltpu.VMEM((head_dim, blocks * width), bf16),
         ]
 
-    cells = rows * cols
     result = array(rows * size, chans)
     first, *others = [*order, 0]
     results = {}
-    results[first], *held = call(
-        functools.partial(main_kernel, first),
-        "main",
-        [array(rows * size + AHEAD, chans), array(cells, chans), array(cells, chans), array(cells, head_dim), array(head_dim, cells)],
-        [owner, counts],
-        slabs + [sent, received, *convs, w_key, w_value, w_query, w_out],
-        [pltpu.VMEM((rows + 2 * HALO, cols, chans), bf16), taps(rows + 2 * HALO), taps(rows + HALO)] + working(1),
-    )
+    message = array(rows * size + AHEAD, chans)
+
+    def kept(count):
+        cells = count * cols
+        return [array(cells, chans), array(cells, chans), array(cells, head_dim), array(head_dim, cells)]
+
+    def window(count):
+        return pltpu.VMEM((count, cols, chans), bf16)
+
+    attention = [w_key, w_value, w_query, w_out]
+    if len(slabs) == 1:
+        results[first], *held = call(
+            functools.partial(main_kernel, first),
+            "main",
+            [message] + kept(rows),
+            [owner, counts],
+            slabs[0] + [sent, received, *convs, *attention],
+            [window(rows + 2 * HALO), taps(rows + 2 * HALO), taps(rows + HALO)] + working(1),
+        )
+    else:
+        ends = array(2 * HALO, cols, 3 * chans)
+        inner = call(
+            inner_kernel,
+            "inner",
+            [ends, ends] + kept(rows - 2 * HALO),
+            [owner, counts],
+            slabs[0] + [sent, *convs, w_key, w_value],
+            [window(rows), taps(rows), taps(rows - HALO)],
+        )
+        results[first], *held = call(
+            functools.partial(outer_kernel, first),
+            "outer",
+            [message] + kept(rows),
+            [owner, counts],
+            slabs[1] + [received, *inner, *convs, *attention],
+            [window(2 * HALO), taps(4 * HALO), taps(4 * HALO)] + working(1),
+        )
     moved = {first: around_by(results[first], first)}
     rest = call(
         functools.partial(rest_kernel, others),

time: 44.7 us -> 46.7 us (1.045)
  starting transfers between devices: 16.7 us -> 23.5 us
  waiting for transfers between devices: 12.9 us -> 7.34 us
    ppermute x9 -> x12, starting transfers between devices: 14.8 us -> 19.8 us  [around_by(): return lax.ppermute(x, 'lon', [(i, (i + d) % n) for i in range(n)])]
    ppermute x9 -> x12, waiting for transfers between devices: 10.8 us -> 7.34 us  [around_by(): return lax.ppermute(x, 'lon', [(i, (i + d) % n) for i in range(n)])]
    ppermute x1, waiting for transfers between devices: 2.06 us -> 0.01 us  [on_device(): received = lax.ppermute(sent, ('lat', 'lon'), pairs)]
    ppermute x1, starting transfers between devices: 1.92 us -> 3.75 us  [on_device(): received = lax.ppermute(sent, ('lat', 'lon'), pairs)]
    pallas_call x6 -> x7, Pallas kernels: 15 us -> 15.4 us  [call(): pl.pallas_call(functools.partial(kernel, n, rows), out_shape=out, in_spec...]
  transfers between devices with their start and end apart: 10 -> 13, of which waited for: 6 -> 4; matrix products, arithmetic and copies ran while one was open for 0% -> 0% of each run, Pallas kernels for 14% -> 19%
where the time goes in v7:
time: 46.7 us; the launch traced here: 46.3 us
  starting transfers between devices  23.5 us (50%)
  Pallas kernels  15.4 us (33%)
  waiting for transfers between devices  7.34 us (16%)
    ppermute x12, starting transfers between devices, around_by(): return lax.ppermute(x, 'lon', [(i, (i + d) % n) for i in range(n)])  19.8 us
    pallas_call x7, Pallas kernels, call(): pl.pallas_call(functools.partial(kernel, n, rows), out_shape=out, in_spec...  15.4 us
    ppermute x12, waiting for transfers between devices, around_by(): return lax.ppermute(x, 'lon', [(i, (i + d) % n) for i in range(n)])  7.34 us
    ppermute x1, starting transfers between devices, on_device(): received = lax.ppermute(sent, ('lat', 'lon'), pairs)  3.75 us
  transfers between devices with their start and end apart: 13, of which 4 were waited for; matrix products, arithmetic and copies ran while one was open for 0% of the time, Pallas kernels for 19%

profile of v7, /device:TPU:0, one launch (start us, length us, event | category | flops | bytes accessed | tf_op | source)
XLA Modules:
  0.0 46.3 jit_solution(13997808912049085797)
XLA Ops:
  0.0 1.4 %send.1 = (bf16[2,32,256]{2,1,0:T(8,128)(2,1)S(1)}, bf16[2,32,256]{2,1,0:T(8,128)(2,1)S(1)}, bf16[2,32,256]{2,1,0:T(8,128)(2,1)S(1)}, bf16[2,32,256]{2,1,0:T(8,1...) custom-call(s32[4,8]{1,0:T(4,128)} %bitcast.12, ...), custom_call_target="tpu_custom_call" | custom-call | tf_op jit(solution)/shard_map/send/pallas_call | solution.py:463
  1.4 3.1 %collective-permute-start = (bf16[2,32,256]{2,1,0:T(8,128)(2,1)S(1)}, bf16[2,32,256]{2,1,0:T(8,128)(2,1)S(1)}, u32[]{:S(2)}, u32[]{:S(2)}) collective-permute-start(bf16[2,32,256]{2,1,0:T(8,128)(2,1)S(1)} %get-tuple-element.48), channel_id=1, source_target_pairs={{0,1},{1,2},{2,3},{3,0},{4,5},{5,6},{6,7},{7,4},{8,9},{9,10},{10,1... | collective-permute-start | bytes 98312 | tf_op jit(solution)/shard_map/ppermute | solution.py:479
  4.5 2.6 %collective-permute-start.1 = (bf16[2,32,256]{2,1,0:T(8,128)(2,1)S(1)}, bf16[2,32,256]{2,1,0:T(8,128)(2,1)S(1)}, u32[]{:S(2)}, u32[]{:S(2)}) collective-permute-start(bf16[2,32,256]{2,1,0:T(8,128)(2,1)S(1)} %get-tuple-element.49), channel_id=1, source_target_pairs={{0,2},{1,3},{2,0},{3,1},{4,6},{5,7},{6,4},{7,5},{8,10},{9,11},{10,... | collective-permute-start | bytes 98312 | tf_op jit(solution)/shard_map/ppermute | solution.py:479
  7.1 1.4 %collective-permute-start.2 = (bf16[2,32,256]{2,1,0:T(8,128)(2,1)S(1)}, bf16[2,32,256]{2,1,0:T(8,128)(2,1)S(1)}, u32[]{:S(2)}, u32[]{:S(2)}) collective-permute-start(bf16[2,32,256]{2,1,0:T(8,128)(2,1)S(1)} %get-tuple-element.50), channel_id=1, source_target_pairs={{0,3},{1,0},{2,1},{3,2},{4,7},{5,4},{6,5},{7,6},{8,11},{9,8},{10,9... | collective-permute-start | bytes 98312 | tf_op jit(solution)/shard_map/ppermute | solution.py:479
  8.5 0.7 %collective-permute-start.7 = (bf16[6,32,256]{2,1,0:T(8,128)(2,1)S(1)}, bf16[6,32,256]{2,1,0:T(8,128)(2,1)S(1)}, u32[]{:S(2)}, u32[]{:S(2)}) collective-permute-start(bf16[6,32,256]{2,1,0:T(8,128)(2,1)S(1)} %get-tuple-element.60), channel_id=1, source_target_pairs={{0,1},{1,2},{2,3},{3,0},{4,5},{5,6},{6,7},{7,4},{8,9},{9,10},{10,1... | collective-permute-start | bytes 294920 | tf_op jit(solution)/shard_map/ppermute | solution.py:479
  9.1 0.3 collective-permute-start.8
  9.5 0.2 collective-permute-done.1.rest_2_
  9.7 1.3 %collective-permute-done.2.rest_3_ = bf16[2,32,256]{2,1,0:T(8,128)(2,1)S(1)} collective-permute-done((bf16[2,32,256]{2,1,0:T(8,128)(2,1)S(1)}, bf16[2,32,256]{2,1,0:T(8,128)(2,1)S(1)}, u32[]{:S(2)}, u32[]{:S(2)}) %collective-permute-start.2) | collective-permute-done | bytes 32800 | tf_op jit(solution)/shard_map/ppermute | solution.py:479
  11.0 0.6 %edge.1.after.rest_4_ = bf16[2,128,256]{2,1,0:T(8,128)(2,1)S(1)} custom-call(s32[4,8]{1,0:T(4,128)S(1)} %get-tuple-element.46.owner, bf16[2,32,256]{2,1,0:T(8,128)(2,1)S(1)} %get-tuple-element.47.rest_0_, bf16[2,32,256]{2,1,0:T(8,128)(2,1)S(1)} %collective-permute-done.rest_1_, bf16[2,32,256]{2,1,0:T(8,128)(2,1)S(1)} %collective-permute-done.1.rest_2_, ...), custom_call_target="tpu_custom_call" | custom-call | tf_op jit(solution)/shard_map/edge/pallas_call | solution.py:463
  11.6 3.8 %collective-permute-start.6 = (bf16[2,128,256]{2,1,0:T(8,128)(2,1)S(1)}, bf16[2,128,256]{2,1,0:T(8,128)(2,1)S(1)}, u32[]{:S(2)}, u32[]{:S(2)}) collective-permute-start(bf16[2,128,256]{2,1,0:T(8,128)(2,1)S(1)} %edge.1.after.rest_4_), channel_id=1, source_target_pairs={{0,1},{1,0},{3,7},{7,3},{4,5},{5,4},{6,10},{10,6},{8,9},{9,8},{11,... | collective-permute-start | bytes 393224 | tf_op jit(solution)/shard_map/ppermute | solution.py:509
  15.4 1.9 %collective-permute-start.9 = (bf16[6,32,256]{2,1,0:T(8,128)(2,1)S(1)}, bf16[6,32,256]{2,1,0:T(8,128)(2,1)S(1)}, u32[]{:S(2)}, u32[]{:S(2)}) collective-permute-start(bf16[6,32,256]{2,1,0:T(8,128)(2,1)S(1)} %get-tuple-element.62), channel_id=1, source_target_pairs={{0,3},{1,0},{2,1},{3,2},{4,7},{5,4},{6,5},{7,6},{8,11},{9,8},{10,9... | collective-permute-start | bytes 294920 | tf_op jit(solution)/shard_map/ppermute | solution.py:479
  17.3 2.0 %load.1 = (s32[256]{0:T(256)S(1)}, bf16[3,768,256]{2,1,0:T(8,128)(2,1)S(1)}, f32[1,256]{1,0:T(1,128)S(1)}, bf16[3,768,256]{2,1,0:T(8,128)(2,1)S(1)}, f32[1,256]{...) custom-call(bf16[2,128,256]{2,1,0:T(8,128)(2,1)S(1)} %edge.1.after.r, ...), custom_call_target="tpu_custom_call" | custom-call | tf_op jit(solution)/shard_map/load/pallas_call | solution.py:463
  19.3 0.2 collective-permute-start.3
  19.5 0.4 collective-permute-start.4
  19.9 3.3 %collective-permute-start.5 = (bf16[2,32,256]{2,1,0:T(8,128)(2,1)S(1)}, bf16[2,32,256]{2,1,0:T(8,128)(2,1)S(1)}, u32[]{:S(2)}, u32[]{:S(2)}) collective-permute-start(bf16[2,32,256]{2,1,0:T(8,128)(2,1)S(1)} %get-tuple-element.58), channel_id=1, source_target_pairs={{0,3},{1,0},{2,1},{3,2},{4,7},{5,4},{6,5},{7,6},{8,11},{9,8},{10,9... | collective-permute-start | bytes 98312 | tf_op jit(solution)/shard_map/ppermute | solution.py:479
  23.2 3.2 %inner.1 = (bf16[4,128,768]{2,1,0:T(8,128)(2,1)S(1)}, bf16[4,128,768]{2,1,0:T(8,128)(2,1)S(1)}, bf16[512,256]{1,0:T(8,128)(2,1)S(1)}, bf16[512,256]{1,0:T(8,128)...) custom-call(s32[4,8]{1,0:T(4,128)S(1)} %get-tuple-element.46.owner, ...), custom_call_target="tpu_custom_call" | custom-call | tf_op jit(solution)/shard_map/inner/pallas_call | solution.py:463
  26.4 3.5 %outer.1 = (bf16[272,256]{1,0:T(8,128)(2,1)S(1)}, bf16[1024,256]{1,0:T(8,128)(2,1)S(1)}, bf16[1024,256]{1,0:T(8,128)(2,1)S(1)}, bf16[1024,64]{1,0:T(8,128)(2,1)S(1)}, bf16[64,1024]{1,0:T(8,128)(2,1)S(1)}) custom-call(s32[4,8]{1,0:T(4,128)S(1)} %get-tuple-element.46.owner, s32[256]{0:T(256)S(1)} %get-tuple-element.54.counts, ...), custom_call_target="tpu_custom_call" | custom-call | tf_op jit(solution)/shard_map/outer/pallas_call | solution.py:463
  30.0 2.0 %collective-permute-start.11 = (bf16[272,256]{1,0:T(8,128)(2,1)S(1)}, bf16[272,256]{1,0:T(8,128)(2,1)S(1)}, u32[]{:S(2)}, u32[]{:S(2)}) collective-permute-start(bf16[272,256]{1,0:T(8,128)(2,1)S(1)} %get-tuple-element.83), channel_id=1, source_target_pairs={{0,2},{1,3},{2,0},{3,1},{4,6},{5,7},{6,4},{7,5},{8,10},{9,11},{10,... | collective-permute-start | bytes 417800 | tf_op jit(solution)/shard_map/ppermute | solution.py:479
  32.0 3.1 %rest.1 = (bf16[256,256]{1,0:T(8,128)(2,1)S(1)}, bf16[256,256]{1,0:T(8,128)(2,1)S(1)}, bf16[256,256]{1,0:T(8,128)(2,1)S(1)}) custom-call(s32[4,8]{1,0:T(4,128)S(1)} %get-tuple-element.46.owner, s32[256]{0:T(256)S(1)} %get-tuple-element.54.counts, bf16[1024,256]{1,0:T(8,128)(2,1)S(1)} %get-tuple-element.77.rest_0_, ...), custom_call_target="tpu_custom_call" | custom-call | tf_op jit(solution)/shard_map/rest/pallas_call | solution.py:463
  35.1 1.1 %collective-permute-start.10 = (bf16[256,256]{1,0:T(8,128)(2,1)S(1)}, bf16[256,256]{1,0:T(8,128)(2,1)S(1)}, u32[]{:S(2)}, u32[]{:S(2)}) collective-permute-start(bf16[256,256]{1,0:T(8,128)(2,1)S(1)} %get-tuple-element.82), channel_id=1, source_target_pairs={{0,1},{1,2},{2,3},{3,0},{4,5},{5,6},{6,7},{7,4},{8,9},{9,10},{10,1... | collective-permute-start | bytes 393224 | tf_op jit(solution)/shard_map/ppermute | solution.py:479
  36.2 2.8 %collective-permute-start.12 = (bf16[256,256]{1,0:T(8,128)(2,1)S(1)}, bf16[256,256]{1,0:T(8,128)(2,1)S(1)}, u32[]{:S(2)}, u32[]{:S(2)}) collective-permute-start(bf16[256,256]{1,0:T(8,128)(2,1)S(1)} %get-tuple-element.84), channel_id=1, source_target_pairs={{0,3},{1,0},{2,1},{3,2},{4,7},{5,4},{6,5},{7,6},{8,11},{9,8},{10,9... | collective-permute-start | bytes 393224 | tf_op jit(solution)/shard_map/ppermute | solution.py:479
  39.0 4.0 %collective-permute-done.10.rest_1_ = bf16[256,256]{1,0:T(8,128)(2,1)S(1)} collective-permute-done((bf16[256,256]{1,0:T(8,128)(2,1)S(1)}, bf16[256,256]{1,0:T(8,128)(2,1)S(1)}, u32[]{:S(2)}, u32[]{:S(2)}) %collective-permute-start.10) | collective-permute-done | bytes 131104 | tf_op jit(solution)/shard_map/ppermute | solution.py:479
  43.0 1.8 %collective-permute-done.12.rest_3_ = bf16[256,256]{1,0:T(8,128)(2,1)S(1)} collective-permute-done((bf16[256,256]{1,0:T(8,128)(2,1)S(1)}, bf16[256,256]{1,0:T(8,128)(2,1)S(1)}, u32[]{:S(2)}, u32[]{:S(2)}) %collective-permute-start.12) | collective-permute-done | bytes 131104 | tf_op jit(solution)/shard_map/ppermute | solution.py:479
  44.8 1.5 %store.1 = bf16[32,32,256]{2,1,0:T(8,128)(2,1)} custom-call(s32[4,8]{1,0:T(4,128)S(1)} %get-tuple-element.45.rotation, bf16[256,256]{1,0:T(8,128)(2,1)S(1)} %get-tuple-element.81.rest_0_, bf16[256,256]{1,0:T(8,128)(2,1)S(1)} %collective-permute-done.10.rest_1_, bf16[272,256]{1,0:T(8,128)(2,1)S(1)} %collective-permute-done.11.rest_2_, ...), custom_call_target="tpu_custom_call" | custom-call | tf_op jit(solution)/shard_map/store/pallas_call | solution.py:463
  (9 shorter events, 0.0 us)
Async XLA Ops:
  1.4 8.0 %collective-permute-start = (bf16[2,32,256]{2,1,0:T(8,128)(2,1)S(1)}, bf16[2,32,256]{2,1,0:T(8,128)(2,1)S(1)}, u32[]{:S(2)}, u32[]{:S(2)}) collective-permute-start(bf16[2,32,256]{2,1,0:T(8,128)(2,1)S(1)} %get-tuple-element.48), channel_id=1, source_target_pairs={{0,1},{1,2},{2,3},{3,0},{4,5},{5,6},{6,7},{7,4},{8,9},{9,10},{10,1... | collective-permute-start | bytes 98312 | tf_op jit(solution)/shard_map/ppermute | solution.py:479
  4.5 5.2 %collective-permute-start.1 = (bf16[2,32,256]{2,1,0:T(8,128)(2,1)S(1)}, bf16[2,32,256]{2,1,0:T(8,128)(2,1)S(1)}, u32[]{:S(2)}, u32[]{:S(2)}) collective-permute-start(bf16[2,32,256]{2,1,0:T(8,128)(2,1)S(1)} %get-tuple-element.49), channel_id=1, source_target_pairs={{0,2},{1,3},{2,0},{3,1},{4,6},{5,7},{6,4},{7,5},{8,10},{9,11},{10,... | collective-permute-start | bytes 98312 | tf_op jit(solution)/shard_map/ppermute | solution.py:479
  7.1 3.9 %collective-permute-start.2 = (bf16[2,32,256]{2,1,0:T(8,128)(2,1)S(1)}, bf16[2,32,256]{2,1,0:T(8,128)(2,1)S(1)}, u32[]{:S(2)}, u32[]{:S(2)}) collective-permute-start(bf16[2,32,256]{2,1,0:T(8,128)(2,1)S(1)} %get-tuple-element.50), channel_id=1, source_target_pairs={{0,3},{1,0},{2,1},{3,2},{4,7},{5,4},{6,5},{7,6},{8,11},{9,8},{10,9... | collective-permute-start | bytes 98312 | tf_op jit(solution)/shard_map/ppermute | solution.py:479
  8.5 11.0 %collective-permute-start.7 = (bf16[6,32,256]{2,1,0:T(8,128)(2,1)S(1)}, bf16[6,32,256]{2,1,0:T(8,128)(2,1)S(1)}, u32[]{:S(2)}, u32[]{:S(2)}) collective-permute-start(bf16[6,32,256]{2,1,0:T(8,128)(2,1)S(1)} %get-tuple-element.60), channel_id=1, source_target_pairs={{0,1},{1,2},{2,3},{3,0},{4,5},{5,6},{6,7},{7,4},{8,9},{9,10},{10,1... | collective-permute-start | bytes 294920 | tf_op jit(solution)/shard_map/ppermute | solution.py:479
  9.1 10.8 %collective-permute-start.8 = (bf16[6,32,256]{2,1,0:T(8,128)(2,1)S(1)}, bf16[6,32,256]{2,1,0:T(8,128)(2,1)S(1)}, u32[]{:S(2)}, u32[]{:S(2)}) collective-permute-start(bf16[6,32,256]{2,1,0:T(8,128)(2,1)S(1)} %get-tuple-element.61), channel_id=1, source_target_pairs={{0,2},{1,3},{2,0},{3,1},{4,6},{5,7},{6,4},{7,5},{8,10},{9,11},{10,... | collective-permute-start | bytes 294920 | tf_op jit(solution)/shard_map/ppermute | solution.py:479
  11.6 14.8 %collective-permute-start.6 = (bf16[2,128,256]{2,1,0:T(8,128)(2,1)S(1)}, bf16[2,128,256]{2,1,0:T(8,128)(2,1)S(1)}, u32[]{:S(2)}, u32[]{:S(2)}) collective-permute-start(bf16[2,128,256]{2,1,0:T(8,128)(2,1)S(1)} %edge.1.after.rest_4_), channel_id=1, source_target_pairs={{0,1},{1,0},{3,7},{7,3},{4,5},{5,4},{6,10},{10,6},{8,9},{9,8},{11,... | collective-permute-start | bytes 393224 | tf_op jit(solution)/shard_map/ppermute | solution.py:509
  15.4 7.8 %collective-permute-start.9 = (bf16[6,32,256]{2,1,0:T(8,128)(2,1)S(1)}, bf16[6,32,256]{2,1,0:T(8,128)(2,1)S(1)}, u32[]{:S(2)}, u32[]{:S(2)}) collective-permute-start(bf16[6,32,256]{2,1,0:T(8,128)(2,1)S(1)} %get-tuple-element.62), channel_id=1, source_target_pairs={{0,3},{1,0},{2,1},{3,2},{4,7},{5,4},{6,5},{7,6},{8,11},{9,8},{10,9... | collective-permute-start | bytes 294920 | tf_op jit(solution)/shard_map/ppermute | solution.py:479
  19.3 7.1 %collective-permute-start.3 = (bf16[2,32,256]{2,1,0:T(8,128)(2,1)S(1)}, bf16[2,32,256]{2,1,0:T(8,128)(2,1)S(1)}, u32[]{:S(2)}, u32[]{:S(2)}) collective-permute-start(bf16[2,32,256]{2,1,0:T(8,128)(2,1)S(1)} %get-tuple-element.56), channel_id=1, source_target_pairs={{0,1},{1,2},{2,3},{3,0},{4,5},{5,6},{6,7},{7,4},{8,9},{9,10},{10,1... | collective-permute-start | bytes 98312 | tf_op jit(solution)/shard_map/ppermute | solution.py:479
  19.5 6.9 %collective-permute-start.4 = (bf16[2,32,256]{2,1,0:T(8,128)(2,1)S(1)}, bf16[2,32,256]{2,1,0:T(8,128)(2,1)S(1)}, u32[]{:S(2)}, u32[]{:S(2)}) collective-permute-start(bf16[2,32,256]{2,1,0:T(8,128)(2,1)S(1)} %get-tuple-element.57), channel_id=1, source_target_pairs={{0,2},{1,3},{2,0},{3,1},{4,6},{5,7},{6,4},{7,5},{8,10},{9,11},{10,... | collective-permute-start | bytes 98312 | tf_op jit(solution)/shard_map/ppermute | solution.py:479
  19.9 6.5 %collective-permute-start.5 = (bf16[2,32,256]{2,1,0:T(8,128)(2,1)S(1)}, bf16[2,32,256]{2,1,0:T(8,128)(2,1)S(1)}, u32[]{:S(2)}, u32[]{:S(2)}) collective-permute-start(bf16[2,32,256]{2,1,0:T(8,128)(2,1)S(1)} %get-tuple-element.58), channel_id=1, source_target_pairs={{0,3},{1,0},{2,1},{3,2},{4,7},{5,4},{6,5},{7,6},{8,11},{9,8},{10,9... | collective-permute-start | bytes 98312 | tf_op jit(solution)/shard_map/ppermute | solution.py:479
  30.0 14.8 %collective-permute-start.11 = (bf16[272,256]{1,0:T(8,128)(2,1)S(1)}, bf16[272,256]{1,0:T(8,128)(2,1)S(1)}, u32[]{:S(2)}, u32[]{:S(2)}) collective-permute-start(bf16[272,256]{1,0:T(8,128)(2,1)S(1)} %get-tuple-element.83), channel_id=1, source_target_pairs={{0,2},{1,3},{2,0},{3,1},{4,6},{5,7},{6,4},{7,5},{8,10},{9,11},{10,... | collective-permute-start | bytes 417800 | tf_op jit(solution)/shard_map/ppermute | solution.py:479
  35.1 7.9 %collective-permute-start.10 = (bf16[256,256]{1,0:T(8,128)(2,1)S(1)}, bf16[256,256]{1,0:T(8,128)(2,1)S(1)}, u32[]{:S(2)}, u32[]{:S(2)}) collective-permute-start(bf16[256,256]{1,0:T(8,128)(2,1)S(1)} %get-tuple-element.82), channel_id=1, source_target_pairs={{0,1},{1,2},{2,3},{3,0},{4,5},{5,6},{6,7},{7,4},{8,9},{9,10},{10,1... | collective-permute-start | bytes 393224 | tf_op jit(solution)/shard_map/ppermute | solution.py:479
  36.2 8.5 %collective-permute-start.12 = (bf16[256,256]{1,0:T(8,128)(2,1)S(1)}, bf16[256,256]{1,0:T(8,128)(2,1)S(1)}, u32[]{:S(2)}, u32[]{:S(2)}) collective-permute-start(bf16[256,256]{1,0:T(8,128)(2,1)S(1)} %get-tuple-element.84), channel_id=1, source_target_pairs={{0,3},{1,0},{2,1},{3,2},{4,7},{5,4},{6,5},{7,6},{8,11},{9,8},{10,9... | collective-permute-start | bytes 393224 | tf_op jit(solution)/shard_map/ppermute | solution.py:479

commit v8 on v6

--- a/solution.py
+++ b/solution.py
@@ -186,53 +186,47 @@
     return lax.dot_general(a, b, (((1,), (1,)), ((), ())), preferred_element_type=jnp.float32)
 
 
-def attend(segments, limits, mixed, normed, keys, values, w_query, w_out, results, here, scores, expo, turned):
+def attend(segments, span, limits, mixed, normed, keys, values, w_query, w_out, results, here, scores, expo, turned):
     rows, chans = len(limits), mixed.shape[1]
     size = here.shape[0] // (rows * len(segments))
     heads, _, head_dim = w_query.shape
     cols = mixed.shape[0] // rows
     width = heads * size
-    blocks = [(s, r) for s in range(len(segments)) for r in range(rows)]
+    blocks = [(s * rows + r, s, r) for s in range(len(segments)) for r in range(*span)]
+    low, high = blocks[0][0], blocks[-1][0] + 1
 
     def cells(s, r):
         return columns_of(segments[s] + r * (cols // size), size)
 
-    for b, (s, r) in enumerate(blocks):
+    for b, s, r in blocks:
         here[b * size : (b + 1) * size, :] = normed[cells(s, r), :]
-    queries = [jnp.dot(here[...], w_query[h], preferred_element_type=jnp.float32) for h in range(heads)]
+    own = here[low * size : high * size, :]
+    queries = [jnp.dot(own, w_query[h], preferred_element_type=jnp.float32) for h in range(heads)]
     queries = [query.astype(jnp.bfloat16) for query in queries]
+    for b, s, r in blocks:
+        part = [query[(b - low) * size : (b - low + 1) * size] for query in queries]
+        scores[b] = by_last(keys[r * cols : (r + 1) * cols, :], jnp.concatenate(part, axis=0))
     key_at = lax.broadcasted_iota(jnp.int32, (cols, width), 0)
     scale = math.log2(math.e) / head_dim**0.5
     shares = {}
-
-    def score(b, r):
-        own = jnp.concatenate([query[b * size : (b + 1) * size] for query in queries], axis=0)
-        scores[b] = by_last(keys[r * cols : (r + 1) * cols, :], own)
-
-    def weigh(b, r):
+    for b, s, r in blocks:
         part = jnp.where(key_at < limits[r], scores[b], -jnp.inf)
         part = jnp.exp2((part - jnp.max(part, axis=0, keepdims=True)) * scale)
         shares[b] = 1.0 / jnp.sum(part, axis=0, keepdims=True)
         expo[b] = part.astype(jnp.bfloat16)
-
-    def add_up(b, r):
+    for b, s, r in blocks:
         summed = jnp.dot(values[:, r * cols : (r + 1) * cols], expo[b], preferred_element_type=jnp.float32)
         turned[:, b * width : (b + 1) * width] = (summed * shares[b]).astype(jnp.bfloat16)
-
-    for turn_at in range(len(blocks) + 4):
-        for lag, step in ((0, score), (2, weigh), (4, add_up)):
-            if 0 <= turn_at - lag < len(blocks):
-                step(turn_at - lag, blocks[turn_at - lag][1])
-    attended = turned[...].T
-    update = jnp.zeros(here.shape, jnp.float32)
+    attended = turned[:, low * width : high * width].T
+    update = jnp.zeros(own.shape, jnp.float32)
     for h in range(heads):
-        starts = [b * width + h * size for b in range(len(blocks))]
+        starts = [(b - low) * width + h * size for b, *_ in blocks]
         part = jnp.concatenate([attended[start : start + size] for start in starts], axis=0)
         weight = w_out[h * head_dim : (h + 1) * head_dim, :]
         update = update + jnp.dot(part, weight, preferred_element_type=jnp.float32)
-    for b, (s, r) in enumerate(blocks):
+    for b, s, r in blocks:
         cell = segments[s] * size + lax.broadcasted_iota(jnp.int32, (size, chans), 0)
-        part = jnp.where(cell < limits[r], update[b * size : (b + 1) * size], 0.0)
+        part = jnp.where(cell < limits[r], update[(b - low) * size : (b - low + 1) * size], 0.0)
         results[s][r * size : (r + 1) * size, :] = (mixed[cells(s, r), :].astype(jnp.float32) + part).astype(jnp.bfloat16)
 
 
@@ -276,7 +270,7 @@
         values[:, at] = by_last(w_value[...], scaled).astype(jnp.bfloat16)
 
     total = rows + HALO
-    half = total // 2
+    half = total // 2 + total // 8
     low = half - HALO
     spread_inputs(0, half + HALO)
     first_low = convolve(taps, w_conv1, b_conv1, 0, half)
@@ -287,13 +281,18 @@
         second_low = convolve(acts, w_conv2, b_conv2, 0, low)
     spread_acts(half, total, first_high)
     second_high = convolve(acts, w_conv2, b_conv2, low, rows - low)
+    result[rows * (cols // n) :, :] = jnp.zeros((AHEAD, chans), result.dtype)
+    segments = [owner[lax.rem(me + first, n), band]]
+
+    def attend_rows(*span):
+        shared = limits[1 : rows + 1], mixed, normed, keys, values, w_query, w_out
+        attend(segments, span, *shared, [result], *scratch)
+
     if low:
         mix(0, low, second_low)
+        attend_rows(0, low)
     mix(low, rows, second_high)
-    limits = limits[1 : rows + 1]
-    result[rows * (cols // n) :, :] = jnp.zeros((AHEAD, chans), result.dtype)
-    segments = [owner[lax.rem(me + first, n), band]]
-    attend(segments, limits, mixed, normed, keys, values, w_query, w_out, [result], *scratch)
+    attend_rows(low, rows)
 
 
 def rest_kernel(moves, n, rows, owner, counts, *rest):
@@ -304,7 +303,7 @@
     first_row = band * (rows * n) + group_of(band, me, n) * rows
     limits = [counts[first_row + r] for r in range(rows)]
     segments = [owner[lax.rem(me + d, n), band] for d in moves]
-    attend(segments, limits, mixed, normed, keys, values, w_query, w_out, results, *scratch)
+    attend(segments, (0, rows), limits, mixed, normed, keys, values, w_query, w_out, results, *scratch)
 
 
 def store_kernel(n, rows, rotation, *rest):

time: 44.7 us -> 44.9 us (level)
    ppermute x1, starting transfers between devices: 1.92 us -> 2.48 us  [on_device(): received = lax.ppermute(sent, ('lat', 'lon'), pairs)]
    ppermute x9, starting transfers between devices: 14.8 us -> 14.3 us  [around_by(): return lax.ppermute(x, 'lon', [(i, (i + d) % n) for i in range(n)])]
  transfers between devices with their start and end apart: 10 -> 10, of which waited for: 6 -> 5; matrix products, arithmetic and copies ran while one was open for 0% -> 0% of each run, Pallas kernels for 14% -> 13%
where the time goes in v8:
time: 44.9 us; the launch traced here: 44.6 us
  starting transfers between devices  16.8 us (37%)
  Pallas kernels  15.2 us (34%)
  waiting for transfers between devices  12.5 us (28%)
    pallas_call x6, Pallas kernels, call(): pl.pallas_call(functools.partial(kernel, n, rows), out_shape=out, in_spec...  15.2 us
    ppermute x9, starting transfers between devices, around_by(): return lax.ppermute(x, 'lon', [(i, (i + d) % n) for i in range(n)])  14.3 us
    ppermute x9, waiting for transfers between devices, around_by(): return lax.ppermute(x, 'lon', [(i, (i + d) % n) for i in range(n)])  10.6 us
    ppermute x1, starting transfers between devices, on_device(): received = lax.ppermute(sent, ('lat', 'lon'), pairs)  2.48 us
    ppermute x1, waiting for transfers between devices, on_device(): received = lax.ppermute(sent, ('lat', 'lon'), pairs)  1.93 us
  transfers between devices with their start and end apart: 10, of which 5 were waited for; matrix products, arithmetic and copies ran while one was open for 0% of the time, Pallas kernels for 13%

profile of v8, /device:TPU:0, one launch (start us, length us, event | category | flops | bytes accessed | tf_op | source)
XLA Modules:
  0.0 44.6 jit_solution(9801654023324106568)
XLA Ops:
  0.0 1.9 %send.1 = (bf16[2,32,256]{2,1,0:T(8,128)(2,1)S(1)}, bf16[2,32,256]{2,1,0:T(8,128)(2,1)S(1)}, bf16[2,32,256]{2,1,0:T(8,128)(2,1)S(1)}, bf16[2,32,256]{2,1,0:T(8,1...) custom-call(s32[4,8]{1,0:T(4,128)} %bitcast.12, ...), custom_call_target="tpu_custom_call" | custom-call | tf_op jit(solution)/shard_map/send/pallas_call | solution.py:357
  1.9 2.4 %collective-permute-start = (bf16[2,32,256]{2,1,0:T(8,128)(2,1)S(1)}, bf16[2,32,256]{2,1,0:T(8,128)(2,1)S(1)}, u32[]{:S(2)}, u32[]{:S(2)}) collective-permute-start(bf16[2,32,256]{2,1,0:T(8,128)(2,1)S(1)} %get-tuple-element.35), channel_id=1, source_target_pairs={{0,1},{1,2},{2,3},{3,0},{4,5},{5,6},{6,7},{7,4},{8,9},{9,10},{10,1... | collective-permute-start | bytes 98312 | tf_op jit(solution)/shard_map/ppermute | solution.py:373
  4.3 2.8 %collective-permute-start.1 = (bf16[2,32,256]{2,1,0:T(8,128)(2,1)S(1)}, bf16[2,32,256]{2,1,0:T(8,128)(2,1)S(1)}, u32[]{:S(2)}, u32[]{:S(2)}) collective-permute-start(bf16[2,32,256]{2,1,0:T(8,128)(2,1)S(1)} %get-tuple-element.36), channel_id=1, source_target_pairs={{0,2},{1,3},{2,0},{3,1},{4,6},{5,7},{6,4},{7,5},{8,10},{9,11},{10,... | collective-permute-start | bytes 98312 | tf_op jit(solution)/shard_map/ppermute | solution.py:373
  7.1 1.4 %collective-permute-start.2 = (bf16[2,32,256]{2,1,0:T(8,128)(2,1)S(1)}, bf16[2,32,256]{2,1,0:T(8,128)(2,1)S(1)}, u32[]{:S(2)}, u32[]{:S(2)}) collective-permute-start(bf16[2,32,256]{2,1,0:T(8,128)(2,1)S(1)} %get-tuple-element.37), channel_id=1, source_target_pairs={{0,3},{1,0},{2,1},{3,2},{4,7},{5,4},{6,5},{7,6},{8,11},{9,8},{10,9... | collective-permute-start | bytes 98312 | tf_op jit(solution)/shard_map/ppermute | solution.py:373
  8.5 0.7 %collective-permute-start.3 = (bf16[8,32,256]{2,1,0:T(8,128)(2,1)S(1)}, bf16[8,32,256]{2,1,0:T(8,128)(2,1)S(1)}, u32[]{:S(2)}, u32[]{:S(2)}) collective-permute-start(bf16[8,32,256]{2,1,0:T(8,128)(2,1)S(1)} %get-tuple-element.40), channel_id=1, source_target_pairs={{0,1},{1,2},{2,3},{3,0},{4,5},{5,6},{6,7},{7,4},{8,9},{9,10},{10,1... | collective-permute-start | bytes 393224 | tf_op jit(solution)/shard_map/ppermute | solution.py:373
  9.1 0.1 collective-permute-start.4
  9.3 0.0 collective-permute-done.rest_1_
  9.3 3.0 %collective-permute-start.5 = (bf16[8,32,256]{2,1,0:T(8,128)(2,1)S(1)}, bf16[8,32,256]{2,1,0:T(8,128)(2,1)S(1)}, u32[]{:S(2)}, u32[]{:S(2)}) collective-permute-start(bf16[8,32,256]{2,1,0:T(8,128)(2,1)S(1)} %get-tuple-element.42), channel_id=1, source_target_pairs={{0,3},{1,0},{2,1},{3,2},{4,7},{5,4},{6,5},{7,6},{8,11},{9,8},{10,9... | collective-permute-start | bytes 393224 | tf_op jit(solution)/shard_map/ppermute | solution.py:373
  12.3 0.0 collective-permute-done.1.rest_2_
  12.3 0.6 %edge.1.after.rest_4_ = bf16[2,128,256]{2,1,0:T(8,128)(2,1)S(1)} custom-call(s32[4,8]{1,0:T(4,128)S(1)} %get-tuple-element.33.owner, bf16[2,32,256]{2,1,0:T(8,128)(2,1)S(1)} %get-tuple-element.34.rest_0_, bf16[2,32,256]{2,1,0:T(8,128)(2,1)S(1)} %collective-permute-done.rest_1_, bf16[2,32,256]{2,1,0:T(8,128)(2,1)S(1)} %collective-permute-done.1.rest_2_, ...), custom_call_target="tpu_custom_call" | custom-call | tf_op jit(solution)/shard_map/edge/pallas_call | solution.py:357
  12.9 2.5 %collective-permute-start.6 = (bf16[2,128,256]{2,1,0:T(8,128)(2,1)S(1)}, bf16[2,128,256]{2,1,0:T(8,128)(2,1)S(1)}, u32[]{:S(2)}, u32[]{:S(2)}) collective-permute-start(bf16[2,128,256]{2,1,0:T(8,128)(2,1)S(1)} %edge.1.after.rest_4_), channel_id=1, source_target_pairs={{0,1},{1,0},{3,7},{7,3},{4,5},{5,4},{6,10},{10,6},{8,9},{9,8},{11,... | collective-permute-start | bytes 393224 | tf_op jit(solution)/shard_map/ppermute | solution.py:402
  15.4 2.0 %load.1 = (s32[256]{0:T(256)S(1)}, bf16[3,768,256]{2,1,0:T(8,128)(2,1)S(1)}, f32[1,256]{1,0:T(1,128)S(1)}, bf16[3,768,256]{2,1,0:T(8,128)(2,1)S(1)}, f32[1,256]{...) custom-call(bf16[2,128,256]{2,1,0:T(8,128)(2,1)S(1)} %edge.1.after.r, ...), custom_call_target="tpu_custom_call" | custom-call | tf_op jit(solution)/shard_map/load/pallas_call | solution.py:357
  17.4 0.0 collective-permute-done.3.rest_1_
  17.4 3.1 %collective-permute-done.4.rest_2_ = bf16[8,32,256]{2,1,0:T(8,128)(2,1)S(1)} collective-permute-done((bf16[8,32,256]{2,1,0:T(8,128)(2,1)S(1)}, bf16[8,32,256]{2,1,0:T(8,128)(2,1)S(1)}, u32[]{:S(2)}, u32[]{:S(2)}) %collective-permute-start.4) | collective-permute-done | bytes 131104 | tf_op jit(solution)/shard_map/ppermute | solution.py:373
  20.5 0.2 collective-permute-done.5.rest_3_
  20.7 1.9 %collective-permute-done.6.rest_5_ = bf16[2,128,256]{2,1,0:T(8,128)(2,1)S(1)} collective-permute-done((bf16[2,128,256]{2,1,0:T(8,128)(2,1)S(1)}, bf16[2,128,256]{2,1,0:T(8,128)(2,1)S(1)}, u32[]{:S(2)}, u32[]{:S(2)}) %collective-permute-start.6) | collective-permute-done | bytes 131104 | tf_op jit(solution)/shard_map/ppermute | solution.py:402
  22.6 5.9 %main.1 = (bf16[272,256]{1,0:T(8,128)(2,1)S(1)}, bf16[1024,256]{1,0:T(8,128)(2,1)S(1)}, bf16[1024,256]{1,0:T(8,128)(2,1)S(1)}, bf16[1024,64]{1,0:T(8,128)(2,1)S(1)}, bf16[64,1024]{1,0:T(8,128)(2,1)S(1)}) custom-call(s32[4,8]{1,0:T(4,128)S(1)} %get-tuple-element.33.owner, s32[256]{0:T(256)S(1)} %get-tuple-element.38.counts, ...), custom_call_target="tpu_custom_call" | custom-call | tf_op jit(solution)/shard_map/main/pallas_call | solution.py:357
  28.5 0.1 collective-permute-start.8
  28.6 3.1 %rest.1 = (bf16[256,256]{1,0:T(8,128)(2,1)S(1)}, bf16[256,256]{1,0:T(8,128)(2,1)S(1)}, bf16[256,256]{1,0:T(8,128)(2,1)S(1)}) custom-call(s32[4,8]{1,0:T(4,128)S(1)} %get-tuple-element.33.owner, s32[256]{0:T(256)S(1)} %get-tuple-element.38.counts, bf16[1024,256]{1,0:T(8,128)(2,1)S(1)} %get-tuple-element.51.rest_0_, ...), custom_call_target="tpu_custom_call" | custom-call | tf_op jit(solution)/shard_map/rest/pallas_call | solution.py:357
  31.7 2.1 %collective-permute-start.7 = (bf16[256,256]{1,0:T(8,128)(2,1)S(1)}, bf16[256,256]{1,0:T(8,128)(2,1)S(1)}, u32[]{:S(2)}, u32[]{:S(2)}) collective-permute-start(bf16[256,256]{1,0:T(8,128)(2,1)S(1)} %get-tuple-element.56), channel_id=1, source_target_pairs={{0,1},{1,2},{2,3},{3,0},{4,5},{5,6},{6,7},{7,4},{8,9},{9,10},{10,1... | collective-permute-start | bytes 393224 | tf_op jit(solution)/shard_map/ppermute | solution.py:373
  33.8 1.8 %collective-permute-start.9 = (bf16[256,256]{1,0:T(8,128)(2,1)S(1)}, bf16[256,256]{1,0:T(8,128)(2,1)S(1)}, u32[]{:S(2)}, u32[]{:S(2)}) collective-permute-start(bf16[256,256]{1,0:T(8,128)(2,1)S(1)} %get-tuple-element.58), channel_id=1, source_target_pairs={{0,3},{1,0},{2,1},{3,2},{4,7},{5,4},{6,5},{7,6},{8,11},{9,8},{10,9... | collective-permute-start | bytes 393224 | tf_op jit(solution)/shard_map/ppermute | solution.py:373
  35.6 4.1 %collective-permute-done.7.rest_1_ = bf16[256,256]{1,0:T(8,128)(2,1)S(1)} collective-permute-done((bf16[256,256]{1,0:T(8,128)(2,1)S(1)}, bf16[256,256]{1,0:T(8,128)(2,1)S(1)}, u32[]{:S(2)}, u32[]{:S(2)}) %collective-permute-start.7) | collective-permute-done | bytes 131104 | tf_op jit(solution)/shard_map/ppermute | solution.py:373
  39.7 3.2 %collective-permute-done.9.rest_3_ = bf16[256,256]{1,0:T(8,128)(2,1)S(1)} collective-permute-done((bf16[256,256]{1,0:T(8,128)(2,1)S(1)}, bf16[256,256]{1,0:T(8,128)(2,1)S(1)}, u32[]{:S(2)}, u32[]{:S(2)}) %collective-permute-start.9) | collective-permute-done | bytes 131104 | tf_op jit(solution)/shard_map/ppermute | solution.py:373
  42.9 1.7 %store.1 = bf16[32,32,256]{2,1,0:T(8,128)(2,1)} custom-call(s32[4,8]{1,0:T(4,128)S(1)} %get-tuple-element.32.rotation, bf16[256,256]{1,0:T(8,128)(2,1)S(1)} %get-tuple-element.55.rest_0_, bf16[256,256]{1,0:T(8,128)(2,1)S(1)} %collective-permute-done.7.rest_1_, bf16[272,256]{1,0:T(8,128)(2,1)S(1)} %collective-permute-done.8.rest_2_, ...), custom_call_target="tpu_custom_call" | custom-call | tf_op jit(solution)/shard_map/store/pallas_call | solution.py:357
  (2 shorter events, 0.0 us)
Async XLA Ops:
  1.9 7.4 %collective-permute-start = (bf16[2,32,256]{2,1,0:T(8,128)(2,1)S(1)}, bf16[2,32,256]{2,1,0:T(8,128)(2,1)S(1)}, u32[]{:S(2)}, u32[]{:S(2)}) collective-permute-start(bf16[2,32,256]{2,1,0:T(8,128)(2,1)S(1)} %get-tuple-element.35), channel_id=1, source_target_pairs={{0,1},{1,2},{2,3},{3,0},{4,5},{5,6},{6,7},{7,4},{8,9},{9,10},{10,1... | collective-permute-start | bytes 98312 | tf_op jit(solution)/shard_map/ppermute | solution.py:373
  4.3 8.0 %collective-permute-start.1 = (bf16[2,32,256]{2,1,0:T(8,128)(2,1)S(1)}, bf16[2,32,256]{2,1,0:T(8,128)(2,1)S(1)}, u32[]{:S(2)}, u32[]{:S(2)}) collective-permute-start(bf16[2,32,256]{2,1,0:T(8,128)(2,1)S(1)} %get-tuple-element.36), channel_id=1, source_target_pairs={{0,2},{1,3},{2,0},{3,1},{4,6},{5,7},{6,4},{7,5},{8,10},{9,11},{10,... | collective-permute-start | bytes 98312 | tf_op jit(solution)/shard_map/ppermute | solution.py:373
  7.1 5.2 %collective-permute-start.2 = (bf16[2,32,256]{2,1,0:T(8,128)(2,1)S(1)}, bf16[2,32,256]{2,1,0:T(8,128)(2,1)S(1)}, u32[]{:S(2)}, u32[]{:S(2)}) collective-permute-start(bf16[2,32,256]{2,1,0:T(8,128)(2,1)S(1)} %get-tuple-element.37), channel_id=1, source_target_pairs={{0,3},{1,0},{2,1},{3,2},{4,7},{5,4},{6,5},{7,6},{8,11},{9,8},{10,9... | collective-permute-start | bytes 98312 | tf_op jit(solution)/shard_map/ppermute | solution.py:373
  8.5 8.9 %collective-permute-start.3 = (bf16[8,32,256]{2,1,0:T(8,128)(2,1)S(1)}, bf16[8,32,256]{2,1,0:T(8,128)(2,1)S(1)}, u32[]{:S(2)}, u32[]{:S(2)}) collective-permute-start(bf16[8,32,256]{2,1,0:T(8,128)(2,1)S(1)} %get-tuple-element.40), channel_id=1, source_target_pairs={{0,1},{1,2},{2,3},{3,0},{4,5},{5,6},{6,7},{7,4},{8,9},{9,10},{10,1... | collective-permute-start | bytes 393224 | tf_op jit(solution)/shard_map/ppermute | solution.py:373
  9.1 11.4 %collective-permute-start.4 = (bf16[8,32,256]{2,1,0:T(8,128)(2,1)S(1)}, bf16[8,32,256]{2,1,0:T(8,128)(2,1)S(1)}, u32[]{:S(2)}, u32[]{:S(2)}) collective-permute-start(bf16[8,32,256]{2,1,0:T(8,128)(2,1)S(1)} %get-tuple-element.41), channel_id=1, source_target_pairs={{0,2},{1,3},{2,0},{3,1},{4,6},{5,7},{6,4},{7,5},{8,10},{9,11},{10,... | collective-permute-start | bytes 393224 | tf_op jit(solution)/shard_map/ppermute | solution.py:373
  9.3 11.4 %collective-permute-start.5 = (bf16[8,32,256]{2,1,0:T(8,128)(2,1)S(1)}, bf16[8,32,256]{2,1,0:T(8,128)(2,1)S(1)}, u32[]{:S(2)}, u32[]{:S(2)}) collective-permute-start(bf16[8,32,256]{2,1,0:T(8,128)(2,1)S(1)} %get-tuple-element.42), channel_id=1, source_target_pairs={{0,3},{1,0},{2,1},{3,2},{4,7},{5,4},{6,5},{7,6},{8,11},{9,8},{10,9... | collective-permute-start | bytes 393224 | tf_op jit(solution)/shard_map/ppermute | solution.py:373
  12.9 9.7 %collective-permute-start.6 = (bf16[2,128,256]{2,1,0:T(8,128)(2,1)S(1)}, bf16[2,128,256]{2,1,0:T(8,128)(2,1)S(1)}, u32[]{:S(2)}, u32[]{:S(2)}) collective-permute-start(bf16[2,128,256]{2,1,0:T(8,128)(2,1)S(1)} %edge.1.after.rest_4_), channel_id=1, source_target_pairs={{0,1},{1,0},{3,7},{7,3},{4,5},{5,4},{6,10},{10,6},{8,9},{9,8},{11,... | collective-permute-start | bytes 393224 | tf_op jit(solution)/shard_map/ppermute | solution.py:402
  28.5 14.4 %collective-permute-start.8 = (bf16[272,256]{1,0:T(8,128)(2,1)S(1)}, bf16[272,256]{1,0:T(8,128)(2,1)S(1)}, u32[]{:S(2)}, u32[]{:S(2)}) collective-permute-start(bf16[272,256]{1,0:T(8,128)(2,1)S(1)} %get-tuple-element.57), channel_id=1, source_target_pairs={{0,2},{1,3},{2,0},{3,1},{4,6},{5,7},{6,4},{7,5},{8,10},{9,11},{10,... | collective-permute-start | bytes 417800 | tf_op jit(solution)/shard_map/ppermute | solution.py:373
  31.7 8.0 %collective-permute-start.7 = (bf16[256,256]{1,0:T(8,128)(2,1)S(1)}, bf16[256,256]{1,0:T(8,128)(2,1)S(1)}, u32[]{:S(2)}, u32[]{:S(2)}) collective-permute-start(bf16[256,256]{1,0:T(8,128)(2,1)S(1)} %get-tuple-element.56), channel_id=1, source_target_pairs={{0,1},{1,2},{2,3},{3,0},{4,5},{5,6},{6,7},{7,4},{8,9},{9,10},{10,1... | collective-permute-start | bytes 393224 | tf_op jit(solution)/shard_map/ppermute | solution.py:373
  33.8 9.1 %collective-permute-start.9 = (bf16[256,256]{1,0:T(8,128)(2,1)S(1)}, bf16[256,256]{1,0:T(8,128)(2,1)S(1)}, u32[]{:S(2)}, u32[]{:S(2)}) collective-permute-start(bf16[256,256]{1,0:T(8,128)(2,1)S(1)} %get-tuple-element.58), channel_id=1, source_target_pairs={{0,3},{1,0},{2,1},{3,2},{4,7},{5,4},{6,5},{7,6},{8,11},{9,8},{10,9... | collective-permute-start | bytes 393224 | tf_op jit(solution)/shard_map/ppermute | solution.py:373

commit v9 on v8

--- a/solution.py
+++ b/solution.py
@@ -87,9 +87,10 @@
                 done(i // depth)
 
 
-def send_kernel(n, rows, rotation_in, owner_in, fields, *rest):
-    edges, slabs, (rotation_out, owner_out) = rest[:n], rest[n : 2 * n], rest[2 * n : 2 * n + 2]
-    staged, block, upright, rotation, scalar_sems, sems = rest[2 * n + 2 :]
+def send_kernel(first, n, rows, rotation_in, owner_in, fields, *rest):
+    edges = [*rest[:first], None, *rest[first : n - 1]]
+    slabs, (rotation_out, owner_out) = rest[n - 1 : 2 * n - 1], rest[2 * n - 1 : 2 * n + 1]
+    staged, block, upright, rotation, scalar_sems, sems = rest[2 * n + 1 :]
     band = lax.axis_index("lat")
     me = lax.axis_index("lon")
     depth = GROUP // fields.shape[0]
@@ -112,6 +113,9 @@
     for d in range(n):
         group = group_of(band, lax.rem(me + d, n), n)
         top, odd = first_held(group, rows), group % 2
+        if d == first:
+            slabs[d][...] = upright[pl.ds(top, rows + HALO)]
+            continue
         edges[d][...] = upright[pl.ds(top + rows * odd, HALO)]
         slabs[d][...] = upright[pl.ds(top + HALO * (1 - odd), rows)]
     scalars[1].wait()
@@ -140,18 +144,19 @@
     return pl.ds(pl.multiple_of(segment * size, size), size)
 
 
-def whole_rows(n, owner, slabs, out, first):
+def whole_rows(n, count, start, owner, slabs, out, first):
     band = lax.axis_index("lat")
     me = lax.axis_index("lon")
-    count, size = slabs[0].shape[:2]
-    for d in range(n):
+    size = slabs[0].shape[1]
+    for d, slab in enumerate(slabs):
         segment = owner[lax.rem(me + n - d, n), band]
-        out[pl.ds(first, count), columns_of(segment, size)] = slabs[d][...]
+        piece = slab[...] if slab.shape[0] == count else slab[pl.ds(start, count)]
+        out[pl.ds(first, count), columns_of(segment, size)] = piece
 
 
 def edge_kernel(n, rows, owner, *rest):
-    del rows
-    whole_rows(n, owner, rest[:n], rest[n], 0)
+    odd = group_of(lax.axis_index("lat"), lax.axis_index("lon"), n) % 2
+    whole_rows(n, HALO, rows * odd, owner, rest[:n], rest[n], 0)
 
 
 def spread(taps, r, row):
@@ -242,7 +247,7 @@
     cols, chans = sent.shape[1:]
     cell = lax.broadcasted_iota(jnp.int32, (cols, chans), 0)
     first_row = band * (rows * n) + group * rows
-    whole_rows(n, owner, slabs, grid, 2 * HALO * (1 - odd))
+    whole_rows(n, rows, HALO * (1 - odd), owner, slabs, grid, 2 * HALO * (1 - odd))
     grid[pl.ds(HALO + (rows - HALO) * odd, HALO)] = sent[...]
     grid[pl.ds((rows + HALO) * odd, HALO)] = received[...]
     limits = [live_count(counts, first_row - 1 + r) for r in range(rows + HALO)]
@@ -270,7 +275,7 @@
         values[:, at] = by_last(w_value[...], scaled).astype(jnp.bfloat16)
 
     total = rows + HALO
-    half = total // 2 + total // 8
+    half = total // 2
     low = half - HALO
     spread_inputs(0, half + HALO)
     first_low = convolve(taps, w_conv1, b_conv1, 0, half)
@@ -283,16 +288,11 @@
     second_high = convolve(acts, w_conv2, b_conv2, low, rows - low)
     result[rows * (cols // n) :, :] = jnp.zeros((AHEAD, chans), result.dtype)
     segments = [owner[lax.rem(me + first, n), band]]
-
-    def attend_rows(*span):
-        shared = limits[1 : rows + 1], mixed, normed, keys, values, w_query, w_out
-        attend(segments, span, *shared, [result], *scratch)
-
     if low:
         mix(0, low, second_low)
-        attend_rows(0, low)
     mix(low, rows, second_high)
-    attend_rows(low, rows)
+    shared = limits[1 : rows + 1], mixed, normed, keys, values, w_query, w_out
+    attend(segments, (0, rows), *shared, [result], *scratch)
 
 
 def rest_kernel(moves, n, rows, owner, counts, *rest):
@@ -388,13 +388,16 @@
     staging = pltpu.VMEM((chans // LANES, size * (size + 8), LANES), jnp.float32)
     block = pltpu.VMEM((size, size, chans), bf16)
 
-    slabs = [array(HALO, size, chans)] * n + [array(rows, size, chans)] * n
+    first = order[0]
+    slabs = [array(HALO, size, chans)] * (n - 1)
+    slabs += [array(rows + (HALO if d == first else 0), size, chans) for d in range(n)]
     scratch = [staging, block, block, pltpu.SMEM(rotation.shape, rotation.dtype)]
     scratch += [pltpu.SemaphoreType.DMA((3,)), pltpu.SemaphoreType.DMA((pieces,))]
     held = slabs + [pltpu.VMEM(x.shape, x.dtype) for x in (rotation, owner)]
-    *slabs, rotation, owner = call(send_kernel, "send", held, [rotation, owner], [in_hbm(fields)], scratch, hbm, hbm)
-    edges = around(slabs[:n])
-    slabs = around(slabs[n:])
+    *slabs, rotation, owner = call(functools.partial(send_kernel, first), "send", held, [rotation, owner], [in_hbm(fields)], scratch, hbm, hbm)
+    edges, slabs = slabs[: n - 1], around(slabs[n - 1 :])
+    edges.insert(first, slabs[first])
+    edges = [x if d in (0, first) else around_by(x, d) for d, x in enumerate(edges)]
 
     snake = [a * n + shard_of(a, g, n) for a in range(bands) for g in range(n)]
     pairs = [(snake[i], snake[i + 1 if i % 2 else i - 1]) for i in range(1, bands * n - 1)]

time: 44.9 us -> 46.6 us (1.038)
  starting transfers between devices: 16.8 us -> 18.9 us
  Pallas kernels: 15.2 us -> 14.1 us
  waiting for transfers between devices: 12.5 us -> 13.1 us
    ppermute x9 -> x8, starting transfers between devices: 14.3 us -> 15.7 us  [around_by(): return lax.ppermute(x, 'lon', [(i, (i + d) % n) for i in range(n)])]
    pallas_call x6, Pallas kernels: 15.2 us -> 14.1 us  [call(): pl.pallas_call(functools.partial(kernel, n, rows), out_shape=out, in_spec...]
    ppermute x9 -> x8, waiting for transfers between devices: 10.6 us -> 11.4 us  [around_by(): return lax.ppermute(x, 'lon', [(i, (i + d) % n) for i in range(n)])]
    ppermute x1, starting transfers between devices: 2.48 us -> 3.18 us  [on_device(): received = lax.ppermute(sent, ('lat', 'lon'), pairs)]
  transfers between devices with their start and end apart: 10 -> 9, of which waited for: 5 -> 5; matrix products, arithmetic and copies ran while one was open for 0% -> 0% of each run, Pallas kernels for 13% -> 12%
where the time goes in v9:
time: 46.6 us; the launch traced here: 46.1 us
  starting transfers between devices  18.9 us (41%)
  Pallas kernels  14.1 us (30%)
  waiting for transfers between devices  13.1 us (28%)
    ppermute x8, starting transfers between devices, around_by(): return lax.ppermute(x, 'lon', [(i, (i + d) % n) for i in range(n)])  15.7 us
    pallas_call x6, Pallas kernels, call(): pl.pallas_call(functools.partial(kernel, n, rows), out_shape=out, in_spec...  14.1 us
    ppermute x8, waiting for transfers between devices, around_by(): return lax.ppermute(x, 'lon', [(i, (i + d) % n) for i in range(n)])  11.4 us
    ppermute x1, starting transfers between devices, on_device(): received = lax.ppermute(sent, ('lat', 'lon'), pairs)  3.18 us
    ppermute x1, waiting for transfers between devices, on_device(): received = lax.ppermute(sent, ('lat', 'lon'), pairs)  1.66 us
  transfers between devices with their start and end apart: 9, of which 5 were waited for; matrix products, arithmetic and copies ran while one was open for 0% of the time, Pallas kernels for 12%

profile of v9, /device:TPU:0, one launch (start us, length us, event | category | flops | bytes accessed | tf_op | source)
XLA Modules:
  0.0 46.1 jit_solution(5827355654220435760)
XLA Ops:
  0.0 1.2 %send.1 = (bf16[2,32,256]{2,1,0:T(8,128)(2,1)S(1)}, bf16[2,32,256]{2,1,0:T(8,128)(2,1)S(1)}, bf16[2,32,256]{2,1,0:T(8,128)(2,1)S(1)}, bf16[8,32,256]{2,1,0:T(8,1...) custom-call(s32[4,8]{1,0:T(4,128)} %bitcast.12, ...), custom_call_target="tpu_custom_call" | custom-call | tf_op jit(solution)/shard_map/send/pallas_call | solution.py:357
  1.2 4.1 %collective-permute-start.1 = (bf16[10,32,256]{2,1,0:T(8,128)(2,1)S(1)}, bf16[10,32,256]{2,1,0:T(8,128)(2,1)S(1)}, u32[]{:S(2)}, u32[]{:S(2)}) collective-permute-start(bf16[10,32,256]{2,1,0:T(8,128)(2,1)S(1)} %get-tuple-element.35), channel_id=1, source_target_pairs={{0,2},{1,3},{2,0},{3,1},{4,6},{5,7},{6,4},{7,5},{8,10},{9,11},{10,... | collective-permute-start | bytes 491528 | tf_op jit(solution)/shard_map/ppermute | solution.py:373
  5.3 2.2 %collective-permute-start = (bf16[2,32,256]{2,1,0:T(8,128)(2,1)S(1)}, bf16[2,32,256]{2,1,0:T(8,128)(2,1)S(1)}, u32[]{:S(2)}, u32[]{:S(2)}) collective-permute-start(bf16[2,32,256]{2,1,0:T(8,128)(2,1)S(1)} %get-tuple-element.34), channel_id=1, source_target_pairs={{0,1},{1,2},{2,3},{3,0},{4,5},{5,6},{6,7},{7,4},{8,9},{9,10},{10,1... | collective-permute-start | bytes 98312 | tf_op jit(solution)/shard_map/ppermute | solution.py:373
  7.6 1.6 %collective-permute-start.2 = (bf16[2,32,256]{2,1,0:T(8,128)(2,1)S(1)}, bf16[2,32,256]{2,1,0:T(8,128)(2,1)S(1)}, u32[]{:S(2)}, u32[]{:S(2)}) collective-permute-start(bf16[2,32,256]{2,1,0:T(8,128)(2,1)S(1)} %get-tuple-element.36), channel_id=1, source_target_pairs={{0,3},{1,0},{2,1},{3,2},{4,7},{5,4},{6,5},{7,6},{8,11},{9,8},{10,9... | collective-permute-start | bytes 98312 | tf_op jit(solution)/shard_map/ppermute | solution.py:373
  9.2 0.4 collective-permute-start.3
  9.6 3.4 %collective-permute-start.4 = (bf16[8,32,256]{2,1,0:T(8,128)(2,1)S(1)}, bf16[8,32,256]{2,1,0:T(8,128)(2,1)S(1)}, u32[]{:S(2)}, u32[]{:S(2)}) collective-permute-start(bf16[8,32,256]{2,1,0:T(8,128)(2,1)S(1)} %get-tuple-element.40), channel_id=1, source_target_pairs={{0,3},{1,0},{2,1},{3,2},{4,7},{5,4},{6,5},{7,6},{8,11},{9,8},{10,9... | collective-permute-start | bytes 393224 | tf_op jit(solution)/shard_map/ppermute | solution.py:373
  13.0 0.0 collective-permute-done.rest_1_
  13.0 3.2 %collective-permute-done.2.rest_3_ = bf16[2,32,256]{2,1,0:T(8,128)(2,1)S(1)} collective-permute-done((bf16[2,32,256]{2,1,0:T(8,128)(2,1)S(1)}, bf16[2,32,256]{2,1,0:T(8,128)(2,1)S(1)}, u32[]{:S(2)}, u32[]{:S(2)}) %collective-permute-start.2) | collective-permute-done | bytes 32800 | tf_op jit(solution)/shard_map/ppermute | solution.py:373
  16.2 1.2 %collective-permute-done.1.rest_2_ = bf16[10,32,256]{2,1,0:T(8,128)(2,1)S(1)} collective-permute-done((bf16[10,32,256]{2,1,0:T(8,128)(2,1)S(1)}, bf16[10,32,256]{2,1,0:T(8,128)(2,1)S(1)}, u32[]{:S(2)}, u32[]{:S(2)}) %collective-permute-start.1) | collective-permute-done | bytes 163872 | tf_op jit(solution)/shard_map/ppermute | solution.py:373
  17.4 0.6 %edge.1.after.rest_4_ = bf16[2,128,256]{2,1,0:T(8,128)(2,1)S(1)} custom-call(s32[4,8]{1,0:T(4,128)S(1)} %get-tuple-element.32.owner, bf16[2,32,256]{2,1,0:T(8,128)(2,1)S(1)} %get-tuple-element.33.rest_0_, bf16[2,32,256]{2,1,0:T(8,128)(2,1)S(1)} %collective-permute-done.rest_1_, bf16[10,32,256]{2,1,0:T(8,128)(2,1)S(1)} %collective-permute-done.1.rest_2_, ...), custom_call_target="tpu_custom_call" | custom-call | tf_op jit(solution)/shard_map/edge/pallas_call | solution.py:357
  18.0 3.2 %collective-permute-start.5 = (bf16[2,128,256]{2,1,0:T(8,128)(2,1)S(1)}, bf16[2,128,256]{2,1,0:T(8,128)(2,1)S(1)}, u32[]{:S(2)}, u32[]{:S(2)}) collective-permute-start(bf16[2,128,256]{2,1,0:T(8,128)(2,1)S(1)} %edge.1.after.rest_4_), channel_id=1, source_target_pairs={{0,1},{1,0},{3,7},{7,3},{4,5},{5,4},{6,10},{10,6},{8,9},{9,8},{11,... | collective-permute-start | bytes 393224 | tf_op jit(solution)/shard_map/ppermute | solution.py:405
  21.2 2.0 %load.1 = (s32[256]{0:T(256)S(1)}, bf16[3,768,256]{2,1,0:T(8,128)(2,1)S(1)}, f32[1,256]{1,0:T(1,128)S(1)}, bf16[3,768,256]{2,1,0:T(8,128)(2,1)S(1)}, f32[1,256]{...) custom-call(bf16[2,128,256]{2,1,0:T(8,128)(2,1)S(1)} %edge.1.after.r, ...), custom_call_target="tpu_custom_call" | custom-call | tf_op jit(solution)/shard_map/load/pallas_call | solution.py:357
  23.2 0.0 collective-permute-done.3.rest_1_
  23.2 0.0 collective-permute-done.4.rest_3_
  23.2 1.7 %collective-permute-done.5.rest_5_ = bf16[2,128,256]{2,1,0:T(8,128)(2,1)S(1)} collective-permute-done((bf16[2,128,256]{2,1,0:T(8,128)(2,1)S(1)}, bf16[2,128,256]{2,1,0:T(8,128)(2,1)S(1)}, u32[]{:S(2)}, u32[]{:S(2)}) %collective-permute-start.5) | collective-permute-done | bytes 131104 | tf_op jit(solution)/shard_map/ppermute | solution.py:405
  24.9 5.7 %main.1 = (bf16[272,256]{1,0:T(8,128)(2,1)S(1)}, bf16[1024,256]{1,0:T(8,128)(2,1)S(1)}, bf16[1024,256]{1,0:T(8,128)(2,1)S(1)}, bf16[1024,64]{1,0:T(8,128)(2,1)S(1)}, bf16[64,1024]{1,0:T(8,128)(2,1)S(1)}) custom-call(s32[4,8]{1,0:T(4,128)S(1)} %get-tuple-element.32.owner, s32[256]{0:T(256)S(1)} %get-tuple-element.37.counts, ...), custom_call_target="tpu_custom_call" | custom-call | tf_op jit(solution)/shard_map/main/pallas_call | solution.py:357
  30.6 0.1 collective-permute-start.7
  30.7 3.1 %rest.1 = (bf16[256,256]{1,0:T(8,128)(2,1)S(1)}, bf16[256,256]{1,0:T(8,128)(2,1)S(1)}, bf16[256,256]{1,0:T(8,128)(2,1)S(1)}) custom-call(s32[4,8]{1,0:T(4,128)S(1)} %get-tuple-element.32.owner, s32[256]{0:T(256)S(1)} %get-tuple-element.37.counts, bf16[1024,256]{1,0:T(8,128)(2,1)S(1)} %get-tuple-element.49.rest_0_, ...), custom_call_target="tpu_custom_call" | custom-call | tf_op jit(solution)/shard_map/rest/pallas_call | solution.py:357
  33.8 1.3 %collective-permute-start.6 = (bf16[256,256]{1,0:T(8,128)(2,1)S(1)}, bf16[256,256]{1,0:T(8,128)(2,1)S(1)}, u32[]{:S(2)}, u32[]{:S(2)}) collective-permute-start(bf16[256,256]{1,0:T(8,128)(2,1)S(1)} %get-tuple-element.54), channel_id=1, source_target_pairs={{0,1},{1,2},{2,3},{3,0},{4,5},{5,6},{6,7},{7,4},{8,9},{9,10},{10,1... | collective-permute-start | bytes 393224 | tf_op jit(solution)/shard_map/ppermute | solution.py:373
  35.1 2.6 %collective-permute-start.8 = (bf16[256,256]{1,0:T(8,128)(2,1)S(1)}, bf16[256,256]{1,0:T(8,128)(2,1)S(1)}, u32[]{:S(2)}, u32[]{:S(2)}) collective-permute-start(bf16[256,256]{1,0:T(8,128)(2,1)S(1)} %get-tuple-element.56), channel_id=1, source_target_pairs={{0,3},{1,0},{2,1},{3,2},{4,7},{5,4},{6,5},{7,6},{8,11},{9,8},{10,9... | collective-permute-start | bytes 393224 | tf_op jit(solution)/shard_map/ppermute | solution.py:373
  37.7 3.1 %collective-permute-done.6.rest_1_ = bf16[256,256]{1,0:T(8,128)(2,1)S(1)} collective-permute-done((bf16[256,256]{1,0:T(8,128)(2,1)S(1)}, bf16[256,256]{1,0:T(8,128)(2,1)S(1)}, u32[]{:S(2)}, u32[]{:S(2)}) %collective-permute-start.6) | collective-permute-done | bytes 131104 | tf_op jit(solution)/shard_map/ppermute | solution.py:373
  40.8 3.9 %collective-permute-done.8.rest_3_ = bf16[256,256]{1,0:T(8,128)(2,1)S(1)} collective-permute-done((bf16[256,256]{1,0:T(8,128)(2,1)S(1)}, bf16[256,256]{1,0:T(8,128)(2,1)S(1)}, u32[]{:S(2)}, u32[]{:S(2)}) %collective-permute-start.8) | collective-permute-done | bytes 131104 | tf_op jit(solution)/shard_map/ppermute | solution.py:373
  44.7 0.0 collective-permute-done.7.rest_2_
  44.7 1.4 %store.1 = bf16[32,32,256]{2,1,0:T(8,128)(2,1)} custom-call(s32[4,8]{1,0:T(4,128)S(1)} %get-tuple-element.31.rotation, bf16[256,256]{1,0:T(8,128)(2,1)S(1)} %get-tuple-element.53.rest_0_, bf16[256,256]{1,0:T(8,128)(2,1)S(1)} %collective-permute-done.6.rest_1_, bf16[272,256]{1,0:T(8,128)(2,1)S(1)} %collective-permute-done.7.rest_2_, ...), custom_call_target="tpu_custom_call" | custom-call | tf_op jit(solution)/shard_map/store/pallas_call | solution.py:357
Async XLA Ops:
  1.2 16.2 %collective-permute-start.1 = (bf16[10,32,256]{2,1,0:T(8,128)(2,1)S(1)}, bf16[10,32,256]{2,1,0:T(8,128)(2,1)S(1)}, u32[]{:S(2)}, u32[]{:S(2)}) collective-permute-start(bf16[10,32,256]{2,1,0:T(8,128)(2,1)S(1)} %get-tuple-element.35), channel_id=1, source_target_pairs={{0,2},{1,3},{2,0},{3,1},{4,6},{5,7},{6,4},{7,5},{8,10},{9,11},{10,... | collective-permute-start | bytes 491528 | tf_op jit(solution)/shard_map/ppermute | solution.py:373
  5.3 7.7 %collective-permute-start = (bf16[2,32,256]{2,1,0:T(8,128)(2,1)S(1)}, bf16[2,32,256]{2,1,0:T(8,128)(2,1)S(1)}, u32[]{:S(2)}, u32[]{:S(2)}) collective-permute-start(bf16[2,32,256]{2,1,0:T(8,128)(2,1)S(1)} %get-tuple-element.34), channel_id=1, source_target_pairs={{0,1},{1,2},{2,3},{3,0},{4,5},{5,6},{6,7},{7,4},{8,9},{9,10},{10,1... | collective-permute-start | bytes 98312 | tf_op jit(solution)/shard_map/ppermute | solution.py:373
  7.6 8.6 %collective-permute-start.2 = (bf16[2,32,256]{2,1,0:T(8,128)(2,1)S(1)}, bf16[2,32,256]{2,1,0:T(8,128)(2,1)S(1)}, u32[]{:S(2)}, u32[]{:S(2)}) collective-permute-start(bf16[2,32,256]{2,1,0:T(8,128)(2,1)S(1)} %get-tuple-element.36), channel_id=1, source_target_pairs={{0,3},{1,0},{2,1},{3,2},{4,7},{5,4},{6,5},{7,6},{8,11},{9,8},{10,9... | collective-permute-start | bytes 98312 | tf_op jit(solution)/shard_map/ppermute | solution.py:373
  9.2 14.0 %collective-permute-start.3 = (bf16[8,32,256]{2,1,0:T(8,128)(2,1)S(1)}, bf16[8,32,256]{2,1,0:T(8,128)(2,1)S(1)}, u32[]{:S(2)}, u32[]{:S(2)}) collective-permute-start(bf16[8,32,256]{2,1,0:T(8,128)(2,1)S(1)} %get-tuple-element.39), channel_id=1, source_target_pairs={{0,1},{1,2},{2,3},{3,0},{4,5},{5,6},{6,7},{7,4},{8,9},{9,10},{10,1... | collective-permute-start | bytes 393224 | tf_op jit(solution)/shard_map/ppermute | solution.py:373
  9.6 13.6 %collective-permute-start.4 = (bf16[8,32,256]{2,1,0:T(8,128)(2,1)S(1)}, bf16[8,32,256]{2,1,0:T(8,128)(2,1)S(1)}, u32[]{:S(2)}, u32[]{:S(2)}) collective-permute-start(bf16[8,32,256]{2,1,0:T(8,128)(2,1)S(1)} %get-tuple-element.40), channel_id=1, source_target_pairs={{0,3},{1,0},{2,1},{3,2},{4,7},{5,4},{6,5},{7,6},{8,11},{9,8},{10,9... | collective-permute-start | bytes 393224 | tf_op jit(solution)/shard_map/ppermute | solution.py:373
  18.0 6.9 %collective-permute-start.5 = (bf16[2,128,256]{2,1,0:T(8,128)(2,1)S(1)}, bf16[2,128,256]{2,1,0:T(8,128)(2,1)S(1)}, u32[]{:S(2)}, u32[]{:S(2)}) collective-permute-start(bf16[2,128,256]{2,1,0:T(8,128)(2,1)S(1)} %edge.1.after.rest_4_), channel_id=1, source_target_pairs={{0,1},{1,0},{3,7},{7,3},{4,5},{5,4},{6,10},{10,6},{8,9},{9,8},{11,... | collective-permute-start | bytes 393224 | tf_op jit(solution)/shard_map/ppermute | solution.py:405
  30.6 14.0 %collective-permute-start.7 = (bf16[272,256]{1,0:T(8,128)(2,1)S(1)}, bf16[272,256]{1,0:T(8,128)(2,1)S(1)}, u32[]{:S(2)}, u32[]{:S(2)}) collective-permute-start(bf16[272,256]{1,0:T(8,128)(2,1)S(1)} %get-tuple-element.55), channel_id=1, source_target_pairs={{0,2},{1,3},{2,0},{3,1},{4,6},{5,7},{6,4},{7,5},{8,10},{9,11},{10,... | collective-permute-start | bytes 417800 | tf_op jit(solution)/shard_map/ppermute | solution.py:373
  33.8 7.0 %collective-permute-start.6 = (bf16[256,256]{1,0:T(8,128)(2,1)S(1)}, bf16[256,256]{1,0:T(8,128)(2,1)S(1)}, u32[]{:S(2)}, u32[]{:S(2)}) collective-permute-start(bf16[256,256]{1,0:T(8,128)(2,1)S(1)} %get-tuple-element.54), channel_id=1, source_target_pairs={{0,1},{1,2},{2,3},{3,0},{4,5},{5,6},{6,7},{7,4},{8,9},{9,10},{10,1... | collective-permute-start | bytes 393224 | tf_op jit(solution)/shard_map/ppermute | solution.py:373
  35.1 9.5 %collective-permute-start.8 = (bf16[256,256]{1,0:T(8,128)(2,1)S(1)}, bf16[256,256]{1,0:T(8,128)(2,1)S(1)}, u32[]{:S(2)}, u32[]{:S(2)}) collective-permute-start(bf16[256,256]{1,0:T(8,128)(2,1)S(1)} %get-tuple-element.56), channel_id=1, source_target_pairs={{0,3},{1,0},{2,1},{3,2},{4,7},{5,4},{6,5},{7,6},{8,11},{9,8},{10,9... | collective-permute-start | bytes 393224 | tf_op jit(solution)/shard_map/ppermute | solution.py:373

commit v10 on v8

--- a/solution.py
+++ b/solution.py
@@ -174,7 +174,8 @@
 
 
 def silu(x):
-    return x / (1.0 + jnp.exp(-x))
+    half = 0.5 * x
+    return half + half * jnp.tanh(half)
 
 
 def live_count(counts, row):
@@ -270,7 +271,7 @@
         values[:, at] = by_last(w_value[...], scaled).astype(jnp.bfloat16)
 
     total = rows + HALO
-    half = total // 2 + total // 8
+    half = total // 2
     low = half - HALO
     spread_inputs(0, half + HALO)
     first_low = convolve(taps, w_conv1, b_conv1, 0, half)
@@ -283,16 +284,11 @@
     second_high = convolve(acts, w_conv2, b_conv2, low, rows - low)
     result[rows * (cols // n) :, :] = jnp.zeros((AHEAD, chans), result.dtype)
     segments = [owner[lax.rem(me + first, n), band]]
-
-    def attend_rows(*span):
-        shared = limits[1 : rows + 1], mixed, normed, keys, values, w_query, w_out
-        attend(segments, span, *shared, [result], *scratch)
-
     if low:
         mix(0, low, second_low)
-        attend_rows(0, low)
     mix(low, rows, second_high)
-    attend_rows(low, rows)
+    shared = limits[1 : rows + 1], mixed, normed, keys, values, w_query, w_out
+    attend(segments, (0, rows), *shared, [result], *scratch)
 
 
 def rest_kernel(moves, n, rows, owner, counts, *rest):

time: 44.9 us -> 44.6 us (level)
  no operation moved by 1% of the time
where the time goes in v10:
time: 44.6 us; the launch traced here: 44.4 us
  starting transfers between devices  16.8 us (38%)
  Pallas kernels  15 us (34%)
  waiting for transfers between devices  12.5 us (28%)
    pallas_call x6, Pallas kernels, call(): pl.pallas_call(functools.partial(kernel, n, rows), out_shape=out, in_spec...  15 us
    ppermute x9, starting transfers between devices, around_by(): return lax.ppermute(x, 'lon', [(i, (i + d) % n) for i in range(n)])  14.3 us
    ppermute x9, waiting for transfers between devices, around_by(): return lax.ppermute(x, 'lon', [(i, (i + d) % n) for i in range(n)])  10.8 us
    ppermute x1, starting transfers between devices, on_device(): received = lax.ppermute(sent, ('lat', 'lon'), pairs)  2.48 us
    ppermute x1, waiting for transfers between devices, on_device(): received = lax.ppermute(sent, ('lat', 'lon'), pairs)  1.74 us
  transfers between devices with their start and end apart: 10, of which 5 were waited for; matrix products, arithmetic and copies ran while one was open for 0% of the time, Pallas kernels for 13%

profile of v10, /device:TPU:0, one launch (start us, length us, event | category | flops | bytes accessed | tf_op | source)
XLA Modules:
  0.0 44.4 jit_solution(17212963984892439299)
XLA Ops:
  0.0 1.9 %send.1 = (bf16[2,32,256]{2,1,0:T(8,128)(2,1)S(1)}, bf16[2,32,256]{2,1,0:T(8,128)(2,1)S(1)}, bf16[2,32,256]{2,1,0:T(8,128)(2,1)S(1)}, bf16[2,32,256]{2,1,0:T(8,1...) custom-call(s32[4,8]{1,0:T(4,128)} %bitcast.12, ...), custom_call_target="tpu_custom_call" | custom-call | tf_op jit(solution)/shard_map/send/pallas_call | solution.py:353
  1.9 2.4 %collective-permute-start = (bf16[2,32,256]{2,1,0:T(8,128)(2,1)S(1)}, bf16[2,32,256]{2,1,0:T(8,128)(2,1)S(1)}, u32[]{:S(2)}, u32[]{:S(2)}) collective-permute-start(bf16[2,32,256]{2,1,0:T(8,128)(2,1)S(1)} %get-tuple-element.35), channel_id=1, source_target_pairs={{0,1},{1,2},{2,3},{3,0},{4,5},{5,6},{6,7},{7,4},{8,9},{9,10},{10,1... | collective-permute-start | bytes 98312 | tf_op jit(solution)/shard_map/ppermute | solution.py:369
  4.3 2.8 %collective-permute-start.1 = (bf16[2,32,256]{2,1,0:T(8,128)(2,1)S(1)}, bf16[2,32,256]{2,1,0:T(8,128)(2,1)S(1)}, u32[]{:S(2)}, u32[]{:S(2)}) collective-permute-start(bf16[2,32,256]{2,1,0:T(8,128)(2,1)S(1)} %get-tuple-element.36), channel_id=1, source_target_pairs={{0,2},{1,3},{2,0},{3,1},{4,6},{5,7},{6,4},{7,5},{8,10},{9,11},{10,... | collective-permute-start | bytes 98312 | tf_op jit(solution)/shard_map/ppermute | solution.py:369
  7.1 1.3 %collective-permute-start.2 = (bf16[2,32,256]{2,1,0:T(8,128)(2,1)S(1)}, bf16[2,32,256]{2,1,0:T(8,128)(2,1)S(1)}, u32[]{:S(2)}, u32[]{:S(2)}) collective-permute-start(bf16[2,32,256]{2,1,0:T(8,128)(2,1)S(1)} %get-tuple-element.37), channel_id=1, source_target_pairs={{0,3},{1,0},{2,1},{3,2},{4,7},{5,4},{6,5},{7,6},{8,11},{9,8},{10,9... | collective-permute-start | bytes 98312 | tf_op jit(solution)/shard_map/ppermute | solution.py:369
  8.5 0.7 %collective-permute-start.3 = (bf16[8,32,256]{2,1,0:T(8,128)(2,1)S(1)}, bf16[8,32,256]{2,1,0:T(8,128)(2,1)S(1)}, u32[]{:S(2)}, u32[]{:S(2)}) collective-permute-start(bf16[8,32,256]{2,1,0:T(8,128)(2,1)S(1)} %get-tuple-element.40), channel_id=1, source_target_pairs={{0,1},{1,2},{2,3},{3,0},{4,5},{5,6},{6,7},{7,4},{8,9},{9,10},{10,1... | collective-permute-start | bytes 393224 | tf_op jit(solution)/shard_map/ppermute | solution.py:369
  9.1 0.1 collective-permute-start.4
  9.3 0.0 collective-permute-done.rest_1_
  9.3 3.0 %collective-permute-start.5 = (bf16[8,32,256]{2,1,0:T(8,128)(2,1)S(1)}, bf16[8,32,256]{2,1,0:T(8,128)(2,1)S(1)}, u32[]{:S(2)}, u32[]{:S(2)}) collective-permute-start(bf16[8,32,256]{2,1,0:T(8,128)(2,1)S(1)} %get-tuple-element.42), channel_id=1, source_target_pairs={{0,3},{1,0},{2,1},{3,2},{4,7},{5,4},{6,5},{7,6},{8,11},{9,8},{10,9... | collective-permute-start | bytes 393224 | tf_op jit(solution)/shard_map/ppermute | solution.py:369
  12.3 0.0 collective-permute-done.1.rest_2_
  12.3 0.0 collective-permute-done.2.rest_3_
  12.3 0.6 %edge.1.after.rest_4_ = bf16[2,128,256]{2,1,0:T(8,128)(2,1)S(1)} custom-call(s32[4,8]{1,0:T(4,128)S(1)} %get-tuple-element.33.owner, bf16[2,32,256]{2,1,0:T(8,128)(2,1)S(1)} %get-tuple-element.34.rest_0_, bf16[2,32,256]{2,1,0:T(8,128)(2,1)S(1)} %collective-permute-done.rest_1_, bf16[2,32,256]{2,1,0:T(8,128)(2,1)S(1)} %collective-permute-done.1.rest_2_, ...), custom_call_target="tpu_custom_call" | custom-call | tf_op jit(solution)/shard_map/edge/pallas_call | solution.py:353
  12.9 2.5 %collective-permute-start.6 = (bf16[2,128,256]{2,1,0:T(8,128)(2,1)S(1)}, bf16[2,128,256]{2,1,0:T(8,128)(2,1)S(1)}, u32[]{:S(2)}, u32[]{:S(2)}) collective-permute-start(bf16[2,128,256]{2,1,0:T(8,128)(2,1)S(1)} %edge.1.after.rest_4_), channel_id=1, source_target_pairs={{0,1},{1,0},{3,7},{7,3},{4,5},{5,4},{6,10},{10,6},{8,9},{9,8},{11,... | collective-permute-start | bytes 393224 | tf_op jit(solution)/shard_map/ppermute | solution.py:398
  15.4 2.0 %load.1 = (s32[256]{0:T(256)S(1)}, bf16[3,768,256]{2,1,0:T(8,128)(2,1)S(1)}, f32[1,256]{1,0:T(1,128)S(1)}, bf16[3,768,256]{2,1,0:T(8,128)(2,1)S(1)}, f32[1,256]{...) custom-call(bf16[2,128,256]{2,1,0:T(8,128)(2,1)S(1)} %edge.1.after.r, ...), custom_call_target="tpu_custom_call" | custom-call | tf_op jit(solution)/shard_map/load/pallas_call | solution.py:353
  17.4 2.9 %collective-permute-done.4.rest_2_ = bf16[8,32,256]{2,1,0:T(8,128)(2,1)S(1)} collective-permute-done((bf16[8,32,256]{2,1,0:T(8,128)(2,1)S(1)}, bf16[8,32,256]{2,1,0:T(8,128)(2,1)S(1)}, u32[]{:S(2)}, u32[]{:S(2)}) %collective-permute-start.4) | collective-permute-done | bytes 131104 | tf_op jit(solution)/shard_map/ppermute | solution.py:369
  20.3 0.9 %collective-permute-done.5.rest_3_ = bf16[8,32,256]{2,1,0:T(8,128)(2,1)S(1)} collective-permute-done((bf16[8,32,256]{2,1,0:T(8,128)(2,1)S(1)}, bf16[8,32,256]{2,1,0:T(8,128)(2,1)S(1)}, u32[]{:S(2)}, u32[]{:S(2)}) %collective-permute-start.5) | collective-permute-done | bytes 131104 | tf_op jit(solution)/shard_map/ppermute | solution.py:369
  21.1 1.7 %collective-permute-done.6.rest_5_ = bf16[2,128,256]{2,1,0:T(8,128)(2,1)S(1)} collective-permute-done((bf16[2,128,256]{2,1,0:T(8,128)(2,1)S(1)}, bf16[2,128,256]{2,1,0:T(8,128)(2,1)S(1)}, u32[]{:S(2)}, u32[]{:S(2)}) %collective-permute-start.6) | collective-permute-done | bytes 131104 | tf_op jit(solution)/shard_map/ppermute | solution.py:398
  22.9 5.7 %main.1 = (bf16[272,256]{1,0:T(8,128)(2,1)S(1)}, bf16[1024,256]{1,0:T(8,128)(2,1)S(1)}, bf16[1024,256]{1,0:T(8,128)(2,1)S(1)}, bf16[1024,64]{1,0:T(8,128)(2,1)S(1)}, bf16[64,1024]{1,0:T(8,128)(2,1)S(1)}) custom-call(s32[4,8]{1,0:T(4,128)S(1)} %get-tuple-element.33.owner, s32[256]{0:T(256)S(1)} %get-tuple-element.38.counts, ...), custom_call_target="tpu_custom_call" | custom-call | tf_op jit(solution)/shard_map/main/pallas_call | solution.py:353
  28.6 0.1 collective-permute-start.8
  28.7 3.1 %rest.1 = (bf16[256,256]{1,0:T(8,128)(2,1)S(1)}, bf16[256,256]{1,0:T(8,128)(2,1)S(1)}, bf16[256,256]{1,0:T(8,128)(2,1)S(1)}) custom-call(s32[4,8]{1,0:T(4,128)S(1)} %get-tuple-element.33.owner, s32[256]{0:T(256)S(1)} %get-tuple-element.38.counts, bf16[1024,256]{1,0:T(8,128)(2,1)S(1)} %get-tuple-element.51.rest_0_, ...), custom_call_target="tpu_custom_call" | custom-call | tf_op jit(solution)/shard_map/rest/pallas_call | solution.py:353
  31.8 1.9 %collective-permute-start.7 = (bf16[256,256]{1,0:T(8,128)(2,1)S(1)}, bf16[256,256]{1,0:T(8,128)(2,1)S(1)}, u32[]{:S(2)}, u32[]{:S(2)}) collective-permute-start(bf16[256,256]{1,0:T(8,128)(2,1)S(1)} %get-tuple-element.56), channel_id=1, source_target_pairs={{0,1},{1,2},{2,3},{3,0},{4,5},{5,6},{6,7},{7,4},{8,9},{9,10},{10,1... | collective-permute-start | bytes 393224 | tf_op jit(solution)/shard_map/ppermute | solution.py:369
  33.7 2.0 %collective-permute-start.9 = (bf16[256,256]{1,0:T(8,128)(2,1)S(1)}, bf16[256,256]{1,0:T(8,128)(2,1)S(1)}, u32[]{:S(2)}, u32[]{:S(2)}) collective-permute-start(bf16[256,256]{1,0:T(8,128)(2,1)S(1)} %get-tuple-element.58), channel_id=1, source_target_pairs={{0,3},{1,0},{2,1},{3,2},{4,7},{5,4},{6,5},{7,6},{8,11},{9,8},{10,9... | collective-permute-start | bytes 393224 | tf_op jit(solution)/shard_map/ppermute | solution.py:369
  35.7 4.2 %collective-permute-done.7.rest_1_ = bf16[256,256]{1,0:T(8,128)(2,1)S(1)} collective-permute-done((bf16[256,256]{1,0:T(8,128)(2,1)S(1)}, bf16[256,256]{1,0:T(8,128)(2,1)S(1)}, u32[]{:S(2)}, u32[]{:S(2)}) %collective-permute-start.7) | collective-permute-done | bytes 131104 | tf_op jit(solution)/shard_map/ppermute | solution.py:369
  39.8 2.9 %collective-permute-done.9.rest_3_ = bf16[256,256]{1,0:T(8,128)(2,1)S(1)} collective-permute-done((bf16[256,256]{1,0:T(8,128)(2,1)S(1)}, bf16[256,256]{1,0:T(8,128)(2,1)S(1)}, u32[]{:S(2)}, u32[]{:S(2)}) %collective-permute-start.9) | collective-permute-done | bytes 131104 | tf_op jit(solution)/shard_map/ppermute | solution.py:369
  42.7 1.7 %store.1 = bf16[32,32,256]{2,1,0:T(8,128)(2,1)} custom-call(s32[4,8]{1,0:T(4,128)S(1)} %get-tuple-element.32.rotation, bf16[256,256]{1,0:T(8,128)(2,1)S(1)} %get-tuple-element.55.rest_0_, bf16[256,256]{1,0:T(8,128)(2,1)S(1)} %collective-permute-done.7.rest_1_, bf16[272,256]{1,0:T(8,128)(2,1)S(1)} %collective-permute-done.8.rest_2_, ...), custom_call_target="tpu_custom_call" | custom-call | tf_op jit(solution)/shard_map/store/pallas_call | solution.py:353
  (2 shorter events, 0.0 us)
Async XLA Ops:
  1.9 7.4 %collective-permute-start = (bf16[2,32,256]{2,1,0:T(8,128)(2,1)S(1)}, bf16[2,32,256]{2,1,0:T(8,128)(2,1)S(1)}, u32[]{:S(2)}, u32[]{:S(2)}) collective-permute-start(bf16[2,32,256]{2,1,0:T(8,128)(2,1)S(1)} %get-tuple-element.35), channel_id=1, source_target_pairs={{0,1},{1,2},{2,3},{3,0},{4,5},{5,6},{6,7},{7,4},{8,9},{9,10},{10,1... | collective-permute-start | bytes 98312 | tf_op jit(solution)/shard_map/ppermute | solution.py:369
  4.3 8.0 %collective-permute-start.1 = (bf16[2,32,256]{2,1,0:T(8,128)(2,1)S(1)}, bf16[2,32,256]{2,1,0:T(8,128)(2,1)S(1)}, u32[]{:S(2)}, u32[]{:S(2)}) collective-permute-start(bf16[2,32,256]{2,1,0:T(8,128)(2,1)S(1)} %get-tuple-element.36), channel_id=1, source_target_pairs={{0,2},{1,3},{2,0},{3,1},{4,6},{5,7},{6,4},{7,5},{8,10},{9,11},{10,... | collective-permute-start | bytes 98312 | tf_op jit(solution)/shard_map/ppermute | solution.py:369
  7.1 5.2 %collective-permute-start.2 = (bf16[2,32,256]{2,1,0:T(8,128)(2,1)S(1)}, bf16[2,32,256]{2,1,0:T(8,128)(2,1)S(1)}, u32[]{:S(2)}, u32[]{:S(2)}) collective-permute-start(bf16[2,32,256]{2,1,0:T(8,128)(2,1)S(1)} %get-tuple-element.37), channel_id=1, source_target_pairs={{0,3},{1,0},{2,1},{3,2},{4,7},{5,4},{6,5},{7,6},{8,11},{9,8},{10,9... | collective-permute-start | bytes 98312 | tf_op jit(solution)/shard_map/ppermute | solution.py:369
  8.5 8.9 %collective-permute-start.3 = (bf16[8,32,256]{2,1,0:T(8,128)(2,1)S(1)}, bf16[8,32,256]{2,1,0:T(8,128)(2,1)S(1)}, u32[]{:S(2)}, u32[]{:S(2)}) collective-permute-start(bf16[8,32,256]{2,1,0:T(8,128)(2,1)S(1)} %get-tuple-element.40), channel_id=1, source_target_pairs={{0,1},{1,2},{2,3},{3,0},{4,5},{5,6},{6,7},{7,4},{8,9},{9,10},{10,1... | collective-permute-start | bytes 393224 | tf_op jit(solution)/shard_map/ppermute | solution.py:369
  9.1 11.1 %collective-permute-start.4 = (bf16[8,32,256]{2,1,0:T(8,128)(2,1)S(1)}, bf16[8,32,256]{2,1,0:T(8,128)(2,1)S(1)}, u32[]{:S(2)}, u32[]{:S(2)}) collective-permute-start(bf16[8,32,256]{2,1,0:T(8,128)(2,1)S(1)} %get-tuple-element.41), channel_id=1, source_target_pairs={{0,2},{1,3},{2,0},{3,1},{4,6},{5,7},{6,4},{7,5},{8,10},{9,11},{10,... | collective-permute-start | bytes 393224 | tf_op jit(solution)/shard_map/ppermute | solution.py:369
  9.3 11.9 %collective-permute-start.5 = (bf16[8,32,256]{2,1,0:T(8,128)(2,1)S(1)}, bf16[8,32,256]{2,1,0:T(8,128)(2,1)S(1)}, u32[]{:S(2)}, u32[]{:S(2)}) collective-permute-start(bf16[8,32,256]{2,1,0:T(8,128)(2,1)S(1)} %get-tuple-element.42), channel_id=1, source_target_pairs={{0,3},{1,0},{2,1},{3,2},{4,7},{5,4},{6,5},{7,6},{8,11},{9,8},{10,9... | collective-permute-start | bytes 393224 | tf_op jit(solution)/shard_map/ppermute | solution.py:369
  12.9 10.0 %collective-permute-start.6 = (bf16[2,128,256]{2,1,0:T(8,128)(2,1)S(1)}, bf16[2,128,256]{2,1,0:T(8,128)(2,1)S(1)}, u32[]{:S(2)}, u32[]{:S(2)}) collective-permute-start(bf16[2,128,256]{2,1,0:T(8,128)(2,1)S(1)} %edge.1.after.rest_4_), channel_id=1, source_target_pairs={{0,1},{1,0},{3,7},{7,3},{4,5},{5,4},{6,10},{10,6},{8,9},{9,8},{11,... | collective-permute-start | bytes 393224 | tf_op jit(solution)/shard_map/ppermute | solution.py:398
  28.6 14.1 %collective-permute-start.8 = (bf16[272,256]{1,0:T(8,128)(2,1)S(1)}, bf16[272,256]{1,0:T(8,128)(2,1)S(1)}, u32[]{:S(2)}, u32[]{:S(2)}) collective-permute-start(bf16[272,256]{1,0:T(8,128)(2,1)S(1)} %get-tuple-element.57), channel_id=1, source_target_pairs={{0,2},{1,3},{2,0},{3,1},{4,6},{5,7},{6,4},{7,5},{8,10},{9,11},{10,... | collective-permute-start | bytes 417800 | tf_op jit(solution)/shard_map/ppermute | solution.py:369
  31.8 8.0 %collective-permute-start.7 = (bf16[256,256]{1,0:T(8,128)(2,1)S(1)}, bf16[256,256]{1,0:T(8,128)(2,1)S(1)}, u32[]{:S(2)}, u32[]{:S(2)}) collective-permute-start(bf16[256,256]{1,0:T(8,128)(2,1)S(1)} %get-tuple-element.56), channel_id=1, source_target_pairs={{0,1},{1,2},{2,3},{3,0},{4,5},{5,6},{6,7},{7,4},{8,9},{9,10},{10,1... | collective-permute-start | bytes 393224 | tf_op jit(solution)/shard_map/ppermute | solution.py:369
  33.7 9.0 %collective-permute-start.9 = (bf16[256,256]{1,0:T(8,128)(2,1)S(1)}, bf16[256,256]{1,0:T(8,128)(2,1)S(1)}, u32[]{:S(2)}, u32[]{:S(2)}) collective-permute-start(bf16[256,256]{1,0:T(8,128)(2,1)S(1)} %get-tuple-element.58), channel_id=1, source_target_pairs={{0,3},{1,0},{2,1},{3,2},{4,7},{5,4},{6,5},{7,6},{8,11},{9,8},{10,9... | collective-permute-start | bytes 393224 | tf_op jit(solution)/shard_map/ppermute | solution.py:369

commit v11 on v10

--- a/solution.py
+++ b/solution.py
@@ -271,22 +271,11 @@
         values[:, at] = by_last(w_value[...], scaled).astype(jnp.bfloat16)
 
     total = rows + HALO
-    half = total // 2
-    low = half - HALO
-    spread_inputs(0, half + HALO)
-    first_low = convolve(taps, w_conv1, b_conv1, 0, half)
-    spread_inputs(half + HALO, total + HALO)
-    first_high = convolve(taps, w_conv1, b_conv1, half, total - half)
-    spread_acts(0, half, first_low)
-    if low:
-        second_low = convolve(acts, w_conv2, b_conv2, 0, low)
-    spread_acts(half, total, first_high)
-    second_high = convolve(acts, w_conv2, b_conv2, low, rows - low)
+    spread_inputs(0, total + HALO)
+    spread_acts(0, total, convolve(taps, w_conv1, b_conv1, 0, total))
+    mix(0, rows, convolve(acts, w_conv2, b_conv2, 0, rows))
     result[rows * (cols // n) :, :] = jnp.zeros((AHEAD, chans), result.dtype)
     segments = [owner[lax.rem(me + first, n), band]]
-    if low:
-        mix(0, low, second_low)
-    mix(low, rows, second_high)
     shared = limits[1 : rows + 1], mixed, normed, keys, values, w_query, w_out
     attend(segments, (0, rows), *shared, [result], *scratch)
 

time: 44.6 us -> 46.6 us (1.045)
  Pallas kernels: 15 us -> 16.5 us
  waiting for transfers between devices: 12.5 us -> 13.1 us
    pallas_call x6, Pallas kernels: 15 us -> 16.5 us  [call(): pl.pallas_call(functools.partial(kernel, n, rows), out_shape=out, in_spec...]
    ppermute x1, starting transfers between devices: 2.48 us -> 1.92 us  [on_device(): received = lax.ppermute(sent, ('lat', 'lon'), pairs)]
  transfers between devices with their start and end apart: 10 -> 10, of which waited for: 5 -> 6; matrix products, arithmetic and copies ran while one was open for 0% -> 0% of each run, Pallas kernels for 13% -> 12%
where the time goes in v11:
time: 46.6 us; the launch traced here: 46.4 us
  starting transfers between devices  16.7 us (36%)
  Pallas kernels  16.5 us (35%)
  waiting for transfers between devices  13.1 us (28%)
    pallas_call x6, Pallas kernels, call(): pl.pallas_call(functools.partial(kernel, n, rows), out_shape=out, in_spec...  16.5 us
    ppermute x9, starting transfers between devices, around_by(): return lax.ppermute(x, 'lon', [(i, (i + d) % n) for i in range(n)])  14.8 us
    ppermute x9, waiting for transfers between devices, around_by(): return lax.ppermute(x, 'lon', [(i, (i + d) % n) for i in range(n)])  11.2 us
    ppermute x1, starting transfers between devices, on_device(): received = lax.ppermute(sent, ('lat', 'lon'), pairs)  1.92 us
    ppermute x1, waiting for transfers between devices, on_device(): received = lax.ppermute(sent, ('lat', 'lon'), pairs)  1.88 us
  transfers between devices with their start and end apart: 10, of which 6 were waited for; matrix products, arithmetic and copies ran while one was open for 0% of the time, Pallas kernels for 12%

profile of v11, /device:TPU:0, one launch (start us, length us, event | category | flops | bytes accessed | tf_op | source)
XLA Modules:
  0.0 46.4 jit_solution(5717472827775378390)
XLA Ops:
  0.0 1.4 %send.1 = (bf16[2,32,256]{2,1,0:T(8,128)(2,1)S(1)}, bf16[2,32,256]{2,1,0:T(8,128)(2,1)S(1)}, bf16[2,32,256]{2,1,0:T(8,128)(2,1)S(1)}, bf16[2,32,256]{2,1,0:T(8,1...) custom-call(s32[4,8]{1,0:T(4,128)} %bitcast.12, ...), custom_call_target="tpu_custom_call" | custom-call | tf_op jit(solution)/shard_map/send/pallas_call | solution.py:342
  1.4 3.1 %collective-permute-start = (bf16[2,32,256]{2,1,0:T(8,128)(2,1)S(1)}, bf16[2,32,256]{2,1,0:T(8,128)(2,1)S(1)}, u32[]{:S(2)}, u32[]{:S(2)}) collective-permute-start(bf16[2,32,256]{2,1,0:T(8,128)(2,1)S(1)} %get-tuple-element.35), channel_id=1, source_target_pairs={{0,1},{1,2},{2,3},{3,0},{4,5},{5,6},{6,7},{7,4},{8,9},{9,10},{10,1... | collective-permute-start | bytes 98312 | tf_op jit(solution)/shard_map/ppermute | solution.py:358
  4.5 3.0 %collective-permute-start.1 = (bf16[2,32,256]{2,1,0:T(8,128)(2,1)S(1)}, bf16[2,32,256]{2,1,0:T(8,128)(2,1)S(1)}, u32[]{:S(2)}, u32[]{:S(2)}) collective-permute-start(bf16[2,32,256]{2,1,0:T(8,128)(2,1)S(1)} %get-tuple-element.36), channel_id=1, source_target_pairs={{0,2},{1,3},{2,0},{3,1},{4,6},{5,7},{6,4},{7,5},{8,10},{9,11},{10,... | collective-permute-start | bytes 98312 | tf_op jit(solution)/shard_map/ppermute | solution.py:358
  7.6 0.9 %collective-permute-start.2 = (bf16[2,32,256]{2,1,0:T(8,128)(2,1)S(1)}, bf16[2,32,256]{2,1,0:T(8,128)(2,1)S(1)}, u32[]{:S(2)}, u32[]{:S(2)}) collective-permute-start(bf16[2,32,256]{2,1,0:T(8,128)(2,1)S(1)} %get-tuple-element.37), channel_id=1, source_target_pairs={{0,3},{1,0},{2,1},{3,2},{4,7},{5,4},{6,5},{7,6},{8,11},{9,8},{10,9... | collective-permute-start | bytes 98312 | tf_op jit(solution)/shard_map/ppermute | solution.py:358
  8.5 1.1 %collective-permute-start.3 = (bf16[8,32,256]{2,1,0:T(8,128)(2,1)S(1)}, bf16[8,32,256]{2,1,0:T(8,128)(2,1)S(1)}, u32[]{:S(2)}, u32[]{:S(2)}) collective-permute-start(bf16[8,32,256]{2,1,0:T(8,128)(2,1)S(1)} %get-tuple-element.40), channel_id=1, source_target_pairs={{0,1},{1,2},{2,3},{3,0},{4,5},{5,6},{6,7},{7,4},{8,9},{9,10},{10,1... | collective-permute-start | bytes 393224 | tf_op jit(solution)/shard_map/ppermute | solution.py:358
  9.6 0.0 collective-permute-start.4
  9.6 2.7 %collective-permute-start.5 = (bf16[8,32,256]{2,1,0:T(8,128)(2,1)S(1)}, bf16[8,32,256]{2,1,0:T(8,128)(2,1)S(1)}, u32[]{:S(2)}, u32[]{:S(2)}) collective-permute-start(bf16[8,32,256]{2,1,0:T(8,128)(2,1)S(1)} %get-tuple-element.42), channel_id=1, source_target_pairs={{0,3},{1,0},{2,1},{3,2},{4,7},{5,4},{6,5},{7,6},{8,11},{9,8},{10,9... | collective-permute-start | bytes 393224 | tf_op jit(solution)/shard_map/ppermute | solution.py:358
  12.3 0.0 collective-permute-done.1.rest_2_
  12.3 1.1 %collective-permute-done.2.rest_3_ = bf16[2,32,256]{2,1,0:T(8,128)(2,1)S(1)} collective-permute-done((bf16[2,32,256]{2,1,0:T(8,128)(2,1)S(1)}, bf16[2,32,256]{2,1,0:T(8,128)(2,1)S(1)}, u32[]{:S(2)}, u32[]{:S(2)}) %collective-permute-start.2) | collective-permute-done | bytes 32800 | tf_op jit(solution)/shard_map/ppermute | solution.py:358
  13.3 0.6 %edge.1.after.rest_4_ = bf16[2,128,256]{2,1,0:T(8,128)(2,1)S(1)} custom-call(s32[4,8]{1,0:T(4,128)S(1)} %get-tuple-element.33.owner, bf16[2,32,256]{2,1,0:T(8,128)(2,1)S(1)} %get-tuple-element.34.rest_0_, bf16[2,32,256]{2,1,0:T(8,128)(2,1)S(1)} %collective-permute-done.rest_1_, bf16[2,32,256]{2,1,0:T(8,128)(2,1)S(1)} %collective-permute-done.1.rest_2_, ...), custom_call_target="tpu_custom_call" | custom-call | tf_op jit(solution)/shard_map/edge/pallas_call | solution.py:342
  13.9 1.9 %collective-permute-start.6 = (bf16[2,128,256]{2,1,0:T(8,128)(2,1)S(1)}, bf16[2,128,256]{2,1,0:T(8,128)(2,1)S(1)}, u32[]{:S(2)}, u32[]{:S(2)}) collective-permute-start(bf16[2,128,256]{2,1,0:T(8,128)(2,1)S(1)} %edge.1.after.rest_4_), channel_id=1, source_target_pairs={{0,1},{1,0},{3,7},{7,3},{4,5},{5,4},{6,10},{10,6},{8,9},{9,8},{11,... | collective-permute-start | bytes 393224 | tf_op jit(solution)/shard_map/ppermute | solution.py:387
  15.9 2.0 %load.1 = (s32[256]{0:T(256)S(1)}, bf16[3,768,256]{2,1,0:T(8,128)(2,1)S(1)}, f32[1,256]{1,0:T(1,128)S(1)}, bf16[3,768,256]{2,1,0:T(8,128)(2,1)S(1)}, f32[1,256]{...) custom-call(bf16[2,128,256]{2,1,0:T(8,128)(2,1)S(1)} %edge.1.after.r, ...), custom_call_target="tpu_custom_call" | custom-call | tf_op jit(solution)/shard_map/load/pallas_call | solution.py:342
  17.9 0.0 collective-permute-done.3.rest_1_
  17.9 2.4 %collective-permute-done.4.rest_2_ = bf16[8,32,256]{2,1,0:T(8,128)(2,1)S(1)} collective-permute-done((bf16[8,32,256]{2,1,0:T(8,128)(2,1)S(1)}, bf16[8,32,256]{2,1,0:T(8,128)(2,1)S(1)}, u32[]{:S(2)}, u32[]{:S(2)}) %collective-permute-start.4) | collective-permute-done | bytes 131104 | tf_op jit(solution)/shard_map/ppermute | solution.py:358
  20.3 0.5 %collective-permute-done.5.rest_3_ = bf16[8,32,256]{2,1,0:T(8,128)(2,1)S(1)} collective-permute-done((bf16[8,32,256]{2,1,0:T(8,128)(2,1)S(1)}, bf16[8,32,256]{2,1,0:T(8,128)(2,1)S(1)}, u32[]{:S(2)}, u32[]{:S(2)}) %collective-permute-start.5) | collective-permute-done | bytes 131104 | tf_op jit(solution)/shard_map/ppermute | solution.py:358
  20.8 1.9 %collective-permute-done.6.rest_5_ = bf16[2,128,256]{2,1,0:T(8,128)(2,1)S(1)} collective-permute-done((bf16[2,128,256]{2,1,0:T(8,128)(2,1)S(1)}, bf16[2,128,256]{2,1,0:T(8,128)(2,1)S(1)}, u32[]{:S(2)}, u32[]{:S(2)}) %collective-permute-start.6) | collective-permute-done | bytes 131104 | tf_op jit(solution)/shard_map/ppermute | solution.py:387
  22.7 7.9 %main.1 = (bf16[272,256]{1,0:T(8,128)(2,1)S(1)}, bf16[1024,256]{1,0:T(8,128)(2,1)S(1)}, bf16[1024,256]{1,0:T(8,128)(2,1)S(1)}, bf16[1024,64]{1,0:T(8,128)(2,1)S(1)}, bf16[64,1024]{1,0:T(8,128)(2,1)S(1)}) custom-call(s32[4,8]{1,0:T(4,128)S(1)} %get-tuple-element.33.owner, s32[256]{0:T(256)S(1)} %get-tuple-element.38.counts, ...), custom_call_target="tpu_custom_call" | custom-call | tf_op jit(solution)/shard_map/main/pallas_call | solution.py:342
  30.6 0.1 collective-permute-start.8
  30.7 3.1 %rest.1 = (bf16[256,256]{1,0:T(8,128)(2,1)S(1)}, bf16[256,256]{1,0:T(8,128)(2,1)S(1)}, bf16[256,256]{1,0:T(8,128)(2,1)S(1)}) custom-call(s32[4,8]{1,0:T(4,128)S(1)} %get-tuple-element.33.owner, s32[256]{0:T(256)S(1)} %get-tuple-element.38.counts, bf16[1024,256]{1,0:T(8,128)(2,1)S(1)} %get-tuple-element.51.rest_0_, ...), custom_call_target="tpu_custom_call" | custom-call | tf_op jit(solution)/shard_map/rest/pallas_call | solution.py:342
  33.8 1.9 %collective-permute-start.7 = (bf16[256,256]{1,0:T(8,128)(2,1)S(1)}, bf16[256,256]{1,0:T(8,128)(2,1)S(1)}, u32[]{:S(2)}, u32[]{:S(2)}) collective-permute-start(bf16[256,256]{1,0:T(8,128)(2,1)S(1)} %get-tuple-element.56), channel_id=1, source_target_pairs={{0,1},{1,2},{2,3},{3,0},{4,5},{5,6},{6,7},{7,4},{8,9},{9,10},{10,1... | collective-permute-start | bytes 393224 | tf_op jit(solution)/shard_map/ppermute | solution.py:358
  35.7 1.9 %collective-permute-start.9 = (bf16[256,256]{1,0:T(8,128)(2,1)S(1)}, bf16[256,256]{1,0:T(8,128)(2,1)S(1)}, u32[]{:S(2)}, u32[]{:S(2)}) collective-permute-start(bf16[256,256]{1,0:T(8,128)(2,1)S(1)} %get-tuple-element.58), channel_id=1, source_target_pairs={{0,3},{1,0},{2,1},{3,2},{4,7},{5,4},{6,5},{7,6},{8,11},{9,8},{10,9... | collective-permute-start | bytes 393224 | tf_op jit(solution)/shard_map/ppermute | solution.py:358
  37.7 4.1 %collective-permute-done.7.rest_1_ = bf16[256,256]{1,0:T(8,128)(2,1)S(1)} collective-permute-done((bf16[256,256]{1,0:T(8,128)(2,1)S(1)}, bf16[256,256]{1,0:T(8,128)(2,1)S(1)}, u32[]{:S(2)}, u32[]{:S(2)}) %collective-permute-start.7) | collective-permute-done | bytes 131104 | tf_op jit(solution)/shard_map/ppermute | solution.py:358
  41.8 3.1 %collective-permute-done.9.rest_3_ = bf16[256,256]{1,0:T(8,128)(2,1)S(1)} collective-permute-done((bf16[256,256]{1,0:T(8,128)(2,1)S(1)}, bf16[256,256]{1,0:T(8,128)(2,1)S(1)}, u32[]{:S(2)}, u32[]{:S(2)}) %collective-permute-start.9) | collective-permute-done | bytes 131104 | tf_op jit(solution)/shard_map/ppermute | solution.py:358
  44.9 1.5 %store.1 = bf16[32,32,256]{2,1,0:T(8,128)(2,1)} custom-call(s32[4,8]{1,0:T(4,128)S(1)} %get-tuple-element.32.rotation, bf16[256,256]{1,0:T(8,128)(2,1)S(1)} %get-tuple-element.55.rest_0_, bf16[256,256]{1,0:T(8,128)(2,1)S(1)} %collective-permute-done.7.rest_1_, bf16[272,256]{1,0:T(8,128)(2,1)S(1)} %collective-permute-done.8.rest_2_, ...), custom_call_target="tpu_custom_call" | custom-call | tf_op jit(solution)/shard_map/store/pallas_call | solution.py:342
  (2 shorter events, 0.0 us)
Async XLA Ops:
  1.4 8.2 %collective-permute-start = (bf16[2,32,256]{2,1,0:T(8,128)(2,1)S(1)}, bf16[2,32,256]{2,1,0:T(8,128)(2,1)S(1)}, u32[]{:S(2)}, u32[]{:S(2)}) collective-permute-start(bf16[2,32,256]{2,1,0:T(8,128)(2,1)S(1)} %get-tuple-element.35), channel_id=1, source_target_pairs={{0,1},{1,2},{2,3},{3,0},{4,5},{5,6},{6,7},{7,4},{8,9},{9,10},{10,1... | collective-permute-start | bytes 98312 | tf_op jit(solution)/shard_map/ppermute | solution.py:358
  4.5 7.8 %collective-permute-start.1 = (bf16[2,32,256]{2,1,0:T(8,128)(2,1)S(1)}, bf16[2,32,256]{2,1,0:T(8,128)(2,1)S(1)}, u32[]{:S(2)}, u32[]{:S(2)}) collective-permute-start(bf16[2,32,256]{2,1,0:T(8,128)(2,1)S(1)} %get-tuple-element.36), channel_id=1, source_target_pairs={{0,2},{1,3},{2,0},{3,1},{4,6},{5,7},{6,4},{7,5},{8,10},{9,11},{10,... | collective-permute-start | bytes 98312 | tf_op jit(solution)/shard_map/ppermute | solution.py:358
  7.6 5.8 %collective-permute-start.2 = (bf16[2,32,256]{2,1,0:T(8,128)(2,1)S(1)}, bf16[2,32,256]{2,1,0:T(8,128)(2,1)S(1)}, u32[]{:S(2)}, u32[]{:S(2)}) collective-permute-start(bf16[2,32,256]{2,1,0:T(8,128)(2,1)S(1)} %get-tuple-element.37), channel_id=1, source_target_pairs={{0,3},{1,0},{2,1},{3,2},{4,7},{5,4},{6,5},{7,6},{8,11},{9,8},{10,9... | collective-permute-start | bytes 98312 | tf_op jit(solution)/shard_map/ppermute | solution.py:358
  8.5 9.4 %collective-permute-start.3 = (bf16[8,32,256]{2,1,0:T(8,128)(2,1)S(1)}, bf16[8,32,256]{2,1,0:T(8,128)(2,1)S(1)}, u32[]{:S(2)}, u32[]{:S(2)}) collective-permute-start(bf16[8,32,256]{2,1,0:T(8,128)(2,1)S(1)} %get-tuple-element.40), channel_id=1, source_target_pairs={{0,1},{1,2},{2,3},{3,0},{4,5},{5,6},{6,7},{7,4},{8,9},{9,10},{10,1... | collective-permute-start | bytes 393224 | tf_op jit(solution)/shard_map/ppermute | solution.py:358
  9.6 10.7 %collective-permute-start.4 = (bf16[8,32,256]{2,1,0:T(8,128)(2,1)S(1)}, bf16[8,32,256]{2,1,0:T(8,128)(2,1)S(1)}, u32[]{:S(2)}, u32[]{:S(2)}) collective-permute-start(bf16[8,32,256]{2,1,0:T(8,128)(2,1)S(1)} %get-tuple-element.41), channel_id=1, source_target_pairs={{0,2},{1,3},{2,0},{3,1},{4,6},{5,7},{6,4},{7,5},{8,10},{9,11},{10,... | collective-permute-start | bytes 393224 | tf_op jit(solution)/shard_map/ppermute | solution.py:358
  9.6 11.2 %collective-permute-start.5 = (bf16[8,32,256]{2,1,0:T(8,128)(2,1)S(1)}, bf16[8,32,256]{2,1,0:T(8,128)(2,1)S(1)}, u32[]{:S(2)}, u32[]{:S(2)}) collective-permute-start(bf16[8,32,256]{2,1,0:T(8,128)(2,1)S(1)} %get-tuple-element.42), channel_id=1, source_target_pairs={{0,3},{1,0},{2,1},{3,2},{4,7},{5,4},{6,5},{7,6},{8,11},{9,8},{10,9... | collective-permute-start | bytes 393224 | tf_op jit(solution)/shard_map/ppermute | solution.py:358
  13.9 8.8 %collective-permute-start.6 = (bf16[2,128,256]{2,1,0:T(8,128)(2,1)S(1)}, bf16[2,128,256]{2,1,0:T(8,128)(2,1)S(1)}, u32[]{:S(2)}, u32[]{:S(2)}) collective-permute-start(bf16[2,128,256]{2,1,0:T(8,128)(2,1)S(1)} %edge.1.after.rest_4_), channel_id=1, source_target_pairs={{0,1},{1,0},{3,7},{7,3},{4,5},{5,4},{6,10},{10,6},{8,9},{9,8},{11,... | collective-permute-start | bytes 393224 | tf_op jit(solution)/shard_map/ppermute | solution.py:387
  30.6 14.2 %collective-permute-start.8 = (bf16[272,256]{1,0:T(8,128)(2,1)S(1)}, bf16[272,256]{1,0:T(8,128)(2,1)S(1)}, u32[]{:S(2)}, u32[]{:S(2)}) collective-permute-start(bf16[272,256]{1,0:T(8,128)(2,1)S(1)} %get-tuple-element.57), channel_id=1, source_target_pairs={{0,2},{1,3},{2,0},{3,1},{4,6},{5,7},{6,4},{7,5},{8,10},{9,11},{10,... | collective-permute-start | bytes 417800 | tf_op jit(solution)/shard_map/ppermute | solution.py:358
  33.8 8.0 %collective-permute-start.7 = (bf16[256,256]{1,0:T(8,128)(2,1)S(1)}, bf16[256,256]{1,0:T(8,128)(2,1)S(1)}, u32[]{:S(2)}, u32[]{:S(2)}) collective-permute-start(bf16[256,256]{1,0:T(8,128)(2,1)S(1)} %get-tuple-element.56), channel_id=1, source_target_pairs={{0,1},{1,2},{2,3},{3,0},{4,5},{5,6},{6,7},{7,4},{8,9},{9,10},{10,1... | collective-permute-start | bytes 393224 | tf_op jit(solution)/shard_map/ppermute | solution.py:358
  35.7 9.1 %collective-permute-start.9 = (bf16[256,256]{1,0:T(8,128)(2,1)S(1)}, bf16[256,256]{1,0:T(8,128)(2,1)S(1)}, u32[]{:S(2)}, u32[]{:S(2)}) collective-permute-start(bf16[256,256]{1,0:T(8,128)(2,1)S(1)} %get-tuple-element.58), channel_id=1, source_target_pairs={{0,3},{1,0},{2,1},{3,2},{4,7},{5,4},{6,5},{7,6},{8,11},{9,8},{10,9... | collective-permute-start | bytes 393224 | tf_op jit(solution)/shard_map/ppermute | solution.py:358

commit v12 on v11

--- a/solution.py
+++ b/solution.py
@@ -11,6 +11,7 @@
 HALO = 2
 LANES = 128
 GROUP = 256
+CHUNKS = 3
 AHEAD = 16
 VMEM_BYTES = 28 * 1024 * 1024
 
@@ -271,9 +272,26 @@
         values[:, at] = by_last(w_value[...], scaled).astype(jnp.bfloat16)
 
     total = rows + HALO
-    spread_inputs(0, total + HALO)
-    spread_acts(0, total, convolve(taps, w_conv1, b_conv1, 0, total))
-    mix(0, rows, convolve(acts, w_conv2, b_conv2, 0, rows))
+    chunks = min(CHUNKS, total // HALO)
+    cuts = [-(-total * c // chunks) for c in range(chunks + 1)]
+    ends = [0] + [cut + HALO for cut in cuts[1:]]
+    lows = [max(cut - HALO, 0) for cut in cuts]
+    firsts, seconds = [], []
+    spread_inputs(ends[0], ends[1])
+    for c in range(chunks):
+        firsts.append(convolve(taps, w_conv1, b_conv1, cuts[c], cuts[c + 1] - cuts[c]))
+        if c:
+            spread_acts(cuts[c - 1], cuts[c], firsts[c - 1])
+        if c + 1 < chunks:
+            spread_inputs(ends[c + 1], ends[c + 2])
+    for c in range(chunks):
+        count = lows[c + 1] - lows[c]
+        seconds.append(convolve(acts, w_conv2, b_conv2, lows[c], count) if count else None)
+        if c == 0:
+            spread_acts(cuts[-2], total, firsts[-1])
+        elif seconds[c - 1] is not None:
+            mix(lows[c - 1], lows[c], seconds[c - 1])
+    mix(lows[-2], rows, seconds[-1])
     result[rows * (cols // n) :, :] = jnp.zeros((AHEAD, chans), result.dtype)
     segments = [owner[lax.rem(me + first, n), band]]
     shared = limits[1 : rows + 1], mixed, normed, keys, values, w_query, w_out

time: 46.6 us -> 44.3 us (0.951)
  Pallas kernels: 16.5 us -> 14.7 us
  waiting for transfers between devices: 13.1 us -> 12 us
  starting transfers between devices: 16.7 us -> 17.3 us
    pallas_call x6, Pallas kernels: 16.5 us -> 14.7 us  [call(): pl.pallas_call(functools.partial(kernel, n, rows), out_shape=out, in_spec...]
    ppermute x9, waiting for transfers between devices: 11.2 us -> 10.3 us  [around_by(): return lax.ppermute(x, 'lon', [(i, (i + d) % n) for i in range(n)])]
    ppermute x1, starting transfers between devices: 1.92 us -> 2.48 us  [on_device(): received = lax.ppermute(sent, ('lat', 'lon'), pairs)]
  transfers between devices with their start and end apart: 10 -> 10, of which waited for: 6 -> 4; matrix products, arithmetic and copies ran while one was open for 0% -> 0% of each run, Pallas kernels for 12% -> 13%
where the time goes in v12:
time: 44.3 us; the launch traced here: 44.1 us
  starting transfers between devices  17.3 us (39%)
  Pallas kernels  14.7 us (33%)
  waiting for transfers between devices  12 us (27%)
    ppermute x9, starting transfers between devices, around_by(): return lax.ppermute(x, 'lon', [(i, (i + d) % n) for i in range(n)])  14.8 us
    pallas_call x6, Pallas kernels, call(): pl.pallas_call(functools.partial(kernel, n, rows), out_shape=out, in_spec...  14.7 us
    ppermute x9, waiting for transfers between devices, around_by(): return lax.ppermute(x, 'lon', [(i, (i + d) % n) for i in range(n)])  10.3 us
    ppermute x1, starting transfers between devices, on_device(): received = lax.ppermute(sent, ('lat', 'lon'), pairs)  2.48 us
    ppermute x1, waiting for transfers between devices, on_device(): received = lax.ppermute(sent, ('lat', 'lon'), pairs)  1.7 us
  transfers between devices with their start and end apart: 10, of which 4 were waited for; matrix products, arithmetic and copies ran while one was open for 0% of the time, Pallas kernels for 13%

profile of v12, /device:TPU:0, one launch (start us, length us, event | category | flops | bytes accessed | tf_op | source)
XLA Modules:
  0.0 44.1 jit_solution(2750565497097452169)
XLA Ops:
  0.0 1.9 %send.1 = (bf16[2,32,256]{2,1,0:T(8,128)(2,1)S(1)}, bf16[2,32,256]{2,1,0:T(8,128)(2,1)S(1)}, bf16[2,32,256]{2,1,0:T(8,128)(2,1)S(1)}, bf16[2,32,256]{2,1,0:T(8,1...) custom-call(s32[4,8]{1,0:T(4,128)} %bitcast.12, ...), custom_call_target="tpu_custom_call" | custom-call | tf_op jit(solution)/shard_map/send/pallas_call | solution.py:360
  1.9 2.6 %collective-permute-start = (bf16[2,32,256]{2,1,0:T(8,128)(2,1)S(1)}, bf16[2,32,256]{2,1,0:T(8,128)(2,1)S(1)}, u32[]{:S(2)}, u32[]{:S(2)}) collective-permute-start(bf16[2,32,256]{2,1,0:T(8,128)(2,1)S(1)} %get-tuple-element.35), channel_id=1, source_target_pairs={{0,1},{1,2},{2,3},{3,0},{4,5},{5,6},{6,7},{7,4},{8,9},{9,10},{10,1... | collective-permute-start | bytes 98312 | tf_op jit(solution)/shard_map/ppermute | solution.py:376
  4.5 2.4 %collective-permute-start.1 = (bf16[2,32,256]{2,1,0:T(8,128)(2,1)S(1)}, bf16[2,32,256]{2,1,0:T(8,128)(2,1)S(1)}, u32[]{:S(2)}, u32[]{:S(2)}) collective-permute-start(bf16[2,32,256]{2,1,0:T(8,128)(2,1)S(1)} %get-tuple-element.36), channel_id=1, source_target_pairs={{0,2},{1,3},{2,0},{3,1},{4,6},{5,7},{6,4},{7,5},{8,10},{9,11},{10,... | collective-permute-start | bytes 98312 | tf_op jit(solution)/shard_map/ppermute | solution.py:376
  6.9 2.0 %collective-permute-start.2 = (bf16[2,32,256]{2,1,0:T(8,128)(2,1)S(1)}, bf16[2,32,256]{2,1,0:T(8,128)(2,1)S(1)}, u32[]{:S(2)}, u32[]{:S(2)}) collective-permute-start(bf16[2,32,256]{2,1,0:T(8,128)(2,1)S(1)} %get-tuple-element.37), channel_id=1, source_target_pairs={{0,3},{1,0},{2,1},{3,2},{4,7},{5,4},{6,5},{7,6},{8,11},{9,8},{10,9... | collective-permute-start | bytes 98312 | tf_op jit(solution)/shard_map/ppermute | solution.py:376
  8.9 0.0 collective-permute-start.3
  8.9 0.5 %collective-permute-start.4 = (bf16[8,32,256]{2,1,0:T(8,128)(2,1)S(1)}, bf16[8,32,256]{2,1,0:T(8,128)(2,1)S(1)}, u32[]{:S(2)}, u32[]{:S(2)}) collective-permute-start(bf16[8,32,256]{2,1,0:T(8,128)(2,1)S(1)} %get-tuple-element.41), channel_id=1, source_target_pairs={{0,2},{1,3},{2,0},{3,1},{4,6},{5,7},{6,4},{7,5},{8,10},{9,11},{10,... | collective-permute-start | bytes 393224 | tf_op jit(solution)/shard_map/ppermute | solution.py:376
  9.5 0.0 collective-permute-done.rest_1_
  9.5 3.3 %collective-permute-start.5 = (bf16[8,32,256]{2,1,0:T(8,128)(2,1)S(1)}, bf16[8,32,256]{2,1,0:T(8,128)(2,1)S(1)}, u32[]{:S(2)}, u32[]{:S(2)}) collective-permute-start(bf16[8,32,256]{2,1,0:T(8,128)(2,1)S(1)} %get-tuple-element.42), channel_id=1, source_target_pairs={{0,3},{1,0},{2,1},{3,2},{4,7},{5,4},{6,5},{7,6},{8,11},{9,8},{10,9... | collective-permute-start | bytes 393224 | tf_op jit(solution)/shard_map/ppermute | solution.py:376
  12.8 0.0 collective-permute-done.2.rest_3_
  12.8 0.6 %edge.1.after.rest_4_ = bf16[2,128,256]{2,1,0:T(8,128)(2,1)S(1)} custom-call(s32[4,8]{1,0:T(4,128)S(1)} %get-tuple-element.33.owner, bf16[2,32,256]{2,1,0:T(8,128)(2,1)S(1)} %get-tuple-element.34.rest_0_, bf16[2,32,256]{2,1,0:T(8,128)(2,1)S(1)} %collective-permute-done.rest_1_, bf16[2,32,256]{2,1,0:T(8,128)(2,1)S(1)} %collective-permute-done.1.rest_2_, ...), custom_call_target="tpu_custom_call" | custom-call | tf_op jit(solution)/shard_map/edge/pallas_call | solution.py:360
  13.4 2.5 %collective-permute-start.6 = (bf16[2,128,256]{2,1,0:T(8,128)(2,1)S(1)}, bf16[2,128,256]{2,1,0:T(8,128)(2,1)S(1)}, u32[]{:S(2)}, u32[]{:S(2)}) collective-permute-start(bf16[2,128,256]{2,1,0:T(8,128)(2,1)S(1)} %edge.1.after.rest_4_), channel_id=1, source_target_pairs={{0,1},{1,0},{3,7},{7,3},{4,5},{5,4},{6,10},{10,6},{8,9},{9,8},{11,... | collective-permute-start | bytes 393224 | tf_op jit(solution)/shard_map/ppermute | solution.py:405
  15.8 2.0 %load.1 = (s32[256]{0:T(256)S(1)}, bf16[3,768,256]{2,1,0:T(8,128)(2,1)S(1)}, f32[1,256]{1,0:T(1,128)S(1)}, bf16[3,768,256]{2,1,0:T(8,128)(2,1)S(1)}, f32[1,256]{...) custom-call(bf16[2,128,256]{2,1,0:T(8,128)(2,1)S(1)} %edge.1.after.r, ...), custom_call_target="tpu_custom_call" | custom-call | tf_op jit(solution)/shard_map/load/pallas_call | solution.py:360
  17.9 3.1 %collective-permute-done.4.rest_2_ = bf16[8,32,256]{2,1,0:T(8,128)(2,1)S(1)} collective-permute-done((bf16[8,32,256]{2,1,0:T(8,128)(2,1)S(1)}, bf16[8,32,256]{2,1,0:T(8,128)(2,1)S(1)}, u32[]{:S(2)}, u32[]{:S(2)}) %collective-permute-start.4) | collective-permute-done | bytes 131104 | tf_op jit(solution)/shard_map/ppermute | solution.py:376
  20.9 0.0 collective-permute-done.5.rest_3_
  20.9 1.7 %collective-permute-done.6.rest_5_ = bf16[2,128,256]{2,1,0:T(8,128)(2,1)S(1)} collective-permute-done((bf16[2,128,256]{2,1,0:T(8,128)(2,1)S(1)}, bf16[2,128,256]{2,1,0:T(8,128)(2,1)S(1)}, u32[]{:S(2)}, u32[]{:S(2)}) %collective-permute-start.6) | collective-permute-done | bytes 131104 | tf_op jit(solution)/shard_map/ppermute | solution.py:405
  22.6 5.5 %main.1 = (bf16[272,256]{1,0:T(8,128)(2,1)S(1)}, bf16[1024,256]{1,0:T(8,128)(2,1)S(1)}, bf16[1024,256]{1,0:T(8,128)(2,1)S(1)}, bf16[1024,64]{1,0:T(8,128)(2,1)S(1)}, bf16[64,1024]{1,0:T(8,128)(2,1)S(1)}) custom-call(s32[4,8]{1,0:T(4,128)S(1)} %get-tuple-element.33.owner, s32[256]{0:T(256)S(1)} %get-tuple-element.38.counts, ...), custom_call_target="tpu_custom_call" | custom-call | tf_op jit(solution)/shard_map/main/pallas_call | solution.py:360
  28.1 0.1 collective-permute-start.8
  28.2 3.1 %rest.1 = (bf16[256,256]{1,0:T(8,128)(2,1)S(1)}, bf16[256,256]{1,0:T(8,128)(2,1)S(1)}, bf16[256,256]{1,0:T(8,128)(2,1)S(1)}) custom-call(s32[4,8]{1,0:T(4,128)S(1)} %get-tuple-element.33.owner, s32[256]{0:T(256)S(1)} %get-tuple-element.38.counts, bf16[1024,256]{1,0:T(8,128)(2,1)S(1)} %get-tuple-element.51.rest_0_, ...), custom_call_target="tpu_custom_call" | custom-call | tf_op jit(solution)/shard_map/rest/pallas_call | solution.py:360
  31.3 1.8 %collective-permute-start.7 = (bf16[256,256]{1,0:T(8,128)(2,1)S(1)}, bf16[256,256]{1,0:T(8,128)(2,1)S(1)}, u32[]{:S(2)}, u32[]{:S(2)}) collective-permute-start(bf16[256,256]{1,0:T(8,128)(2,1)S(1)} %get-tuple-element.56), channel_id=1, source_target_pairs={{0,1},{1,2},{2,3},{3,0},{4,5},{5,6},{6,7},{7,4},{8,9},{9,10},{10,1... | collective-permute-start | bytes 393224 | tf_op jit(solution)/shard_map/ppermute | solution.py:376
  33.1 2.0 %collective-permute-start.9 = (bf16[256,256]{1,0:T(8,128)(2,1)S(1)}, bf16[256,256]{1,0:T(8,128)(2,1)S(1)}, u32[]{:S(2)}, u32[]{:S(2)}) collective-permute-start(bf16[256,256]{1,0:T(8,128)(2,1)S(1)} %get-tuple-element.58), channel_id=1, source_target_pairs={{0,3},{1,0},{2,1},{3,2},{4,7},{5,4},{6,5},{7,6},{8,11},{9,8},{10,9... | collective-permute-start | bytes 393224 | tf_op jit(solution)/shard_map/ppermute | solution.py:376
  35.2 4.1 %collective-permute-done.7.rest_1_ = bf16[256,256]{1,0:T(8,128)(2,1)S(1)} collective-permute-done((bf16[256,256]{1,0:T(8,128)(2,1)S(1)}, bf16[256,256]{1,0:T(8,128)(2,1)S(1)}, u32[]{:S(2)}, u32[]{:S(2)}) %collective-permute-start.7) | collective-permute-done | bytes 131104 | tf_op jit(solution)/shard_map/ppermute | solution.py:376
  39.3 3.1 %collective-permute-done.9.rest_3_ = bf16[256,256]{1,0:T(8,128)(2,1)S(1)} collective-permute-done((bf16[256,256]{1,0:T(8,128)(2,1)S(1)}, bf16[256,256]{1,0:T(8,128)(2,1)S(1)}, u32[]{:S(2)}, u32[]{:S(2)}) %collective-permute-start.9) | collective-permute-done | bytes 131104 | tf_op jit(solution)/shard_map/ppermute | solution.py:376
  42.4 0.0 collective-permute-done.8.rest_2_
  42.4 1.7 %store.1 = bf16[32,32,256]{2,1,0:T(8,128)(2,1)} custom-call(s32[4,8]{1,0:T(4,128)S(1)} %get-tuple-element.32.rotation, bf16[256,256]{1,0:T(8,128)(2,1)S(1)} %get-tuple-element.55.rest_0_, bf16[256,256]{1,0:T(8,128)(2,1)S(1)} %collective-permute-done.7.rest_1_, bf16[272,256]{1,0:T(8,128)(2,1)S(1)} %collective-permute-done.8.rest_2_, ...), custom_call_target="tpu_custom_call" | custom-call | tf_op jit(solution)/shard_map/store/pallas_call | solution.py:360
  (2 shorter events, 0.0 us)
Async XLA Ops:
  1.9 7.6 %collective-permute-start = (bf16[2,32,256]{2,1,0:T(8,128)(2,1)S(1)}, bf16[2,32,256]{2,1,0:T(8,128)(2,1)S(1)}, u32[]{:S(2)}, u32[]{:S(2)}) collective-permute-start(bf16[2,32,256]{2,1,0:T(8,128)(2,1)S(1)} %get-tuple-element.35), channel_id=1, source_target_pairs={{0,1},{1,2},{2,3},{3,0},{4,5},{5,6},{6,7},{7,4},{8,9},{9,10},{10,1... | collective-permute-start | bytes 98312 | tf_op jit(solution)/shard_map/ppermute | solution.py:376
  4.5 8.2 %collective-permute-start.1 = (bf16[2,32,256]{2,1,0:T(8,128)(2,1)S(1)}, bf16[2,32,256]{2,1,0:T(8,128)(2,1)S(1)}, u32[]{:S(2)}, u32[]{:S(2)}) collective-permute-start(bf16[2,32,256]{2,1,0:T(8,128)(2,1)S(1)} %get-tuple-element.36), channel_id=1, source_target_pairs={{0,2},{1,3},{2,0},{3,1},{4,6},{5,7},{6,4},{7,5},{8,10},{9,11},{10,... | collective-permute-start | bytes 98312 | tf_op jit(solution)/shard_map/ppermute | solution.py:376
  6.9 5.8 %collective-permute-start.2 = (bf16[2,32,256]{2,1,0:T(8,128)(2,1)S(1)}, bf16[2,32,256]{2,1,0:T(8,128)(2,1)S(1)}, u32[]{:S(2)}, u32[]{:S(2)}) collective-permute-start(bf16[2,32,256]{2,1,0:T(8,128)(2,1)S(1)} %get-tuple-element.37), channel_id=1, source_target_pairs={{0,3},{1,0},{2,1},{3,2},{4,7},{5,4},{6,5},{7,6},{8,11},{9,8},{10,9... | collective-permute-start | bytes 98312 | tf_op jit(solution)/shard_map/ppermute | solution.py:376
  8.9 8.9 %collective-permute-start.3 = (bf16[8,32,256]{2,1,0:T(8,128)(2,1)S(1)}, bf16[8,32,256]{2,1,0:T(8,128)(2,1)S(1)}, u32[]{:S(2)}, u32[]{:S(2)}) collective-permute-start(bf16[8,32,256]{2,1,0:T(8,128)(2,1)S(1)} %get-tuple-element.40), channel_id=1, source_target_pairs={{0,1},{1,2},{2,3},{3,0},{4,5},{5,6},{6,7},{7,4},{8,9},{9,10},{10,1... | collective-permute-start | bytes 393224 | tf_op jit(solution)/shard_map/ppermute | solution.py:376
  8.9 12.0 %collective-permute-start.4 = (bf16[8,32,256]{2,1,0:T(8,128)(2,1)S(1)}, bf16[8,32,256]{2,1,0:T(8,128)(2,1)S(1)}, u32[]{:S(2)}, u32[]{:S(2)}) collective-permute-start(bf16[8,32,256]{2,1,0:T(8,128)(2,1)S(1)} %get-tuple-element.41), channel_id=1, source_target_pairs={{0,2},{1,3},{2,0},{3,1},{4,6},{5,7},{6,4},{7,5},{8,10},{9,11},{10,... | collective-permute-start | bytes 393224 | tf_op jit(solution)/shard_map/ppermute | solution.py:376
  9.5 11.5 %collective-permute-start.5 = (bf16[8,32,256]{2,1,0:T(8,128)(2,1)S(1)}, bf16[8,32,256]{2,1,0:T(8,128)(2,1)S(1)}, u32[]{:S(2)}, u32[]{:S(2)}) collective-permute-start(bf16[8,32,256]{2,1,0:T(8,128)(2,1)S(1)} %get-tuple-element.42), channel_id=1, source_target_pairs={{0,3},{1,0},{2,1},{3,2},{4,7},{5,4},{6,5},{7,6},{8,11},{9,8},{10,9... | collective-permute-start | bytes 393224 | tf_op jit(solution)/shard_map/ppermute | solution.py:376
  13.4 9.3 %collective-permute-start.6 = (bf16[2,128,256]{2,1,0:T(8,128)(2,1)S(1)}, bf16[2,128,256]{2,1,0:T(8,128)(2,1)S(1)}, u32[]{:S(2)}, u32[]{:S(2)}) collective-permute-start(bf16[2,128,256]{2,1,0:T(8,128)(2,1)S(1)} %edge.1.after.rest_4_), channel_id=1, source_target_pairs={{0,1},{1,0},{3,7},{7,3},{4,5},{5,4},{6,10},{10,6},{8,9},{9,8},{11,... | collective-permute-start | bytes 393224 | tf_op jit(solution)/shard_map/ppermute | solution.py:405
  28.1 14.2 %collective-permute-start.8 = (bf16[272,256]{1,0:T(8,128)(2,1)S(1)}, bf16[272,256]{1,0:T(8,128)(2,1)S(1)}, u32[]{:S(2)}, u32[]{:S(2)}) collective-permute-start(bf16[272,256]{1,0:T(8,128)(2,1)S(1)} %get-tuple-element.57), channel_id=1, source_target_pairs={{0,2},{1,3},{2,0},{3,1},{4,6},{5,7},{6,4},{7,5},{8,10},{9,11},{10,... | collective-permute-start | bytes 417800 | tf_op jit(solution)/shard_map/ppermute | solution.py:376
  31.3 8.0 %collective-permute-start.7 = (bf16[256,256]{1,0:T(8,128)(2,1)S(1)}, bf16[256,256]{1,0:T(8,128)(2,1)S(1)}, u32[]{:S(2)}, u32[]{:S(2)}) collective-permute-start(bf16[256,256]{1,0:T(8,128)(2,1)S(1)} %get-tuple-element.56), channel_id=1, source_target_pairs={{0,1},{1,2},{2,3},{3,0},{4,5},{5,6},{6,7},{7,4},{8,9},{9,10},{10,1... | collective-permute-start | bytes 393224 | tf_op jit(solution)/shard_map/ppermute | solution.py:376
  33.1 9.2 %collective-permute-start.9 = (bf16[256,256]{1,0:T(8,128)(2,1)S(1)}, bf16[256,256]{1,0:T(8,128)(2,1)S(1)}, u32[]{:S(2)}, u32[]{:S(2)}) collective-permute-start(bf16[256,256]{1,0:T(8,128)(2,1)S(1)} %get-tuple-element.58), channel_id=1, source_target_pairs={{0,3},{1,0},{2,1},{3,2},{4,7},{5,4},{6,5},{7,6},{8,11},{9,8},{10,9... | collective-permute-start | bytes 393224 | tf_op jit(solution)/shard_map/ppermute | solution.py:376

commit v13 on v12

--- a/solution.py
+++ b/solution.py
@@ -11,7 +11,7 @@
 HALO = 2
 LANES = 128
 GROUP = 256
-CHUNKS = 3
+CHUNKS = 4
 AHEAD = 16
 VMEM_BYTES = 28 * 1024 * 1024
 

time: 44.3 us -> 44 us (level)
  starting transfers between devices: 17.3 us -> 16.8 us
    ppermute x9, starting transfers between devices: 14.8 us -> 14.3 us  [around_by(): return lax.ppermute(x, 'lon', [(i, (i + d) % n) for i in range(n)])]
where the time goes in v13:
time: 44 us; the launch traced here: 44.1 us
  starting transfers between devices  16.8 us (38%)
  Pallas kernels  14.8 us (34%)
  waiting for transfers between devices  12.4 us (28%)
    pallas_call x6, Pallas kernels, call(): pl.pallas_call(functools.partial(kernel, n, rows), out_shape=out, in_spec...  14.8 us
    ppermute x9, starting transfers between devices, around_by(): return lax.ppermute(x, 'lon', [(i, (i + d) % n) for i in range(n)])  14.3 us
    ppermute x9, waiting for transfers between devices, around_by(): return lax.ppermute(x, 'lon', [(i, (i + d) % n) for i in range(n)])  10.7 us
    ppermute x1, starting transfers between devices, on_device(): received = lax.ppermute(sent, ('lat', 'lon'), pairs)  2.48 us
    ppermute x1, waiting for transfers between devices, on_device(): received = lax.ppermute(sent, ('lat', 'lon'), pairs)  1.75 us
  transfers between devices with their start and end apart: 10, of which 4 were waited for; matrix products, arithmetic and copies ran while one was open for 0% of the time, Pallas kernels for 13%

profile of v13, /device:TPU:0, one launch (start us, length us, event | category | flops | bytes accessed | tf_op | source)
XLA Modules:
  0.0 44.1 jit_solution(16333315890499193017)
XLA Ops:
  0.0 1.9 %send.1 = (bf16[2,32,256]{2,1,0:T(8,128)(2,1)S(1)}, bf16[2,32,256]{2,1,0:T(8,128)(2,1)S(1)}, bf16[2,32,256]{2,1,0:T(8,128)(2,1)S(1)}, bf16[2,32,256]{2,1,0:T(8,1...) custom-call(s32[4,8]{1,0:T(4,128)} %bitcast.12, ...), custom_call_target="tpu_custom_call" | custom-call | tf_op jit(solution)/shard_map/send/pallas_call | solution.py:360
  1.9 2.4 %collective-permute-start = (bf16[2,32,256]{2,1,0:T(8,128)(2,1)S(1)}, bf16[2,32,256]{2,1,0:T(8,128)(2,1)S(1)}, u32[]{:S(2)}, u32[]{:S(2)}) collective-permute-start(bf16[2,32,256]{2,1,0:T(8,128)(2,1)S(1)} %get-tuple-element.35), channel_id=1, source_target_pairs={{0,1},{1,2},{2,3},{3,0},{4,5},{5,6},{6,7},{7,4},{8,9},{9,10},{10,1... | collective-permute-start | bytes 98312 | tf_op jit(solution)/shard_map/ppermute | solution.py:376
  4.3 2.8 %collective-permute-start.1 = (bf16[2,32,256]{2,1,0:T(8,128)(2,1)S(1)}, bf16[2,32,256]{2,1,0:T(8,128)(2,1)S(1)}, u32[]{:S(2)}, u32[]{:S(2)}) collective-permute-start(bf16[2,32,256]{2,1,0:T(8,128)(2,1)S(1)} %get-tuple-element.36), channel_id=1, source_target_pairs={{0,2},{1,3},{2,0},{3,1},{4,6},{5,7},{6,4},{7,5},{8,10},{9,11},{10,... | collective-permute-start | bytes 98312 | tf_op jit(solution)/shard_map/ppermute | solution.py:376
  7.1 1.3 %collective-permute-start.2 = (bf16[2,32,256]{2,1,0:T(8,128)(2,1)S(1)}, bf16[2,32,256]{2,1,0:T(8,128)(2,1)S(1)}, u32[]{:S(2)}, u32[]{:S(2)}) collective-permute-start(bf16[2,32,256]{2,1,0:T(8,128)(2,1)S(1)} %get-tuple-element.37), channel_id=1, source_target_pairs={{0,3},{1,0},{2,1},{3,2},{4,7},{5,4},{6,5},{7,6},{8,11},{9,8},{10,9... | collective-permute-start | bytes 98312 | tf_op jit(solution)/shard_map/ppermute | solution.py:376
  8.5 0.7 %collective-permute-start.3 = (bf16[8,32,256]{2,1,0:T(8,128)(2,1)S(1)}, bf16[8,32,256]{2,1,0:T(8,128)(2,1)S(1)}, u32[]{:S(2)}, u32[]{:S(2)}) collective-permute-start(bf16[8,32,256]{2,1,0:T(8,128)(2,1)S(1)} %get-tuple-element.40), channel_id=1, source_target_pairs={{0,1},{1,2},{2,3},{3,0},{4,5},{5,6},{6,7},{7,4},{8,9},{9,10},{10,1... | collective-permute-start | bytes 393224 | tf_op jit(solution)/shard_map/ppermute | solution.py:376
  9.1 0.1 collective-permute-start.4
  9.3 0.0 collective-permute-done.rest_1_
  9.3 3.0 %collective-permute-start.5 = (bf16[8,32,256]{2,1,0:T(8,128)(2,1)S(1)}, bf16[8,32,256]{2,1,0:T(8,128)(2,1)S(1)}, u32[]{:S(2)}, u32[]{:S(2)}) collective-permute-start(bf16[8,32,256]{2,1,0:T(8,128)(2,1)S(1)} %get-tuple-element.42), channel_id=1, source_target_pairs={{0,3},{1,0},{2,1},{3,2},{4,7},{5,4},{6,5},{7,6},{8,11},{9,8},{10,9... | collective-permute-start | bytes 393224 | tf_op jit(solution)/shard_map/ppermute | solution.py:376
  12.3 0.0 collective-permute-done.1.rest_2_
  12.3 0.0 collective-permute-done.2.rest_3_
  12.3 0.6 %edge.1.after.rest_4_ = bf16[2,128,256]{2,1,0:T(8,128)(2,1)S(1)} custom-call(s32[4,8]{1,0:T(4,128)S(1)} %get-tuple-element.33.owner, bf16[2,32,256]{2,1,0:T(8,128)(2,1)S(1)} %get-tuple-element.34.rest_0_, bf16[2,32,256]{2,1,0:T(8,128)(2,1)S(1)} %collective-permute-done.rest_1_, bf16[2,32,256]{2,1,0:T(8,128)(2,1)S(1)} %collective-permute-done.1.rest_2_, ...), custom_call_target="tpu_custom_call" | custom-call | tf_op jit(solution)/shard_map/edge/pallas_call | solution.py:360
  12.9 2.5 %collective-permute-start.6 = (bf16[2,128,256]{2,1,0:T(8,128)(2,1)S(1)}, bf16[2,128,256]{2,1,0:T(8,128)(2,1)S(1)}, u32[]{:S(2)}, u32[]{:S(2)}) collective-permute-start(bf16[2,128,256]{2,1,0:T(8,128)(2,1)S(1)} %edge.1.after.rest_4_), channel_id=1, source_target_pairs={{0,1},{1,0},{3,7},{7,3},{4,5},{5,4},{6,10},{10,6},{8,9},{9,8},{11,... | collective-permute-start | bytes 393224 | tf_op jit(solution)/shard_map/ppermute | solution.py:405
  15.4 2.0 %load.1 = (s32[256]{0:T(256)S(1)}, bf16[3,768,256]{2,1,0:T(8,128)(2,1)S(1)}, f32[1,256]{1,0:T(1,128)S(1)}, bf16[3,768,256]{2,1,0:T(8,128)(2,1)S(1)}, f32[1,256]{...) custom-call(bf16[2,128,256]{2,1,0:T(8,128)(2,1)S(1)} %edge.1.after.r, ...), custom_call_target="tpu_custom_call" | custom-call | tf_op jit(solution)/shard_map/load/pallas_call | solution.py:360
  17.4 3.5 %collective-permute-done.4.rest_2_ = bf16[8,32,256]{2,1,0:T(8,128)(2,1)S(1)} collective-permute-done((bf16[8,32,256]{2,1,0:T(8,128)(2,1)S(1)}, bf16[8,32,256]{2,1,0:T(8,128)(2,1)S(1)}, u32[]{:S(2)}, u32[]{:S(2)}) %collective-permute-start.4) | collective-permute-done | bytes 131104 | tf_op jit(solution)/shard_map/ppermute | solution.py:376
  20.9 1.7 %collective-permute-done.6.rest_5_ = bf16[2,128,256]{2,1,0:T(8,128)(2,1)S(1)} collective-permute-done((bf16[2,128,256]{2,1,0:T(8,128)(2,1)S(1)}, bf16[2,128,256]{2,1,0:T(8,128)(2,1)S(1)}, u32[]{:S(2)}, u32[]{:S(2)}) %collective-permute-start.6) | collective-permute-done | bytes 131104 | tf_op jit(solution)/shard_map/ppermute | solution.py:405
  22.6 5.5 %main.1 = (bf16[272,256]{1,0:T(8,128)(2,1)S(1)}, bf16[1024,256]{1,0:T(8,128)(2,1)S(1)}, bf16[1024,256]{1,0:T(8,128)(2,1)S(1)}, bf16[1024,64]{1,0:T(8,128)(2,1)S(1)}, bf16[64,1024]{1,0:T(8,128)(2,1)S(1)}) custom-call(s32[4,8]{1,0:T(4,128)S(1)} %get-tuple-element.33.owner, s32[256]{0:T(256)S(1)} %get-tuple-element.38.counts, ...), custom_call_target="tpu_custom_call" | custom-call | tf_op jit(solution)/shard_map/main/pallas_call | solution.py:360
  28.2 0.1 collective-permute-start.8
  28.3 3.1 %rest.1 = (bf16[256,256]{1,0:T(8,128)(2,1)S(1)}, bf16[256,256]{1,0:T(8,128)(2,1)S(1)}, bf16[256,256]{1,0:T(8,128)(2,1)S(1)}) custom-call(s32[4,8]{1,0:T(4,128)S(1)} %get-tuple-element.33.owner, s32[256]{0:T(256)S(1)} %get-tuple-element.38.counts, bf16[1024,256]{1,0:T(8,128)(2,1)S(1)} %get-tuple-element.51.rest_0_, ...), custom_call_target="tpu_custom_call" | custom-call | tf_op jit(solution)/shard_map/rest/pallas_call | solution.py:360
  31.3 1.8 %collective-permute-start.7 = (bf16[256,256]{1,0:T(8,128)(2,1)S(1)}, bf16[256,256]{1,0:T(8,128)(2,1)S(1)}, u32[]{:S(2)}, u32[]{:S(2)}) collective-permute-start(bf16[256,256]{1,0:T(8,128)(2,1)S(1)} %get-tuple-element.56), channel_id=1, source_target_pairs={{0,1},{1,2},{2,3},{3,0},{4,5},{5,6},{6,7},{7,4},{8,9},{9,10},{10,1... | collective-permute-start | bytes 393224 | tf_op jit(solution)/shard_map/ppermute | solution.py:376
  33.1 2.1 %collective-permute-start.9 = (bf16[256,256]{1,0:T(8,128)(2,1)S(1)}, bf16[256,256]{1,0:T(8,128)(2,1)S(1)}, u32[]{:S(2)}, u32[]{:S(2)}) collective-permute-start(bf16[256,256]{1,0:T(8,128)(2,1)S(1)} %get-tuple-element.58), channel_id=1, source_target_pairs={{0,3},{1,0},{2,1},{3,2},{4,7},{5,4},{6,5},{7,6},{8,11},{9,8},{10,9... | collective-permute-start | bytes 393224 | tf_op jit(solution)/shard_map/ppermute | solution.py:376
  35.2 4.4 %collective-permute-done.7.rest_1_ = bf16[256,256]{1,0:T(8,128)(2,1)S(1)} collective-permute-done((bf16[256,256]{1,0:T(8,128)(2,1)S(1)}, bf16[256,256]{1,0:T(8,128)(2,1)S(1)}, u32[]{:S(2)}, u32[]{:S(2)}) %collective-permute-start.7) | collective-permute-done | bytes 131104 | tf_op jit(solution)/shard_map/ppermute | solution.py:376
  39.6 2.8 %collective-permute-done.9.rest_3_ = bf16[256,256]{1,0:T(8,128)(2,1)S(1)} collective-permute-done((bf16[256,256]{1,0:T(8,128)(2,1)S(1)}, bf16[256,256]{1,0:T(8,128)(2,1)S(1)}, u32[]{:S(2)}, u32[]{:S(2)}) %collective-permute-start.9) | collective-permute-done | bytes 131104 | tf_op jit(solution)/shard_map/ppermute | solution.py:376
  42.4 0.0 collective-permute-done.8.rest_2_
  42.4 1.7 %store.1 = bf16[32,32,256]{2,1,0:T(8,128)(2,1)} custom-call(s32[4,8]{1,0:T(4,128)S(1)} %get-tuple-element.32.rotation, bf16[256,256]{1,0:T(8,128)(2,1)S(1)} %get-tuple-element.55.rest_0_, bf16[256,256]{1,0:T(8,128)(2,1)S(1)} %collective-permute-done.7.rest_1_, bf16[272,256]{1,0:T(8,128)(2,1)S(1)} %collective-permute-done.8.rest_2_, ...), custom_call_target="tpu_custom_call" | custom-call | tf_op jit(solution)/shard_map/store/pallas_call | solution.py:360
  (2 shorter events, 0.0 us)
Async XLA Ops:
  1.9 7.4 %collective-permute-start = (bf16[2,32,256]{2,1,0:T(8,128)(2,1)S(1)}, bf16[2,32,256]{2,1,0:T(8,128)(2,1)S(1)}, u32[]{:S(2)}, u32[]{:S(2)}) collective-permute-start(bf16[2,32,256]{2,1,0:T(8,128)(2,1)S(1)} %get-tuple-element.35), channel_id=1, source_target_pairs={{0,1},{1,2},{2,3},{3,0},{4,5},{5,6},{6,7},{7,4},{8,9},{9,10},{10,1... | collective-permute-start | bytes 98312 | tf_op jit(solution)/shard_map/ppermute | solution.py:376
  4.3 8.0 %collective-permute-start.1 = (bf16[2,32,256]{2,1,0:T(8,128)(2,1)S(1)}, bf16[2,32,256]{2,1,0:T(8,128)(2,1)S(1)}, u32[]{:S(2)}, u32[]{:S(2)}) collective-permute-start(bf16[2,32,256]{2,1,0:T(8,128)(2,1)S(1)} %get-tuple-element.36), channel_id=1, source_target_pairs={{0,2},{1,3},{2,0},{3,1},{4,6},{5,7},{6,4},{7,5},{8,10},{9,11},{10,... | collective-permute-start | bytes 98312 | tf_op jit(solution)/shard_map/ppermute | solution.py:376
  7.1 5.2 %collective-permute-start.2 = (bf16[2,32,256]{2,1,0:T(8,128)(2,1)S(1)}, bf16[2,32,256]{2,1,0:T(8,128)(2,1)S(1)}, u32[]{:S(2)}, u32[]{:S(2)}) collective-permute-start(bf16[2,32,256]{2,1,0:T(8,128)(2,1)S(1)} %get-tuple-element.37), channel_id=1, source_target_pairs={{0,3},{1,0},{2,1},{3,2},{4,7},{5,4},{6,5},{7,6},{8,11},{9,8},{10,9... | collective-permute-start | bytes 98312 | tf_op jit(solution)/shard_map/ppermute | solution.py:376
  8.5 8.9 %collective-permute-start.3 = (bf16[8,32,256]{2,1,0:T(8,128)(2,1)S(1)}, bf16[8,32,256]{2,1,0:T(8,128)(2,1)S(1)}, u32[]{:S(2)}, u32[]{:S(2)}) collective-permute-start(bf16[8,32,256]{2,1,0:T(8,128)(2,1)S(1)} %get-tuple-element.40), channel_id=1, source_target_pairs={{0,1},{1,2},{2,3},{3,0},{4,5},{5,6},{6,7},{7,4},{8,9},{9,10},{10,1... | collective-permute-start | bytes 393224 | tf_op jit(solution)/shard_map/ppermute | solution.py:376
  9.1 11.8 %collective-permute-start.4 = (bf16[8,32,256]{2,1,0:T(8,128)(2,1)S(1)}, bf16[8,32,256]{2,1,0:T(8,128)(2,1)S(1)}, u32[]{:S(2)}, u32[]{:S(2)}) collective-permute-start(bf16[8,32,256]{2,1,0:T(8,128)(2,1)S(1)} %get-tuple-element.41), channel_id=1, source_target_pairs={{0,2},{1,3},{2,0},{3,1},{4,6},{5,7},{6,4},{7,5},{8,10},{9,11},{10,... | collective-permute-start | bytes 393224 | tf_op jit(solution)/shard_map/ppermute | solution.py:376
  9.3 11.6 %collective-permute-start.5 = (bf16[8,32,256]{2,1,0:T(8,128)(2,1)S(1)}, bf16[8,32,256]{2,1,0:T(8,128)(2,1)S(1)}, u32[]{:S(2)}, u32[]{:S(2)}) collective-permute-start(bf16[8,32,256]{2,1,0:T(8,128)(2,1)S(1)} %get-tuple-element.42), channel_id=1, source_target_pairs={{0,3},{1,0},{2,1},{3,2},{4,7},{5,4},{6,5},{7,6},{8,11},{9,8},{10,9... | collective-permute-start | bytes 393224 | tf_op jit(solution)/shard_map/ppermute | solution.py:376
  12.9 9.7 %collective-permute-start.6 = (bf16[2,128,256]{2,1,0:T(8,128)(2,1)S(1)}, bf16[2,128,256]{2,1,0:T(8,128)(2,1)S(1)}, u32[]{:S(2)}, u32[]{:S(2)}) collective-permute-start(bf16[2,128,256]{2,1,0:T(8,128)(2,1)S(1)} %edge.1.after.rest_4_), channel_id=1, source_target_pairs={{0,1},{1,0},{3,7},{7,3},{4,5},{5,4},{6,10},{10,6},{8,9},{9,8},{11,... | collective-permute-start | bytes 393224 | tf_op jit(solution)/shard_map/ppermute | solution.py:405
  28.2 14.2 %collective-permute-start.8 = (bf16[272,256]{1,0:T(8,128)(2,1)S(1)}, bf16[272,256]{1,0:T(8,128)(2,1)S(1)}, u32[]{:S(2)}, u32[]{:S(2)}) collective-permute-start(bf16[272,256]{1,0:T(8,128)(2,1)S(1)} %get-tuple-element.57), channel_id=1, source_target_pairs={{0,2},{1,3},{2,0},{3,1},{4,6},{5,7},{6,4},{7,5},{8,10},{9,11},{10,... | collective-permute-start | bytes 417800 | tf_op jit(solution)/shard_map/ppermute | solution.py:376
  31.3 8.3 %collective-permute-start.7 = (bf16[256,256]{1,0:T(8,128)(2,1)S(1)}, bf16[256,256]{1,0:T(8,128)(2,1)S(1)}, u32[]{:S(2)}, u32[]{:S(2)}) collective-permute-start(bf16[256,256]{1,0:T(8,128)(2,1)S(1)} %get-tuple-element.56), channel_id=1, source_target_pairs={{0,1},{1,2},{2,3},{3,0},{4,5},{5,6},{6,7},{7,4},{8,9},{9,10},{10,1... | collective-permute-start | bytes 393224 | tf_op jit(solution)/shard_map/ppermute | solution.py:376
  33.1 9.2 %collective-permute-start.9 = (bf16[256,256]{1,0:T(8,128)(2,1)S(1)}, bf16[256,256]{1,0:T(8,128)(2,1)S(1)}, u32[]{:S(2)}, u32[]{:S(2)}) collective-permute-start(bf16[256,256]{1,0:T(8,128)(2,1)S(1)} %get-tuple-element.58), channel_id=1, source_target_pairs={{0,3},{1,0},{2,1},{3,2},{4,7},{5,4},{6,5},{7,6},{8,11},{9,8},{10,9... | collective-permute-start | bytes 393224 | tf_op jit(solution)/shard_map/ppermute | solution.py:376

commit v14 on v12

--- a/solution.py
+++ b/solution.py
@@ -125,7 +125,6 @@
     direct, (query, key) = refs[:count], refs[count : count + 2]
     loaded, (w_query, w_key) = refs[count + 2 : 2 * count + 2], refs[2 * count + 2 : 2 * count + 4]
     query_in, key_in, sems = refs[2 * count + 4 :]
-    heads, _, head_dim = w_query.shape
     pairs = list(zip(direct, loaded)) + [(query, query_in), (key, key_in)]
     copies = [pltpu.make_async_copy(*pair, sems.at[i]) for i, pair in enumerate(pairs)]
     for copy in copies:
@@ -133,8 +132,7 @@
     for copy in copies:
         copy.wait()
     w_key[...] = key_in[...].T
-    for h in range(heads):
-        w_query[h] = query_in[:, h * head_dim : (h + 1) * head_dim]
+    w_query[...] = query_in[...]
 
 
 def columns_of(segment, size):
@@ -191,7 +189,8 @@
 def attend(segments, span, limits, mixed, normed, keys, values, w_query, w_out, results, here, scores, expo, turned):
     rows, chans = len(limits), mixed.shape[1]
     size = here.shape[0] // (rows * len(segments))
-    heads, _, head_dim = w_query.shape
+    head_dim = keys.shape[1]
+    heads = chans // head_dim
     cols = mixed.shape[0] // rows
     width = heads * size
     blocks = [(s * rows + r, s, r) for s in range(len(segments)) for r in range(*span)]
@@ -203,8 +202,8 @@
     for b, s, r in blocks:
         here[b * size : (b + 1) * size, :] = normed[cells(s, r), :]
     own = here[low * size : high * size, :]
-    queries = [jnp.dot(own, w_query[h], preferred_element_type=jnp.float32) for h in range(heads)]
-    queries = [query.astype(jnp.bfloat16) for query in queries]
+    query = jnp.dot(own, w_query[...], preferred_element_type=jnp.float32).astype(jnp.bfloat16)
+    queries = [query[:, h * head_dim : (h + 1) * head_dim] for h in range(heads)]
     for b, s, r in blocks:
         part = [query[(b - low) * size : (b - low + 1) * size] for query in queries]
         scores[b] = by_last(keys[r * cols : (r + 1) * cols, :], jnp.concatenate(part, axis=0))
@@ -220,12 +219,11 @@
         summed = jnp.dot(values[:, r * cols : (r + 1) * cols], expo[b], preferred_element_type=jnp.float32)
         turned[:, b * width : (b + 1) * width] = (summed * shares[b]).astype(jnp.bfloat16)
     attended = turned[:, low * width : high * width].T
-    update = jnp.zeros(own.shape, jnp.float32)
+    parts = []
     for h in range(heads):
         starts = [(b - low) * width + h * size for b, *_ in blocks]
-        part = jnp.concatenate([attended[start : start + size] for start in starts], axis=0)
-        weight = w_out[h * head_dim : (h + 1) * head_dim, :]
-        update = update + jnp.dot(part, weight, preferred_element_type=jnp.float32)
+        parts.append(jnp.concatenate([attended[start : start + size] for start in starts], axis=0))
+    update = jnp.dot(jnp.concatenate(parts, axis=1), w_out[...], preferred_element_type=jnp.float32)
     for b, s, r in blocks:
         cell = segments[s] * size + lax.broadcasted_iota(jnp.int32, (size, chans), 0)
         part = jnp.where(cell < limits[r], update[(b - low) * size : (b - low + 1) * size], 0.0)
@@ -407,7 +405,7 @@
     head_dim = w_key.shape[1]
     heads = chans // head_dim
     held = [pltpu.VMEM(x.shape, x.dtype) for x in loaded]
-    held += [pltpu.VMEM((heads, chans, head_dim), bf16), pltpu.VMEM(w_key.shape, bf16)]
+    held += [pltpu.VMEM(w_query.shape, bf16), pltpu.VMEM(w_key.shape, bf16)]
     scratch = [pltpu.VMEM(x.shape, bf16) for x in turned] + [pltpu.SemaphoreType.DMA((len(loaded) + 2,))]
     loaded = call(load_kernel, "load", held, [sent], loaded + turned, scratch, hbm, hbm)
     counts, *convs, w_value, w_out, w_query, w_key = loaded

time: 44.3 us -> 43.2 us (0.975)
  Pallas kernels: 14.7 us -> 12.8 us
  waiting for transfers between devices: 12 us -> 13 us
    pallas_call x6, Pallas kernels: 14.7 us -> 12.8 us  [call(): pl.pallas_call(functools.partial(kernel, n, rows), out_shape=out, in_spec...]
    ppermute x9, waiting for transfers between devices: 10.3 us -> 11.1 us  [around_by(): return lax.ppermute(x, 'lon', [(i, (i + d) % n) for i in range(n)])]
  transfers between devices with their start and end apart: 10 -> 10, of which waited for: 4 -> 4; matrix products, arithmetic and copies ran while one was open for 0% -> 0% of each run, Pallas kernels for 13% -> 11%
where the time goes in v14:
time: 43.2 us; the launch traced here: 43.3 us
  starting transfers between devices  17.5 us (41%)
  waiting for transfers between devices  13 us (30%)
  Pallas kernels  12.8 us (30%)
    ppermute x9, starting transfers between devices, around_by(): return lax.ppermute(x, 'lon', [(i, (i + d) % n) for i in range(n)])  15 us
    pallas_call x6, Pallas kernels, call(): pl.pallas_call(functools.partial(kernel, n, rows), out_shape=out, in_spec...  12.8 us
    ppermute x9, waiting for transfers between devices, around_by(): return lax.ppermute(x, 'lon', [(i, (i + d) % n) for i in range(n)])  11.1 us
    ppermute x1, starting transfers between devices, on_device(): received = lax.ppermute(sent, ('lat', 'lon'), pairs)  2.48 us
    ppermute x1, waiting for transfers between devices, on_device(): received = lax.ppermute(sent, ('lat', 'lon'), pairs)  1.89 us
  transfers between devices with their start and end apart: 10, of which 4 were waited for; matrix products, arithmetic and copies ran while one was open for 0% of the time, Pallas kernels for 11%

profile of v14, /device:TPU:0, one launch (start us, length us, event | category | flops | bytes accessed | tf_op | source)
XLA Modules:
  0.0 43.3 jit_solution(10437889929221819346)
XLA Ops:
  0.0 1.2 %send.1 = (bf16[2,32,256]{2,1,0:T(8,128)(2,1)S(1)}, bf16[2,32,256]{2,1,0:T(8,128)(2,1)S(1)}, bf16[2,32,256]{2,1,0:T(8,128)(2,1)S(1)}, bf16[2,32,256]{2,1,0:T(8,1...) custom-call(s32[4,8]{1,0:T(4,128)} %bitcast.12, ...), custom_call_target="tpu_custom_call" | custom-call | tf_op jit(solution)/shard_map/send/pallas_call | solution.py:358
  1.2 3.1 %collective-permute-start = (bf16[2,32,256]{2,1,0:T(8,128)(2,1)S(1)}, bf16[2,32,256]{2,1,0:T(8,128)(2,1)S(1)}, u32[]{:S(2)}, u32[]{:S(2)}) collective-permute-start(bf16[2,32,256]{2,1,0:T(8,128)(2,1)S(1)} %get-tuple-element.35), channel_id=1, source_target_pairs={{0,1},{1,2},{2,3},{3,0},{4,5},{5,6},{6,7},{7,4},{8,9},{9,10},{10,1... | collective-permute-start | bytes 98312 | tf_op jit(solution)/shard_map/ppermute | solution.py:374
  4.3 2.6 %collective-permute-start.1 = (bf16[2,32,256]{2,1,0:T(8,128)(2,1)S(1)}, bf16[2,32,256]{2,1,0:T(8,128)(2,1)S(1)}, u32[]{:S(2)}, u32[]{:S(2)}) collective-permute-start(bf16[2,32,256]{2,1,0:T(8,128)(2,1)S(1)} %get-tuple-element.36), channel_id=1, source_target_pairs={{0,2},{1,3},{2,0},{3,1},{4,6},{5,7},{6,4},{7,5},{8,10},{9,11},{10,... | collective-permute-start | bytes 98312 | tf_op jit(solution)/shard_map/ppermute | solution.py:374
  6.9 1.5 %collective-permute-start.2 = (bf16[2,32,256]{2,1,0:T(8,128)(2,1)S(1)}, bf16[2,32,256]{2,1,0:T(8,128)(2,1)S(1)}, u32[]{:S(2)}, u32[]{:S(2)}) collective-permute-start(bf16[2,32,256]{2,1,0:T(8,128)(2,1)S(1)} %get-tuple-element.37), channel_id=1, source_target_pairs={{0,3},{1,0},{2,1},{3,2},{4,7},{5,4},{6,5},{7,6},{8,11},{9,8},{10,9... | collective-permute-start | bytes 98312 | tf_op jit(solution)/shard_map/ppermute | solution.py:374
  8.5 0.5 %collective-permute-start.3 = (bf16[8,32,256]{2,1,0:T(8,128)(2,1)S(1)}, bf16[8,32,256]{2,1,0:T(8,128)(2,1)S(1)}, u32[]{:S(2)}, u32[]{:S(2)}) collective-permute-start(bf16[8,32,256]{2,1,0:T(8,128)(2,1)S(1)} %get-tuple-element.40), channel_id=1, source_target_pairs={{0,1},{1,2},{2,3},{3,0},{4,5},{5,6},{6,7},{7,4},{8,9},{9,10},{10,1... | collective-permute-start | bytes 393224 | tf_op jit(solution)/shard_map/ppermute | solution.py:374
  8.9 0.3 collective-permute-start.4
  9.3 0.0 collective-permute-done.rest_1_
  9.3 3.0 %collective-permute-start.5 = (bf16[8,32,256]{2,1,0:T(8,128)(2,1)S(1)}, bf16[8,32,256]{2,1,0:T(8,128)(2,1)S(1)}, u32[]{:S(2)}, u32[]{:S(2)}) collective-permute-start(bf16[8,32,256]{2,1,0:T(8,128)(2,1)S(1)} %get-tuple-element.42), channel_id=1, source_target_pairs={{0,3},{1,0},{2,1},{3,2},{4,7},{5,4},{6,5},{7,6},{8,11},{9,8},{10,9... | collective-permute-start | bytes 393224 | tf_op jit(solution)/shard_map/ppermute | solution.py:374
  12.3 0.0 collective-permute-done.1.rest_2_
  12.3 0.0 collective-permute-done.2.rest_3_
  12.3 0.6 %edge.1.after.rest_4_ = bf16[2,128,256]{2,1,0:T(8,128)(2,1)S(1)} custom-call(s32[4,8]{1,0:T(4,128)S(1)} %get-tuple-element.33.owner, bf16[2,32,256]{2,1,0:T(8,128)(2,1)S(1)} %get-tuple-element.34.rest_0_, bf16[2,32,256]{2,1,0:T(8,128)(2,1)S(1)} %collective-permute-done.rest_1_, bf16[2,32,256]{2,1,0:T(8,128)(2,1)S(1)} %collective-permute-done.1.rest_2_, ...), custom_call_target="tpu_custom_call" | custom-call | tf_op jit(solution)/shard_map/edge/pallas_call | solution.py:358
  12.9 2.5 %collective-permute-start.6 = (bf16[2,128,256]{2,1,0:T(8,128)(2,1)S(1)}, bf16[2,128,256]{2,1,0:T(8,128)(2,1)S(1)}, u32[]{:S(2)}, u32[]{:S(2)}) collective-permute-start(bf16[2,128,256]{2,1,0:T(8,128)(2,1)S(1)} %edge.1.after.rest_4_), channel_id=1, source_target_pairs={{0,1},{1,0},{3,7},{7,3},{4,5},{5,4},{6,10},{10,6},{8,9},{9,8},{11,... | collective-permute-start | bytes 393224 | tf_op jit(solution)/shard_map/ppermute | solution.py:403
  15.4 1.9 %load.1 = (s32[256]{0:T(256)S(1)}, bf16[3,768,256]{2,1,0:T(8,128)(2,1)S(1)}, f32[1,256]{1,0:T(1,128)S(1)}, bf16[3,768,256]{2,1,0:T(8,128)(2,1)S(1)}, f32[1,256]{...) custom-call(bf16[2,128,256]{2,1,0:T(8,128)(2,1)S(1)} %edge.1.after.r, ...), custom_call_target="tpu_custom_call" | custom-call | tf_op jit(solution)/shard_map/load/pallas_call | solution.py:358
  17.3 0.0 collective-permute-done.3.rest_1_
  17.3 3.2 %collective-permute-done.4.rest_2_ = bf16[8,32,256]{2,1,0:T(8,128)(2,1)S(1)} collective-permute-done((bf16[8,32,256]{2,1,0:T(8,128)(2,1)S(1)}, bf16[8,32,256]{2,1,0:T(8,128)(2,1)S(1)}, u32[]{:S(2)}, u32[]{:S(2)}) %collective-permute-start.4) | collective-permute-done | bytes 131104 | tf_op jit(solution)/shard_map/ppermute | solution.py:374
  20.5 1.9 %collective-permute-done.6.rest_5_ = bf16[2,128,256]{2,1,0:T(8,128)(2,1)S(1)} collective-permute-done((bf16[2,128,256]{2,1,0:T(8,128)(2,1)S(1)}, bf16[2,128,256]{2,1,0:T(8,128)(2,1)S(1)}, u32[]{:S(2)}, u32[]{:S(2)}) %collective-permute-start.6) | collective-permute-done | bytes 131104 | tf_op jit(solution)/shard_map/ppermute | solution.py:403
  22.4 5.3 %main.1 = (bf16[272,256]{1,0:T(8,128)(2,1)S(1)}, bf16[1024,256]{1,0:T(8,128)(2,1)S(1)}, bf16[1024,256]{1,0:T(8,128)(2,1)S(1)}, bf16[1024,64]{1,0:T(8,128)(2,1)S(1)}, bf16[64,1024]{1,0:T(8,128)(2,1)S(1)}) custom-call(s32[4,8]{1,0:T(4,128)S(1)} %get-tuple-element.33.owner, s32[256]{0:T(256)S(1)} %get-tuple-element.38.counts, ...), custom_call_target="tpu_custom_call" | custom-call | tf_op jit(solution)/shard_map/main/pallas_call | solution.py:358
  27.7 0.1 collective-permute-start.8
  27.8 2.3 %rest.1 = (bf16[256,256]{1,0:T(8,128)(2,1)S(1)}, bf16[256,256]{1,0:T(8,128)(2,1)S(1)}, bf16[256,256]{1,0:T(8,128)(2,1)S(1)}) custom-call(s32[4,8]{1,0:T(4,128)S(1)} %get-tuple-element.33.owner, s32[256]{0:T(256)S(1)} %get-tuple-element.38.counts, bf16[1024,256]{1,0:T(8,128)(2,1)S(1)} %get-tuple-element.51.rest_0_, ...), custom_call_target="tpu_custom_call" | custom-call | tf_op jit(solution)/shard_map/rest/pallas_call | solution.py:358
  30.1 2.1 %collective-permute-start.7 = (bf16[256,256]{1,0:T(8,128)(2,1)S(1)}, bf16[256,256]{1,0:T(8,128)(2,1)S(1)}, u32[]{:S(2)}, u32[]{:S(2)}) collective-permute-start(bf16[256,256]{1,0:T(8,128)(2,1)S(1)} %get-tuple-element.56), channel_id=1, source_target_pairs={{0,1},{1,2},{2,3},{3,0},{4,5},{5,6},{6,7},{7,4},{8,9},{9,10},{10,1... | collective-permute-start | bytes 393224 | tf_op jit(solution)/shard_map/ppermute | solution.py:374
  32.1 1.8 %collective-permute-start.9 = (bf16[256,256]{1,0:T(8,128)(2,1)S(1)}, bf16[256,256]{1,0:T(8,128)(2,1)S(1)}, u32[]{:S(2)}, u32[]{:S(2)}) collective-permute-start(bf16[256,256]{1,0:T(8,128)(2,1)S(1)} %get-tuple-element.58), channel_id=1, source_target_pairs={{0,3},{1,0},{2,1},{3,2},{4,7},{5,4},{6,5},{7,6},{8,11},{9,8},{10,9... | collective-permute-start | bytes 393224 | tf_op jit(solution)/shard_map/ppermute | solution.py:374
  33.9 4.1 %collective-permute-done.7.rest_1_ = bf16[256,256]{1,0:T(8,128)(2,1)S(1)} collective-permute-done((bf16[256,256]{1,0:T(8,128)(2,1)S(1)}, bf16[256,256]{1,0:T(8,128)(2,1)S(1)}, u32[]{:S(2)}, u32[]{:S(2)}) %collective-permute-start.7) | collective-permute-done | bytes 131104 | tf_op jit(solution)/shard_map/ppermute | solution.py:374
  38.1 3.8 %collective-permute-done.9.rest_3_ = bf16[256,256]{1,0:T(8,128)(2,1)S(1)} collective-permute-done((bf16[256,256]{1,0:T(8,128)(2,1)S(1)}, bf16[256,256]{1,0:T(8,128)(2,1)S(1)}, u32[]{:S(2)}, u32[]{:S(2)}) %collective-permute-start.9) | collective-permute-done | bytes 131104 | tf_op jit(solution)/shard_map/ppermute | solution.py:374
  41.8 1.4 %store.1 = bf16[32,32,256]{2,1,0:T(8,128)(2,1)} custom-call(s32[4,8]{1,0:T(4,128)S(1)} %get-tuple-element.32.rotation, bf16[256,256]{1,0:T(8,128)(2,1)S(1)} %get-tuple-element.55.rest_0_, bf16[256,256]{1,0:T(8,128)(2,1)S(1)} %collective-permute-done.7.rest_1_, bf16[272,256]{1,0:T(8,128)(2,1)S(1)} %collective-permute-done.8.rest_2_, ...), custom_call_target="tpu_custom_call" | custom-call | tf_op jit(solution)/shard_map/store/pallas_call | solution.py:358
  (2 shorter events, 0.0 us)
Async XLA Ops:
  1.2 8.0 %collective-permute-start = (bf16[2,32,256]{2,1,0:T(8,128)(2,1)S(1)}, bf16[2,32,256]{2,1,0:T(8,128)(2,1)S(1)}, u32[]{:S(2)}, u32[]{:S(2)}) collective-permute-start(bf16[2,32,256]{2,1,0:T(8,128)(2,1)S(1)} %get-tuple-element.35), channel_id=1, source_target_pairs={{0,1},{1,2},{2,3},{3,0},{4,5},{5,6},{6,7},{7,4},{8,9},{9,10},{10,1... | collective-permute-start | bytes 98312 | tf_op jit(solution)/shard_map/ppermute | solution.py:374
  4.3 8.0 %collective-permute-start.1 = (bf16[2,32,256]{2,1,0:T(8,128)(2,1)S(1)}, bf16[2,32,256]{2,1,0:T(8,128)(2,1)S(1)}, u32[]{:S(2)}, u32[]{:S(2)}) collective-permute-start(bf16[2,32,256]{2,1,0:T(8,128)(2,1)S(1)} %get-tuple-element.36), channel_id=1, source_target_pairs={{0,2},{1,3},{2,0},{3,1},{4,6},{5,7},{6,4},{7,5},{8,10},{9,11},{10,... | collective-permute-start | bytes 98312 | tf_op jit(solution)/shard_map/ppermute | solution.py:374
  6.9 5.4 %collective-permute-start.2 = (bf16[2,32,256]{2,1,0:T(8,128)(2,1)S(1)}, bf16[2,32,256]{2,1,0:T(8,128)(2,1)S(1)}, u32[]{:S(2)}, u32[]{:S(2)}) collective-permute-start(bf16[2,32,256]{2,1,0:T(8,128)(2,1)S(1)} %get-tuple-element.37), channel_id=1, source_target_pairs={{0,3},{1,0},{2,1},{3,2},{4,7},{5,4},{6,5},{7,6},{8,11},{9,8},{10,9... | collective-permute-start | bytes 98312 | tf_op jit(solution)/shard_map/ppermute | solution.py:374
  8.5 8.8 %collective-permute-start.3 = (bf16[8,32,256]{2,1,0:T(8,128)(2,1)S(1)}, bf16[8,32,256]{2,1,0:T(8,128)(2,1)S(1)}, u32[]{:S(2)}, u32[]{:S(2)}) collective-permute-start(bf16[8,32,256]{2,1,0:T(8,128)(2,1)S(1)} %get-tuple-element.40), channel_id=1, source_target_pairs={{0,1},{1,2},{2,3},{3,0},{4,5},{5,6},{6,7},{7,4},{8,9},{9,10},{10,1... | collective-permute-start | bytes 393224 | tf_op jit(solution)/shard_map/ppermute | solution.py:374
  8.9 11.5 %collective-permute-start.4 = (bf16[8,32,256]{2,1,0:T(8,128)(2,1)S(1)}, bf16[8,32,256]{2,1,0:T(8,128)(2,1)S(1)}, u32[]{:S(2)}, u32[]{:S(2)}) collective-permute-start(bf16[8,32,256]{2,1,0:T(8,128)(2,1)S(1)} %get-tuple-element.41), channel_id=1, source_target_pairs={{0,2},{1,3},{2,0},{3,1},{4,6},{5,7},{6,4},{7,5},{8,10},{9,11},{10,... | collective-permute-start | bytes 393224 | tf_op jit(solution)/shard_map/ppermute | solution.py:374
  9.3 11.2 %collective-permute-start.5 = (bf16[8,32,256]{2,1,0:T(8,128)(2,1)S(1)}, bf16[8,32,256]{2,1,0:T(8,128)(2,1)S(1)}, u32[]{:S(2)}, u32[]{:S(2)}) collective-permute-start(bf16[8,32,256]{2,1,0:T(8,128)(2,1)S(1)} %get-tuple-element.42), channel_id=1, source_target_pairs={{0,3},{1,0},{2,1},{3,2},{4,7},{5,4},{6,5},{7,6},{8,11},{9,8},{10,9... | collective-permute-start | bytes 393224 | tf_op jit(solution)/shard_map/ppermute | solution.py:374
  12.9 9.5 %collective-permute-start.6 = (bf16[2,128,256]{2,1,0:T(8,128)(2,1)S(1)}, bf16[2,128,256]{2,1,0:T(8,128)(2,1)S(1)}, u32[]{:S(2)}, u32[]{:S(2)}) collective-permute-start(bf16[2,128,256]{2,1,0:T(8,128)(2,1)S(1)} %edge.1.after.rest_4_), channel_id=1, source_target_pairs={{0,1},{1,0},{3,7},{7,3},{4,5},{5,4},{6,10},{10,6},{8,9},{9,8},{11,... | collective-permute-start | bytes 393224 | tf_op jit(solution)/shard_map/ppermute | solution.py:403
  27.7 14.1 %collective-permute-start.8 = (bf16[272,256]{1,0:T(8,128)(2,1)S(1)}, bf16[272,256]{1,0:T(8,128)(2,1)S(1)}, u32[]{:S(2)}, u32[]{:S(2)}) collective-permute-start(bf16[272,256]{1,0:T(8,128)(2,1)S(1)} %get-tuple-element.57), channel_id=1, source_target_pairs={{0,2},{1,3},{2,0},{3,1},{4,6},{5,7},{6,4},{7,5},{8,10},{9,11},{10,... | collective-permute-start | bytes 417800 | tf_op jit(solution)/shard_map/ppermute | solution.py:374
  30.1 8.0 %collective-permute-start.7 = (bf16[256,256]{1,0:T(8,128)(2,1)S(1)}, bf16[256,256]{1,0:T(8,128)(2,1)S(1)}, u32[]{:S(2)}, u32[]{:S(2)}) collective-permute-start(bf16[256,256]{1,0:T(8,128)(2,1)S(1)} %get-tuple-element.56), channel_id=1, source_target_pairs={{0,1},{1,2},{2,3},{3,0},{4,5},{5,6},{6,7},{7,4},{8,9},{9,10},{10,1... | collective-permute-start | bytes 393224 | tf_op jit(solution)/shard_map/ppermute | solution.py:374
  32.1 9.7 %collective-permute-start.9 = (bf16[256,256]{1,0:T(8,128)(2,1)S(1)}, bf16[256,256]{1,0:T(8,128)(2,1)S(1)}, u32[]{:S(2)}, u32[]{:S(2)}) collective-permute-start(bf16[256,256]{1,0:T(8,128)(2,1)S(1)} %get-tuple-element.58), channel_id=1, source_target_pairs={{0,3},{1,0},{2,1},{3,2},{4,7},{5,4},{6,5},{7,6},{8,11},{9,8},{10,9... | collective-permute-start | bytes 393224 | tf_op jit(solution)/shard_map/ppermute | solution.py:374

commit v15 on v14

--- a/solution.py
+++ b/solution.py
@@ -271,7 +271,7 @@
 
     total = rows + HALO
     chunks = min(CHUNKS, total // HALO)
-    cuts = [-(-total * c // chunks) for c in range(chunks + 1)]
+    cuts = [min(-(-total // chunks) * c, total) for c in range(chunks + 1)]
     ends = [0] + [cut + HALO for cut in cuts[1:]]
     lows = [max(cut - HALO, 0) for cut in cuts]
     firsts, seconds = [], []

time: 43.2 us -> 43.5 us (level)
  Pallas kernels: 12.8 us -> 13.8 us
  waiting for transfers between devices: 13 us -> 12 us
    pallas_call x6, Pallas kernels: 12.8 us -> 13.8 us  [call(): pl.pallas_call(functools.partial(kernel, n, rows), out_shape=out, in_spec...]
    ppermute x9, waiting for transfers between devices: 11.1 us -> 10.6 us  [around_by(): return lax.ppermute(x, 'lon', [(i, (i + d) % n) for i in range(n)])]
  transfers between devices with their start and end apart: 10 -> 10, of which waited for: 4 -> 5; matrix products, arithmetic and copies ran while one was open for 0% -> 0% of each run, Pallas kernels for 11% -> 11%
where the time goes in v15:
time: 43.5 us; the launch traced here: 43.2 us
  starting transfers between devices  17.3 us (40%)
  Pallas kernels  13.8 us (32%)
  waiting for transfers between devices  12 us (28%)
    ppermute x9, starting transfers between devices, around_by(): return lax.ppermute(x, 'lon', [(i, (i + d) % n) for i in range(n)])  14.8 us
    pallas_call x6, Pallas kernels, call(): pl.pallas_call(functools.partial(kernel, n, rows), out_shape=out, in_spec...  13.8 us
    ppermute x9, waiting for transfers between devices, around_by(): return lax.ppermute(x, 'lon', [(i, (i + d) % n) for i in range(n)])  10.6 us
    ppermute x1, starting transfers between devices, on_device(): received = lax.ppermute(sent, ('lat', 'lon'), pairs)  2.48 us
    ppermute x1, waiting for transfers between devices, on_device(): received = lax.ppermute(sent, ('lat', 'lon'), pairs)  1.48 us
  transfers between devices with their start and end apart: 10, of which 5 were waited for; matrix products, arithmetic and copies ran while one was open for 0% of the time, Pallas kernels for 11%

profile of v15, /device:TPU:0, one launch (start us, length us, event | category | flops | bytes accessed | tf_op | source)
XLA Modules:
  0.0 43.2 jit_solution(6043682385145501455)
XLA Ops:
  0.0 1.9 %send.1 = (bf16[2,32,256]{2,1,0:T(8,128)(2,1)S(1)}, bf16[2,32,256]{2,1,0:T(8,128)(2,1)S(1)}, bf16[2,32,256]{2,1,0:T(8,128)(2,1)S(1)}, bf16[2,32,256]{2,1,0:T(8,1...) custom-call(s32[4,8]{1,0:T(4,128)} %bitcast.12, ...), custom_call_target="tpu_custom_call" | custom-call | tf_op jit(solution)/shard_map/send/pallas_call | solution.py:358
  1.9 2.6 %collective-permute-start = (bf16[2,32,256]{2,1,0:T(8,128)(2,1)S(1)}, bf16[2,32,256]{2,1,0:T(8,128)(2,1)S(1)}, u32[]{:S(2)}, u32[]{:S(2)}) collective-permute-start(bf16[2,32,256]{2,1,0:T(8,128)(2,1)S(1)} %get-tuple-element.35), channel_id=1, source_target_pairs={{0,1},{1,2},{2,3},{3,0},{4,5},{5,6},{6,7},{7,4},{8,9},{9,10},{10,1... | collective-permute-start | bytes 98312 | tf_op jit(solution)/shard_map/ppermute | solution.py:374
  4.5 2.4 %collective-permute-start.1 = (bf16[2,32,256]{2,1,0:T(8,128)(2,1)S(1)}, bf16[2,32,256]{2,1,0:T(8,128)(2,1)S(1)}, u32[]{:S(2)}, u32[]{:S(2)}) collective-permute-start(bf16[2,32,256]{2,1,0:T(8,128)(2,1)S(1)} %get-tuple-element.36), channel_id=1, source_target_pairs={{0,2},{1,3},{2,0},{3,1},{4,6},{5,7},{6,4},{7,5},{8,10},{9,11},{10,... | collective-permute-start | bytes 98312 | tf_op jit(solution)/shard_map/ppermute | solution.py:374
  6.9 2.0 %collective-permute-start.2 = (bf16[2,32,256]{2,1,0:T(8,128)(2,1)S(1)}, bf16[2,32,256]{2,1,0:T(8,128)(2,1)S(1)}, u32[]{:S(2)}, u32[]{:S(2)}) collective-permute-start(bf16[2,32,256]{2,1,0:T(8,128)(2,1)S(1)} %get-tuple-element.37), channel_id=1, source_target_pairs={{0,3},{1,0},{2,1},{3,2},{4,7},{5,4},{6,5},{7,6},{8,11},{9,8},{10,9... | collective-permute-start | bytes 98312 | tf_op jit(solution)/shard_map/ppermute | solution.py:374
  8.9 0.0 collective-permute-start.3
  8.9 0.5 %collective-permute-start.4 = (bf16[8,32,256]{2,1,0:T(8,128)(2,1)S(1)}, bf16[8,32,256]{2,1,0:T(8,128)(2,1)S(1)}, u32[]{:S(2)}, u32[]{:S(2)}) collective-permute-start(bf16[8,32,256]{2,1,0:T(8,128)(2,1)S(1)} %get-tuple-element.41), channel_id=1, source_target_pairs={{0,2},{1,3},{2,0},{3,1},{4,6},{5,7},{6,4},{7,5},{8,10},{9,11},{10,... | collective-permute-start | bytes 393224 | tf_op jit(solution)/shard_map/ppermute | solution.py:374
  9.5 0.0 collective-permute-done.rest_1_
  9.5 3.3 %collective-permute-start.5 = (bf16[8,32,256]{2,1,0:T(8,128)(2,1)S(1)}, bf16[8,32,256]{2,1,0:T(8,128)(2,1)S(1)}, u32[]{:S(2)}, u32[]{:S(2)}) collective-permute-start(bf16[8,32,256]{2,1,0:T(8,128)(2,1)S(1)} %get-tuple-element.42), channel_id=1, source_target_pairs={{0,3},{1,0},{2,1},{3,2},{4,7},{5,4},{6,5},{7,6},{8,11},{9,8},{10,9... | collective-permute-start | bytes 393224 | tf_op jit(solution)/shard_map/ppermute | solution.py:374
  12.8 0.0 collective-permute-done.1.rest_2_
  12.8 0.0 collective-permute-done.2.rest_3_
  12.8 0.6 %edge.1.after.rest_4_ = bf16[2,128,256]{2,1,0:T(8,128)(2,1)S(1)} custom-call(s32[4,8]{1,0:T(4,128)S(1)} %get-tuple-element.33.owner, bf16[2,32,256]{2,1,0:T(8,128)(2,1)S(1)} %get-tuple-element.34.rest_0_, bf16[2,32,256]{2,1,0:T(8,128)(2,1)S(1)} %collective-permute-done.rest_1_, bf16[2,32,256]{2,1,0:T(8,128)(2,1)S(1)} %collective-permute-done.1.rest_2_, ...), custom_call_target="tpu_custom_call" | custom-call | tf_op jit(solution)/shard_map/edge/pallas_call | solution.py:358
  13.4 2.5 %collective-permute-start.6 = (bf16[2,128,256]{2,1,0:T(8,128)(2,1)S(1)}, bf16[2,128,256]{2,1,0:T(8,128)(2,1)S(1)}, u32[]{:S(2)}, u32[]{:S(2)}) collective-permute-start(bf16[2,128,256]{2,1,0:T(8,128)(2,1)S(1)} %edge.1.after.rest_4_), channel_id=1, source_target_pairs={{0,1},{1,0},{3,7},{7,3},{4,5},{5,4},{6,10},{10,6},{8,9},{9,8},{11,... | collective-permute-start | bytes 393224 | tf_op jit(solution)/shard_map/ppermute | solution.py:403
  15.8 1.9 %load.1 = (s32[256]{0:T(256)S(1)}, bf16[3,768,256]{2,1,0:T(8,128)(2,1)S(1)}, f32[1,256]{1,0:T(1,128)S(1)}, bf16[3,768,256]{2,1,0:T(8,128)(2,1)S(1)}, f32[1,256]{...) custom-call(bf16[2,128,256]{2,1,0:T(8,128)(2,1)S(1)} %edge.1.after.r, ...), custom_call_target="tpu_custom_call" | custom-call | tf_op jit(solution)/shard_map/load/pallas_call | solution.py:358
  17.8 2.5 %collective-permute-done.4.rest_2_ = bf16[8,32,256]{2,1,0:T(8,128)(2,1)S(1)} collective-permute-done((bf16[8,32,256]{2,1,0:T(8,128)(2,1)S(1)}, bf16[8,32,256]{2,1,0:T(8,128)(2,1)S(1)}, u32[]{:S(2)}, u32[]{:S(2)}) %collective-permute-start.4) | collective-permute-done | bytes 131104 | tf_op jit(solution)/shard_map/ppermute | solution.py:374
  20.3 0.6 %collective-permute-done.5.rest_3_ = bf16[8,32,256]{2,1,0:T(8,128)(2,1)S(1)} collective-permute-done((bf16[8,32,256]{2,1,0:T(8,128)(2,1)S(1)}, bf16[8,32,256]{2,1,0:T(8,128)(2,1)S(1)}, u32[]{:S(2)}, u32[]{:S(2)}) %collective-permute-start.5) | collective-permute-done | bytes 131104 | tf_op jit(solution)/shard_map/ppermute | solution.py:374
  20.9 1.5 %collective-permute-done.6.rest_5_ = bf16[2,128,256]{2,1,0:T(8,128)(2,1)S(1)} collective-permute-done((bf16[2,128,256]{2,1,0:T(8,128)(2,1)S(1)}, bf16[2,128,256]{2,1,0:T(8,128)(2,1)S(1)}, u32[]{:S(2)}, u32[]{:S(2)}) %collective-permute-start.6) | collective-permute-done | bytes 131104 | tf_op jit(solution)/shard_map/ppermute | solution.py:403
  22.4 5.5 %main.1 = (bf16[272,256]{1,0:T(8,128)(2,1)S(1)}, bf16[1024,256]{1,0:T(8,128)(2,1)S(1)}, bf16[1024,256]{1,0:T(8,128)(2,1)S(1)}, bf16[1024,64]{1,0:T(8,128)(2,1)S(1)}, bf16[64,1024]{1,0:T(8,128)(2,1)S(1)}) custom-call(s32[4,8]{1,0:T(4,128)S(1)} %get-tuple-element.33.owner, s32[256]{0:T(256)S(1)} %get-tuple-element.38.counts, ...), custom_call_target="tpu_custom_call" | custom-call | tf_op jit(solution)/shard_map/main/pallas_call | solution.py:358
  27.9 0.1 collective-permute-start.8
  27.9 2.3 %rest.1 = (bf16[256,256]{1,0:T(8,128)(2,1)S(1)}, bf16[256,256]{1,0:T(8,128)(2,1)S(1)}, bf16[256,256]{1,0:T(8,128)(2,1)S(1)}) custom-call(s32[4,8]{1,0:T(4,128)S(1)} %get-tuple-element.33.owner, s32[256]{0:T(256)S(1)} %get-tuple-element.38.counts, bf16[1024,256]{1,0:T(8,128)(2,1)S(1)} %get-tuple-element.51.rest_0_, ...), custom_call_target="tpu_custom_call" | custom-call | tf_op jit(solution)/shard_map/rest/pallas_call | solution.py:358
  30.2 2.1 %collective-permute-start.7 = (bf16[256,256]{1,0:T(8,128)(2,1)S(1)}, bf16[256,256]{1,0:T(8,128)(2,1)S(1)}, u32[]{:S(2)}, u32[]{:S(2)}) collective-permute-start(bf16[256,256]{1,0:T(8,128)(2,1)S(1)} %get-tuple-element.56), channel_id=1, source_target_pairs={{0,1},{1,2},{2,3},{3,0},{4,5},{5,6},{6,7},{7,4},{8,9},{9,10},{10,1... | collective-permute-start | bytes 393224 | tf_op jit(solution)/shard_map/ppermute | solution.py:374
  32.3 1.8 %collective-permute-start.9 = (bf16[256,256]{1,0:T(8,128)(2,1)S(1)}, bf16[256,256]{1,0:T(8,128)(2,1)S(1)}, u32[]{:S(2)}, u32[]{:S(2)}) collective-permute-start(bf16[256,256]{1,0:T(8,128)(2,1)S(1)} %get-tuple-element.58), channel_id=1, source_target_pairs={{0,3},{1,0},{2,1},{3,2},{4,7},{5,4},{6,5},{7,6},{8,11},{9,8},{10,9... | collective-permute-start | bytes 393224 | tf_op jit(solution)/shard_map/ppermute | solution.py:374
  34.1 4.4 %collective-permute-done.7.rest_1_ = bf16[256,256]{1,0:T(8,128)(2,1)S(1)} collective-permute-done((bf16[256,256]{1,0:T(8,128)(2,1)S(1)}, bf16[256,256]{1,0:T(8,128)(2,1)S(1)}, u32[]{:S(2)}, u32[]{:S(2)}) %collective-permute-start.7) | collective-permute-done | bytes 131104 | tf_op jit(solution)/shard_map/ppermute | solution.py:374
  38.5 3.0 %collective-permute-done.9.rest_3_ = bf16[256,256]{1,0:T(8,128)(2,1)S(1)} collective-permute-done((bf16[256,256]{1,0:T(8,128)(2,1)S(1)}, bf16[256,256]{1,0:T(8,128)(2,1)S(1)}, u32[]{:S(2)}, u32[]{:S(2)}) %collective-permute-start.9) | collective-permute-done | bytes 131104 | tf_op jit(solution)/shard_map/ppermute | solution.py:374
  41.5 1.7 %store.1 = bf16[32,32,256]{2,1,0:T(8,128)(2,1)} custom-call(s32[4,8]{1,0:T(4,128)S(1)} %get-tuple-element.32.rotation, bf16[256,256]{1,0:T(8,128)(2,1)S(1)} %get-tuple-element.55.rest_0_, bf16[256,256]{1,0:T(8,128)(2,1)S(1)} %collective-permute-done.7.rest_1_, bf16[272,256]{1,0:T(8,128)(2,1)S(1)} %collective-permute-done.8.rest_2_, ...), custom_call_target="tpu_custom_call" | custom-call | tf_op jit(solution)/shard_map/store/pallas_call | solution.py:358
  (2 shorter events, 0.0 us)
Async XLA Ops:
  1.9 7.6 %collective-permute-start = (bf16[2,32,256]{2,1,0:T(8,128)(2,1)S(1)}, bf16[2,32,256]{2,1,0:T(8,128)(2,1)S(1)}, u32[]{:S(2)}, u32[]{:S(2)}) collective-permute-start(bf16[2,32,256]{2,1,0:T(8,128)(2,1)S(1)} %get-tuple-element.35), channel_id=1, source_target_pairs={{0,1},{1,2},{2,3},{3,0},{4,5},{5,6},{6,7},{7,4},{8,9},{9,10},{10,1... | collective-permute-start | bytes 98312 | tf_op jit(solution)/shard_map/ppermute | solution.py:374
  4.5 8.2 %collective-permute-start.1 = (bf16[2,32,256]{2,1,0:T(8,128)(2,1)S(1)}, bf16[2,32,256]{2,1,0:T(8,128)(2,1)S(1)}, u32[]{:S(2)}, u32[]{:S(2)}) collective-permute-start(bf16[2,32,256]{2,1,0:T(8,128)(2,1)S(1)} %get-tuple-element.36), channel_id=1, source_target_pairs={{0,2},{1,3},{2,0},{3,1},{4,6},{5,7},{6,4},{7,5},{8,10},{9,11},{10,... | collective-permute-start | bytes 98312 | tf_op jit(solution)/shard_map/ppermute | solution.py:374
  6.9 5.8 %collective-permute-start.2 = (bf16[2,32,256]{2,1,0:T(8,128)(2,1)S(1)}, bf16[2,32,256]{2,1,0:T(8,128)(2,1)S(1)}, u32[]{:S(2)}, u32[]{:S(2)}) collective-permute-start(bf16[2,32,256]{2,1,0:T(8,128)(2,1)S(1)} %get-tuple-element.37), channel_id=1, source_target_pairs={{0,3},{1,0},{2,1},{3,2},{4,7},{5,4},{6,5},{7,6},{8,11},{9,8},{10,9... | collective-permute-start | bytes 98312 | tf_op jit(solution)/shard_map/ppermute | solution.py:374
  8.9 8.8 %collective-permute-start.3 = (bf16[8,32,256]{2,1,0:T(8,128)(2,1)S(1)}, bf16[8,32,256]{2,1,0:T(8,128)(2,1)S(1)}, u32[]{:S(2)}, u32[]{:S(2)}) collective-permute-start(bf16[8,32,256]{2,1,0:T(8,128)(2,1)S(1)} %get-tuple-element.40), channel_id=1, source_target_pairs={{0,1},{1,2},{2,3},{3,0},{4,5},{5,6},{6,7},{7,4},{8,9},{9,10},{10,1... | collective-permute-start | bytes 393224 | tf_op jit(solution)/shard_map/ppermute | solution.py:374
  8.9 11.3 %collective-permute-start.4 = (bf16[8,32,256]{2,1,0:T(8,128)(2,1)S(1)}, bf16[8,32,256]{2,1,0:T(8,128)(2,1)S(1)}, u32[]{:S(2)}, u32[]{:S(2)}) collective-permute-start(bf16[8,32,256]{2,1,0:T(8,128)(2,1)S(1)} %get-tuple-element.41), channel_id=1, source_target_pairs={{0,2},{1,3},{2,0},{3,1},{4,6},{5,7},{6,4},{7,5},{8,10},{9,11},{10,... | collective-permute-start | bytes 393224 | tf_op jit(solution)/shard_map/ppermute | solution.py:374
  9.5 11.4 %collective-permute-start.5 = (bf16[8,32,256]{2,1,0:T(8,128)(2,1)S(1)}, bf16[8,32,256]{2,1,0:T(8,128)(2,1)S(1)}, u32[]{:S(2)}, u32[]{:S(2)}) collective-permute-start(bf16[8,32,256]{2,1,0:T(8,128)(2,1)S(1)} %get-tuple-element.42), channel_id=1, source_target_pairs={{0,3},{1,0},{2,1},{3,2},{4,7},{5,4},{6,5},{7,6},{8,11},{9,8},{10,9... | collective-permute-start | bytes 393224 | tf_op jit(solution)/shard_map/ppermute | solution.py:374
  13.4 9.0 %collective-permute-start.6 = (bf16[2,128,256]{2,1,0:T(8,128)(2,1)S(1)}, bf16[2,128,256]{2,1,0:T(8,128)(2,1)S(1)}, u32[]{:S(2)}, u32[]{:S(2)}) collective-permute-start(bf16[2,128,256]{2,1,0:T(8,128)(2,1)S(1)} %edge.1.after.rest_4_), channel_id=1, source_target_pairs={{0,1},{1,0},{3,7},{7,3},{4,5},{5,4},{6,10},{10,6},{8,9},{9,8},{11,... | collective-permute-start | bytes 393224 | tf_op jit(solution)/shard_map/ppermute | solution.py:403
  27.9 13.6 %collective-permute-start.8 = (bf16[272,256]{1,0:T(8,128)(2,1)S(1)}, bf16[272,256]{1,0:T(8,128)(2,1)S(1)}, u32[]{:S(2)}, u32[]{:S(2)}) collective-permute-start(bf16[272,256]{1,0:T(8,128)(2,1)S(1)} %get-tuple-element.57), channel_id=1, source_target_pairs={{0,2},{1,3},{2,0},{3,1},{4,6},{5,7},{6,4},{7,5},{8,10},{9,11},{10,... | collective-permute-start | bytes 417800 | tf_op jit(solution)/shard_map/ppermute | solution.py:374
  30.2 8.3 %collective-permute-start.7 = (bf16[256,256]{1,0:T(8,128)(2,1)S(1)}, bf16[256,256]{1,0:T(8,128)(2,1)S(1)}, u32[]{:S(2)}, u32[]{:S(2)}) collective-permute-start(bf16[256,256]{1,0:T(8,128)(2,1)S(1)} %get-tuple-element.56), channel_id=1, source_target_pairs={{0,1},{1,2},{2,3},{3,0},{4,5},{5,6},{6,7},{7,4},{8,9},{9,10},{10,1... | collective-permute-start | bytes 393224 | tf_op jit(solution)/shard_map/ppermute | solution.py:374
  32.3 9.2 %collective-permute-start.9 = (bf16[256,256]{1,0:T(8,128)(2,1)S(1)}, bf16[256,256]{1,0:T(8,128)(2,1)S(1)}, u32[]{:S(2)}, u32[]{:S(2)}) collective-permute-start(bf16[256,256]{1,0:T(8,128)(2,1)S(1)} %get-tuple-element.58), channel_id=1, source_target_pairs={{0,3},{1,0},{2,1},{3,2},{4,7},{5,4},{6,5},{7,6},{8,11},{9,8},{10,9... | collective-permute-start | bytes 393224 | tf_op jit(solution)/shard_map/ppermute | solution.py:374

commit v16 on v15

--- a/solution.py
+++ b/solution.py
@@ -435,16 +435,17 @@
         [pltpu.VMEM((rows + 2 * HALO, cols, chans), bf16), taps(rows + 2 * HALO), taps(rows + HALO)] + working(1),
     )
     moved = {first: around_by(results[first], first)}
-    rest = call(
-        functools.partial(rest_kernel, others),
-        "rest",
-        [result] * len(others),
-        [owner, counts],
-        held + [w_query, w_out],
-        working(len(others)),
-    )
-    for d, x in zip(others, rest):
-        moved[d] = around_by(x, d) if d else x
+    for name, group in (("rest", others[:-1]), ("own", others[-1:])):
+        parts = call(
+            functools.partial(rest_kernel, group),
+            name,
+            [result] * len(group),
+            [owner, counts],
+            held + [w_query, w_out],
+            working(len(group)),
+        )
+        for d, x in zip(group, parts):
+            moved[d] = around_by(x, d) if d else x
     slabs = [moved[d] for d in range(n)]
     scratch = [staging, block, block, pltpu.SemaphoreType.DMA((pieces,))]
     return call(store_kernel, "store", array(*fields.shape), [rotation], slabs, scratch, out_spec=hbm)

time: 43.5 us -> 44.2 us (1.016)
  starting transfers between devices: 17.3 us -> 16 us
  Pallas kernels: 13.8 us -> 15.1 us
  waiting for transfers between devices: 12 us -> 12.6 us
    pallas_call x6 -> x7, Pallas kernels: 13.8 us -> 15.1 us  [call(): pl.pallas_call(functools.partial(kernel, n, rows), out_shape=out, in_spec...]
    ppermute x1, waiting for transfers between devices: 1.48 us -> 2.27 us  [on_device(): received = lax.ppermute(sent, ('lat', 'lon'), pairs)]
    ppermute x9, starting transfers between devices: 14.8 us -> 14.1 us  [around_by(): return lax.ppermute(x, 'lon', [(i, (i + d) % n) for i in range(n)])]
    ppermute x1, starting transfers between devices: 2.48 us -> 1.92 us  [on_device(): received = lax.ppermute(sent, ('lat', 'lon'), pairs)]
  transfers between devices with their start and end apart: 10 -> 10, of which waited for: 5 -> 6; matrix products, arithmetic and copies ran while one was open for 0% -> 0% of each run, Pallas kernels for 11% -> 14%
where the time goes in v16:
time: 44.2 us; the launch traced here: 43.9 us
  starting transfers between devices  16 us (36%)
  Pallas kernels  15.1 us (34%)
  waiting for transfers between devices  12.6 us (29%)
    pallas_call x7, Pallas kernels, call(): pl.pallas_call(functools.partial(kernel, n, rows), out_shape=out, in_spec...  15.1 us
    ppermute x9, starting transfers between devices, around_by(): return lax.ppermute(x, 'lon', [(i, (i + d) % n) for i in range(n)])  14.1 us
    ppermute x9, waiting for transfers between devices, around_by(): return lax.ppermute(x, 'lon', [(i, (i + d) % n) for i in range(n)])  10.3 us
    ppermute x1, waiting for transfers between devices, on_device(): received = lax.ppermute(sent, ('lat', 'lon'), pairs)  2.27 us
    ppermute x1, starting transfers between devices, on_device(): received = lax.ppermute(sent, ('lat', 'lon'), pairs)  1.92 us
  transfers between devices with their start and end apart: 10, of which 6 were waited for; matrix products, arithmetic and copies ran while one was open for 0% of the time, Pallas kernels for 14%

profile of v16, /device:TPU:0, one launch (start us, length us, event | category | flops | bytes accessed | tf_op | source)
XLA Modules:
  0.0 43.9 jit_solution(11931411529698523231)
XLA Ops:
  0.0 1.9 %send.1 = (bf16[2,32,256]{2,1,0:T(8,128)(2,1)S(1)}, bf16[2,32,256]{2,1,0:T(8,128)(2,1)S(1)}, bf16[2,32,256]{2,1,0:T(8,128)(2,1)S(1)}, bf16[2,32,256]{2,1,0:T(8,1...) custom-call(s32[4,8]{1,0:T(4,128)} %bitcast.12, ...), custom_call_target="tpu_custom_call" | custom-call | tf_op jit(solution)/shard_map/send/pallas_call | solution.py:358
  1.9 3.1 %collective-permute-start = (bf16[2,32,256]{2,1,0:T(8,128)(2,1)S(1)}, bf16[2,32,256]{2,1,0:T(8,128)(2,1)S(1)}, u32[]{:S(2)}, u32[]{:S(2)}) collective-permute-start(bf16[2,32,256]{2,1,0:T(8,128)(2,1)S(1)} %get-tuple-element.34), channel_id=1, source_target_pairs={{0,1},{1,2},{2,3},{3,0},{4,5},{5,6},{6,7},{7,4},{8,9},{9,10},{10,1... | collective-permute-start | bytes 98312 | tf_op jit(solution)/shard_map/ppermute | solution.py:374
  5.0 2.6 %collective-permute-start.1 = (bf16[2,32,256]{2,1,0:T(8,128)(2,1)S(1)}, bf16[2,32,256]{2,1,0:T(8,128)(2,1)S(1)}, u32[]{:S(2)}, u32[]{:S(2)}) collective-permute-start(bf16[2,32,256]{2,1,0:T(8,128)(2,1)S(1)} %get-tuple-element.35), channel_id=1, source_target_pairs={{0,2},{1,3},{2,0},{3,1},{4,6},{5,7},{6,4},{7,5},{8,10},{9,11},{10,... | collective-permute-start | bytes 98312 | tf_op jit(solution)/shard_map/ppermute | solution.py:374
  7.6 0.7 %collective-permute-start.2 = (bf16[2,32,256]{2,1,0:T(8,128)(2,1)S(1)}, bf16[2,32,256]{2,1,0:T(8,128)(2,1)S(1)}, u32[]{:S(2)}, u32[]{:S(2)}) collective-permute-start(bf16[2,32,256]{2,1,0:T(8,128)(2,1)S(1)} %get-tuple-element.36), channel_id=1, source_target_pairs={{0,3},{1,0},{2,1},{3,2},{4,7},{5,4},{6,5},{7,6},{8,11},{9,8},{10,9... | collective-permute-start | bytes 98312 | tf_op jit(solution)/shard_map/ppermute | solution.py:374
  8.3 1.3 %collective-permute-start.3 = (bf16[8,32,256]{2,1,0:T(8,128)(2,1)S(1)}, bf16[8,32,256]{2,1,0:T(8,128)(2,1)S(1)}, u32[]{:S(2)}, u32[]{:S(2)}) collective-permute-start(bf16[8,32,256]{2,1,0:T(8,128)(2,1)S(1)} %get-tuple-element.39), channel_id=1, source_target_pairs={{0,1},{1,2},{2,3},{3,0},{4,5},{5,6},{6,7},{7,4},{8,9},{9,10},{10,1... | collective-permute-start | bytes 393224 | tf_op jit(solution)/shard_map/ppermute | solution.py:374
  9.6 0.3 collective-permute-start.4
  9.9 0.0 collective-permute-done.rest_1_
  9.9 2.2 %collective-permute-start.5 = (bf16[8,32,256]{2,1,0:T(8,128)(2,1)S(1)}, bf16[8,32,256]{2,1,0:T(8,128)(2,1)S(1)}, u32[]{:S(2)}, u32[]{:S(2)}) collective-permute-start(bf16[8,32,256]{2,1,0:T(8,128)(2,1)S(1)} %get-tuple-element.41), channel_id=1, source_target_pairs={{0,3},{1,0},{2,1},{3,2},{4,7},{5,4},{6,5},{7,6},{8,11},{9,8},{10,9... | collective-permute-start | bytes 393224 | tf_op jit(solution)/shard_map/ppermute | solution.py:374
  12.1 1.6 %collective-permute-done.2.rest_3_ = bf16[2,32,256]{2,1,0:T(8,128)(2,1)S(1)} collective-permute-done((bf16[2,32,256]{2,1,0:T(8,128)(2,1)S(1)}, bf16[2,32,256]{2,1,0:T(8,128)(2,1)S(1)}, u32[]{:S(2)}, u32[]{:S(2)}) %collective-permute-start.2) | collective-permute-done | bytes 32800 | tf_op jit(solution)/shard_map/ppermute | solution.py:374
  13.7 0.6 %edge.1.after.rest_4_ = bf16[2,128,256]{2,1,0:T(8,128)(2,1)S(1)} custom-call(s32[4,8]{1,0:T(4,128)S(1)} %get-tuple-element.32.owner, bf16[2,32,256]{2,1,0:T(8,128)(2,1)S(1)} %get-tuple-element.33.rest_0_, bf16[2,32,256]{2,1,0:T(8,128)(2,1)S(1)} %collective-permute-done.rest_1_, bf16[2,32,256]{2,1,0:T(8,128)(2,1)S(1)} %collective-permute-done.1.rest_2_, ...), custom_call_target="tpu_custom_call" | custom-call | tf_op jit(solution)/shard_map/edge/pallas_call | solution.py:358
  14.3 1.9 %collective-permute-start.6 = (bf16[2,128,256]{2,1,0:T(8,128)(2,1)S(1)}, bf16[2,128,256]{2,1,0:T(8,128)(2,1)S(1)}, u32[]{:S(2)}, u32[]{:S(2)}) collective-permute-start(bf16[2,128,256]{2,1,0:T(8,128)(2,1)S(1)} %edge.1.after.rest_4_), channel_id=1, source_target_pairs={{0,1},{1,0},{3,7},{7,3},{4,5},{5,4},{6,10},{10,6},{8,9},{9,8},{11,... | collective-permute-start | bytes 393224 | tf_op jit(solution)/shard_map/ppermute | solution.py:403
  16.3 1.9 %load.1 = (s32[256]{0:T(256)S(1)}, bf16[3,768,256]{2,1,0:T(8,128)(2,1)S(1)}, f32[1,256]{1,0:T(1,128)S(1)}, bf16[3,768,256]{2,1,0:T(8,128)(2,1)S(1)}, f32[1,256]{...) custom-call(bf16[2,128,256]{2,1,0:T(8,128)(2,1)S(1)} %edge.1.after.r, ...), custom_call_target="tpu_custom_call" | custom-call | tf_op jit(solution)/shard_map/load/pallas_call | solution.py:358
  18.2 2.2 %collective-permute-done.4.rest_2_ = bf16[8,32,256]{2,1,0:T(8,128)(2,1)S(1)} collective-permute-done((bf16[8,32,256]{2,1,0:T(8,128)(2,1)S(1)}, bf16[8,32,256]{2,1,0:T(8,128)(2,1)S(1)}, u32[]{:S(2)}, u32[]{:S(2)}) %collective-permute-start.4) | collective-permute-done | bytes 131104 | tf_op jit(solution)/shard_map/ppermute | solution.py:374
  20.3 0.1 collective-permute-done.5.rest_3_
  20.4 2.3 %collective-permute-done.6.rest_5_ = bf16[2,128,256]{2,1,0:T(8,128)(2,1)S(1)} collective-permute-done((bf16[2,128,256]{2,1,0:T(8,128)(2,1)S(1)}, bf16[2,128,256]{2,1,0:T(8,128)(2,1)S(1)}, u32[]{:S(2)}, u32[]{:S(2)}) %collective-permute-start.6) | collective-permute-done | bytes 131104 | tf_op jit(solution)/shard_map/ppermute | solution.py:403
  22.7 5.5 %main.1 = (bf16[272,256]{1,0:T(8,128)(2,1)S(1)}, bf16[1024,256]{1,0:T(8,128)(2,1)S(1)}, bf16[1024,256]{1,0:T(8,128)(2,1)S(1)}, bf16[1024,64]{1,0:T(8,128)(2,1)S(1)}, bf16[64,1024]{1,0:T(8,128)(2,1)S(1)}) custom-call(s32[4,8]{1,0:T(4,128)S(1)} %get-tuple-element.32.owner, s32[256]{0:T(256)S(1)} %get-tuple-element.37.counts, ...), custom_call_target="tpu_custom_call" | custom-call | tf_op jit(solution)/shard_map/main/pallas_call | solution.py:358
  28.2 0.1 collective-permute-start.8
  28.3 2.0 %rest.1 = (bf16[256,256]{1,0:T(8,128)(2,1)S(1)}, bf16[256,256]{1,0:T(8,128)(2,1)S(1)}) custom-call(s32[4,8]{1,0:T(4,128)S(1)} %get-tuple-element.32.owner, s32[256]{0:T(256)S(1)} %get-tuple-element.37.counts, bf16[1024,256]{1,0:T(8,128)(2,1)S(1)} %get-tuple-element.50.rest_0_, bf16[1024,256]{1,0:T(8,128)(2,1)S(1)} %get-tuple-element.51.rest_1_, ...), custom_call_target="tpu_custom_call" | custom-call | tf_op jit(solution)/shard_map/rest/pallas_call | solution.py:358
  30.3 1.7 %collective-permute-start.7 = (bf16[256,256]{1,0:T(8,128)(2,1)S(1)}, bf16[256,256]{1,0:T(8,128)(2,1)S(1)}, u32[]{:S(2)}, u32[]{:S(2)}) collective-permute-start(bf16[256,256]{1,0:T(8,128)(2,1)S(1)} %get-tuple-element.54), channel_id=1, source_target_pairs={{0,1},{1,2},{2,3},{3,0},{4,5},{5,6},{6,7},{7,4},{8,9},{9,10},{10,1... | collective-permute-start | bytes 393224 | tf_op jit(solution)/shard_map/ppermute | solution.py:374
  32.0 2.1 %collective-permute-start.9 = (bf16[256,256]{1,0:T(8,128)(2,1)S(1)}, bf16[256,256]{1,0:T(8,128)(2,1)S(1)}, u32[]{:S(2)}, u32[]{:S(2)}) collective-permute-start(bf16[256,256]{1,0:T(8,128)(2,1)S(1)} %get-tuple-element.56), channel_id=1, source_target_pairs={{0,3},{1,0},{2,1},{3,2},{4,7},{5,4},{6,5},{7,6},{8,11},{9,8},{10,9... | collective-permute-start | bytes 393224 | tf_op jit(solution)/shard_map/ppermute | solution.py:374
  34.2 1.6 %own.1.rest_0_ = bf16[256,256]{1,0:T(8,128)(2,1)S(1)} custom-call(s32[4,8]{1,0:T(4,128)S(1)} %get-tuple-element.32.owner, s32[256]{0:T(256)S(1)} %get-tuple-element.37.counts, bf16[1024,256]{1,0:T(8,128)(2,1)S(1)} %get-tuple-element.50.rest_0_, bf16[1024,256]{1,0:T(8,128)(2,1)S(1)} %get-tuple-element.51.rest_1_, ...), custom_call_target="tpu_custom_call" | custom-call | tf_op jit(solution)/shard_map/own/pallas_call | solution.py:358
  35.7 2.8 %collective-permute-done.7.rest_1_ = bf16[256,256]{1,0:T(8,128)(2,1)S(1)} collective-permute-done((bf16[256,256]{1,0:T(8,128)(2,1)S(1)}, bf16[256,256]{1,0:T(8,128)(2,1)S(1)}, u32[]{:S(2)}, u32[]{:S(2)}) %collective-permute-start.7) | collective-permute-done | bytes 131104 | tf_op jit(solution)/shard_map/ppermute | solution.py:374
  38.6 3.6 %collective-permute-done.9.rest_3_ = bf16[256,256]{1,0:T(8,128)(2,1)S(1)} collective-permute-done((bf16[256,256]{1,0:T(8,128)(2,1)S(1)}, bf16[256,256]{1,0:T(8,128)(2,1)S(1)}, u32[]{:S(2)}, u32[]{:S(2)}) %collective-permute-start.9) | collective-permute-done | bytes 131104 | tf_op jit(solution)/shard_map/ppermute | solution.py:374
  42.2 1.7 %store.1 = bf16[32,32,256]{2,1,0:T(8,128)(2,1)} custom-call(s32[4,8]{1,0:T(4,128)S(1)} %get-tuple-element.31.rotation, bf16[256,256]{1,0:T(8,128)(2,1)S(1)} %own.1.rest_0_, bf16[256,256]{1,0:T(8,128)(2,1)S(1)} %collective-permute-done.7.rest_1_, bf16[272,256]{1,0:T(8,128)(2,1)S(1)} %collective-permute-done.8.rest_2_, ...), custom_call_target="tpu_custom_call" | custom-call | tf_op jit(solution)/shard_map/store/pallas_call | solution.py:358
  (3 shorter events, 0.0 us)
Async XLA Ops:
  1.9 8.0 %collective-permute-start = (bf16[2,32,256]{2,1,0:T(8,128)(2,1)S(1)}, bf16[2,32,256]{2,1,0:T(8,128)(2,1)S(1)}, u32[]{:S(2)}, u32[]{:S(2)}) collective-permute-start(bf16[2,32,256]{2,1,0:T(8,128)(2,1)S(1)} %get-tuple-element.34), channel_id=1, source_target_pairs={{0,1},{1,2},{2,3},{3,0},{4,5},{5,6},{6,7},{7,4},{8,9},{9,10},{10,1... | collective-permute-start | bytes 98312 | tf_op jit(solution)/shard_map/ppermute | solution.py:374
  5.0 7.1 %collective-permute-start.1 = (bf16[2,32,256]{2,1,0:T(8,128)(2,1)S(1)}, bf16[2,32,256]{2,1,0:T(8,128)(2,1)S(1)}, u32[]{:S(2)}, u32[]{:S(2)}) collective-permute-start(bf16[2,32,256]{2,1,0:T(8,128)(2,1)S(1)} %get-tuple-element.35), channel_id=1, source_target_pairs={{0,2},{1,3},{2,0},{3,1},{4,6},{5,7},{6,4},{7,5},{8,10},{9,11},{10,... | collective-permute-start | bytes 98312 | tf_op jit(solution)/shard_map/ppermute | solution.py:374
  7.6 6.2 %collective-permute-start.2 = (bf16[2,32,256]{2,1,0:T(8,128)(2,1)S(1)}, bf16[2,32,256]{2,1,0:T(8,128)(2,1)S(1)}, u32[]{:S(2)}, u32[]{:S(2)}) collective-permute-start(bf16[2,32,256]{2,1,0:T(8,128)(2,1)S(1)} %get-tuple-element.36), channel_id=1, source_target_pairs={{0,3},{1,0},{2,1},{3,2},{4,7},{5,4},{6,5},{7,6},{8,11},{9,8},{10,9... | collective-permute-start | bytes 98312 | tf_op jit(solution)/shard_map/ppermute | solution.py:374
  8.3 9.9 %collective-permute-start.3 = (bf16[8,32,256]{2,1,0:T(8,128)(2,1)S(1)}, bf16[8,32,256]{2,1,0:T(8,128)(2,1)S(1)}, u32[]{:S(2)}, u32[]{:S(2)}) collective-permute-start(bf16[8,32,256]{2,1,0:T(8,128)(2,1)S(1)} %get-tuple-element.39), channel_id=1, source_target_pairs={{0,1},{1,2},{2,3},{3,0},{4,5},{5,6},{6,7},{7,4},{8,9},{9,10},{10,1... | collective-permute-start | bytes 393224 | tf_op jit(solution)/shard_map/ppermute | solution.py:374
  9.6 10.7 %collective-permute-start.4 = (bf16[8,32,256]{2,1,0:T(8,128)(2,1)S(1)}, bf16[8,32,256]{2,1,0:T(8,128)(2,1)S(1)}, u32[]{:S(2)}, u32[]{:S(2)}) collective-permute-start(bf16[8,32,256]{2,1,0:T(8,128)(2,1)S(1)} %get-tuple-element.40), channel_id=1, source_target_pairs={{0,2},{1,3},{2,0},{3,1},{4,6},{5,7},{6,4},{7,5},{8,10},{9,11},{10,... | collective-permute-start | bytes 393224 | tf_op jit(solution)/shard_map/ppermute | solution.py:374
  9.9 10.5 %collective-permute-start.5 = (bf16[8,32,256]{2,1,0:T(8,128)(2,1)S(1)}, bf16[8,32,256]{2,1,0:T(8,128)(2,1)S(1)}, u32[]{:S(2)}, u32[]{:S(2)}) collective-permute-start(bf16[8,32,256]{2,1,0:T(8,128)(2,1)S(1)} %get-tuple-element.41), channel_id=1, source_target_pairs={{0,3},{1,0},{2,1},{3,2},{4,7},{5,4},{6,5},{7,6},{8,11},{9,8},{10,9... | collective-permute-start | bytes 393224 | tf_op jit(solution)/shard_map/ppermute | solution.py:374
  14.3 8.4 %collective-permute-start.6 = (bf16[2,128,256]{2,1,0:T(8,128)(2,1)S(1)}, bf16[2,128,256]{2,1,0:T(8,128)(2,1)S(1)}, u32[]{:S(2)}, u32[]{:S(2)}) collective-permute-start(bf16[2,128,256]{2,1,0:T(8,128)(2,1)S(1)} %edge.1.after.rest_4_), channel_id=1, source_target_pairs={{0,1},{1,0},{3,7},{7,3},{4,5},{5,4},{6,10},{10,6},{8,9},{9,8},{11,... | collective-permute-start | bytes 393224 | tf_op jit(solution)/shard_map/ppermute | solution.py:403
  28.2 14.0 %collective-permute-start.8 = (bf16[272,256]{1,0:T(8,128)(2,1)S(1)}, bf16[272,256]{1,0:T(8,128)(2,1)S(1)}, u32[]{:S(2)}, u32[]{:S(2)}) collective-permute-start(bf16[272,256]{1,0:T(8,128)(2,1)S(1)} %get-tuple-element.55), channel_id=1, source_target_pairs={{0,2},{1,3},{2,0},{3,1},{4,6},{5,7},{6,4},{7,5},{8,10},{9,11},{10,... | collective-permute-start | bytes 417800 | tf_op jit(solution)/shard_map/ppermute | solution.py:374
  30.3 8.3 %collective-permute-start.7 = (bf16[256,256]{1,0:T(8,128)(2,1)S(1)}, bf16[256,256]{1,0:T(8,128)(2,1)S(1)}, u32[]{:S(2)}, u32[]{:S(2)}) collective-permute-start(bf16[256,256]{1,0:T(8,128)(2,1)S(1)} %get-tuple-element.54), channel_id=1, source_target_pairs={{0,1},{1,2},{2,3},{3,0},{4,5},{5,6},{6,7},{7,4},{8,9},{9,10},{10,1... | collective-permute-start | bytes 393224 | tf_op jit(solution)/shard_map/ppermute | solution.py:374
  32.0 10.1 %collective-permute-start.9 = (bf16[256,256]{1,0:T(8,128)(2,1)S(1)}, bf16[256,256]{1,0:T(8,128)(2,1)S(1)}, u32[]{:S(2)}, u32[]{:S(2)}) collective-permute-start(bf16[256,256]{1,0:T(8,128)(2,1)S(1)} %get-tuple-element.56), channel_id=1, source_target_pairs={{0,3},{1,0},{2,1},{3,2},{4,7},{5,4},{6,5},{7,6},{8,11},{9,8},{10,9... | collective-permute-start | bytes 393224 | tf_op jit(solution)/shard_map/ppermute | solution.py:374

commit v17 on v16

--- a/solution.py
+++ b/solution.py
@@ -368,7 +368,7 @@
     def array(*shape):
         return jax.ShapeDtypeStruct(shape, bf16)
 
-    order = sorted(range(1, n), key=lambda d: -min(d, n - d))
+    order = sorted(range(1, n), key=lambda d: (-min(d, n - d), -d))
 
     def around_by(x, d):
         return lax.ppermute(x, "lon", [(i, (i + d) % n) for i in range(n)])

time: 44.2 us -> 43.7 us (0.989)
  waiting for transfers between devices: 12.6 us -> 10.6 us
  starting transfers between devices: 16 us -> 17.3 us
    ppermute x9, waiting for transfers between devices: 10.3 us -> 9.07 us  [around_by(): return lax.ppermute(x, 'lon', [(i, (i + d) % n) for i in range(n)])]
    ppermute x1, waiting for transfers between devices: 2.27 us -> 1.5 us  [on_device(): received = lax.ppermute(sent, ('lat', 'lon'), pairs)]
    ppermute x9, starting transfers between devices: 14.1 us -> 14.8 us  [around_by(): return lax.ppermute(x, 'lon', [(i, (i + d) % n) for i in range(n)])]
    ppermute x1, starting transfers between devices: 1.92 us -> 2.48 us  [on_device(): received = lax.ppermute(sent, ('lat', 'lon'), pairs)]
  transfers between devices with their start and end apart: 10 -> 10, of which waited for: 6 -> 5; matrix products, arithmetic and copies ran while one was open for 0% -> 0% of each run, Pallas kernels for 14% -> 14%
where the time goes in v17:
time: 43.7 us; the launch traced here: 43 us
  starting transfers between devices  17.3 us (40%)
  Pallas kernels  15.1 us (35%)
  waiting for transfers between devices  10.6 us (24%)
    pallas_call x7, Pallas kernels, call(): pl.pallas_call(functools.partial(kernel, n, rows), out_shape=out, in_spec...  15.1 us
    ppermute x9, starting transfers between devices, around_by(): return lax.ppermute(x, 'lon', [(i, (i + d) % n) for i in range(n)])  14.8 us
    ppermute x9, waiting for transfers between devices, around_by(): return lax.ppermute(x, 'lon', [(i, (i + d) % n) for i in range(n)])  9.07 us
    ppermute x1, starting transfers between devices, on_device(): received = lax.ppermute(sent, ('lat', 'lon'), pairs)  2.48 us
    ppermute x1, waiting for transfers between devices, on_device(): received = lax.ppermute(sent, ('lat', 'lon'), pairs)  1.5 us
  transfers between devices with their start and end apart: 10, of which 5 were waited for; matrix products, arithmetic and copies ran while one was open for 0% of the time, Pallas kernels for 14%

profile of v17, /device:TPU:0, one launch (start us, length us, event | category | flops | bytes accessed | tf_op | source)
XLA Modules:
  0.0 43.0 jit_solution(1693878731865491623)
XLA Ops:
  0.0 1.9 %send.1 = (bf16[2,32,256]{2,1,0:T(8,128)(2,1)S(1)}, bf16[2,32,256]{2,1,0:T(8,128)(2,1)S(1)}, bf16[2,32,256]{2,1,0:T(8,128)(2,1)S(1)}, bf16[2,32,256]{2,1,0:T(8,1...) custom-call(s32[4,8]{1,0:T(4,128)} %bitcast.12, ...), custom_call_target="tpu_custom_call" | custom-call | tf_op jit(solution)/shard_map/send/pallas_call | solution.py:358
  1.9 3.1 %collective-permute-start = (bf16[2,32,256]{2,1,0:T(8,128)(2,1)S(1)}, bf16[2,32,256]{2,1,0:T(8,128)(2,1)S(1)}, u32[]{:S(2)}, u32[]{:S(2)}) collective-permute-start(bf16[2,32,256]{2,1,0:T(8,128)(2,1)S(1)} %get-tuple-element.34), channel_id=1, source_target_pairs={{0,1},{1,2},{2,3},{3,0},{4,5},{5,6},{6,7},{7,4},{8,9},{9,10},{10,1... | collective-permute-start | bytes 98312 | tf_op jit(solution)/shard_map/ppermute | solution.py:374
  5.0 2.6 %collective-permute-start.1 = (bf16[2,32,256]{2,1,0:T(8,128)(2,1)S(1)}, bf16[2,32,256]{2,1,0:T(8,128)(2,1)S(1)}, u32[]{:S(2)}, u32[]{:S(2)}) collective-permute-start(bf16[2,32,256]{2,1,0:T(8,128)(2,1)S(1)} %get-tuple-element.35), channel_id=1, source_target_pairs={{0,2},{1,3},{2,0},{3,1},{4,6},{5,7},{6,4},{7,5},{8,10},{9,11},{10,... | collective-permute-start | bytes 98312 | tf_op jit(solution)/shard_map/ppermute | solution.py:374
  7.6 1.3 %collective-permute-start.2 = (bf16[2,32,256]{2,1,0:T(8,128)(2,1)S(1)}, bf16[2,32,256]{2,1,0:T(8,128)(2,1)S(1)}, u32[]{:S(2)}, u32[]{:S(2)}) collective-permute-start(bf16[2,32,256]{2,1,0:T(8,128)(2,1)S(1)} %get-tuple-element.36), channel_id=1, source_target_pairs={{0,3},{1,0},{2,1},{3,2},{4,7},{5,4},{6,5},{7,6},{8,11},{9,8},{10,9... | collective-permute-start | bytes 98312 | tf_op jit(solution)/shard_map/ppermute | solution.py:374
  8.9 0.7 %collective-permute-start.3 = (bf16[8,32,256]{2,1,0:T(8,128)(2,1)S(1)}, bf16[8,32,256]{2,1,0:T(8,128)(2,1)S(1)}, u32[]{:S(2)}, u32[]{:S(2)}) collective-permute-start(bf16[8,32,256]{2,1,0:T(8,128)(2,1)S(1)} %get-tuple-element.39), channel_id=1, source_target_pairs={{0,1},{1,2},{2,3},{3,0},{4,5},{5,6},{6,7},{7,4},{8,9},{9,10},{10,1... | collective-permute-start | bytes 393224 | tf_op jit(solution)/shard_map/ppermute | solution.py:374
  9.6 0.3 collective-permute-start.4
  9.9 2.8 %collective-permute-start.5 = (bf16[8,32,256]{2,1,0:T(8,128)(2,1)S(1)}, bf16[8,32,256]{2,1,0:T(8,128)(2,1)S(1)}, u32[]{:S(2)}, u32[]{:S(2)}) collective-permute-start(bf16[8,32,256]{2,1,0:T(8,128)(2,1)S(1)} %get-tuple-element.41), channel_id=1, source_target_pairs={{0,3},{1,0},{2,1},{3,2},{4,7},{5,4},{6,5},{7,6},{8,11},{9,8},{10,9... | collective-permute-start | bytes 393224 | tf_op jit(solution)/shard_map/ppermute | solution.py:374
  12.8 0.0 collective-permute-done.1.rest_2_
  12.8 0.0 collective-permute-done.2.rest_3_
  12.8 0.6 %edge.1.after.rest_4_ = bf16[2,128,256]{2,1,0:T(8,128)(2,1)S(1)} custom-call(s32[4,8]{1,0:T(4,128)S(1)} %get-tuple-element.32.owner, bf16[2,32,256]{2,1,0:T(8,128)(2,1)S(1)} %get-tuple-element.33.rest_0_, bf16[2,32,256]{2,1,0:T(8,128)(2,1)S(1)} %collective-permute-done.rest_1_, bf16[2,32,256]{2,1,0:T(8,128)(2,1)S(1)} %collective-permute-done.1.rest_2_, ...), custom_call_target="tpu_custom_call" | custom-call | tf_op jit(solution)/shard_map/edge/pallas_call | solution.py:358
  13.4 2.5 %collective-permute-start.6 = (bf16[2,128,256]{2,1,0:T(8,128)(2,1)S(1)}, bf16[2,128,256]{2,1,0:T(8,128)(2,1)S(1)}, u32[]{:S(2)}, u32[]{:S(2)}) collective-permute-start(bf16[2,128,256]{2,1,0:T(8,128)(2,1)S(1)} %edge.1.after.rest_4_), channel_id=1, source_target_pairs={{0,1},{1,0},{3,7},{7,3},{4,5},{5,4},{6,10},{10,6},{8,9},{9,8},{11,... | collective-permute-start | bytes 393224 | tf_op jit(solution)/shard_map/ppermute | solution.py:403
  15.8 1.9 %load.1 = (s32[256]{0:T(256)S(1)}, bf16[3,768,256]{2,1,0:T(8,128)(2,1)S(1)}, f32[1,256]{1,0:T(1,128)S(1)}, bf16[3,768,256]{2,1,0:T(8,128)(2,1)S(1)}, f32[1,256]{...) custom-call(bf16[2,128,256]{2,1,0:T(8,128)(2,1)S(1)} %edge.1.after.r, ...), custom_call_target="tpu_custom_call" | custom-call | tf_op jit(solution)/shard_map/load/pallas_call | solution.py:358
  17.8 2.7 %collective-permute-done.4.rest_2_ = bf16[8,32,256]{2,1,0:T(8,128)(2,1)S(1)} collective-permute-done((bf16[8,32,256]{2,1,0:T(8,128)(2,1)S(1)}, bf16[8,32,256]{2,1,0:T(8,128)(2,1)S(1)}, u32[]{:S(2)}, u32[]{:S(2)}) %collective-permute-start.4) | collective-permute-done | bytes 131104 | tf_op jit(solution)/shard_map/ppermute | solution.py:374
  20.5 1.1 %collective-permute-done.5.rest_3_ = bf16[8,32,256]{2,1,0:T(8,128)(2,1)S(1)} collective-permute-done((bf16[8,32,256]{2,1,0:T(8,128)(2,1)S(1)}, bf16[8,32,256]{2,1,0:T(8,128)(2,1)S(1)}, u32[]{:S(2)}, u32[]{:S(2)}) %collective-permute-start.5) | collective-permute-done | bytes 131104 | tf_op jit(solution)/shard_map/ppermute | solution.py:374
  21.5 1.5 %collective-permute-done.6.rest_5_ = bf16[2,128,256]{2,1,0:T(8,128)(2,1)S(1)} collective-permute-done((bf16[2,128,256]{2,1,0:T(8,128)(2,1)S(1)}, bf16[2,128,256]{2,1,0:T(8,128)(2,1)S(1)}, u32[]{:S(2)}, u32[]{:S(2)}) %collective-permute-start.6) | collective-permute-done | bytes 131104 | tf_op jit(solution)/shard_map/ppermute | solution.py:403
  23.0 5.5 %main.1 = (bf16[272,256]{1,0:T(8,128)(2,1)S(1)}, bf16[1024,256]{1,0:T(8,128)(2,1)S(1)}, bf16[1024,256]{1,0:T(8,128)(2,1)S(1)}, bf16[1024,64]{1,0:T(8,128)(2,1)S(1)}, bf16[64,1024]{1,0:T(8,128)(2,1)S(1)}) custom-call(s32[4,8]{1,0:T(4,128)S(1)} %get-tuple-element.32.owner, s32[256]{0:T(256)S(1)} %get-tuple-element.37.counts, ...), custom_call_target="tpu_custom_call" | custom-call | tf_op jit(solution)/shard_map/main/pallas_call | solution.py:358
  28.5 0.1 collective-permute-start.8
  28.6 2.0 %rest.1 = (bf16[256,256]{1,0:T(8,128)(2,1)S(1)}, bf16[256,256]{1,0:T(8,128)(2,1)S(1)}) custom-call(s32[4,8]{1,0:T(4,128)S(1)} %get-tuple-element.32.owner, s32[256]{0:T(256)S(1)} %get-tuple-element.37.counts, bf16[1024,256]{1,0:T(8,128)(2,1)S(1)} %get-tuple-element.50.rest_0_, bf16[1024,256]{1,0:T(8,128)(2,1)S(1)} %get-tuple-element.51.rest_1_, ...), custom_call_target="tpu_custom_call" | custom-call | tf_op jit(solution)/shard_map/rest/pallas_call | solution.py:358
  30.6 2.1 %collective-permute-start.7 = (bf16[256,256]{1,0:T(8,128)(2,1)S(1)}, bf16[256,256]{1,0:T(8,128)(2,1)S(1)}, u32[]{:S(2)}, u32[]{:S(2)}) collective-permute-start(bf16[256,256]{1,0:T(8,128)(2,1)S(1)} %get-tuple-element.54), channel_id=1, source_target_pairs={{0,1},{1,2},{2,3},{3,0},{4,5},{5,6},{6,7},{7,4},{8,9},{9,10},{10,1... | collective-permute-start | bytes 393224 | tf_op jit(solution)/shard_map/ppermute | solution.py:374
  32.7 1.8 %collective-permute-start.9 = (bf16[256,256]{1,0:T(8,128)(2,1)S(1)}, bf16[256,256]{1,0:T(8,128)(2,1)S(1)}, u32[]{:S(2)}, u32[]{:S(2)}) collective-permute-start(bf16[256,256]{1,0:T(8,128)(2,1)S(1)} %get-tuple-element.56), channel_id=1, source_target_pairs={{0,3},{1,0},{2,1},{3,2},{4,7},{5,4},{6,5},{7,6},{8,11},{9,8},{10,9... | collective-permute-start | bytes 393224 | tf_op jit(solution)/shard_map/ppermute | solution.py:374
  34.5 1.6 %own.1.rest_0_ = bf16[256,256]{1,0:T(8,128)(2,1)S(1)} custom-call(s32[4,8]{1,0:T(4,128)S(1)} %get-tuple-element.32.owner, s32[256]{0:T(256)S(1)} %get-tuple-element.37.counts, bf16[1024,256]{1,0:T(8,128)(2,1)S(1)} %get-tuple-element.50.rest_0_, bf16[1024,256]{1,0:T(8,128)(2,1)S(1)} %get-tuple-element.51.rest_1_, ...), custom_call_target="tpu_custom_call" | custom-call | tf_op jit(solution)/shard_map/own/pallas_call | solution.py:358
  36.1 2.8 %collective-permute-done.7.rest_1_ = bf16[256,256]{1,0:T(8,128)(2,1)S(1)} collective-permute-done((bf16[256,256]{1,0:T(8,128)(2,1)S(1)}, bf16[256,256]{1,0:T(8,128)(2,1)S(1)}, u32[]{:S(2)}, u32[]{:S(2)}) %collective-permute-start.7) | collective-permute-done | bytes 131104 | tf_op jit(solution)/shard_map/ppermute | solution.py:374
  38.9 2.5 %collective-permute-done.9.rest_3_ = bf16[256,256]{1,0:T(8,128)(2,1)S(1)} collective-permute-done((bf16[256,256]{1,0:T(8,128)(2,1)S(1)}, bf16[256,256]{1,0:T(8,128)(2,1)S(1)}, u32[]{:S(2)}, u32[]{:S(2)}) %collective-permute-start.9) | collective-permute-done | bytes 131104 | tf_op jit(solution)/shard_map/ppermute | solution.py:374
  41.3 1.7 %store.1 = bf16[32,32,256]{2,1,0:T(8,128)(2,1)} custom-call(s32[4,8]{1,0:T(4,128)S(1)} %get-tuple-element.31.rotation, bf16[256,256]{1,0:T(8,128)(2,1)S(1)} %own.1.rest_0_, bf16[256,256]{1,0:T(8,128)(2,1)S(1)} %collective-permute-done.7.rest_1_, bf16[272,256]{1,0:T(8,128)(2,1)S(1)} %collective-permute-done.8.rest_2_, ...), custom_call_target="tpu_custom_call" | custom-call | tf_op jit(solution)/shard_map/store/pallas_call | solution.py:358
  (3 shorter events, 0.0 us)
Async XLA Ops:
  1.9 8.0 %collective-permute-start = (bf16[2,32,256]{2,1,0:T(8,128)(2,1)S(1)}, bf16[2,32,256]{2,1,0:T(8,128)(2,1)S(1)}, u32[]{:S(2)}, u32[]{:S(2)}) collective-permute-start(bf16[2,32,256]{2,1,0:T(8,128)(2,1)S(1)} %get-tuple-element.34), channel_id=1, source_target_pairs={{0,1},{1,2},{2,3},{3,0},{4,5},{5,6},{6,7},{7,4},{8,9},{9,10},{10,1... | collective-permute-start | bytes 98312 | tf_op jit(solution)/shard_map/ppermute | solution.py:374
  5.0 7.8 %collective-permute-start.1 = (bf16[2,32,256]{2,1,0:T(8,128)(2,1)S(1)}, bf16[2,32,256]{2,1,0:T(8,128)(2,1)S(1)}, u32[]{:S(2)}, u32[]{:S(2)}) collective-permute-start(bf16[2,32,256]{2,1,0:T(8,128)(2,1)S(1)} %get-tuple-element.35), channel_id=1, source_target_pairs={{0,2},{1,3},{2,0},{3,1},{4,6},{5,7},{6,4},{7,5},{8,10},{9,11},{10,... | collective-permute-start | bytes 98312 | tf_op jit(solution)/shard_map/ppermute | solution.py:374
  7.6 5.2 %collective-permute-start.2 = (bf16[2,32,256]{2,1,0:T(8,128)(2,1)S(1)}, bf16[2,32,256]{2,1,0:T(8,128)(2,1)S(1)}, u32[]{:S(2)}, u32[]{:S(2)}) collective-permute-start(bf16[2,32,256]{2,1,0:T(8,128)(2,1)S(1)} %get-tuple-element.36), channel_id=1, source_target_pairs={{0,3},{1,0},{2,1},{3,2},{4,7},{5,4},{6,5},{7,6},{8,11},{9,8},{10,9... | collective-permute-start | bytes 98312 | tf_op jit(solution)/shard_map/ppermute | solution.py:374
  8.9 8.8 %collective-permute-start.3 = (bf16[8,32,256]{2,1,0:T(8,128)(2,1)S(1)}, bf16[8,32,256]{2,1,0:T(8,128)(2,1)S(1)}, u32[]{:S(2)}, u32[]{:S(2)}) collective-permute-start(bf16[8,32,256]{2,1,0:T(8,128)(2,1)S(1)} %get-tuple-element.39), channel_id=1, source_target_pairs={{0,1},{1,2},{2,3},{3,0},{4,5},{5,6},{6,7},{7,4},{8,9},{9,10},{10,1... | collective-permute-start | bytes 393224 | tf_op jit(solution)/shard_map/ppermute | solution.py:374
  9.6 10.9 %collective-permute-start.4 = (bf16[8,32,256]{2,1,0:T(8,128)(2,1)S(1)}, bf16[8,32,256]{2,1,0:T(8,128)(2,1)S(1)}, u32[]{:S(2)}, u32[]{:S(2)}) collective-permute-start(bf16[8,32,256]{2,1,0:T(8,128)(2,1)S(1)} %get-tuple-element.40), channel_id=1, source_target_pairs={{0,2},{1,3},{2,0},{3,1},{4,6},{5,7},{6,4},{7,5},{8,10},{9,11},{10,... | collective-permute-start | bytes 393224 | tf_op jit(solution)/shard_map/ppermute | solution.py:374
  9.9 11.6 %collective-permute-start.5 = (bf16[8,32,256]{2,1,0:T(8,128)(2,1)S(1)}, bf16[8,32,256]{2,1,0:T(8,128)(2,1)S(1)}, u32[]{:S(2)}, u32[]{:S(2)}) collective-permute-start(bf16[8,32,256]{2,1,0:T(8,128)(2,1)S(1)} %get-tuple-element.41), channel_id=1, source_target_pairs={{0,3},{1,0},{2,1},{3,2},{4,7},{5,4},{6,5},{7,6},{8,11},{9,8},{10,9... | collective-permute-start | bytes 393224 | tf_op jit(solution)/shard_map/ppermute | solution.py:374
  13.4 9.7 %collective-permute-start.6 = (bf16[2,128,256]{2,1,0:T(8,128)(2,1)S(1)}, bf16[2,128,256]{2,1,0:T(8,128)(2,1)S(1)}, u32[]{:S(2)}, u32[]{:S(2)}) collective-permute-start(bf16[2,128,256]{2,1,0:T(8,128)(2,1)S(1)} %edge.1.after.rest_4_), channel_id=1, source_target_pairs={{0,1},{1,0},{3,7},{7,3},{4,5},{5,4},{6,10},{10,6},{8,9},{9,8},{11,... | collective-permute-start | bytes 393224 | tf_op jit(solution)/shard_map/ppermute | solution.py:403
  28.5 12.8 %collective-permute-start.8 = (bf16[272,256]{1,0:T(8,128)(2,1)S(1)}, bf16[272,256]{1,0:T(8,128)(2,1)S(1)}, u32[]{:S(2)}, u32[]{:S(2)}) collective-permute-start(bf16[272,256]{1,0:T(8,128)(2,1)S(1)} %get-tuple-element.55), channel_id=1, source_target_pairs={{0,2},{1,3},{2,0},{3,1},{4,6},{5,7},{6,4},{7,5},{8,10},{9,11},{10,... | collective-permute-start | bytes 417800 | tf_op jit(solution)/shard_map/ppermute | solution.py:374
  30.6 8.3 %collective-permute-start.7 = (bf16[256,256]{1,0:T(8,128)(2,1)S(1)}, bf16[256,256]{1,0:T(8,128)(2,1)S(1)}, u32[]{:S(2)}, u32[]{:S(2)}) collective-permute-start(bf16[256,256]{1,0:T(8,128)(2,1)S(1)} %get-tuple-element.54), channel_id=1, source_target_pairs={{0,1},{1,2},{2,3},{3,0},{4,5},{5,6},{6,7},{7,4},{8,9},{9,10},{10,1... | collective-permute-start | bytes 393224 | tf_op jit(solution)/shard_map/ppermute | solution.py:374
  32.7 8.7 %collective-permute-start.9 = (bf16[256,256]{1,0:T(8,128)(2,1)S(1)}, bf16[256,256]{1,0:T(8,128)(2,1)S(1)}, u32[]{:S(2)}, u32[]{:S(2)}) collective-permute-start(bf16[256,256]{1,0:T(8,128)(2,1)S(1)} %get-tuple-element.56), channel_id=1, source_target_pairs={{0,3},{1,0},{2,1},{3,2},{4,7},{5,4},{6,5},{7,6},{8,11},{9,8},{10,9... | collective-permute-start | bytes 393224 | tf_op jit(solution)/shard_map/ppermute | solution.py:374
